TPU v7x, 32 devices: a whole 2x2x4 slice. The times are simulated.
32 devices in a mesh: gx: 2 (over y), gy: 8 (over z, core), gz: 2 (over x).
Axes of the slice: x: 2, y: 2, z: 4, core: 2. Of those that a mesh axis runs over, the one named last changes fastest.
Arguments:
- velocity: float32 [3, 256, 256, 256], P(None, 'gx', 'gy', 'gz'), may hold values from -6 to 6
- adjoint_seed: float32 [3, 256, 256, 256], P(None, 'gx', 'gy', 'gz'), may hold values from -6 to 6
- susceptibility: float32 [256, 256, 256], P('gx', 'gy', 'gz'), may hold values from 0.5 to 4
- remanence: float32 [256, 256, 256], P('gx', 'gy', 'gz'), may hold values from 0.2 to 1.5
- region_bounds: int32 [2, 3], replicated, may hold values from 0 to 128, as said below
- step_id: int32 [1], replicated, may hold values from 0 to 999
Outputs:
- next_velocity: float32 [3, 256, 256, 256], P(None, 'gx', 'gy', 'gz')
- velocity_adjoint: float32 [3, 256, 256, 256], P(None, 'gx', 'gy', 'gz')
- design_gradient: float32 [256, 256, 256], P('gx', 'gy', 'gz')
Inputs may be any that keep to these rules, and one draw needn't show every extreme that they name: Along every dimension the design region is nonempty and lies in the lower half of the box: region_bounds[0, d] < region_bounds[1, d] <= half the cells along d.
All inputs are finite; a program needn't handle non-finite values.
Results may differ from a plain program's by a relative error of at most 0.000096.
Values sent between devices are 32-bit elements; how exact they have to be, the bound alone decides.
No kernel may reach another device: no remote copies, remote signals or barrier semaphores. Data moves between devices by JAX's collectives and lax.ppermute only.
A program may use at most 320 MiB of HBM per device.

v0:
```python
import jax
import jax.numpy as jnp
from jax import lax
from jax.sharding import PartitionSpec as P

NX = 256
NY = 256
NZ = 256


time_step = 0.5
viscosity = 0.2
field_period = 24
full_turn = 6.283185307179586
highest = lax.Precision.HIGHEST


def passed_along(array, axis, by):
    peers = lax.axis_size(axis)
    pairs = [(i, i + by) for i in range(peers) if 0 <= i + by < peers]
    return lax.ppermute(array, axis, pairs)


def padded_2(block, sides, width):
    for axis, dim in sides:
        count = lax.axis_size(axis)
        forward = [(i, i + 1) for i in range(count - 1)]
        backward = [(target, source) for source, target in forward]
        low = lax.ppermute(
            lax.slice_in_dim(block, block.shape[dim] - width, None, axis=dim), axis, forward
        )
        high = lax.ppermute(lax.slice_in_dim(block, 0, width, axis=dim), axis, backward)
        block = jnp.concatenate([low, block, high], axis=dim)
    return block


def phase_tables(row_index, col_index, length):
    phase_turns = row_index[:, None] * col_index[None, :] % length
    phase_angle = full_turn * phase_turns.astype(jnp.float32) / length
    return (jnp.cos(phase_angle), jnp.sin(phase_angle))


def folded_index(cell_index, length):
    return jnp.where(cell_index < length // 2, cell_index, cell_index - length)


def arrival_order(length):
    position = jnp.arange(length, dtype=jnp.int32)
    return position


def depth_sum(partial_term):
    return lax.psum_scatter(partial_term, "gz", scatter_dimension=3, tiled=True)


def column_turn(real_part, imag_part):
    return (
        lax.all_to_all(real_part, "gy", split_axis=1, concat_axis=2, tiled=True),
        lax.all_to_all(imag_part, "gy", split_axis=1, concat_axis=2, tiled=True),
    )


def row_turn(real_part, imag_part):
    return (
        lax.all_to_all(real_part, ("gx", "gy"), split_axis=2, concat_axis=1, tiled=True),
        lax.all_to_all(imag_part, ("gx", "gy"), split_axis=2, concat_axis=1, tiled=True),
    )


def rotate(real_part, imag_part, cosine, sine, form, direction):
    real_cos = jnp.einsum(form, real_part, cosine, precision=highest)
    real_sin = jnp.einsum(form, real_part, sine, precision=highest)
    imag_cos = jnp.einsum(form, imag_part, cosine, precision=highest)
    imag_sin = jnp.einsum(form, imag_part, sine, precision=highest)
    return (real_cos - direction * imag_sin, imag_cos + direction * real_sin)


def depth_section(real_part, imag_part, magnet_only):
    if magnet_only:
        half_depth = NZ // 2
        moved_real, moved_imag = passed_along(
            (real_part[..., half_depth:], imag_part[..., half_depth:]), "gz", 1
        )
        lower_device = lax.axis_index("gz") == 0
        return (
            jnp.where(lower_device, real_part[..., :half_depth], moved_real),
            jnp.where(lower_device, imag_part[..., :half_depth], moved_imag),
        )
    field_count = real_part.shape[0]
    summed = depth_sum(jnp.concatenate([real_part, imag_part], axis=0))
    return (summed[:field_count], summed[field_count:])


def forward_spectrum(fields, magnet_only):
    depth_cells = fields.shape[3]
    depth_index = lax.axis_index("gz") * depth_cells + jnp.arange(depth_cells, dtype=jnp.int32)
    cosine, sine = phase_tables(depth_index, jnp.arange(NZ, dtype=jnp.int32), NZ)
    real_part = jnp.einsum("fabc,ck->fabk", fields, cosine, precision=highest)
    imag_part = -jnp.einsum("fabc,ck->fabk", fields, sine, precision=highest)
    real_part, imag_part = depth_section(real_part, imag_part, magnet_only)
    real_part, imag_part = column_turn(real_part, imag_part)
    second_index = jnp.arange(NY, dtype=jnp.int32)
    cosine, sine = phase_tables(second_index, second_index, NY)
    real_part, imag_part = rotate(real_part, imag_part, cosine, sine, "fabk,bq->faqk", -1.0)
    real_part, imag_part = row_turn(real_part, imag_part)
    cosine, sine = phase_tables(arrival_order(NX), jnp.arange(NX, dtype=jnp.int32), NX)
    return rotate(real_part, imag_part, cosine, sine, "fapk,aq->fqpk", -1.0)


def inverse_field(real_part, imag_part, magnet_only):
    first_index = jnp.arange(NX, dtype=jnp.int32)
    cosine, sine = phase_tables(first_index, first_index, NX)
    real_part, imag_part = rotate(real_part, imag_part, cosine, sine, "fqpk,qa->fpak", 1.0)
    real_part, imag_part = row_turn(real_part, imag_part)
    cosine, sine = phase_tables(arrival_order(NY), jnp.arange(NY, dtype=jnp.int32), NY)
    real_part, imag_part = rotate(real_part, imag_part, cosine, sine, "fpak,pb->fbak", 1.0)
    real_part, imag_part = column_turn(real_part, imag_part)
    depth_cells = real_part.shape[3]
    depth_index = lax.axis_index("gz") * depth_cells + jnp.arange(depth_cells, dtype=jnp.int32)
    norm_scale = 1.0 / (NX * NY * NZ)
    if magnet_only:
        cosine, sine = phase_tables(depth_index, jnp.arange(NZ // 2, dtype=jnp.int32), NZ)
        own_term = jnp.einsum("fbak,kc->fabc", real_part, cosine, precision=highest) - jnp.einsum(
            "fbak,kc->fabc", imag_part, sine, precision=highest
        )
        own_term = own_term * norm_scale
        arrived = passed_along(own_term, "gz", -1)
        return own_term + arrived
    cosine, sine = phase_tables(depth_index, jnp.arange(NZ, dtype=jnp.int32), NZ)
    partial_term = jnp.einsum("fbak,kc->fabc", real_part, cosine, precision=highest) - jnp.einsum(
        "fbak,kc->fabc", imag_part, sine, precision=highest
    )
    return depth_sum(partial_term * norm_scale)


def spectral_kernels(run_second, depth_cells):
    fold_first = folded_index(jnp.arange(NX, dtype=jnp.int32), NX)[:, None, None]
    second_index = (
        lax.axis_index("gx") * lax.axis_size("gy") + lax.axis_index("gy")
    ) * run_second + jnp.arange(run_second, dtype=jnp.int32)
    fold_second = folded_index(second_index, NY)[None, :, None]
    third_index = lax.axis_index("gz") * depth_cells + jnp.arange(depth_cells, dtype=jnp.int32)
    fold_third = folded_index(third_index, NZ)[None, None, :]
    wave_first = full_turn * fold_first.astype(jnp.float32) / NX
    wave_second = full_turn * fold_second.astype(jnp.float32) / NY
    wave_third = full_turn * fold_third.astype(jnp.float32) / NZ
    anchor = (fold_first == 0) & (fold_second == 0) & (fold_third == 0)
    square = wave_first * wave_first + wave_second * wave_second + wave_third * wave_third
    safe_square = jnp.where(anchor, 1.0, square)
    return [
        jnp.where(anchor, 0.0, -(component_wave * wave_third) / safe_square)
        for component_wave in (wave_first, wave_second, wave_third)
    ]


def central_slope(padded, axis_number):
    if axis_number == 0:
        return (padded[..., 2:, 1:-1, 1:-1] - padded[..., :-2, 1:-1, 1:-1]) * 0.5
    if axis_number == 1:
        return (padded[..., 1:-1, 2:, 1:-1] - padded[..., 1:-1, :-2, 1:-1]) * 0.5
    return (padded[..., 1:-1, 1:-1, 2:] - padded[..., 1:-1, 1:-1, :-2]) * 0.5


def laplace(padded):
    beside = padded[..., 2:, 1:-1, 1:-1] + padded[..., :-2, 1:-1, 1:-1]
    beside = beside + padded[..., 1:-1, 2:, 1:-1] + padded[..., 1:-1, :-2, 1:-1]
    beside = beside + padded[..., 1:-1, 1:-1, 2:] + padded[..., 1:-1, 1:-1, :-2]
    return beside - 6.0 * padded[..., 1:-1, 1:-1, 1:-1]


def on_device(velocity, adjoint_seed, susceptibility, remanence, region_bounds, step_id):
    span_first, span_second, span_third = susceptibility.shape
    place_first = lax.axis_index("gx") * span_first + jnp.arange(span_first, dtype=jnp.int32)
    place_second = lax.axis_index("gy") * span_second + jnp.arange(span_second, dtype=jnp.int32)
    place_third = lax.axis_index("gz") * span_third + jnp.arange(span_third, dtype=jnp.int32)
    inside_first = (place_first >= region_bounds[0, 0]) & (place_first < region_bounds[1, 0])
    inside_second = (place_second >= region_bounds[0, 1]) & (place_second < region_bounds[1, 1])
    inside_third = (place_third >= region_bounds[0, 2]) & (place_third < region_bounds[1, 2])
    region_mask = (
        inside_first[:, None, None] & inside_second[None, :, None] & inside_third[None, None, :]
    ).astype(jnp.float32)
    stacked = jnp.concatenate([velocity, adjoint_seed, susceptibility[None]], axis=0)
    padded_all = padded_2(stacked, (("gx", 1), ("gy", 2), ("gz", 3)), 1)
    magnet_real, magnet_imag = forward_spectrum((remanence * region_mask)[None], True)
    kernels = spectral_kernels(magnet_real.shape[2], magnet_real.shape[3])
    demag_field = inverse_field(
        jnp.stack([kernel * magnet_real[0] for kernel in kernels]),
        jnp.stack([kernel * magnet_imag[0] for kernel in kernels]),
        False,
    )
    phase_angle = full_turn * (step_id[0] % field_period).astype(jnp.float32) / field_period
    applied = jnp.stack([jnp.cos(phase_angle), jnp.sin(phase_angle), jnp.zeros((), jnp.float32)])
    total_field = demag_field + applied[:, None, None, None]
    energy = 0.5 * jnp.sum(total_field * total_field, axis=0)
    padded_energy = padded_2(energy, (("gx", 0), ("gy", 1), ("gz", 2)), 1)
    padded_velocity = padded_all[0:3]
    padded_seed = padded_all[3:6]
    padded_suscept = padded_all[6]
    advect = jnp.stack(
        [
            velocity[0] * central_slope(padded_velocity[comp], 0)
            + velocity[1] * central_slope(padded_velocity[comp], 1)
            + velocity[2] * central_slope(padded_velocity[comp], 2)
            for comp in range(3)
        ]
    )
    pushed = jnp.stack(
        [susceptibility * central_slope(padded_energy, axis_number) for axis_number in range(3)]
    )
    next_velocity = velocity + time_step * (viscosity * laplace(padded_velocity) - advect + pushed)
    flux_terms = padded_suscept[None] * padded_seed
    source = (
        central_slope(flux_terms[0], 0)
        + central_slope(flux_terms[1], 1)
        + central_slope(flux_terms[2], 2)
    )
    source = -time_step * source
    field_adjoint = source[None] * total_field
    adjoint_real, adjoint_imag = forward_spectrum(field_adjoint, False)
    combined_real = (
        kernels[0] * adjoint_real[0] + kernels[1] * adjoint_real[1] + kernels[2] * adjoint_real[2]
    )
    combined_imag = (
        kernels[0] * adjoint_imag[0] + kernels[1] * adjoint_imag[1] + kernels[2] * adjoint_imag[2]
    )
    magnet_adjoint = inverse_field(combined_real[None], combined_imag[None], True)[0]
    design_gradient = region_mask * magnet_adjoint
    shear_terms = jnp.stack(
        [
            adjoint_seed[0] * central_slope(padded_velocity[0], comp)
            + adjoint_seed[1] * central_slope(padded_velocity[1], comp)
            + adjoint_seed[2] * central_slope(padded_velocity[2], comp)
            for comp in range(3)
        ]
    )
    carried = jnp.stack(
        [
            central_slope(padded_velocity[0] * padded_seed[comp], 0)
            + central_slope(padded_velocity[1] * padded_seed[comp], 1)
            + central_slope(padded_velocity[2] * padded_seed[comp], 2)
            for comp in range(3)
        ]
    )
    velocity_adjoint = adjoint_seed + time_step * (
        viscosity * laplace(padded_seed) - shear_terms + carried
    )
    return (next_velocity, velocity_adjoint, design_gradient)


def solution(mesh):
    return jax.shard_map(
        on_device,
        mesh=mesh,
        in_specs=(
            P(None, "gx", "gy", "gz"),
            P(None, "gx", "gy", "gz"),
            P("gx", "gy", "gz"),
            P("gx", "gy", "gz"),
            P(),
            P(),
        ),
        out_specs=(P(None, "gx", "gy", "gz"), P(None, "gx", "gy", "gz"), P("gx", "gy", "gz")),
        check_vma=False,
    )
```

profile of v0, /device:TPU:12, one launch (start us, length us, event | category | flops | bytes accessed | tf_op | source)
XLA Modules:
  0.0 2548.6 jit_solution(14170455124143179268)
XLA Ops:
  26.1 43.9 %collective-permute-done.7 = f32[1,128,32,128]{3,1,2,0:T(8,128)} collective-permute-done((f32[1,128,32,128]{3,1,2,0:T(8,128)}, f32[1,128,32,128]{3,1,2,0:T(8,128)}, u32[]{:S(2)}, u32[]{:S(2)}) %collective-permute-start.7) | collective-permute-done | bytes 2097184 | tf_op jit(solution)/shard_map/ppermute | solution.py:21
  89.6 44.6 %collective-permute-done.6 = f32[1,128,32,128]{3,1,2,0:T(8,128)S(1)} collective-permute-done((f32[1,128,32,128]{3,1,2,0:T(8,128)S(1)}, f32[1,128,32,128]{3,1,2,0:T(8,128)S(1)}, u32[]{:S(2)}, u32[]{:S(2)}) %collective-permute-start.6) | collective-permute-done | bytes 2097184 | tf_op jit(solution)/shard_map/ppermute | solution.py:21
  148.2 39.6 %all-to-all-done = f32[1,128,32,128]{3,2,0,1:T(8,128)} async-done(((f32[1,128,32,128]{3,2,0,1:T(8,128)}), f32[1,128,32,128]{3,2,0,1:T(8,128)}, u32[]{:S(2)}, u32[]{:S(2)}) %all-to-all-start) | async-done | bytes 2097184 | tf_op jit(solution)/shard_map/all_to_all | solution.py:58
  195.6 7.8 all-to-all-start.3
  213.5 37.2 %all-to-all-done.3 = f32[1,16,256,128]{3,1,0,2:T(8,128)} async-done(((f32[1,16,256,128]{3,1,0,2:T(8,128)}), f32[1,16,256,128]{3,1,0,2:T(8,128)}, u32[]{:S(2)}, u32[]{:S(2)}) %all-to-all-start.3) | async-done | bytes 2097184 | tf_op jit(solution)/shard_map/all_to_all | solution.py:66
  257.9 44.8 %all-to-all-done.2 = f32[1,16,256,128]{3,1,0,2:T(8,128)} async-done(((f32[1,16,256,128]{3,1,0,2:T(8,128)}), f32[1,16,256,128]{3,1,0,2:T(8,128)}, u32[]{:S(2)}, u32[]{:S(2)}) %all-to-all-start.2) | async-done | bytes 2097184 | tf_op jit(solution)/shard_map/all_to_all | solution.py:65
  317.8 7.3 fusion.22
  325.1 7.8 subtract_bitcast_fusion.3
  344.0 10.1 fusion.21
  354.2 7.4 add_bitcast_fusion.3
  367.9 113.3 %all-to-all-done.4 = f32[3,16,256,128]{3,1,0,2:T(8,128)} async-done(((f32[3,16,256,128]{3,1,0,2:T(8,128)}), f32[3,16,256,128]{3,1,0,2:T(8,128)}, u32[]{:S(2)}, u32[]{:S(2)}) %all-to-all-start.4) | async-done | bytes 6291488 | tf_op jit(solution)/shard_map/all_to_all | solution.py:65
  492.5 130.6 %all-to-all-done.5 = f32[3,16,256,128]{3,1,0,2:T(8,128)} async-done(((f32[3,16,256,128]{3,1,0,2:T(8,128)}), f32[3,16,256,128]{3,1,0,2:T(8,128)}, u32[]{:S(2)}, u32[]{:S(2)}) %all-to-all-start.5) | async-done | bytes 6291488 | tf_op jit(solution)/shard_map/all_to_all | solution.py:66
  626.9 7.3 fusion.132
  634.3 7.9 add_bitcast_fusion.2
  653.3 10.2 fusion.135
  663.5 7.4 subtract_bitcast_fusion.2
  677.3 110.5 %all-to-all-done.7 = f32[3,256,16,128]{3,2,0,1:T(8,128)} async-done(((f32[3,256,16,128]{3,2,0,1:T(8,128)}), f32[3,256,16,128]{3,2,0,1:T(8,128)}, u32[]{:S(2)}, u32[]{:S(2)}) %all-to-all-start.7) | async-done | bytes 6291488 | tf_op jit(solution)/shard_map/all_to_all | solution.py:59
  787.8 8.7 all-to-all-start.6
  803.2 128.8 %all-to-all-done.6 = f32[3,256,16,128]{3,2,0,1:T(8,128)} async-done(((f32[3,256,16,128]{3,2,0,1:T(8,128)}), f32[3,256,16,128]{3,2,0,1:T(8,128)}, u32[]{:S(2)}, u32[]{:S(2)}) %all-to-all-start.6) | async-done | bytes 6291488 | tf_op jit(solution)/shard_map/all_to_all | solution.py:58
  935.9 11.9 fusion.149
  947.8 15.2 multiply_bitcast_fusion
  965.1 7.3 copy.141
  972.5 7.0 copy.94
  985.4 11.2 fusion.379
  996.5 9.0 copy.97
  1006.9 9.1 copy.95
  1020.6 7.9 copy.98
  1028.6 8.0 copy.96
  1072.4 7.8 collective-permute-done.4
  1081.7 44.2 %pad_maximum_fusion.1 = f32[7,130,34,130]{1,3,2,0:T(8,128)} fusion(f32[7,130,34,1]{1,3,2,0:T(1,128)S(1)} %collective-permute-done.4, f32[7,130,1,128]{1,3,2,0:T(8,128)S(1)} %copy.102, f32[7,1,32,128]{1,3,2,0:T(8,128)} %copy.96, f32[1,128,32,128]{1,3,2,0:T(8,128)S(1)} %bitcast.403, f32[3,128,32,128]{1,3,2,0:T(8,128)} %copy.94, f32[3,128,32,128]{1,3,2,0:T(8,128)} %copy.141, ...), kind=kLoop, calls=%fused_computation.2 | loop fusion | flops 32177600 | bytes 32177600 | tf_op jit(solution)/shard_map/concatenate | solution.py:33
  1125.9 12.0 slice_bitcast_fusion.3
  1137.9 10.3 slice_multiply_fusion
  1148.2 10.5 slice_bitcast_fusion.2
  1158.7 10.8 fusion.48
  1169.6 14.2 fusion.25
  1183.8 14.0 fusion.17
  1197.8 14.4 pad_maximum_fusion.2
  1212.3 279.3 %reduce-scatter.5.cloned.1.call-done = f32[6,128,32,128]{3,1,2,0:T(8,128)} async-done(((f32[6,128,32,256]{3,1,2,0:T(8,128)}), f32[6,128,32,128]{3,1,2,0:T(8,128)}) %reduce-scatter.5.cloned.1.call-update) | async-done | bytes 12582928 | tf_op jit(solution)/shard_map/reduce_scatter | solution.py:53
  1491.6 8.9 fusion.380
  1511.9 9.0 copy.149
  1520.9 126.5 %all-to-all-done.9 = f32[3,128,32,128]{3,2,0,1:T(8,128)} async-done(((f32[3,128,32,128]{3,2,0,1:T(8,128)}), f32[3,128,32,128]{3,2,0,1:T(8,128)}, u32[]{:S(2)}, u32[]{:S(2)}) %all-to-all-start.9) | async-done | bytes 6291488 | tf_op jit(solution)/shard_map/all_to_all | solution.py:59
  1647.4 8.2 all-to-all-start.8
  1661.8 10.4 fusion.126
  1672.2 118.9 %all-to-all-done.8 = f32[3,128,32,128]{3,2,0,1:T(8,128)} async-done(((f32[3,128,32,128]{3,2,0,1:T(8,128)}), f32[3,128,32,128]{3,2,0,1:T(8,128)}, u32[]{:S(2)}, u32[]{:S(2)}) %all-to-all-start.8) | async-done | bytes 6291488 | tf_op jit(solution)/shard_map/all_to_all | solution.py:58
  1795.7 8.1 add_bitcast_fusion.1
  1810.1 8.4 all-to-all-start.11
  1818.5 10.0 fusion.130
  1828.5 8.0 subtract_bitcast_fusion.1
  1842.8 112.9 %all-to-all-done.11 = f32[3,16,256,128]{3,1,0,2:T(8,128)} async-done(((f32[3,16,256,128]{3,1,0,2:T(8,128)}), f32[3,16,256,128]{3,1,0,2:T(8,128)}, u32[]{:S(2)}, u32[]{:S(2)}) %all-to-all-start.11) | async-done | bytes 6291488 | tf_op jit(solution)/shard_map/all_to_all | solution.py:66
  1967.1 130.4 %all-to-all-done.10 = f32[3,16,256,128]{3,1,0,2:T(8,128)} async-done(((f32[3,16,256,128]{3,1,0,2:T(8,128)}), f32[3,16,256,128]{3,1,0,2:T(8,128)}, u32[]{:S(2)}, u32[]{:S(2)}) %all-to-all-start.10) | async-done | bytes 6291488 | tf_op jit(solution)/shard_map/all_to_all | solution.py:65
  2101.4 7.3 fusion.128
  2108.7 7.5 fusion.124
  2116.2 8.1 subtract_bitcast_fusion
  2124.4 8.5 add_bitcast_fusion
  2148.3 23.1 fusion.30
  2171.5 19.9 fusion.52
  2208.2 69.2 %pad_maximum_fusion = (f32[7,130,34,129]{1,3,2,0:T(8,128)}, f32[7,130,34,129]{1,3,2,0:T(8,128)}) fusion(f32[7,130,34,1]{1,3,2,0:T(1,128)S(1)} %copy-done.30, f32[7,130,1,128]{1,3,2,0:T(8,128)S(1)} %copy-done.11, f32[7,1,32,128]{1,3,2,0:T(8,128)} %copy.96, f32[1,128,32,128]{1,3,2,0:T(8,128)S(1)} %bitcast.404, f32[3,128,32,128]{1,3,2,0:T(8,128)} %copy.94, ...), kind=kLoop, calls=%fused_computation | loop fusion | flops 55877640 | bytes 48018880 | tf_op jit(solution)/shard_map/concatenate | solution.py:33
  2296.1 12.2 fusion.60
  2308.3 22.5 add_bitcast_fusion.8
  2330.8 21.3 add_bitcast_fusion.7
  2382.5 34.8 %fusion.5 = f32[3,128,32,128]{1,3,2,0:T(8,128)} fusion(f32[3,128,32,128]{1,3,2,0:T(8,128)} %copy.94, f32[7,130,34,129]{1,3,2,0:T(8,128)} %get-tuple-element.13, f32[7,130,34,129]{1,3,2,0:T(8,128)} %get-tuple-element.12, f32[7,130,1,128]{1,3,2,0:T(8,128)} %copy.104, f32[7,1,32,128]{1,3,2,0:T(8,128)} %copy.96, f32[7,1,32,128]{1,3,2,0:T(8,128)} %copy.98, ...), kind=kLoop, calls=%fused_computation.13 | loop fusion | flops 50331648 | bytes 47298560 | tf_op jit(solution)/shard_map/add | solution.py:244
  2428.5 24.5 add_bitcast_fusion.12
  2469.8 6.9 fusion.73
  2489.3 34.7 %fusion.14 = f32[3,128,32,128]{1,3,2,0:T(8,128)} fusion(f32[3,128,32,128]{1,3,2,0:T(8,128)} %copy.141, f32[7,130,34,129]{1,3,2,0:T(8,128)} %get-tuple-element.13, f32[7,130,34,129]{1,3,2,0:T(8,128)} %get-tuple-element.12, f32[7,130,1,128]{1,3,2,0:T(8,128)S(1)} %copy-done.12, f32[7,1,32,128]{1,3,2,0:T(8,128)} %copy.96, f32[7,1,32,128]{1,3,2,0:T(8,128)} %copy.98, ...), kind=kLoop, calls=%fused_computation.40 | loop fusion | flops 50331648 | bytes 47298560 | tf_op jit(solution)/shard_map/add | solution.py:210
  (282 shorter events, 392.5 us)
Async XLA Ops:
  7.2 1176.6 %copy-start.39 = (s32[128]{0:T(128)}, s32[128]{0:T(128)S(1)}, u32[]{:S(2)}) copy-start(s32[128]{0:T(128)S(1)} %iota_add_fusion) | copy-start | bytes 1540
  11.9 67.8 %copy-start.47 = (pred[128]{0:T(512)(128)(4,1)}, pred[128]{0:T(512)(128)(4,1)S(1)}, u32[]{:S(2)}) copy-start(pred[128]{0:T(512)(128)(4,1)S(1)} %compare_and_fusion) | copy-start | bytes 388
  14.5 65.2 %copy-start.37 = (pred[128,32]{0,1:T(8,128)(4,1)}, pred[128,32]{0,1:T(8,128)(4,1)S(1)}, u32[]{:S(2)}) copy-start(pred[128,32]{0,1:T(8,128)(4,1)S(1)} %broadcast_and_fusion) | copy-start | bytes 12292
  21.4 48.6 %collective-permute-start.7 = (f32[1,128,32,128]{3,1,2,0:T(8,128)}, f32[1,128,32,128]{3,1,2,0:T(8,128)}, u32[]{:S(2)}, u32[]{:S(2)}) collective-permute-start(f32[1,128,32,128]{3,1,2,0:T(8,128)} %slice.578), channel_id=1, source_target_pairs={{0,1},{2,3},{4,5},{6,7},{8,9},{10,11},{12,13},{14,15},{16,17},{18,... | collective-permute-start | bytes 6291464 | tf_op jit(solution)/shard_map/ppermute | solution.py:21
  74.4 62.7 %all-to-all-start.1 = ((f32[1,128,32,128]{3,2,0,1:T(8,128)}), f32[1,128,32,128]{3,2,0,1:T(8,128)}, u32[]{:S(2)}, u32[]{:S(2)}) async-start(f32[1,128,32,128]{3,2,0,1:T(8,128)} %copy.116), calls=%async_computation.1 | async-start | bytes 4194304 | tf_op jit(solution)/shard_map/all_to_all | solution.py:59
  84.0 50.2 %collective-permute-start.6 = (f32[1,128,32,128]{3,1,2,0:T(8,128)S(1)}, f32[1,128,32,128]{3,1,2,0:T(8,128)S(1)}, u32[]{:S(2)}, u32[]{:S(2)}) collective-permute-start(f32[1,128,32,128]{3,1,2,0:T(8,128)S(1)} %slice.576), channel_id=1, source_target_pairs={{0,1},{2,3},{4,5},{6,7},{8,9},{10,11},{12,13},{14,15},{16,17},{18,... | collective-permute-start | bytes 6291464 | tf_op jit(solution)/shard_map/ppermute | solution.py:21
  137.1 50.7 %all-to-all-start = ((f32[1,128,32,128]{3,2,0,1:T(8,128)}), f32[1,128,32,128]{3,2,0,1:T(8,128)}, u32[]{:S(2)}, u32[]{:S(2)}) async-start(f32[1,128,32,128]{3,2,0,1:T(8,128)} %copy.113), calls=%async_computation | async-start | bytes 4194304 | tf_op jit(solution)/shard_map/all_to_all | solution.py:58
  195.6 55.0 %all-to-all-start.3 = ((f32[1,16,256,128]{3,1,0,2:T(8,128)}), f32[1,16,256,128]{3,1,0,2:T(8,128)}, u32[]{:S(2)}, u32[]{:S(2)}) async-start(f32[1,16,256,128]{3,1,0,2:T(8,128)} %copy.120), calls=%async_computation.3 | async-start | bytes 4194304 | tf_op jit(solution)/shard_map/all_to_all | solution.py:66
  250.7 51.9 %all-to-all-start.2 = ((f32[1,16,256,128]{3,1,0,2:T(8,128)}), f32[1,16,256,128]{3,1,0,2:T(8,128)}, u32[]{:S(2)}, u32[]{:S(2)}) async-start(f32[1,16,256,128]{3,1,0,2:T(8,128)} %copy.118), calls=%async_computation.2 | async-start | bytes 4194304 | tf_op jit(solution)/shard_map/all_to_all | solution.py:65
  255.5 57.8 %copy-start.49 = (f32[128]{0:T(128)}, f32[128]{0:T(128)S(1)}, u32[]{:S(2)}) copy-start(f32[128]{0:T(128)S(1)} %fusion.378) | copy-start | bytes 1540
  255.5 57.8 %copy-start.51 = (pred[128]{0:T(512)(128)(4,1)}, pred[128]{0:T(512)(128)(4,1)S(1)}, u32[]{:S(2)}) copy-start(pred[128]{0:T(512)(128)(4,1)S(1)} %broadcast_compare_fusion) | copy-start | bytes 388
  255.6 57.7 %copy-start.53 = (f32[128]{0:T(128)}, f32[128]{0:T(128)S(1)}, u32[]{:S(2)}) copy-start(f32[128]{0:T(128)S(1)} %get-tuple-element.70) | copy-start | bytes 1540
  255.7 57.6 %copy-start.45 = (pred[256,16]{0,1:T(8,128)(4,1)}, pred[256,16]{0,1:T(8,128)(4,1)S(1)}, u32[]{:S(2)}) copy-start(pred[256,16]{0,1:T(8,128)(4,1)S(1)} %broadcast_and_fusion.1) | copy-start | bytes 12292
  255.8 57.5 %copy-start.43 = (f32[16,128]{1,0:T(8,128)}, f32[16,128]{1,0:T(8,128)S(1)}, u32[]{:S(2)}) copy-start(f32[16,128]{1,0:T(8,128)S(1)} %multiply_negate_fusion.1) | copy-start | bytes 24580
  255.9 57.5 %copy-start.35 = (f32[256,16]{0,1:T(8,128)}, f32[256,16]{0,1:T(8,128)S(1)}, u32[]{:S(2)}) copy-start(f32[256,16]{0,1:T(8,128)S(1)} %broadcast_add_fusion) | copy-start | bytes 49156
  256.0 57.4 %copy-start.33 = (f32[256,128]{1,0:T(8,128)}, f32[256,128]{1,0:T(8,128)S(1)}, u32[]{:S(2)}) copy-start(f32[256,128]{1,0:T(8,128)S(1)} %multiply_negate_fusion) | copy-start | bytes 393220
  339.3 141.9 %all-to-all-start.4 = ((f32[3,16,256,128]{3,1,0,2:T(8,128)}), f32[3,16,256,128]{3,1,0,2:T(8,128)}, u32[]{:S(2)}, u32[]{:S(2)}) async-start(f32[3,16,256,128]{3,1,0,2:T(8,128)} %copy.122), calls=%async_computation.4 | async-start | bytes 12582912 | tf_op jit(solution)/shard_map/all_to_all | solution.py:65
  344.0 10.1 copy-start.21
  344.0 10.1 copy-start.23
  481.2 141.9 %all-to-all-start.5 = ((f32[3,16,256,128]{3,1,0,2:T(8,128)}), f32[3,16,256,128]{3,1,0,2:T(8,128)}, u32[]{:S(2)}, u32[]{:S(2)}) async-start(f32[3,16,256,128]{3,1,0,2:T(8,128)} %copy.124), calls=%async_computation.5 | async-start | bytes 12582912 | tf_op jit(solution)/shard_map/all_to_all | solution.py:66
  623.1 11.2 slice-start.2
  648.5 15.0 slice-start.4
  648.5 139.3 %all-to-all-start.7 = ((f32[3,256,16,128]{3,2,0,1:T(8,128)}), f32[3,256,16,128]{3,2,0,1:T(8,128)}, u32[]{:S(2)}, u32[]{:S(2)}) async-start(f32[3,256,16,128]{3,2,0,1:T(8,128)} %copy.129), calls=%async_computation.7 | async-start | bytes 12582912 | tf_op jit(solution)/shard_map/all_to_all | solution.py:59
  653.3 10.2 slice-start.5
  787.8 144.1 %all-to-all-start.6 = ((f32[3,256,16,128]{3,2,0,1:T(8,128)}), f32[3,256,16,128]{3,2,0,1:T(8,128)}, u32[]{:S(2)}, u32[]{:S(2)}) async-start(f32[3,256,16,128]{3,2,0,1:T(8,128)} %copy.126), calls=%async_computation.6 | async-start | bytes 12582912 | tf_op jit(solution)/shard_map/all_to_all | solution.py:58
  796.5 373.1 %reduce-scatter.3.cloned.1.call-start = ((), (), s32[]{:S(2)}) async-start(), calls=%async_computation.18 | async-start | bytes 18874368 | tf_op jit(solution)/shard_map/reduce_scatter | solution.py:53
  932.0 15.8 slice-start.8
  935.9 11.9 slice-start.9
  963.0 528.5 %reduce-scatter.5.cloned.1.call-start = ((), (), s32[]{:S(2)}) async-start(), calls=%async_computation.19 | async-start | bytes 37748736 | tf_op jit(solution)/shard_map/reduce_scatter | solution.py:53
  965.1 116.5 %copy-start = (f32[128,32,128]{0,2,1:T(8,128)}, f32[128,32,128]{0,2,1:T(8,128)S(1)}, u32[]{:S(2)}) copy-start(f32[128,32,128]{0,2,1:T(8,128)S(1)} %copy.92) | copy-start | bytes 6291460
  1005.6 15.1 collective-permute-start.1
  1016.0 12.6 collective-permute-start
  1041.7 11.1 collective-permute-start.2
  1048.0 10.2 collective-permute-start.3
  1054.4 27.3 %copy-start.10 = (f32[7,130,1,128]{1,3,2,0:T(8,128)}, f32[7,130,1,128]{1,3,2,0:T(8,128)S(1)}, u32[]{:S(2)}) copy-start(f32[7,130,1,128]{1,3,2,0:T(8,128)S(1)} %copy.102) | copy-start | bytes 1397764
  1065.6 14.6 collective-permute-start.4
  1066.9 14.7 collective-permute-start.5
  1072.4 111.4 %copy-start.41 = (f32[3]{0:T(128)}, f32[3]{0:T(128)S(1)}, u32[]{:S(2)}) copy-start(f32[3]{0:T(128)S(1)} %pad_maximum_fusion.68) | copy-start | bytes 40
  1080.2 45.7 %copy-start.29 = (f32[7,130,34,1]{1,3,2,0:T(1,128)}, f32[7,130,34,1]{1,3,2,0:T(1,128)S(1)}, u32[]{:S(2)}) copy-start(f32[7,130,34,1]{1,3,2,0:T(1,128)S(1)} %collective-permute-done.4) | copy-start | bytes 371284
  1081.7 44.2 %copy-start.31 = (f32[7,130,34,1]{1,3,2,0:T(1,128)}, f32[7,130,34,1]{1,3,2,0:T(1,128)S(1)}, u32[]{:S(2)}) copy-start(f32[7,130,34,1]{1,3,2,0:T(1,128)S(1)} %collective-permute-done.5) | copy-start | bytes 371284
  1169.6 14.2 copy-start.7
  1506.7 140.6 %all-to-all-start.9 = ((f32[3,128,32,128]{3,2,0,1:T(8,128)}), f32[3,128,32,128]{3,2,0,1:T(8,128)}, u32[]{:S(2)}, u32[]{:S(2)}) async-start(f32[3,128,32,128]{3,2,0,1:T(8,128)} %copy.151), calls=%async_computation.11 | async-start | bytes 12582912 | tf_op jit(solution)/shard_map/all_to_all | solution.py:59
  1647.4 143.7 %all-to-all-start.8 = ((f32[3,128,32,128]{3,2,0,1:T(8,128)}), f32[3,128,32,128]{3,2,0,1:T(8,128)}, u32[]{:S(2)}, u32[]{:S(2)}) async-start(f32[3,128,32,128]{3,2,0,1:T(8,128)} %copy.149), calls=%async_computation.10 | async-start | bytes 12582912 | tf_op jit(solution)/shard_map/all_to_all | solution.py:58
  1794.8 9.0 copy-start.6
  1810.1 18.4 slice-start
  1810.1 145.6 %all-to-all-start.11 = ((f32[3,16,256,128]{3,1,0,2:T(8,128)}), f32[3,16,256,128]{3,1,0,2:T(8,128)}, u32[]{:S(2)}, u32[]{:S(2)}) async-start(f32[3,16,256,128]{3,1,0,2:T(8,128)} %copy.155), calls=%async_computation.13 | async-start | bytes 12582912 | tf_op jit(solution)/shard_map/all_to_all | solution.py:66
  1818.5 10.0 slice-start.1
  1955.7 141.8 %all-to-all-start.10 = ((f32[3,16,256,128]{3,1,0,2:T(8,128)}), f32[3,16,256,128]{3,1,0,2:T(8,128)}, u32[]{:S(2)}, u32[]{:S(2)}) async-start(f32[3,16,256,128]{3,1,0,2:T(8,128)} %copy.153), calls=%async_computation.12 | async-start | bytes 12582912 | tf_op jit(solution)/shard_map/all_to_all | solution.py:65
  2097.5 11.2 slice-start.6
  2143.3 57.9 %all-to-all-start.13 = ((f32[1,16,256,128]{3,1,0,2:T(8,128)}), f32[1,16,256,128]{3,1,0,2:T(8,128)}, u32[]{:S(2)}, u32[]{:S(2)}) async-start(f32[1,16,256,128]{3,1,0,2:T(8,128)} %copy.159), calls=%async_computation.15 | async-start | bytes 4194304 | tf_op jit(solution)/shard_map/all_to_all | solution.py:66
  2201.3 79.3 %all-to-all-start.12 = ((f32[1,16,256,128]{3,1,0,2:T(8,128)}), f32[1,16,256,128]{3,1,0,2:T(8,128)}, u32[]{:S(2)}, u32[]{:S(2)}) async-start(f32[1,16,256,128]{3,1,0,2:T(8,128)} %copy.157), calls=%async_computation.14 | async-start | bytes 4194304 | tf_op jit(solution)/shard_map/all_to_all | solution.py:65
  2290.7 86.7 %all-to-all-start.14 = ((f32[1,256,16,128]{3,2,0,1:T(8,128)}), f32[1,256,16,128]{3,2,0,1:T(8,128)}, u32[]{:S(2)}, u32[]{:S(2)}) async-start(f32[1,256,16,128]{3,2,0,1:T(8,128)} %copy.161), calls=%async_computation.16 | async-start | bytes 4194304 | tf_op jit(solution)/shard_map/all_to_all | solution.py:58
  2330.8 21.3 copy-start.42
  2363.4 8.6 copy-start.17
  2363.4 55.9 %collective-permute-start.8 = (f32[1,32,128]{2,1,0:T(8,128)S(1)}, f32[1,32,128]{2,1,0:T(8,128)S(1)}, u32[]{:S(2)}, u32[]{:S(2)}) collective-permute-start(f32[1,32,128]{2,1,0:T(8,128)S(1)} %copy.132), channel_id=1, source_target_pairs={{16,0},{17,1},{18,2},{19,3},{20,4},{21,5},{22,6},{23,7},{24,8},{25... | collective-permute-start | bytes 49160 | tf_op jit(solution)/shard_map/ppermute | solution.py:32
  2366.0 51.3 %collective-permute-start.9 = (f32[1,32,128]{2,1,0:T(8,128)S(1)}, f32[1,32,128]{2,1,0:T(8,128)S(1)}, u32[]{:S(2)}, u32[]{:S(2)}) collective-permute-start(f32[1,32,128]{2,1,0:T(8,128)S(1)} %copy.134), channel_id=1, source_target_pairs={{0,16},{1,17},{2,18},{3,19},{4,20},{5,21},{6,22},{7,23},{8,24},{9,... | collective-permute-start | bytes 49160 | tf_op jit(solution)/shard_map/ppermute | solution.py:29
  2377.4 104.6 %all-to-all-start.15 = ((f32[1,256,16,128]{3,2,0,1:T(8,128)}), f32[1,256,16,128]{3,2,0,1:T(8,128)}, u32[]{:S(2)}, u32[]{:S(2)}) async-start(f32[1,256,16,128]{3,2,0,1:T(8,128)} %copy.163), calls=%async_computation.17 | async-start | bytes 4194304 | tf_op jit(solution)/shard_map/all_to_all | solution.py:59
  2422.5 37.1 %collective-permute-start.11 = (f32[130,1,128]{0,2,1:T(8,128)S(1)}, f32[130,1,128]{0,2,1:T(8,128)S(1)}, u32[]{:S(2)}, u32[]{:S(2)}) collective-permute-start(f32[130,1,128]{0,2,1:T(8,128)S(1)} %get-tuple-element.44), channel_id=1, source_target_pairs={{0,2},{2,4},{4,6},{6,8},{8,10},{10,12},{12,14},{1,3},{3,5},{5,7},{... | collective-permute-start | bytes 199688 | tf_op jit(solution)/shard_map/ppermute | solution.py:29
  2424.6 35.0 %collective-permute-start.10 = (f32[130,1,128]{0,2,1:T(8,128)S(1)}, f32[130,1,128]{0,2,1:T(8,128)S(1)}, u32[]{:S(2)}, u32[]{:S(2)}) collective-permute-start(f32[130,1,128]{0,2,1:T(8,128)S(1)} %get-tuple-element.45), channel_id=1, source_target_pairs={{2,0},{4,2},{6,4},{8,6},{10,8},{12,10},{14,12},{3,1},{5,3},{7,5},{... | collective-permute-start | bytes 199688 | tf_op jit(solution)/shard_map/ppermute | solution.py:32
  2461.2 8.5 collective-permute-start.12
  2462.7 7.1 collective-permute-start.13
  2487.8 49.0 %collective-permute-start.14 = (f32[1,128,32,128]{1,3,2,0:T(8,128)}, f32[1,128,32,128]{1,3,2,0:T(8,128)}, u32[]{:S(2)}, u32[]{:S(2)}) collective-permute-start(f32[1,128,32,128]{1,3,2,0:T(8,128)} %multiply_bitcast_fusion.1), channel_id=1, source_target_pairs={{1,0},{3,2},{5,4},{7,6},{9,8},{11,10},{13,12},{15,14},{17,16},{19,... | collective-permute-start | bytes 6291464 | tf_op jit(solution)/shard_map/ppermute | solution.py:21
  2524.0 12.8 copy-start.38
  2524.0 12.8 copy-start.48
  (34 other events, 205.2 us)
Sparse Core Ops, SparseCore 0:
  963.2 152.5 reduce-scatter.2
  1212.4 279.0 reduce-scatter.4
where the time goes:
time: 2560 us; the launch traced here: 2550 us
  waiting for transfers between devices  1480 us (58%)
  other arithmetic  384 us (15%)
  local copies, waits for them, and re-layouts  264 us (10%)
  matrix products  258 us (10%)
  starting transfers between devices  142 us (6%)
    all_to_all x4, waiting for transfers between devices, row_turn(): lax.all_to_all(real_part, ('gx', 'gy'), split_axis=2, concat_axis=1, tile...  289 us
    all_to_all x4, waiting for transfers between devices, column_turn(): lax.all_to_all(real_part, 'gy', split_axis=1, concat_axis=2, tiled=True)  287 us
    all_to_all x4, waiting for transfers between devices, row_turn(): lax.all_to_all(imag_part, ('gx', 'gy'), split_axis=2, concat_axis=1, tile...  281 us
    reduce_scatter x2, waiting for transfers between devices, depth_sum(): return lax.psum_scatter(partial_term, 'gz', scatter_dimension=3, tiled=True)  279 us
    all_to_all x4, waiting for transfers between devices, column_turn(): lax.all_to_all(imag_part, 'gy', split_axis=1, concat_axis=2, tiled=True)  237 us
    concatenate x4, other arithmetic, padded_2(): block = jnp.concatenate([low, block, high], axis=dim)  118 us
    ppermute x3, waiting for transfers between devices, passed_along(): return lax.ppermute(array, axis, pairs)  94.7 us
  transfers between devices with their start and end apart: 33, of which 19 were waited for; matrix products, arithmetic and copies ran while one was open for 25% of the time, Pallas kernels for 0%

commit v1 on v0

v1 whole, which is shorter than its diff:
```python
import functools
import math

import jax
import jax.numpy as jnp
import ml_dtypes
import numpy as np
from jax import lax
from jax.experimental import pallas as pl
from jax.experimental.pallas import tpu as pltpu
from jax.sharding import PartitionSpec as P

time_step = 0.5
viscosity = 0.2
field_period = 24
full_turn = 2.0 * math.pi
bf16 = ml_dtypes.bfloat16
axes = ("gx", "gy", "gz")


def wave_tables(length):
    half = length // 2
    slot = np.arange(length)
    wave = np.where(slot <= half, slot, slot - half)
    angle = full_turn * (wave[:, None] * np.arange(length)[None, :] % length) / length
    weight = np.sqrt(np.where(slot % half == 0, 1.0, 2.0) / length)[:, None]
    odd = (slot > half)[:, None]
    kappa = full_turn * wave / length
    basis = np.where(odd, np.sin(angle), np.cos(angle)) * weight
    slope = np.where(odd, np.cos(angle), -np.sin(angle)) * weight * kappa[:, None]
    slope[half] = 0.0
    return basis, slope, kappa


def two_parts(table):
    high = table.astype(bf16)
    low = (table - high.astype(np.float64)).astype(bf16)
    return high, low


def split(value):
    high = value.astype(jnp.bfloat16)
    low = (value - high.astype(jnp.float32)).astype(jnp.bfloat16)
    return high, low


def dot(left, right):
    return jnp.dot(left, right, preferred_element_type=jnp.float32)


def own_rows(table, axis, count):
    return lax.dynamic_slice_in_dim(jnp.asarray(table), lax.axis_index(axis) * count, count, 0)


def own_cols(table, axis, count):
    return lax.dynamic_slice_in_dim(jnp.asarray(table), lax.axis_index(axis) * count, count, 1)


class Plan:
    def __init__(self, mesh, local):
        self.gx, self.gy, self.gz = (mesh.shape[a] for a in axes)
        self.xl, self.yl, self.zl = local
        self.nx, self.ny, self.nz = self.xl * self.gx, self.yl * self.gy, self.zl * self.gz
        self.x2, self.y2, self.z2 = self.nx // 2, self.ny // 2, self.nz // 2
        self.px, self.py = self.xl // 4, self.yl // 2

    def piece_rows(self, y):
        across, inside = lax.div(y, self.py), lax.rem(y, self.py)
        runs = []
        for depth in range(self.gz // 2):
            runs.append([])
            for first in range(self.gx):
                for side in range(2):
                    piece = (first * self.gy + across) * self.gz + 2 * depth + side
                    runs[-1].append(piece * (self.px * self.py) + inside)
        return runs


def forward_tables(plan):
    bx, dx, wx = wave_tables(plan.nx)
    by, dy, wy = wave_tables(plan.ny)
    bz, dz, wz = wave_tables(plan.nz)
    hx, hy, hz = plan.nx // 2, plan.ny // 2, plan.nz // 2
    ez = bz.copy()
    ez[0] = bz[hz]
    z1 = dz.copy()
    z1[0] = 0.0
    z2 = dz.copy()
    z2[0] = -(np.pi**2) * bz[hz]
    z3 = -(wz**2)[:, None] * bz
    z3[0] = 0.0
    z1n = np.zeros_like(z1)
    z1n[hz] = -np.pi * bz[hz]
    xs = dx.copy()
    xs[hx] = np.pi * bx[hx]
    w3 = wz.copy()
    w3[0] = np.pi
    base = wy[:, None] ** 2 + w3[None, :] ** 2
    keep = np.ones_like(base, bool)
    keep[:, 0] = False
    keep[hy, 0] = True
    base = np.where(keep, base, 1e30).astype(np.float32)
    return dict(
        fx=bx[:, : plan.x2],
        ez=ez[:, : plan.z2],
        fy=by[:, : plan.y2],
        by=by,
        dy=dy,
        bx=bx,
        xs=xs,
        z1=z1,
        z2=z2,
        z3=z3,
        z1n=z1n,
        base=base,
        w1=(wx**2).astype(np.float32),
    )


def pair_lanes(a, b):
    return jnp.concatenate([a, b], axis=1)


def pair_rows(a, b):
    return jnp.concatenate([a, b], axis=0)


def load_plane(ref, plan, y):
    blocks = [
        [ref[pl.ds(start, plan.px, stride=plan.py), :] for start in runs]
        for runs in plan.piece_rows(y)
    ]
    blocks = [jnp.concatenate(rows, axis=0) for rows in blocks]
    return blocks[0] if len(blocks) == 1 else jnp.concatenate(blocks, axis=1)


def store_plane(ref, plan, y, value):
    for depth, runs in enumerate(plan.piece_rows(y)):
        for place, start in enumerate(runs):
            ref[pl.ds(start, plan.px, stride=plan.py), :] = value[
                place * plan.px : (place + 1) * plan.px, depth * plan.zl : (depth + 1) * plan.zl
            ]


def field_body(
    plan, w1_ref, app_ref, m_ref, src_ref, fx_ref, fxl_ref, ez_ref, ezl_ref, fy_ref, fyl_ref,
    g_ref, z13_ref, z13l_ref, z2_ref, z1n_ref, xs_ref, xb_ref, base_ref,
    f_ref, e_ref, s_ref, r_ref, kern_ref,
):
    nx, hx, y2, z2, xl, yl, zl = plan.nx, plan.nx // 2, plan.y2, plan.z2, plan.xl, plan.yl, plan.zl
    span, block = yl * nx, xl * yl

    def along_x(pair, carry):
        plane = pair_lanes(load_plane(m_ref, plan, 2 * pair), load_plane(m_ref, plan, 2 * pair + 1))
        high, low = split(plane)
        out = dot(fx_ref[...], pair_rows(high, low)) + dot(fxl_ref[...], high)
        s_ref[pl.ds(2 * pair * nx, nx), :] = out[:, :z2]
        s_ref[pl.ds((2 * pair + 1) * nx, nx), :] = out[:, z2:]
        return carry

    lax.fori_loop(0, y2 // 2, along_x, 0)

    def one_slab(plane, kern):
        high, low = split(plane)
        spectrum = dot(fy_ref[...], pair_rows(high, low)) + dot(fyl_ref[...], high)
        high, low = split(spectrum * kern)
        both = dot(g_ref[...], high)
        return both[: 2 * yl] + both[2 * yl :] + dot(g_ref[: 2 * yl], low)

    def slabs(i, edge):
        rows = pair_rows(
            s_ref[pl.ds(i, y2, stride=nx), :], s_ref[pl.ds(i + hx, y2, stride=nx), :]
        )
        high, low = split(rows)
        planes = dot(pair_lanes(high, low), ez_ref[...]) + dot(high, ezl_ref[...])
        kern_ref[...] = 1.0 / (base_ref[...] + w1_ref[i])
        even = one_slab(planes[:y2], kern_ref[...])
        if edge:
            kern_ref[...] = 1.0 / (base_ref[...] + w1_ref[hx])
        odd = one_slab(planes[y2:], kern_ref[...])
        q1 = pair_rows(even[:yl], odd[:yl])
        q2 = pair_rows(even[yl:], odd[yl:])
        lane = lax.broadcasted_iota(jnp.int32, q1.shape, 1)
        q2 = jnp.where(lane == 0, q1, q2)
        high, low = split(q1)
        r13 = dot(high, z13_ref[...]) + dot(low, z13_ref[...]) + dot(high, z13l_ref[...])
        high2, low2 = split(q2)
        r2 = dot(high2, z2_ref[...])
        r2 = r2[:, :zl] + r2[:, zl:] + dot(low2, z2_ref[:, :zl])
        for part, slot in ((0, i), (1, i + hx)):
            take = slice(part * yl, (part + 1) * yl)
            r1 = r13[take, :zl]
            if edge and part == 1:
                r1 = dot(high[yl:], z1n_ref[...])
                r1 = r1[:, :zl] + r1[:, zl:] + dot(low[yl:], z1n_ref[:, :zl])
            r_ref[pl.ds(slot, yl, stride=nx), :] = r1
            r_ref[pl.ds(span + slot, yl, stride=nx), :] = r2[take]
            r_ref[pl.ds(2 * span + slot, yl, stride=nx), :] = r13[take, zl:]

    def later_slabs(i, carry):
        slabs(i, False)
        return carry

    slabs(0, True)
    lax.fori_loop(1, hx, later_slabs, 0)

    def back_x(mat_ref, values):
        high, low = split(values)
        both = dot(mat_ref[...], high)
        return both[:xl] + both[xl:] + dot(mat_ref[:xl], low)

    def cells(pair, carry):
        here = [[pl.ds(j * span + (2 * pair + k) * nx, nx) for k in range(2)] for j in range(3)]
        h1 = back_x(xs_ref, pair_lanes(r_ref[here[0][0], :], r_ref[here[0][1], :]))
        for k in range(2):
            h23 = back_x(xb_ref, pair_lanes(r_ref[here[1][k], :], r_ref[here[2][k], :]))
            t1 = h1[:, k * zl : (k + 1) * zl] + app_ref[0]
            t2 = h23[:, :zl] + app_ref[1]
            t3 = h23[:, zl:]
            out = pl.ds(2 * pair + k, xl, stride=yl)
            source = src_ref[out, :]
            e_ref[out, :] = 0.5 * (t1 * t1 + t2 * t2 + t3 * t3)
            f_ref[pl.ds(2 * pair + k, xl, stride=yl), :] = source * t1
            f_ref[pl.ds(block + 2 * pair + k, xl, stride=yl), :] = source * t2
            f_ref[pl.ds(2 * block + 2 * pair + k, xl, stride=yl), :] = source * t3
        return carry

    lax.fori_loop(0, yl // 2, cells, 0)


def adjoint_body(
    plan, w1_ref, f_ref, xs_ref, xsl_ref, xb_ref, xbl_ref, z13_ref, z13l_ref, z2_ref, z2l_ref, z1n_ref, z1nl_ref,
    g_ref, fy_ref, ez_ref, fx_ref, base_ref,
    m_ref, s_ref, r_ref, kern_ref,
):
    nx, hx, y2, z2, xl, yl, zl = plan.nx, plan.nx // 2, plan.y2, plan.z2, plan.xl, plan.yl, plan.zl
    span, block = yl * nx, xl * yl

    def along_x(mat_ref, low_ref, values):
        high, low = split(values)
        return dot(mat_ref[...], pair_rows(high, low)) + dot(low_ref[...], high)

    def cells(pair, carry):
        here = [[pl.ds(j * block + 2 * pair + k, xl, stride=yl) for k in range(2)] for j in range(3)]
        u1 = along_x(xs_ref, xsl_ref, pair_lanes(f_ref[here[0][0], :], f_ref[here[0][1], :]))
        for k in range(2):
            u23 = along_x(xb_ref, xbl_ref, pair_lanes(f_ref[here[1][k], :], f_ref[here[2][k], :]))
            row = (2 * pair + k) * nx
            r_ref[pl.ds(row, nx), :] = u1[:, k * zl : (k + 1) * zl]
            r_ref[pl.ds(span + row, nx), :] = u23[:, :zl]
            r_ref[pl.ds(2 * span + row, nx), :] = u23[:, zl:]
        return carry

    lax.fori_loop(0, yl // 2, cells, 0)

    def one_slab(q, kern):
        high, low = split(q)
        spectrum = dot(g_ref[...], jnp.concatenate([high, high, low], axis=0))
        high, low = split(spectrum * kern)
        both = dot(fy_ref[...], high)
        return both[:y2] + both[y2:] + dot(fy_ref[:y2], low)

    def slabs(i, edge):
        u = [
            pair_rows(
                r_ref[pl.ds(j * span + i, yl, stride=nx), :],
                r_ref[pl.ds(j * span + i + hx, yl, stride=nx), :],
            )
            for j in range(3)
        ]
        high1, low1 = split(u[0])
        high3, low3 = split(u[2])
        high, low = pair_lanes(high1, high3), pair_lanes(low1, low3)
        q1 = dot(high, z13_ref[...]) + dot(low, z13_ref[...]) + dot(high, z13l_ref[...])
        if edge:
            mid = dot(pair_lanes(high1, low1), z1n_ref[...]) + dot(high1, z1nl_ref[...])
            q1 = pair_rows(q1[:yl], q1[yl:] + mid[yl:])
        high2, low2 = split(u[1])
        q2 = dot(pair_lanes(high2, low2), z2_ref[...]) + dot(high2, z2l_ref[...])
        first = lax.broadcasted_iota(jnp.int32, q1.shape, 1) == 0
        q1, q2 = jnp.where(first, q2, q1), jnp.where(first, 0.0, q2)
        kern_ref[...] = 1.0 / (base_ref[...] + w1_ref[i])
        even = one_slab(pair_rows(q1[:yl], q2[:yl]), kern_ref[...])
        if edge:
            kern_ref[...] = 1.0 / (base_ref[...] + w1_ref[hx])
        odd = one_slab(pair_rows(q1[yl:], q2[yl:]), kern_ref[...])
        high, low = split(pair_rows(even, odd))
        out = dot(high, ez_ref[...])
        out = out[:, :z2] + out[:, z2:] + dot(low, ez_ref[:, :z2])
        s_ref[pl.ds(i, y2, stride=nx), :] = out[:y2]
        s_ref[pl.ds(i + hx, y2, stride=nx), :] = out[y2:]

    def later_slabs(i, carry):
        slabs(i, False)
        return carry

    slabs(0, True)
    lax.fori_loop(1, hx, later_slabs, 0)

    def back_x(pair, carry):
        planes = pair_lanes(
            s_ref[pl.ds(2 * pair * nx, nx), :], s_ref[pl.ds((2 * pair + 1) * nx, nx), :]
        )
        high, low = split(planes)
        both = dot(fx_ref[...], high)
        out = both[: plan.x2] + both[plan.x2 :] + dot(fx_ref[: plan.x2], low)
        store_plane(m_ref, plan, 2 * pair, out[:, :z2])
        store_plane(m_ref, plan, 2 * pair + 1, out[:, z2:])
        return carry

    lax.fori_loop(0, y2 // 2, back_x, 0)


def spread(block, axis, dim):
    count = lax.axis_size(axis)
    halves = jnp.split(block, 2, axis=dim)
    moved = [
        lax.ppermute(half, axis, [(s, 2 * s + k) for s in range(count // 2)])
        for k, half in enumerate(halves)
    ]
    return moved[0] + moved[1]


def unspread(piece, axis, dim):
    count = lax.axis_size(axis)
    moved = [
        lax.ppermute(piece, axis, [(2 * s + k, s) for s in range(count // 2)]) for k in range(2)
    ]
    return jnp.concatenate(moved, axis=dim)


def halves_of(high_low, axis=0):
    return np.concatenate(high_low, axis=axis)


vmem = pl.BlockSpec(memory_space=pltpu.VMEM)
smem = pl.BlockSpec(memory_space=pltpu.SMEM)
kernel_params = pltpu.CompilerParams(vmem_limit_bytes=60 * 2**20)


def scratch_of(plan):
    return [
        pltpu.VMEM((plan.y2 * plan.nx, plan.z2), jnp.float32),
        pltpu.VMEM((3 * plan.yl * plan.nx, plan.zl), jnp.float32),
        pltpu.VMEM((plan.ny, plan.nz), jnp.float32),
    ]


def field_call(plan, tables, magnet, source, applied):
    t = tables
    xl, yl, zl = plan.xl, plan.yl, plan.zl

    def cat(*arrays):
        return jnp.concatenate(arrays, axis=0)

    fx, fxl = two_parts(t["fx"])
    ez, ezl = two_parts(t["ez"].T)
    fy, fyl = two_parts(t["fy"])
    g1, g1l = [own_rows(p, "gy", yl) for p in two_parts(t["by"].T)]
    g2, g2l = [own_rows(p, "gy", yl) for p in two_parts(t["dy"].T)]
    z1, z1l = [own_cols(p, "gz", zl) for p in two_parts(t["z1"])]
    z2, z2l = [own_cols(p, "gz", zl) for p in two_parts(t["z2"])]
    z3, z3l = [own_cols(p, "gz", zl) for p in two_parts(t["z3"])]
    z1n, z1nl = [own_cols(p, "gz", zl) for p in two_parts(t["z1n"])]
    xs, xsl = [own_rows(p, "gx", xl) for p in two_parts(t["xs"].T)]
    xb, xbl = [own_rows(p, "gx", xl) for p in two_parts(t["bx"].T)]
    rows = xl * yl
    return pl.pallas_call(
        functools.partial(field_body, plan),
        out_shape=[
            jax.ShapeDtypeStruct((3 * rows, zl), jnp.float32),
            jax.ShapeDtypeStruct((rows, zl), jnp.float32),
        ],
        in_specs=[smem, smem] + [vmem] * 16,
        out_specs=[vmem, vmem],
        scratch_shapes=scratch_of(plan),
        compiler_params=kernel_params,
    )(
        jnp.asarray(t["w1"]), applied, magnet.reshape(-1, zl), source.reshape(rows, zl),
        np.concatenate([fx, fx], axis=1), fxl, np.concatenate([ez, ez]), ezl, np.concatenate([fy, fy], axis=1), fyl,
        cat(g1, g2, g1l, g2l), pair_lanes(z1, z3), pair_lanes(z1l, z3l), pair_lanes(z2, z2l),
        pair_lanes(z1n, z1nl), cat(xs, xsl), cat(xb, xbl), jnp.asarray(t["base"]),
    )


def adjoint_call(plan, tables, field):
    t = tables
    xl, yl, zl = plan.xl, plan.yl, plan.zl

    def cat(*arrays):
        return jnp.concatenate(arrays, axis=0)

    xs, xsl = [own_cols(p, "gx", xl) for p in two_parts(t["xs"])]
    xb, xbl = [own_cols(p, "gx", xl) for p in two_parts(t["bx"])]
    z1, z1l = [own_rows(p, "gz", zl) for p in two_parts(t["z1"].T)]
    z2, z2l = [own_rows(p, "gz", zl) for p in two_parts(t["z2"].T)]
    z3, z3l = [own_rows(p, "gz", zl) for p in two_parts(t["z3"].T)]
    z1n, z1nl = [own_rows(p, "gz", zl) for p in two_parts((t["z1n"] - t["z1"]).T)]
    g1, g1l = [own_cols(p, "gy", yl) for p in two_parts(t["by"])]
    g2, g2l = [own_cols(p, "gy", yl) for p in two_parts(t["dy"])]
    fy, fyl = two_parts(t["fy"].T)
    ez, ezl = two_parts(t["ez"])
    fx, fxl = two_parts(t["fx"].T)
    return pl.pallas_call(
        functools.partial(adjoint_body, plan),
        out_shape=jax.ShapeDtypeStruct((plan.x2 * plan.y2 * plan.z2 // zl, zl), jnp.float32),
        in_specs=[smem] + [vmem] * 16,
        out_specs=vmem,
        scratch_shapes=scratch_of(plan),
        compiler_params=kernel_params,
    )(
        jnp.asarray(t["w1"]), field,
        pair_lanes(xs, xs), xsl, pair_lanes(xb, xb), xbl, cat(z1, z3), cat(z1l, z3l), cat(z2, z2), z2l, cat(z1n, z1n), z1nl,
        jnp.concatenate([g1, g2, g1l, g2l, g1, g2], axis=1), np.concatenate([fy, fyl]),
        np.concatenate([ez, ezl], axis=1), np.concatenate([fx, fxl]), jnp.asarray(t["base"]),
    )


def lanes_of(count):
    return -(-count // 128) * 128


def faces_body(chunk, v_ref, a_ref, c_ref, ylo_ref, yhi_ref, zlo_ref, zhi_ref):
    yl, zl = v_ref.shape[2:]
    step = pl.program_id(0)

    @pl.when(step == 0)
    def _():
        zlo_ref[...] = jnp.zeros_like(zlo_ref)
        zhi_ref[...] = jnp.zeros_like(zhi_ref)

    lane = lax.broadcasted_iota(jnp.int32, zlo_ref.shape[1:], 1)
    for field in range(7):
        low, high = zlo_ref[field], zhi_ref[field]
        for k in range(chunk):
            plane = v_ref[field, k] if field < 3 else a_ref[field - 3, k] if field < 6 else c_ref[k]
            ylo_ref[field, k : k + 1, :] = plane[:1]
            yhi_ref[field, k : k + 1, :] = plane[yl - 1 :]
            here = lane == step * chunk + k
            low = jnp.where(here, plane[:, :1], low)
            high = jnp.where(here, plane[:, zl - 1 :], high)
        zlo_ref[field] = low
        zhi_ref[field] = high


def faces_call(velocity, adjoint_seed, susceptibility):
    xl, yl, zl = susceptibility.shape
    chunk = 8
    three = pl.BlockSpec((3, chunk, yl, zl), lambda i: (0, i, 0, 0))
    y_spec = pl.BlockSpec((7, chunk, zl), lambda i: (0, i, 0))
    z_spec = pl.BlockSpec((7, yl, lanes_of(max(xl, zl))), lambda i: (0, 0, 0))
    y_shape = jax.ShapeDtypeStruct((7, xl, zl), jnp.float32)
    z_shape = jax.ShapeDtypeStruct((7, yl, lanes_of(max(xl, zl))), jnp.float32)
    return pl.pallas_call(
        functools.partial(faces_body, chunk),
        grid=(xl // chunk,),
        in_specs=[three, three, pl.BlockSpec((chunk, yl, zl), lambda i: (i, 0, 0))],
        out_specs=[y_spec, y_spec, z_spec, z_spec],
        out_shape=[y_shape, y_shape, z_shape, z_shape],
        compiler_params=kernel_params,
    )(velocity, adjoint_seed, susceptibility)


def to_neighbours(low_face, high_face, axis):
    count = lax.axis_size(axis)
    below = lax.ppermute(high_face, axis, [(i, i + 1) for i in range(count - 1)])
    above = lax.ppermute(low_face, axis, [(i + 1, i) for i in range(count - 1)])
    return below, above


class Around:
    def __init__(self, ref, k, x, y_below, y_above, z_below, z_above):
        mid = ref[k + 1]
        yl, zl = mid.shape
        row = lax.broadcasted_iota(jnp.int32, mid.shape, 0)
        lane = lax.broadcasted_iota(jnp.int32, mid.shape, 1)
        width = z_below.shape[1]
        left = pltpu.roll(z_below, lax.rem(width - x, width), 1)[:, :zl]
        right = pltpu.roll(z_above, lax.rem(width + zl - 1 - x, width), 1)[:, :zl]
        self.mid = mid
        self.less = [
            ref[k],
            jnp.where(row == 0, y_below, pltpu.roll(mid, 1, 0)),
            jnp.where(lane == 0, left, pltpu.roll(mid, 1, 1)),
        ]
        self.more = [
            ref[k + 2],
            jnp.where(row == yl - 1, y_above, pltpu.roll(mid, yl - 1, 0)),
            jnp.where(lane == zl - 1, right, pltpu.roll(mid, zl - 1, 1)),
        ]

    def slope(self, d):
        return (self.more[d] - self.less[d]) * 0.5

    def laplace(self):
        beside = self.more[0] + self.less[0] + self.more[1] + self.less[1]
        return beside + self.more[2] + self.less[2] - 6.0 * self.mid


def fill_window(window, chunk, field, before, block, after, x_below, x_above):
    step, last = pl.program_id(0), pl.num_programs(0) - 1
    for k in range(chunk):
        window[field, k + 1] = block(k)
    window[field, 0] = jnp.where(step == 0, x_below, before)
    window[field, chunk + 1] = jnp.where(step == last, x_above, after)


def adjoint_cells_body(
    chunk, v_ref, vb_ref, va_ref, a_ref, ab_ref, aa_ref, c_ref, cb_ref, ca_ref,
    xlo_ref, xhi_ref, ylo_ref, yhi_ref, zlo_ref, zhi_ref, out_ref, source_ref, window,
):
    for j in range(3):
        fill_window(window, chunk, j, vb_ref[j, 0], lambda k: v_ref[j, k], va_ref[j, 0], xlo_ref[j], xhi_ref[j])
        fill_window(window, chunk, 3 + j, ab_ref[j, 0], lambda k: a_ref[j, k], aa_ref[j, 0], xlo_ref[3 + j], xhi_ref[3 + j])
    fill_window(window, chunk, 6, cb_ref[0], lambda k: c_ref[k], ca_ref[0], xlo_ref[6], xhi_ref[6])
    start = pl.program_id(0) * chunk

    def plane(k, carry):
        at = [
            Around(
                window.at[f], k, start + k,
                ylo_ref[f, pl.ds(k, 1), :], yhi_ref[f, pl.ds(k, 1), :], zlo_ref[f], zhi_ref[f],
            )
            for f in range(7)
        ]
        v, a, c = at[:3], at[3:6], at[6]
        flux = [c.more[i] * a[i].more[i] - c.less[i] * a[i].less[i] for i in range(3)]
        source_ref[k] = (-0.5 * time_step) * (flux[0] + flux[1] + flux[2])
        for j in range(3):
            shear = sum(a[i].mid * (v[i].more[j] - v[i].less[j]) for i in range(3))
            carried = sum(v[i].more[i] * a[j].more[i] - v[i].less[i] * a[j].less[i] for i in range(3))
            out_ref[j, k] = a[j].mid + time_step * (
                viscosity * a[j].laplace() + 0.5 * (carried - shear)
            )
        return carry

    lax.fori_loop(0, chunk, plane, 0)


def next_cells_body(
    chunk, v_ref, vb_ref, va_ref, e_ref, eb_ref, ea_ref, c_ref,
    xlo_ref, xhi_ref, ylo_ref, yhi_ref, zlo_ref, zhi_ref,
    exlo_ref, exhi_ref, eylo_ref, eyhi_ref, ezlo_ref, ezhi_ref, out_ref, window,
):
    for j in range(3):
        fill_window(window, chunk, j, vb_ref[j, 0], lambda k: v_ref[j, k], va_ref[j, 0], xlo_ref[j], xhi_ref[j])
    fill_window(window, chunk, 3, eb_ref[0], lambda k: e_ref[k], ea_ref[0], exlo_ref[...], exhi_ref[...])
    start = pl.program_id(0) * chunk

    def plane(k, carry):
        v = [
            Around(
                window.at[f], k, start + k,
                ylo_ref[f, pl.ds(k, 1), :], yhi_ref[f, pl.ds(k, 1), :], zlo_ref[f], zhi_ref[f],
            )
            for f in range(3)
        ]
        e = Around(
            window.at[3], k, start + k,
            eylo_ref[pl.ds(k, 1), :], eyhi_ref[pl.ds(k, 1), :], ezlo_ref[...], ezhi_ref[...],
        )
        for j in range(3):
            advect = sum(v[i].mid * (v[j].more[i] - v[j].less[i]) for i in range(3))
            pushed = c_ref[k] * (e.more[j] - e.less[j])
            out_ref[j, k] = v[j].mid + time_step * (
                viscosity * v[j].laplace() + 0.5 * (pushed - advect)
            )
        return carry

    lax.fori_loop(0, chunk, plane, 0)


def cell_specs(chunk, xl, yl, zl, lead):
    def at(block, place):
        if lead:
            return pl.BlockSpec((3, block, yl, zl), lambda i: (0, place(i), 0, 0))
        return pl.BlockSpec((block, yl, zl), lambda i: (place(i), 0, 0))

    return [
        at(chunk, lambda i: i),
        at(1, lambda i: jnp.maximum(i * chunk - 1, 0)),
        at(1, lambda i: jnp.minimum((i + 1) * chunk, xl - 1)),
    ]


def face_specs(chunk, yl, zl, width, fields):
    def spec(shape, index):
        return pl.BlockSpec((fields, *shape), lambda i: (0, *index(i)))

    x_spec = spec((yl, zl), lambda i: (0, 0))
    y_spec = spec((chunk, zl), lambda i: (i, 0))
    z_spec = spec((yl, width), lambda i: (0, 0))
    return [x_spec, x_spec, y_spec, y_spec, z_spec, z_spec]


def adjoint_cells_call(velocity, adjoint_seed, susceptibility, faces):
    xl, yl, zl = susceptibility.shape
    chunk = 8
    three = cell_specs(chunk, xl, yl, zl, True)
    one = cell_specs(chunk, xl, yl, zl, False)
    v, a, c = velocity, adjoint_seed, susceptibility
    return pl.pallas_call(
        functools.partial(adjoint_cells_body, chunk),
        grid=(xl // chunk,),
        in_specs=three + three + one + face_specs(chunk, yl, zl, lanes_of(max(xl, zl)), 7),
        out_specs=[three[0], one[0]],
        out_shape=[
            jax.ShapeDtypeStruct(v.shape, jnp.float32),
            jax.ShapeDtypeStruct(c.shape, jnp.float32),
        ],
        scratch_shapes=[pltpu.VMEM((7, chunk + 2, yl, zl), jnp.float32)],
        compiler_params=kernel_params,
    )(v, v, v, a, a, a, c, c, c, *faces)


def next_cells_call(velocity, energy, susceptibility, faces, energy_faces):
    xl, yl, zl = susceptibility.shape
    chunk = 8
    three = cell_specs(chunk, xl, yl, zl, True)
    one = cell_specs(chunk, xl, yl, zl, False)
    width = lanes_of(max(xl, zl))
    energy_specs = [
        pl.BlockSpec((yl, zl), lambda i: (0, 0)),
        pl.BlockSpec((chunk, zl), lambda i: (i, 0)),
        pl.BlockSpec((yl, width), lambda i: (0, 0)),
    ]
    energy_specs = [spec for spec in energy_specs for _ in range(2)]
    v, e, c = velocity, energy, susceptibility
    return pl.pallas_call(
        functools.partial(next_cells_body, chunk),
        grid=(xl // chunk,),
        in_specs=three + one + one[:1] + face_specs(chunk, yl, zl, width, 3) + energy_specs,
        out_specs=three[0],
        out_shape=jax.ShapeDtypeStruct(v.shape, jnp.float32),
        scratch_shapes=[pltpu.VMEM((4, chunk + 2, yl, zl), jnp.float32)],
        compiler_params=kernel_params,
    )(v, v, v, e, e, e, c, *faces, *energy_faces)


def on_device(mesh, velocity, adjoint_seed, susceptibility, remanence, region_bounds, step_id):
    plan = Plan(mesh, susceptibility.shape)
    tables = forward_tables(plan)
    places = [
        lax.axis_index(a) * n + jnp.arange(n, dtype=jnp.int32)
        for a, n in zip(axes, susceptibility.shape)
    ]
    inside = [
        (place >= region_bounds[0, d]) & (place < region_bounds[1, d])
        for d, place in enumerate(places)
    ]
    region_mask = (
        inside[0][:, None, None] & inside[1][None, :, None] & inside[2][None, None, :]
    ).astype(jnp.float32)
    magnet = spread(spread(spread(remanence * region_mask, "gx", 0), "gz", 0), "gy", 1)
    magnet = lax.all_gather(magnet, axes)
    stacked = [
        jnp.concatenate([velocity[:, x], adjoint_seed[:, x], susceptibility[None, x]], axis=0)
        for x in (0, plan.xl - 1)
    ]
    ylo, yhi, zlo, zhi = faces_call(velocity, adjoint_seed, susceptibility)
    faces = [
        *to_neighbours(*stacked, "gx"), *to_neighbours(ylo, yhi, "gy"), *to_neighbours(zlo, zhi, "gz"),
    ]
    velocity_adjoint, source = adjoint_cells_call(velocity, adjoint_seed, susceptibility, faces)
    phase_angle = full_turn * (step_id[0] % field_period).astype(jnp.float32) / field_period
    applied = jnp.stack([jnp.cos(phase_angle), jnp.sin(phase_angle)])
    field_adjoint, energy = field_call(plan, tables, magnet, source, applied)
    partial_sums = adjoint_call(plan, tables, field_adjoint)
    piece = lax.psum_scatter(
        partial_sums.reshape(-1, plan.px, plan.py, plan.zl), axes, scatter_dimension=0
    )
    magnet_adjoint = unspread(unspread(unspread(piece, "gy", 1), "gz", 0), "gx", 0)
    design_gradient = region_mask * magnet_adjoint
    energy = energy.reshape(susceptibility.shape)
    ends = [energy[..., z].T for z in (0, plan.zl - 1)]
    ends = [jnp.pad(end, ((0, 0), (0, lanes_of(max(plan.xl, plan.zl)) - plan.xl))) for end in ends]
    energy_faces = [
        *to_neighbours(energy[0], energy[-1], "gx"),
        *to_neighbours(energy[:, 0], energy[:, -1], "gy"),
        *to_neighbours(*ends, "gz"),
    ]
    next_velocity = next_cells_call(velocity, energy, susceptibility, faces, energy_faces)
    return (next_velocity, velocity_adjoint, design_gradient)


def solution(mesh):
    cells = P(*axes)
    vectors = P(None, *axes)
    return jax.shard_map(
        functools.partial(on_device, mesh),
        mesh=mesh,
        in_specs=(vectors, vectors, cells, cells, P(), P()),
        out_specs=(vectors, vectors, cells),
        check_vma=False,
    )
```

time: 2560 us -> 838 us (0.33)
  waiting for transfers between devices: 1480 us -> 265 us
  Pallas kernels: 0 us -> 455 us
  other arithmetic: 384 us -> 20.2 us
  matrix products: 258 us -> 0 us
  local copies, waits for them, and re-layouts: 264 us -> 24.7 us
  starting transfers between devices: 142 us -> 50 us
    all_to_all x16 -> x0, waiting for transfers between devices: 1090 us -> none  [the longest x4 289 us: row_turn(): lax.all_to_all(real_part, ('gx', 'gy'), split_axis=2, concat_axis=1, tile...]
    pallas_call x0 -> x5, Pallas kernels: none -> 455 us  [the longest x1 195 us: field_call(): pl.pallas_call(functools.partial(field_body, plan), out_shape=[jax.ShapeD...]
    dot_general x40 -> x0, matrix products: 258 us -> none  [the longest x8 50 us: rotate(): real_cos = jnp.einsum(form, real_part, cosine, precision=highest)]
    concatenate x6 -> x15, other arithmetic: 138 us -> 8.57 us  [the longest x7 4.58 us: cat(): return jnp.concatenate(arrays, axis=0)]
    another operation x9 -> x1, other arithmetic: 112 us -> 0.56 us  [on_device(): applied = jnp.stack([jnp.cos(phase_angle), jnp.sin(phase_angle)])]
    reduce_scatter x2 -> x1, waiting for transfers between devices: 279 us -> 182 us  [on_device(): lax.psum_scatter(partial_sums.reshape(-1, plan.px, plan.py, plan.zl), axe...]
    all_to_all x16 -> x0, starting transfers between devices: 95 us -> none  [the longest x4 27.3 us: column_turn(): lax.all_to_all(real_part, 'gy', split_axis=1, concat_axis=2, tiled=True)]
    add x4 -> x3, other arithmetic: 69.6 us -> 1.02 us  [spread(): return moved[0] + moved[1]]
  transfers between devices with their start and end apart: 33 -> 26, of which waited for: 19 -> 11; matrix products, arithmetic and copies ran while one was open for 25% -> 3% of each run, Pallas kernels for 0% -> 9%
where the time goes in v1:
time: 838 us; the launch traced here: 830 us
  Pallas kernels  455 us (54%)
  waiting for transfers between devices  265 us (32%)
  starting transfers between devices  50 us (6%)
  local copies, waits for them, and re-layouts  24.7 us (3%)
  other arithmetic  20.2 us (2%)
  between operations  15.6 us (2%)
    pallas_call x1, Pallas kernels, field_call(): pl.pallas_call(functools.partial(field_body, plan), out_shape=[jax.ShapeD...  195 us
    pallas_call x1, Pallas kernels, adjoint_call(): pl.pallas_call(functools.partial(adjoint_body, plan), out_shape=jax.Shape...  189 us
    reduce_scatter x1, waiting for transfers between devices, on_device(): lax.psum_scatter(partial_sums.reshape(-1, plan.px, plan.py, plan.zl), axe...  182 us
    ppermute x6, waiting for transfers between devices, spread(): lax.ppermute(half, axis, [(s, 2 * s + k) for s in range(count // 2)])  46.4 us
    pallas_call x1, Pallas kernels, adjoint_cells_call(): pl.pallas_call(functools.partial(adjoint_cells_body, chunk), grid=(xl //...  30.4 us
    pallas_call x1, Pallas kernels, next_cells_call(): pl.pallas_call(functools.partial(next_cells_body, chunk), grid=(xl // chu...  23.6 us
    ppermute x6, waiting for transfers between devices, unspread(): lax.ppermute(piece, axis, [(2 * s + k, s) for s in range(count // 2)])  22.6 us
    pallas_call x1, Pallas kernels, faces_call(): pl.pallas_call(functools.partial(faces_body, chunk), grid=(xl // chunk,),...  16.9 us
  transfers between devices with their start and end apart: 26, of which 11 were waited for; matrix products, arithmetic and copies ran while one was open for 3% of the time, Pallas kernels for 9%

profile of v1, /device:TPU:12, one launch (start us, length us, event | category | flops | bytes accessed | tf_op | source)
XLA Modules:
  0.0 830.5 jit_solution(11546961275738149271)
XLA Ops:
  7.2 1.6 fusion.7
  8.8 1.3 compare_and_fusion.1
  10.1 1.3 compare_and_fusion.2
  11.5 1.3 compare_and_fusion
  12.7 2.9 and_select_fusion.1
  15.8 0.7 collective-permute-start
  16.6 1.3 collective-permute-start.1
  17.9 25.5 %collective-permute-done.1 = f32[64,32,128]{2,1,0:T(8,128)S(1)} collective-permute-done((f32[64,32,128]{2,1,0:T(8,128)S(1)}, f32[64,32,128]{2,1,0:T(8,128)S(1)}, u32[]{:S(2)}, u32[]{:S(2)}) %collective-permute-start.1) | collective-permute-done | bytes 1048608 | tf_op jit(solution)/shard_map/ppermute | solution.py:318
  43.6 0.7 collective-permute-start.2
  44.3 3.4 collective-permute-start.3
  47.8 10.2 %collective-permute-done.3 = f32[32,32,128]{2,1,0:T(8,128)S(1)} collective-permute-done((f32[32,32,128]{2,1,0:T(8,128)S(1)}, f32[32,32,128]{2,1,0:T(8,128)S(1)}, u32[]{:S(2)}, u32[]{:S(2)}) %collective-permute-start.3) | collective-permute-done | bytes 524320 | tf_op jit(solution)/shard_map/ppermute | solution.py:318
  58.2 3.5 collective-permute-start.4
  61.6 1.3 collective-permute-start.5
  63.0 5.0 collective-permute-done.4
  68.0 5.6 collective-permute-done.5
  73.6 0.7 add.92
  74.4 0.7 fusion.3
  75.1 0.9 slice_bitcast_fusion
  76.0 1.3 collective-permute-start.6
  77.4 4.7 collective-permute-start.7
  82.1 16.9 %shard_map.472 = (f32[7,128,128]{2,1,0:T(8,128)}, f32[7,128,128]{2,1,0:T(8,128)}, f32[7,32,128]{2,1,0:T(8,128)}, f32[7,32,128]{2,1,0:T(8,128)}) custom-call(f32[3,128,32,128]{3,2,1,0:T(8,128)} %va_ref.3, f32[3,128,32,128]{3,2,1,0:T(8,128)} %aa_ref.1, f32[128,32,128]{2,1,0:T(8,128)} %c_ref.5), custom_call_target="tpu_custom_call" | custom-call | tf_op jit(solution)/shard_map/pallas_call | solution.py:454
  99.1 2.1 collective-permute-start.8
  101.2 3.6 collective-permute-start.9
  104.8 4.4 collective-permute-start.10
  110.3 0.8 concatenate.72.g_ref
  111.2 0.8 constant_dynamic-slice_fusion.30
  112.6 0.9 constant_dynamic-slice_fusion.24
  113.5 0.9 constant_dynamic-slice_fusion.8
  114.4 0.9 constant_dynamic-slice_fusion.5
  116.6 0.8 constant_dynamic-slice_fusion.13
  118.9 1.5 constant_dynamic-slice_fusion.12
  120.4 0.8 constant_dynamic-slice_fusion.26
  121.2 0.7 pad_maximum_fusion.z13_ref
  127.1 1.3 collective-permute-start.11
  128.5 0.7 constant_dynamic-slice_fusion.4
  129.1 7.4 collective-permute-done.11.zhi_ref
  137.4 0.8 copy-done.2
  138.2 30.4 %shard_map.473 = (f32[3,128,32,128]{3,2,1,0:T(8,128)}, f32[128,32,128]{2,1,0:T(8,128)}) custom-call(f32[3,128,32,128]{3,2,1,0:T(8,128)} %va_ref.3, f32[3,128,32,128]{3,2,1,0:T(8,128)} %va_ref.3, f32[3,128,32,128]{3,2,1,0:T(8,128)} %va_ref.3, f32[3,128,32,128]{3,2,1,0:T(8,128)} %aa_ref.1, f32[3,128,32,128]{3,2,1,0:T(8,128)} %aa_ref.1, ...), custom_call_target="tpu_custom_call" | custom-call | tf_op jit(solution)/shard_map/pallas_call | solution.py:602
  168.6 195.4 %shard_map.474 = (f32[12288,128]{1,0:T(8,128)}, f32[4096,128]{1,0:T(8,128)}) custom-call(f32[256]{0:T(256)} %constant.121.clone.w1_ref, f32[2]{0:T(128)} %pad_maximum_fusion.15.app_ref, f32[16384,128]{1,0:T(8,128)} %bitcast.48, f32[4096,128]{1,0:T(8,128)} %bitcast.49, bf16[256,256]{1,0:T(8,128)(2,1)} %constant.123.clone.fx_ref.fy_ref, ...), custom_call_target="tpu_custom_call" | custom-call | tf_op jit(solution)/shard_map/pallas_call | solution.py:368
  364.1 189.0 %shard_map.476 = f32[16384,128]{1,0:T(8,128)} custom-call(f32[256]{0:T(256)} %constant.121.clone.w1_ref, f32[12288,128]{1,0:T(8,128)} %get-tuple-element.18.f_ref, bf16[256,256]{1,0:T(8,128)(2,1)} %pad_maximum_fusion.6.xs_ref, bf16[256,128]{1,0:T(8,128)(2,1)} %get-tuple-element.70.xsl_ref, bf16[256,256]{1,0:T(8,128)(2,1)} %pad_maximum_fusion.7.xb_ref, ...), custom_call_target="tpu_custom_call" | custom-call | tf_op jit(solution)/shard_map/pallas_call | solution.py:404
  553.1 182.5 %reduce-scatter.2.cloned.1.call-done = f32[1,32,16,128]{3,2,1,0:T(8,128)} async-done(((f32[32,32,16,128]{3,2,1,0:T(8,128)}), f32[1,32,16,128]{3,2,1,0:T(8,128)}) %reduce-scatter.2.cloned.1.call-update) | async-done | bytes 262160 | tf_op jit(solution)/shard_map/reduce_scatter | solution.py:669
  735.6 1.9 collective-permute-start.18
  737.5 1.3 collective-permute-start.19
  738.8 13.6 %collective-permute-done.18 = f32[32,16,128]{2,1,0:T(8,128)S(1)} collective-permute-done((f32[32,16,128]{2,1,0:T(8,128)}, f32[32,16,128]{2,1,0:T(8,128)S(1)}, u32[]{:S(2)}, u32[]{:S(2)}) %collective-permute-start.18) | collective-permute-done | bytes 262176 | tf_op jit(solution)/shard_map/ppermute | solution.py:327
  752.5 0.7 collective-permute-start.20
  753.2 1.3 collective-permute-start.21
  754.5 0.8 constant_dynamic-update-slice_fusion.3
  755.3 8.9 %collective-permute-done.21 = f32[32,32,128]{2,1,0:T(8,128)S(1)} collective-permute-done((f32[32,32,128]{2,1,0:T(8,128)S(1)}, f32[32,32,128]{2,1,0:T(8,128)S(1)}, u32[]{:S(2)}, u32[]{:S(2)}) %collective-permute-start.21) | collective-permute-done | bytes 524320 | tf_op jit(solution)/shard_map/ppermute | solution.py:327
  764.3 0.8 constant_dynamic-update-slice_fusion.2
  765.1 0.7 collective-permute-start.22
  765.8 4.6 collective-permute-start.23
  770.4 2.8 fusion
  773.1 2.7 copy.83
  775.8 1.4 collective-permute-start.16
  777.3 2.7 copy.84
  780.0 1.3 collective-permute-start.17
  781.3 1.9 collective-permute-start.14
  783.2 3.6 collective-permute-start.15
  786.9 1.3 collective-permute-start.12
  788.2 4.3 collective-permute-done.12.exlo_ref
  792.5 1.6 collective-permute-start.13
  794.2 1.4 collective-permute-done.13.exhi_ref
  796.8 23.6 %shard_map.475 = f32[3,128,32,128]{3,2,1,0:T(8,128)} custom-call(f32[3,128,32,128]{3,2,1,0:T(8,128)} %va_ref.3, f32[3,128,32,128]{3,2,1,0:T(8,128)} %va_ref.3, f32[3,128,32,128]{3,2,1,0:T(8,128)} %va_ref.3, f32[128,32,128]{2,1,0:T(8,128)} %bitcast.42, f32[128,32,128]{2,1,0:T(8,128)} %bitcast.43, f32[128,32,128]{2,1,0:T(8,128)} %bitcast.44, ...), custom_call_target="tpu_custom_call" | custom-call | tf_op jit(solution)/shard_map/pallas_call | solution.py:629
  820.5 3.2 and_select_fusion
  (116 shorter events, 11.9 us)
Async XLA Ops:
  7.2 161.5 %all-gather.3.cloned.1.call-start = ((), (), s32[]{:S(2)}) async-start(), calls=%async_computation.2 | async-start | bytes 8650752 | tf_op jit(solution)/shard_map/all_gather | solution.py:655
  15.8 2.0 collective-permute-start
  16.6 26.8 %collective-permute-start.1 = (f32[64,32,128]{2,1,0:T(8,128)S(1)}, f32[64,32,128]{2,1,0:T(8,128)S(1)}, u32[]{:S(2)}, u32[]{:S(2)}) collective-permute-start(f32[64,32,128]{2,1,0:T(8,128)S(1)} %get-tuple-element.31), channel_id=1, source_target_pairs={{0,16},{1,17},{2,18},{3,19},{4,20},{5,21},{6,22},{7,23},{8,24},{9,... | collective-permute-start | bytes 3145736 | tf_op jit(solution)/shard_map/ppermute | solution.py:318
  43.6 4.1 collective-permute-start.2
  44.3 13.7 %collective-permute-start.3 = (f32[32,32,128]{2,1,0:T(8,128)S(1)}, f32[32,32,128]{2,1,0:T(8,128)S(1)}, u32[]{:S(2)}, u32[]{:S(2)}) collective-permute-start(f32[32,32,128]{2,1,0:T(8,128)S(1)} %get-tuple-element.33), channel_id=1, source_target_pairs={{0,1},{2,3},{4,5},{6,7},{8,9},{10,11},{12,13},{14,15},{16,17},{18,... | collective-permute-start | bytes 1572872 | tf_op jit(solution)/shard_map/ppermute | solution.py:318
  58.2 9.8 %collective-permute-start.4 = (f32[32,16,128]{2,1,0:T(8,128)S(1)}, f32[32,16,128]{2,1,0:T(8,128)S(1)}, u32[]{:S(2)}, u32[]{:S(2)}) collective-permute-start(f32[32,16,128]{2,1,0:T(8,128)S(1)} %get-tuple-element.36), channel_id=1, source_target_pairs={{0,0},{2,4},{4,8},{6,12},{1,1},{3,5},{5,9},{7,13},{16,16},{18,20},... | collective-permute-start | bytes 786440 | tf_op jit(solution)/shard_map/ppermute | solution.py:318
  61.6 11.9 %collective-permute-start.5 = (f32[32,16,128]{2,1,0:T(8,128)S(1)}, f32[32,16,128]{2,1,0:T(8,128)S(1)}, u32[]{:S(2)}, u32[]{:S(2)}) collective-permute-start(f32[32,16,128]{2,1,0:T(8,128)S(1)} %get-tuple-element.35), channel_id=1, source_target_pairs={{0,2},{2,6},{4,10},{6,14},{1,3},{3,7},{5,11},{7,15},{16,18},{18,22... | collective-permute-start | bytes 786440 | tf_op jit(solution)/shard_map/ppermute | solution.py:318
  74.3 661.3 %reduce-scatter.2.cloned.1.call-start = ((), (), s32[]{:S(2)}) async-start(), calls=%async_computation.1 | async-start | bytes 8650752 | tf_op jit(solution)/shard_map/reduce_scatter | solution.py:669
  76.0 51.1 %collective-permute-start.6 = (f32[7,32,128]{2,1,0:T(8,128)S(1)}, f32[7,32,128]{2,1,0:T(8,128)S(1)}, u32[]{:S(2)}, u32[]{:S(2)}) collective-permute-start(f32[7,32,128]{2,1,0:T(8,128)S(1)} %pad_maximum_fusion.12), channel_id=1, source_target_pairs={{0,16},{1,17},{2,18},{3,19},{4,20},{5,21},{6,22},{7,23},{8,24},{9,... | collective-permute-start | bytes 344072 | tf_op jit(solution)/shard_map/ppermute | solution.py:466
  77.4 32.6 %copy-start.7 = (bf16[256,256]{1,0:T(8,128)(2,1)S(1)}, bf16[256,256]{1,0:T(8,128)(2,1)}, u32[]{:S(2)}) copy-start(bf16[256,256]{1,0:T(8,128)(2,1)} %constant.130.clone) | copy-start | bytes 393220
  77.4 32.6 %copy-start.9 = (bf16[256,256]{1,0:T(8,128)(2,1)S(1)}, bf16[256,256]{1,0:T(8,128)(2,1)}, u32[]{:S(2)}) copy-start(bf16[256,256]{1,0:T(8,128)(2,1)} %constant.112.clone) | copy-start | bytes 393220
  77.4 32.8 %copy-start.8 = (bf16[256,256]{1,0:T(8,128)(2,1)S(1)}, bf16[256,256]{1,0:T(8,128)(2,1)}, u32[]{:S(2)}) copy-start(bf16[256,256]{1,0:T(8,128)(2,1)} %constant.129.clone) | copy-start | bytes 393220
  77.4 32.7 %copy-start.26 = (bf16[256,256]{1,0:T(8,128)(2,1)S(1)}, bf16[256,256]{1,0:T(8,128)(2,1)}, u32[]{:S(2)}) copy-start(bf16[256,256]{1,0:T(8,128)(2,1)} %constant.138.clone) | copy-start | bytes 393220
  77.4 33.7 %copy-start.12 = (bf16[256,256]{1,0:T(8,128)(2,1)S(1)}, bf16[256,256]{1,0:T(8,128)(2,1)}, u32[]{:S(2)}) copy-start(bf16[256,256]{1,0:T(8,128)(2,1)} %constant.110.clone) | copy-start | bytes 393220
  77.4 33.7 %copy-start.13 = (bf16[256,256]{1,0:T(8,128)(2,1)S(1)}, bf16[256,256]{1,0:T(8,128)(2,1)}, u32[]{:S(2)}) copy-start(bf16[256,256]{1,0:T(8,128)(2,1)} %constant.108.clone) | copy-start | bytes 393220
  77.4 33.7 %copy-start.14 = (bf16[256,256]{1,0:T(8,128)(2,1)S(1)}, bf16[256,256]{1,0:T(8,128)(2,1)}, u32[]{:S(2)}) copy-start(bf16[256,256]{1,0:T(8,128)(2,1)} %constant.107.clone) | copy-start | bytes 393220
  77.4 51.7 %collective-permute-start.7 = (f32[7,32,128]{2,1,0:T(8,128)S(1)}, f32[7,32,128]{2,1,0:T(8,128)S(1)}, u32[]{:S(2)}, u32[]{:S(2)}) collective-permute-start(f32[7,32,128]{2,1,0:T(8,128)S(1)} %pad_maximum_fusion.13), channel_id=1, source_target_pairs={{16,0},{17,1},{18,2},{19,3},{20,4},{21,5},{22,6},{23,7},{24,8},{25... | collective-permute-start | bytes 344072 | tf_op jit(solution)/shard_map/ppermute | solution.py:467
  99.1 21.3 %copy-start.25 = (bf16[256,256]{1,0:T(8,128)(2,1)S(1)}, bf16[256,256]{1,0:T(8,128)(2,1)}, u32[]{:S(2)}) copy-start(bf16[256,256]{1,0:T(8,128)(2,1)} %constant.111.clone) | copy-start | bytes 393220
  99.1 37.5 %collective-permute-start.8 = (f32[7,128,128]{2,1,0:T(8,128)}, f32[7,128,128]{2,1,0:T(8,128)S(1)}, u32[]{:S(2)}, u32[]{:S(2)}) collective-permute-start(f32[7,128,128]{2,1,0:T(8,128)} %get-tuple-element.11), channel_id=1, source_target_pairs={{0,2},{2,4},{4,6},{6,8},{8,10},{10,12},{12,14},{1,3},{3,5},{5,7},{... | collective-permute-start | bytes 1376264 | tf_op jit(solution)/shard_map/ppermute | solution.py:466
  101.2 35.4 %collective-permute-start.9 = (f32[7,128,128]{2,1,0:T(8,128)}, f32[7,128,128]{2,1,0:T(8,128)S(1)}, u32[]{:S(2)}, u32[]{:S(2)}) collective-permute-start(f32[7,128,128]{2,1,0:T(8,128)} %get-tuple-element.12), channel_id=1, source_target_pairs={{2,0},{4,2},{6,4},{8,6},{10,8},{12,10},{14,12},{3,1},{5,3},{7,5},{... | collective-permute-start | bytes 1376264 | tf_op jit(solution)/shard_map/ppermute | solution.py:467
  104.8 24.3 %collective-permute-start.10 = (f32[7,32,128]{2,1,0:T(8,128)}, f32[7,32,128]{2,1,0:T(8,128)S(1)}, u32[]{:S(2)}, u32[]{:S(2)}) collective-permute-start(f32[7,32,128]{2,1,0:T(8,128)} %get-tuple-element.13), channel_id=1, source_target_pairs={{0,1},{2,3},{4,5},{6,7},{8,9},{10,11},{12,13},{14,15},{16,17},{18,... | collective-permute-start | bytes 344072 | tf_op jit(solution)/shard_map/ppermute | solution.py:466
  110.1 12.4 %copy-start.23 = (bf16[256,256]{1,0:T(8,128)(2,1)S(1)}, bf16[256,256]{1,0:T(8,128)(2,1)}, u32[]{:S(2)}) copy-start(bf16[256,256]{1,0:T(8,128)(2,1)} %constant.113.clone) | copy-start | bytes 393220
  110.2 12.4 %copy-start.24 = (bf16[256,256]{1,0:T(8,128)(2,1)S(1)}, bf16[256,256]{1,0:T(8,128)(2,1)}, u32[]{:S(2)}) copy-start(bf16[256,256]{1,0:T(8,128)(2,1)} %constant.114.clone) | copy-start | bytes 393220
  111.1 12.1 %copy-start.21 = (bf16[256,256]{1,0:T(8,128)(2,1)S(1)}, bf16[256,256]{1,0:T(8,128)(2,1)}, u32[]{:S(2)}) copy-start(bf16[256,256]{1,0:T(8,128)(2,1)} %constant.117.clone) | copy-start | bytes 393220
  111.1 12.1 %copy-start.22 = (bf16[256,256]{1,0:T(8,128)(2,1)S(1)}, bf16[256,256]{1,0:T(8,128)(2,1)}, u32[]{:S(2)}) copy-start(bf16[256,256]{1,0:T(8,128)(2,1)} %constant.118.clone) | copy-start | bytes 393220
  112.6 11.3 %copy-start.19 = (bf16[256,256]{1,0:T(8,128)(2,1)S(1)}, bf16[256,256]{1,0:T(8,128)(2,1)}, u32[]{:S(2)}) copy-start(bf16[256,256]{1,0:T(8,128)(2,1)} %constant.119.clone) | copy-start | bytes 393220
  112.6 11.3 %copy-start.20 = (bf16[256,256]{1,0:T(8,128)(2,1)S(1)}, bf16[256,256]{1,0:T(8,128)(2,1)}, u32[]{:S(2)}) copy-start(bf16[256,256]{1,0:T(8,128)(2,1)} %constant.120.clone) | copy-start | bytes 393220
  114.4 10.9 %copy-start.17 = (bf16[256,256]{1,0:T(8,128)(2,1)S(1)}, bf16[256,256]{1,0:T(8,128)(2,1)}, u32[]{:S(2)}) copy-start(bf16[256,256]{1,0:T(8,128)(2,1)} %constant.131.clone) | copy-start | bytes 393220
  114.4 10.9 %copy-start.18 = (bf16[256,256]{1,0:T(8,128)(2,1)S(1)}, bf16[256,256]{1,0:T(8,128)(2,1)}, u32[]{:S(2)}) copy-start(bf16[256,256]{1,0:T(8,128)(2,1)} %constant.134.clone) | copy-start | bytes 393220
  117.5 9.6 %copy-start.31 = (f32[7,32,128]{2,1,0:T(8,128)S(1)}, f32[7,32,128]{2,1,0:T(8,128)}, u32[]{:S(2)}) copy-start(f32[7,32,128]{2,1,0:T(8,128)} %get-tuple-element.14) | copy-start | bytes 344068
  117.5 10.9 %copy-start.15 = (bf16[256,256]{1,0:T(8,128)(2,1)S(1)}, bf16[256,256]{1,0:T(8,128)(2,1)}, u32[]{:S(2)}) copy-start(bf16[256,256]{1,0:T(8,128)(2,1)} %constant.133.clone) | copy-start | bytes 393220
  117.5 10.9 %copy-start.16 = (bf16[256,256]{1,0:T(8,128)(2,1)S(1)}, bf16[256,256]{1,0:T(8,128)(2,1)}, u32[]{:S(2)}) copy-start(bf16[256,256]{1,0:T(8,128)(2,1)} %constant.137.clone) | copy-start | bytes 393220
  127.1 9.5 %copy-start.3 = (f32[7,32,128]{2,1,0:T(8,128)}, f32[7,32,128]{2,1,0:T(8,128)S(1)}, u32[]{:S(2)}) copy-start(f32[7,32,128]{2,1,0:T(8,128)S(1)} %collective-permute-done.6.xlo_ref) | copy-start | bytes 344068
  127.1 9.4 %collective-permute-start.11 = (f32[7,32,128]{2,1,0:T(8,128)S(1)}, f32[7,32,128]{2,1,0:T(8,128)S(1)}, u32[]{:S(2)}, u32[]{:S(2)}) collective-permute-start(f32[7,32,128]{2,1,0:T(8,128)S(1)} %copy-done.31), channel_id=1, source_target_pairs={{1,0},{3,2},{5,4},{7,6},{9,8},{11,10},{13,12},{15,14},{17,16},{19,... | collective-permute-start | bytes 344072 | tf_op jit(solution)/shard_map/ppermute | solution.py:467
  129.1 7.5 copy-start.4
  129.1 7.5 copy-start.5
  136.6 0.7 copy-start.6
  136.6 0.8 copy-start.1
  137.4 0.8 copy-start.2
  553.1 217.3 %copy-start = (f32[4096,128]{1,0:T(8,128)S(1)}, f32[4096,128]{1,0:T(8,128)}, u32[]{:S(2)}) copy-start(f32[4096,128]{1,0:T(8,128)} %get-tuple-element.16) | copy-start | bytes 6291460
  735.6 16.8 %collective-permute-start.18 = (f32[32,16,128]{2,1,0:T(8,128)}, f32[32,16,128]{2,1,0:T(8,128)S(1)}, u32[]{:S(2)}, u32[]{:S(2)}) collective-permute-start(f32[32,16,128]{2,1,0:T(8,128)} %bitcast.54), channel_id=1, source_target_pairs={{0,0},{4,2},{8,4},{12,6},{1,1},{5,3},{9,5},{13,7},{16,16},{20,18},... | collective-permute-start | bytes 786440 | tf_op jit(solution)/shard_map/ppermute | solution.py:327
  737.5 15.0 %collective-permute-start.19 = (f32[32,16,128]{2,1,0:T(8,128)}, f32[32,16,128]{2,1,0:T(8,128)S(1)}, u32[]{:S(2)}, u32[]{:S(2)}) collective-permute-start(f32[32,16,128]{2,1,0:T(8,128)} %bitcast.55), channel_id=1, source_target_pairs={{2,0},{6,2},{10,4},{14,6},{3,1},{7,3},{11,5},{15,7},{18,16},{22,18... | collective-permute-start | bytes 786440 | tf_op jit(solution)/shard_map/ppermute | solution.py:327
  752.5 2.0 collective-permute-start.20
  753.2 11.1 %collective-permute-start.21 = (f32[32,32,128]{2,1,0:T(8,128)S(1)}, f32[32,32,128]{2,1,0:T(8,128)S(1)}, u32[]{:S(2)}, u32[]{:S(2)}) collective-permute-start(f32[32,32,128]{2,1,0:T(8,128)S(1)} %constant_dynamic-update-slice_fusion), channel_id=1, source_target_pairs={{1,0},{3,2},{5,4},{7,6},{9,8},{11,10},{13,12},{15,14},{17,16},{19,... | collective-permute-start | bytes 1572872 | tf_op jit(solution)/shard_map/ppermute | solution.py:327
  765.1 55.3 %collective-permute-start.22 = (f32[64,32,128]{2,1,0:T(8,128)}, f32[64,32,128]{2,1,0:T(8,128)S(1)}, u32[]{:S(2)}, u32[]{:S(2)}) collective-permute-start(f32[64,32,128]{2,1,0:T(8,128)} %constant_dynamic-update-slice_fusion.2), channel_id=1, source_target_pairs={{0,0},{1,1},{2,2},{3,3},{4,4},{5,5},{6,6},{7,7},{8,8},{9,9},{10,10... | collective-permute-start | bytes 3145736 | tf_op jit(solution)/shard_map/ppermute | solution.py:327
  765.8 54.6 %collective-permute-start.23 = (f32[64,32,128]{2,1,0:T(8,128)}, f32[64,32,128]{2,1,0:T(8,128)}, u32[]{:S(2)}, u32[]{:S(2)}) collective-permute-start(f32[64,32,128]{2,1,0:T(8,128)} %constant_dynamic-update-slice_fusion.2), channel_id=1, source_target_pairs={{16,0},{17,1},{18,2},{19,3},{20,4},{21,5},{22,6},{23,7},{24,8},{25... | collective-permute-start | bytes 3145736 | tf_op jit(solution)/shard_map/ppermute | solution.py:327
  775.8 7.4 collective-permute-start.16
  780.0 6.9 collective-permute-start.17
  781.3 14.3 %collective-permute-start.14 = (f32[128,128]{1,0:T(8,128)S(1)}, f32[128,128]{1,0:T(8,128)S(1)}, u32[]{:S(2)}, u32[]{:S(2)}) collective-permute-start(f32[128,128]{1,0:T(8,128)S(1)} %bitcast.51), channel_id=1, source_target_pairs={{0,2},{2,4},{4,6},{6,8},{8,10},{10,12},{12,14},{1,3},{3,5},{5,7},{... | collective-permute-start | bytes 196616 | tf_op jit(solution)/shard_map/ppermute | solution.py:466
  783.2 12.4 %copy-start.27 = (f32[32,128]{1,0:T(8,128)}, f32[32,128]{1,0:T(8,128)S(1)}, u32[]{:S(2)}) copy-start(f32[32,128]{1,0:T(8,128)S(1)} %collective-permute-done.16.ezlo_ref) | copy-start | bytes 49156
  783.2 12.4 %collective-permute-start.15 = (f32[128,128]{1,0:T(8,128)S(1)}, f32[128,128]{1,0:T(8,128)S(1)}, u32[]{:S(2)}, u32[]{:S(2)}) collective-permute-start(f32[128,128]{1,0:T(8,128)S(1)} %bitcast.50), channel_id=1, source_target_pairs={{2,0},{4,2},{6,4},{8,6},{10,8},{12,10},{14,12},{3,1},{5,3},{7,5},{... | collective-permute-start | bytes 196616 | tf_op jit(solution)/shard_map/ppermute | solution.py:467
  786.9 8.7 %copy-start.28 = (f32[32,128]{1,0:T(8,128)}, f32[32,128]{1,0:T(8,128)S(1)}, u32[]{:S(2)}) copy-start(f32[32,128]{1,0:T(8,128)S(1)} %collective-permute-done.17.ezhi_ref) | copy-start | bytes 49156
  786.9 5.6 collective-permute-start.12
  792.5 3.1 copy-start.29
  792.5 3.1 collective-permute-start.13
  795.6 0.6 copy-start.30
  795.6 0.6 copy-start.10
  796.2 0.6 copy-start.11
Sparse Core Ops, SparseCore 0:
  74.5 85.5 all-gather.2
  553.2 182.3 reduce-scatter.1

commit v2 on v1

v2 whole, which is shorter than its diff:
```python
import functools
import math

import jax
import jax.numpy as jnp
import ml_dtypes
import numpy as np
from jax import lax
from jax.experimental import pallas as pl
from jax.experimental.pallas import tpu as pltpu
from jax.sharding import PartitionSpec as P

time_step = 0.5
viscosity = 0.2
field_period = 24
full_turn = 2.0 * math.pi
bf16 = ml_dtypes.bfloat16
axes = ("gx", "gy", "gz")


def wave_tables(length):
    half = length // 2
    slot = np.arange(length)
    wave = np.where(slot <= half, slot, slot - half)
    angle = full_turn * (wave[:, None] * np.arange(length)[None, :] % length) / length
    weight = np.sqrt(np.where(slot % half == 0, 1.0, 2.0) / length)[:, None]
    odd = (slot > half)[:, None]
    kappa = full_turn * wave / length
    basis = np.where(odd, np.sin(angle), np.cos(angle)) * weight
    slope = np.where(odd, np.cos(angle), -np.sin(angle)) * weight * kappa[:, None]
    slope[half] = 0.0
    return basis, slope, kappa


def two_parts(table):
    high = table.astype(bf16)
    low = (table - high.astype(np.float64)).astype(bf16)
    return high, low


def split(value):
    high = value.astype(jnp.bfloat16)
    low = (value - high.astype(jnp.float32)).astype(jnp.bfloat16)
    return high, low


def dot(left, right):
    return jnp.dot(left, right, preferred_element_type=jnp.float32)


class Plan:
    def __init__(self, mesh, local):
        self.gx, self.gy, self.gz = (mesh.shape[a] for a in axes)
        self.xl, self.yl, self.zl = local
        self.nx, self.ny, self.nz = self.xl * self.gx, self.yl * self.gy, self.zl * self.gz
        self.x2, self.y2, self.z2 = self.nx // 2, self.ny // 2, self.nz // 2
        self.kx, self.kh = self.nx // 2, self.nx // 4
        self.yc = 2 * self.yl
        self.pitch = self.kx + 8
        self.px, self.py = self.xl // 4, self.yl // 2
        self.relay = (self.gx, self.gy, self.gz) == (2, 8, 2)
        self.arrays = 16 if self.relay else 1
        self.segments = self.relay_segments() if self.relay else self.gathered_segments()

    def gathered_segments(self):
        size = self.py * self.px
        return [
            [
                [
                    (0, ((first * self.gy + across) * self.gz + 2 * depth + side) * size)
                    for first in range(self.gx)
                    for side in range(2)
                ]
                for depth in range(self.gz // 2)
            ]
            for across in range(self.gy)
        ]

    def relay_segments(self):
        size = self.py * self.px
        segments = []
        for at in range(0, 16, 4):
            segments.append([[(at, 0), (at, size), (at + 1, 0), (at + 1, size)]])
            segments.append([[(at + 2, 0), (at + 3, 0), (at + 2, size), (at + 3, size)]])
        return segments

    def orders(self):
        x_orders = [
            np.concatenate([np.arange(self.px) + (column ^ r) * self.px for r in range(4)])
            for column in range(4)
        ]
        y_orders = []
        for side in range(2):
            for later in range(2):
                blocks = [2 * (half ^ later) + (side ^ far) for far in range(2) for half in range(2)]
                y_orders.append(np.concatenate([np.arange(self.yl) + block * self.yl for block in blocks]))
        return x_orders, y_orders


def make_tables(plan):
    bx, dx, wx = wave_tables(plan.nx)
    by, dy, wy = wave_tables(plan.ny)
    bz, dz, wz = wave_tables(plan.nz)
    hx, hy, hz = plan.nx // 2, plan.ny // 2, plan.nz // 2
    ez = bz.copy()
    ez[0] = bz[hz]
    z1 = dz.copy()
    z1[0] = 0.0
    z2 = dz.copy()
    z2[0] = -(np.pi**2) * bz[hz]
    z3 = -(wz**2)[:, None] * bz
    z3[0] = 0.0
    z1n = np.zeros_like(z1)
    z1n[hz] = -np.pi * bz[hz]
    xs = dx.copy()
    xs[hx] = np.pi * bx[hx]
    w3 = wz.copy()
    w3[0] = np.pi
    base = wy[:, None] ** 2 + w3[None, :] ** 2
    keep = np.ones_like(base, bool)
    keep[:, 0] = False
    keep[hy, 0] = True
    base = np.where(keep, base, 1e30).astype(np.float32)
    own = [np.arange(c * plan.kh, (c + 1) * plan.kh) for c in range(2)]
    own = [np.concatenate([cosines, hx + cosines]) for cosines in own]

    def by_side(table):
        return np.stack([table[slots] for slots in own])

    fx, fy = by_side(bx[:, : plan.x2]), by[None, :, : plan.y2]
    if plan.relay:
        x_orders, y_orders = plan.orders()
        fx = np.stack([part[:, order] for part in fx for order in x_orders])
        fy = np.stack([fy[0][:, order] for order in y_orders])
    return dict(
        fx=fx,
        fy=fy,
        xb=by_side(bx),
        xs=by_side(xs),
        w1=by_side((wx**2).astype(np.float32)),
        z1n=np.stack([z1n, z1]),
        ez=ez[:, : plan.z2],
        by=by,
        dy=dy,
        z1=z1,
        z2=z2,
        z3=z3,
        base=base,
    )


def pair_lanes(*arrays):
    return jnp.concatenate(arrays, axis=1)


def pair_rows(*arrays):
    return jnp.concatenate(arrays, axis=0)


def load_plane(refs, plan, segment, i):
    blocks = [
        pair_rows(*[refs[array][pl.ds(start + i * plan.px, plan.px), :] for array, start in runs])
        for runs in segment
    ]
    return blocks[0] if len(blocks) == 1 else pair_lanes(*blocks)


def store_plane(refs, plan, segment, i, value):
    for depth, runs in enumerate(segment):
        for place, (array, start) in enumerate(runs):
            refs[array][pl.ds(start + i * plan.px, plan.px), :] = value[
                place * plan.px : (place + 1) * plan.px, depth * plan.zl : (depth + 1) * plan.zl
            ]


def field_body(
    plan, group, w1_ref, fx_ref, ez_ref, fy_ref, g_ref, z13_ref, z2_ref, z1n_ref, xs_ref, xb_ref, base_ref, *refs,
):
    kx, kh, pitch = plan.kx, plan.kh, plan.pitch
    y2, z2, xl, yl, yc, zl = plan.y2, plan.z2, plan.xl, plan.yl, plan.yc, plan.zl
    span = yc * pitch
    m_refs, (own_ref, other_ref, s_ref, r_ref) = refs[: plan.arrays], refs[plan.arrays :]

    def along_x(number, segment):
        def body(pair, carry):
            planes = [load_plane(m_refs, plan, segment, 2 * pair + k) for k in range(2)]
            high, low = split(pair_lanes(*planes))
            out = dot(fx_ref[...], pair_rows(high, low, high))
            row = (number * plan.py + 2 * pair) * pitch
            s_ref[pl.ds(row, kx), :] = out[:, :z2]
            s_ref[pl.ds(row + pitch, kx), :] = out[:, z2:]
            return carry

        lax.fori_loop(0, plan.py // 2, body, 0)

    for number, segment in enumerate(plan.segments):
        along_x(number, segment)

    def depth_waves(slots):
        rows = pair_rows(*[s_ref[pl.ds(slot, y2, stride=pitch), :] for slot in slots])
        high, low = split(rows)
        return dot(pair_lanes(high, low, high), ez_ref[...])

    def one_slab(plane, kern):
        high, low = split(plane)
        high, low = split(dot(fy_ref[...], pair_rows(high, low, high)) * kern)
        both = dot(g_ref[...], high)
        return both[: 2 * yc] + both[2 * yc :] + dot(g_ref[: 2 * yc], low)

    def two_products(high, low, table_ref):
        both = dot(high, table_ref[...])
        return both[:, :zl] + both[:, zl:] + dot(low, table_ref[:, :zl])

    def store(slots, cells, j):
        for place, slot in enumerate(slots):
            r_ref[pl.ds(j * span + slot, yc, stride=pitch), :] = cells[place * yc : (place + 1) * yc]

    def depth_cells(slots, slabs, edge):
        q1 = pair_rows(*[slab[:yc] for slab in slabs])
        q2 = pair_rows(*[slab[yc:] for slab in slabs])
        lane = lax.broadcasted_iota(jnp.int32, q1.shape, 1)
        q2 = jnp.where(lane == 0, q1, q2)
        high, low = split(q1)
        r13 = dot(pair_lanes(high, low, high), z13_ref[...])
        store(slots, two_products(high, low, z1n_ref) if edge else r13[:, :zl], 0)
        store(slots, r13[:, zl:], 2)
        store(slots, two_products(*split(q2), z2_ref), 1)

    def waves(step, carry):
        first = step * group
        slots = [first + k + part for k in range(group) for part in (0, kh)]
        planes = depth_waves(slots)
        slabs = []
        for k in range(group):
            kern = 1.0 / (base_ref[...] + w1_ref[first + k])
            for part in range(2):
                at = (2 * k + part) * y2
                slabs.append(one_slab(planes[at : at + y2], kern))
        depth_cells(slots, slabs, False)
        return carry

    lax.fori_loop(0, kh // group, waves, 0)

    slab = one_slab(depth_waves([kh]), 1.0 / (base_ref[...] + w1_ref[kh]))
    depth_cells([kh], [slab], True)

    def back_x(mat_ref, values):
        high, low = split(values)
        return dot(mat_ref[...], pair_rows(high, low, high))

    def cells(out_ref, shift):
        def body(pair, carry):
            here = [
                [pl.ds(j * span + (shift + 2 * pair + k) * pitch, kx) for k in range(2)]
                for j in range(3)
            ]
            h1 = back_x(xs_ref, pair_lanes(r_ref[here[0][0], :], r_ref[here[0][1], :]))
            for k in range(2):
                h23 = back_x(xb_ref, pair_lanes(r_ref[here[1][k], :], r_ref[here[2][k], :]))
                at = (2 * pair + k) * xl
                out_ref[pl.ds(at, xl), :] = h1[:, k * zl : (k + 1) * zl]
                out_ref[pl.ds(yl * xl + at, xl), :] = h23[:, :zl]
                out_ref[pl.ds(2 * yl * xl + at, xl), :] = h23[:, zl:]
            return carry

        lax.fori_loop(0, yl // 2, body, 0)

    cells(other_ref, yl)
    cells(own_ref, 0)


def adjoint_body(
    plan, group, w1_ref, own_ref, other_ref, xs_ref, xb_ref, z13_ref, z2_ref, z1n_ref, g_ref, fy_ref, ez_ref, fx_ref, base_ref, *refs,
):
    kx, kh, pitch = plan.kx, plan.kh, plan.pitch
    y2, z2, xl, yl, yc, zl = plan.y2, plan.z2, plan.xl, plan.yl, plan.yc, plan.zl
    span = yc * pitch
    m_refs, (s_ref, r_ref) = refs[: plan.arrays], refs[plan.arrays :]

    def along_x(mat_ref, values):
        high, low = split(values)
        return dot(mat_ref[...], pair_rows(high, low, high))

    def cells(f_ref, shift):
        def body(pair, carry):
            here = [
                [pl.ds((j * yl + 2 * pair + k) * xl, xl) for k in range(2)] for j in range(3)
            ]
            u1 = along_x(xs_ref, pair_lanes(f_ref[here[0][0], :], f_ref[here[0][1], :]))
            for k in range(2):
                u23 = along_x(xb_ref, pair_lanes(f_ref[here[1][k], :], f_ref[here[2][k], :]))
                row = (shift + 2 * pair + k) * pitch
                r_ref[pl.ds(row, kx), :] = u1[:, k * zl : (k + 1) * zl]
                r_ref[pl.ds(span + row, kx), :] = u23[:, :zl]
                r_ref[pl.ds(2 * span + row, kx), :] = u23[:, zl:]
            return carry

        lax.fori_loop(0, yl // 2, body, 0)

    cells(own_ref, 0)
    cells(other_ref, yl)

    def depth_waves(slots, edge):
        u = [
            pair_rows(*[r_ref[pl.ds(j * span + slot, yc, stride=pitch), :] for slot in slots])
            for j in range(3)
        ]
        high1, low1 = split(u[0])
        high2, low2 = split(u[1])
        high3, low3 = split(u[2])
        high = pair_lanes(high1, high3)
        q1 = dot(pair_lanes(high, low1, low3, high), z13_ref[...])
        if edge:
            q1 = q1 + dot(pair_lanes(high1, low1, high1), z1n_ref[...])
        q2 = dot(pair_lanes(high2, low2, high2), z2_ref[...])
        first = lax.broadcasted_iota(jnp.int32, q1.shape, 1) == 0
        return jnp.where(first, q2, q1), jnp.where(first, 0.0, q2)

    def one_slab(q1, q2, kern):
        high, low = split(pair_rows(q1, q2))
        high, low = split(dot(g_ref[...], pair_rows(high, low, high)) * kern)
        both = dot(fy_ref[...], high)
        return both[:y2] + both[y2:] + dot(fy_ref[:y2], low)

    def depth_cells(slots, slabs):
        high, low = split(pair_rows(*slabs))
        out = dot(high, ez_ref[...])
        out = out[:, :z2] + out[:, z2:] + dot(low, ez_ref[:, :z2])
        for place, slot in enumerate(slots):
            s_ref[pl.ds(slot, y2, stride=pitch), :] = out[place * y2 : (place + 1) * y2]

    def waves(step, carry):
        first = step * group
        slots = [first + k + part for k in range(group) for part in (0, kh)]
        q1, q2 = depth_waves(slots, False)
        slabs = []
        for k in range(group):
            kern = 1.0 / (base_ref[...] + w1_ref[first + k])
            for part in range(2):
                take = slice((2 * k + part) * yc, (2 * k + part + 1) * yc)
                slabs.append(one_slab(q1[take], q2[take], kern))
        depth_cells(slots, slabs)
        return carry

    lax.fori_loop(0, kh // group, waves, 0)

    q1, q2 = depth_waves([kh], True)
    depth_cells([kh], [one_slab(q1, q2, 1.0 / (base_ref[...] + w1_ref[kh]))])

    def back_x(number, segment):
        def body(pair, carry):
            row = (number * plan.py + 2 * pair) * pitch
            planes = [s_ref[pl.ds(row + k * pitch, kx), :] for k in range(2)]
            high, low = split(pair_lanes(*planes))
            out = dot(fx_ref[...], pair_rows(high, low, high))
            store_plane(m_refs, plan, segment, 2 * pair, out[:, :z2])
            store_plane(m_refs, plan, segment, 2 * pair + 1, out[:, z2:])
            return carry

        lax.fori_loop(0, plan.py // 2, body, 0)

    for number, segment in enumerate(plan.segments):
        back_x(number, segment)


vmem = pl.BlockSpec(memory_space=pltpu.VMEM)
smem = pl.BlockSpec(memory_space=pltpu.SMEM)
kernel_params = pltpu.CompilerParams(vmem_limit_bytes=60 * 2**20)


def scratch_of(plan):
    return [
        pltpu.VMEM((plan.y2 * plan.pitch, plan.z2), jnp.float32),
        pltpu.VMEM((3 * plan.yc * plan.pitch, plan.zl), jnp.float32),
    ]


def side_of(plan):
    return lax.rem(lax.axis_index("gy"), 2)


def of_side(plan, stack):
    return lax.dynamic_index_in_dim(jnp.asarray(stack), side_of(plan), 0, keepdims=False)


def of_place(plan, stack, name):
    side, place = side_of(plan), 0
    if plan.relay and name == "fx":
        side, place = 4 * side, 2 * lax.axis_index("gx") + lax.axis_index("gz")
    elif plan.relay:
        side, place = 2 * side, jnp.minimum(lax.axis_index("gy") // 2, 1)
    elif name == "fy":
        side = 0
    return lax.dynamic_index_in_dim(jnp.asarray(stack), side + place, 0, keepdims=False)


def own_block(plan, table, axis, count, dim):
    table = jnp.asarray(table)
    place = lax.axis_index(axis)
    if axis != "gy":
        return lax.dynamic_slice_in_dim(table, place * count, count, dim)
    partner = place + 1 - 2 * lax.rem(place, 2)
    both = [lax.dynamic_slice_in_dim(table, p * count, count, dim) for p in (place, partner)]
    return jnp.concatenate(both, axis=dim)


def thrice_lanes(table):
    high, low = two_parts(table)
    return np.concatenate([high, high, low], axis=-1)


def thrice_rows(table):
    high, low = two_parts(table)
    return np.concatenate([high, high, low], axis=-2)


def field_tables(plan, t):
    xl, yl, zl = plan.xl, plan.yl, plan.zl

    def y_cells(part):
        return own_block(plan, part, "gy", yl, 0)

    def z_cells(part):
        return own_block(plan, part, "gz", zl, 1)

    def x_table(name):
        high, low = [
            own_block(plan, of_side(plan, part.swapaxes(1, 2)), "gx", xl, 0) for part in two_parts(t[name])
        ]
        return pair_lanes(high, high, low)

    b, bl = [y_cells(part) for part in two_parts(t["by"].T)]
    d, dl = [y_cells(part) for part in two_parts(t["dy"].T)]
    z1, z1l = [z_cells(part) for part in two_parts(t["z1"])]
    z2, z2l = [z_cells(part) for part in two_parts(t["z2"])]
    z3, z3l = [z_cells(part) for part in two_parts(t["z3"])]
    z1n, z1nl = [z_cells(of_side(plan, part)) for part in two_parts(t["z1n"])]
    z13, z13l = pair_lanes(z1, z3), pair_lanes(z1l, z3l)
    return [
        of_side(plan, t["w1"]), of_place(plan, thrice_lanes(t["fx"]), "fx"), jnp.asarray(thrice_rows(t["ez"].T)),
        of_place(plan, thrice_lanes(t["fy"]), "fy"), pair_rows(b, d, bl, dl), pair_rows(z13, z13, z13l), pair_lanes(z2, z2l),
        pair_lanes(z1n, z1nl), x_table("xs"), x_table("xb"), jnp.asarray(t["base"]),
    ]


def field_call(plan, tables, octant):
    xl, yl, zl = plan.xl, plan.yl, plan.zl
    group = 4
    shape = jax.ShapeDtypeStruct((3 * yl * xl, zl), jnp.float32)
    own, other = pl.pallas_call(
        functools.partial(field_body, plan, group),
        out_shape=[shape, shape],
        in_specs=[smem] + [vmem] * (10 + plan.arrays),
        out_specs=[vmem, vmem],
        scratch_shapes=scratch_of(plan),
        compiler_params=kernel_params,
    )(*tables, *octant)
    return own.reshape(3, yl, xl, zl), other.reshape(3, yl, xl, zl)


def adjoint_tables(plan, t):
    xl, yl, zl = plan.xl, plan.yl, plan.zl

    def y_cells(part):
        return own_block(plan, part, "gy", yl, 1)

    def z_cells(part):
        return own_block(plan, part, "gz", zl, 0)

    def x_table(name):
        high, low = [
            own_block(plan, of_side(plan, part), "gx", xl, 1) for part in two_parts(t[name])
        ]
        return pair_lanes(high, high, low)

    b, bl = [y_cells(part) for part in two_parts(t["by"])]
    d, dl = [y_cells(part) for part in two_parts(t["dy"])]
    z1, z1l = [z_cells(part) for part in two_parts(t["z1"].T)]
    z2, z2l = [z_cells(part) for part in two_parts(t["z2"].T)]
    z3, z3l = [z_cells(part) for part in two_parts(t["z3"].T)]
    z1n, z1nl = [
        z_cells(of_side(plan, part)) for part in two_parts((t["z1n"] - t["z1"]).swapaxes(1, 2))
    ]
    fy, fyl = two_parts(t["fy"].swapaxes(1, 2))
    ez, ezl = two_parts(t["ez"])
    return [
        of_side(plan, t["w1"]), x_table("xs"), x_table("xb"),
        pair_rows(z1, z3, z1, z3, z1l, z3l), pair_rows(z2, z2, z2l), pair_rows(z1n, z1n, z1nl),
        pair_lanes(b, d, b, d, bl, dl), of_place(plan, np.concatenate([fy, fyl], axis=1), "fy"), jnp.concatenate([ez, ezl], axis=1),
        of_place(plan, thrice_lanes(t["fx"].swapaxes(1, 2)), "fx"), jnp.asarray(t["base"]),
    ]


def adjoint_call(plan, tables, own, other):
    zl = plan.zl
    group = 4
    return pl.pallas_call(
        functools.partial(adjoint_body, plan, group),
        out_shape=[
            jax.ShapeDtypeStruct((plan.x2 * plan.y2 * plan.z2 // zl // plan.arrays, zl), jnp.float32)
        ] * plan.arrays,
        in_specs=[smem] + [vmem] * 12,
        out_specs=[vmem] * plan.arrays,
        scratch_shapes=scratch_of(plan),
        compiler_params=kernel_params,
    )(tables[0], own.reshape(-1, zl), other.reshape(-1, zl), *tables[1:])


def swapped(array):
    count = lax.axis_size("gy")
    return lax.ppermute(array, "gy", [(i, i + 1 - 2 * (i % 2)) for i in range(count)])


def spread(block, axis, dim):
    count = lax.axis_size(axis)
    halves = jnp.split(block, 2, axis=dim)
    moved = [
        lax.ppermute(half, axis, [(s, 2 * s + k) for s in range(count // 2)])
        for k, half in enumerate(halves)
    ]
    return moved[0] + moved[1]


def unspread(piece, axis, dim):
    count = lax.axis_size(axis)
    moved = [
        lax.ppermute(piece, axis, [(2 * s + k, s) for s in range(count // 2)]) for k in range(2)
    ]
    return jnp.concatenate(moved, axis=dim)


def gather_octant(plan, block, work):
    if plan.relay:
        return relay_octant(plan, block, work)
    done = []
    for step in work:
        done.append(step(done))
    piece = block
    for axis, dim in (("gx", 1), ("gz", 1), ("gy", 0)):
        piece = spread(piece, axis, dim)
    return [lax.all_gather(piece.reshape(plan.py * plan.px, plan.zl), axes, tiled=True)], done


def owners_sum(plan, sums, work):
    if plan.relay:
        return relay_sums(plan, sums, work)
    done = [step() for step in work]
    piece = lax.psum_scatter(sums[0], axes, scatter_dimension=0, tiled=True)
    piece = piece.reshape(plan.py, plan.px, plan.zl)
    return unspread(unspread(unspread(piece, "gy", 0), "gz", 1), "gx", 1), done


flip = [(0, 1), (1, 0)]


def along(array, pairs):
    return lax.ppermute(array, "gy", [(2 * a + c, 2 * b + c) for a, b in pairs for c in range(2)])


def together(*values):
    return lax.optimization_barrier(values)


def relay_octant(plan, block, work):
    z = lax.axis_index("gy") // 2
    done = []
    quarters = [block[:, r * plan.px : (r + 1) * plan.px].reshape(-1, plan.zl) for r in range(4)]
    moved = [lax.ppermute(quarters[r], ("gx", "gz"), [(0, r)]) for r in range(1, 4)]
    moved, result = together(moved, work[0](done))
    done.append(result)
    piece = quarters[0] + moved[0] + moved[1] + moved[2]
    up = along(piece, [(0, 1), (1, 2)])
    down = along(piece, [(1, 0)])
    up, result = together(up, work[1](done))
    done.append(result)
    up2 = along(up, [(1, 2), (2, 3)])
    up2, result = together(up2, work[2](done))
    done.append(result)
    up3 = along(up2, [(2, 3)])
    first = across(plan, jnp.where(z < 2, piece, jnp.where(z == 2, up, up2)))
    up3, result = together(up3, work[3](done))
    done.append(result)
    second = jnp.where(z == 0, down, jnp.where(z == 1, up, jnp.where(z == 2, up2, up3)))
    own = first + across(plan, second)
    return own + [swapped(array) for array in own], done


def across(plan, piece):
    half = plan.py * plan.px
    low, high = piece[:half], piece[half:]
    a = pair_rows(low, lax.ppermute(low, "gz", flip))
    b = pair_rows(high, lax.ppermute(high, "gx", flip))
    return [a, lax.ppermute(a, "gx", flip), b, lax.ppermute(b, "gz", flip)]


def across_sums(plan, arrays):
    half = plan.py * plan.px
    a, ay, b, bx = arrays
    a = a + lax.ppermute(ay, "gx", flip)
    b = b + lax.ppermute(bx, "gz", flip)
    low = a[:half] + lax.ppermute(a[half:], "gz", flip)
    high = b[:half] + lax.ppermute(b[half:], "gx", flip)
    return pair_rows(low, high)


def relay_sums(plan, sums, work):
    z = lax.axis_index("gy") // 2
    own = [sums[i] + swapped(sums[i + 8]) for i in range(8)]
    second = across_sums(plan, own[4:])
    moved = along(second, [(3, 2)])
    moved, result0 = together(moved, work[0]())
    first = across_sums(plan, own[:4])
    second = second + moved
    moved = along(jnp.where(z == 3, first, second), [(3, 2), (2, 1)])
    moved, result1 = together(moved, work[1]())
    first = first + jnp.where(z == 2, moved, 0.0)
    second = second + jnp.where(z == 1, moved, 0.0)
    first = first + along(second, [(0, 1)]) + along(jnp.where(z == 2, first, second), [(2, 1), (1, 0)])
    quarters = [first] + [lax.ppermute(first, ("gx", "gz"), [(r, 0)]) for r in range(1, 4)]
    block = jnp.concatenate([q.reshape(plan.yl, plan.px, plan.zl) for q in quarters], axis=1)
    return block, [result0, result1]


def lanes_of(count):
    return -(-count // 128) * 128


def faces_body(chunk, v_ref, a_ref, c_ref, ylo_ref, yhi_ref, zlo_ref, zhi_ref):
    yl, zl = v_ref.shape[2:]
    step = pl.program_id(0)

    @pl.when(step == 0)
    def _():
        zlo_ref[...] = jnp.zeros_like(zlo_ref)
        zhi_ref[...] = jnp.zeros_like(zhi_ref)

    lane = lax.broadcasted_iota(jnp.int32, zlo_ref.shape[1:], 1)
    for field in range(7):
        low, high = zlo_ref[field], zhi_ref[field]
        for k in range(chunk):
            plane = v_ref[field, k] if field < 3 else a_ref[field - 3, k] if field < 6 else c_ref[k]
            ylo_ref[field, k : k + 1, :] = plane[:1]
            yhi_ref[field, k : k + 1, :] = plane[yl - 1 :]
            here = lane == step * chunk + k
            low = jnp.where(here, plane[:, :1], low)
            high = jnp.where(here, plane[:, zl - 1 :], high)
        zlo_ref[field] = low
        zhi_ref[field] = high


def faces_call(velocity, adjoint_seed, susceptibility):
    xl, yl, zl = susceptibility.shape
    chunk = 8
    three = pl.BlockSpec((3, chunk, yl, zl), lambda i: (0, i, 0, 0))
    y_spec = pl.BlockSpec((7, chunk, zl), lambda i: (0, i, 0))
    z_spec = pl.BlockSpec((7, yl, lanes_of(max(xl, zl))), lambda i: (0, 0, 0))
    y_shape = jax.ShapeDtypeStruct((7, xl, zl), jnp.float32)
    z_shape = jax.ShapeDtypeStruct((7, yl, lanes_of(max(xl, zl))), jnp.float32)
    return pl.pallas_call(
        functools.partial(faces_body, chunk),
        grid=(xl // chunk,),
        in_specs=[three, three, pl.BlockSpec((chunk, yl, zl), lambda i: (i, 0, 0))],
        out_specs=[y_spec, y_spec, z_spec, z_spec],
        out_shape=[y_shape, y_shape, z_shape, z_shape],
        compiler_params=kernel_params,
    )(velocity, adjoint_seed, susceptibility)


def to_neighbours(low_face, high_face, axis):
    count = lax.axis_size(axis)
    below = lax.ppermute(high_face, axis, [(i, i + 1) for i in range(count - 1)])
    above = lax.ppermute(low_face, axis, [(i + 1, i) for i in range(count - 1)])
    return below, above


def combine_body(chunk, app_ref, own_ref, arrived_ref, source_ref, f_ref, e_ref, ylo_ref, yhi_ref, zlo_ref, zhi_ref):
    yl, _, zl = source_ref.shape
    step = pl.program_id(0)

    @pl.when(step == 0)
    def _():
        zlo_ref[...] = jnp.zeros_like(zlo_ref)
        zhi_ref[...] = jnp.zeros_like(zhi_ref)

    energy = 0.0
    for j in range(3):
        total = own_ref[j] + arrived_ref[j] + app_ref[j]
        f_ref[j] = source_ref[...] * total
        energy = energy + total * total
    energy = 0.5 * energy
    lane = lax.broadcasted_iota(jnp.int32, zlo_ref.shape, 1)
    low, high = zlo_ref[...], zhi_ref[...]
    for k in range(chunk):
        plane = energy[:, k, :]
        e_ref[k] = plane
        ylo_ref[k : k + 1, :] = plane[:1]
        yhi_ref[k : k + 1, :] = plane[yl - 1 :]
        here = lane == step * chunk + k
        low = jnp.where(here, plane[:, :1], low)
        high = jnp.where(here, plane[:, zl - 1 :], high)
    zlo_ref[...] = low
    zhi_ref[...] = high


def combine_call(applied, own, arrived, source):
    _, yl, xl, zl = own.shape
    chunk = 8
    width = lanes_of(max(xl, zl))
    three = pl.BlockSpec((3, yl, chunk, zl), lambda i: (0, 0, i, 0))
    y_spec = pl.BlockSpec((chunk, zl), lambda i: (i, 0))
    z_spec = pl.BlockSpec((yl, width), lambda i: (0, 0))
    shapes = [(3, yl, xl, zl), (xl, yl, zl), (xl, zl), (xl, zl), (yl, width), (yl, width)]
    return pl.pallas_call(
        functools.partial(combine_body, chunk),
        grid=(xl // chunk,),
        in_specs=[smem, three, three, pl.BlockSpec((yl, chunk, zl), lambda i: (0, i, 0))],
        out_specs=[
            three, pl.BlockSpec((chunk, yl, zl), lambda i: (i, 0, 0)), y_spec, y_spec, z_spec, z_spec,
        ],
        out_shape=[jax.ShapeDtypeStruct(shape, jnp.float32) for shape in shapes],
        compiler_params=kernel_params,
    )(applied, own, arrived, source)


class Around:
    def __init__(self, ref, k, x, y_below, y_above, z_below, z_above):
        mid = ref[k + 1]
        yl, zl = mid.shape
        row = lax.broadcasted_iota(jnp.int32, mid.shape, 0)
        lane = lax.broadcasted_iota(jnp.int32, mid.shape, 1)
        width = z_below.shape[1]
        left = pltpu.roll(z_below, lax.rem(width - x, width), 1)[:, :zl]
        right = pltpu.roll(z_above, lax.rem(width + zl - 1 - x, width), 1)[:, :zl]
        self.mid = mid
        self.less = [
            ref[k],
            jnp.where(row == 0, y_below, pltpu.roll(mid, 1, 0)),
            jnp.where(lane == 0, left, pltpu.roll(mid, 1, 1)),
        ]
        self.more = [
            ref[k + 2],
            jnp.where(row == yl - 1, y_above, pltpu.roll(mid, yl - 1, 0)),
            jnp.where(lane == zl - 1, right, pltpu.roll(mid, zl - 1, 1)),
        ]

    def slope(self, d):
        return (self.more[d] - self.less[d]) * 0.5

    def laplace(self):
        beside = self.more[0] + self.less[0] + self.more[1] + self.less[1]
        return beside + self.more[2] + self.less[2] - 6.0 * self.mid


def fill_window(window, chunk, field, before, block, after, x_below, x_above):
    step, last = pl.program_id(0), pl.num_programs(0) - 1
    for k in range(chunk):
        window[field, k + 1] = block(k)
    window[field, 0] = jnp.where(step == 0, x_below, before)
    window[field, chunk + 1] = jnp.where(step == last, x_above, after)


def source_body(
    chunk, a_ref, ab_ref, aa_ref, c_ref, cb_ref, ca_ref,
    xlo_ref, xhi_ref, ylo_ref, yhi_ref, zlo_ref, zhi_ref, source_ref, window,
):
    for j in range(3):
        fill_window(window, chunk, j, ab_ref[j, 0], lambda k: a_ref[j, k], aa_ref[j, 0], xlo_ref[3 + j], xhi_ref[3 + j])
    fill_window(window, chunk, 3, cb_ref[0], lambda k: c_ref[k], ca_ref[0], xlo_ref[6], xhi_ref[6])
    start = pl.program_id(0) * chunk

    def plane(k, carry):
        at = [
            Around(
                window.at[f], k, start + k,
                ylo_ref[3 + f, pl.ds(k, 1), :], yhi_ref[3 + f, pl.ds(k, 1), :], zlo_ref[3 + f], zhi_ref[3 + f],
            )
            for f in range(4)
        ]
        a, c = at[:3], at[3]
        flux = [c.more[i] * a[i].more[i] - c.less[i] * a[i].less[i] for i in range(3)]
        source_ref[:, k, :] = (-0.5 * time_step) * (flux[0] + flux[1] + flux[2])
        return carry

    lax.fori_loop(0, chunk, plane, 0)


def adjoint_cells_body(
    chunk, v_ref, vb_ref, va_ref, a_ref, ab_ref, aa_ref,
    xlo_ref, xhi_ref, ylo_ref, yhi_ref, zlo_ref, zhi_ref, out_ref, window,
):
    for j in range(3):
        fill_window(window, chunk, j, vb_ref[j, 0], lambda k: v_ref[j, k], va_ref[j, 0], xlo_ref[j], xhi_ref[j])
        fill_window(window, chunk, 3 + j, ab_ref[j, 0], lambda k: a_ref[j, k], aa_ref[j, 0], xlo_ref[3 + j], xhi_ref[3 + j])
    start = pl.program_id(0) * chunk

    def plane(k, carry):
        at = [
            Around(
                window.at[f], k, start + k,
                ylo_ref[f, pl.ds(k, 1), :], yhi_ref[f, pl.ds(k, 1), :], zlo_ref[f], zhi_ref[f],
            )
            for f in range(6)
        ]
        v, a = at[:3], at[3:]
        for j in range(3):
            shear = sum(a[i].mid * (v[i].more[j] - v[i].less[j]) for i in range(3))
            carried = sum(v[i].more[i] * a[j].more[i] - v[i].less[i] * a[j].less[i] for i in range(3))
            out_ref[j, k] = a[j].mid + time_step * (
                viscosity * a[j].laplace() + 0.5 * (carried - shear)
            )
        return carry

    lax.fori_loop(0, chunk, plane, 0)


def next_cells_body(
    chunk, v_ref, vb_ref, va_ref, e_ref, eb_ref, ea_ref, c_ref,
    xlo_ref, xhi_ref, ylo_ref, yhi_ref, zlo_ref, zhi_ref,
    exlo_ref, exhi_ref, eylo_ref, eyhi_ref, ezlo_ref, ezhi_ref, out_ref, window,
):
    for j in range(3):
        fill_window(window, chunk, j, vb_ref[j, 0], lambda k: v_ref[j, k], va_ref[j, 0], xlo_ref[j], xhi_ref[j])
    fill_window(window, chunk, 3, eb_ref[0], lambda k: e_ref[k], ea_ref[0], exlo_ref[...], exhi_ref[...])
    start = pl.program_id(0) * chunk

    def plane(k, carry):
        v = [
            Around(
                window.at[f], k, start + k,
                ylo_ref[f, pl.ds(k, 1), :], yhi_ref[f, pl.ds(k, 1), :], zlo_ref[f], zhi_ref[f],
            )
            for f in range(3)
        ]
        e = Around(
            window.at[3], k, start + k,
            eylo_ref[pl.ds(k, 1), :], eyhi_ref[pl.ds(k, 1), :], ezlo_ref[...], ezhi_ref[...],
        )
        for j in range(3):
            advect = sum(v[i].mid * (v[j].more[i] - v[j].less[i]) for i in range(3))
            pushed = c_ref[k] * (e.more[j] - e.less[j])
            out_ref[j, k] = v[j].mid + time_step * (
                viscosity * v[j].laplace() + 0.5 * (pushed - advect)
            )
        return carry

    lax.fori_loop(0, chunk, plane, 0)


def cell_specs(chunk, xl, yl, zl, lead):
    def at(block, place):
        if lead:
            return pl.BlockSpec((3, block, yl, zl), lambda i: (0, place(i), 0, 0))
        return pl.BlockSpec((block, yl, zl), lambda i: (place(i), 0, 0))

    return [
        at(chunk, lambda i: i),
        at(1, lambda i: jnp.maximum(i * chunk - 1, 0)),
        at(1, lambda i: jnp.minimum((i + 1) * chunk, xl - 1)),
    ]


def face_specs(chunk, yl, zl, width, fields):
    def spec(shape, index):
        return pl.BlockSpec((fields, *shape), lambda i: (0, *index(i)))

    x_spec = spec((yl, zl), lambda i: (0, 0))
    y_spec = spec((chunk, zl), lambda i: (i, 0))
    z_spec = spec((yl, width), lambda i: (0, 0))
    return [x_spec, x_spec, y_spec, y_spec, z_spec, z_spec]


def source_call(adjoint_seed, susceptibility, faces):
    xl, yl, zl = susceptibility.shape
    chunk = 8
    a, c = adjoint_seed, susceptibility
    return pl.pallas_call(
        functools.partial(source_body, chunk),
        grid=(xl // chunk,),
        in_specs=cell_specs(chunk, xl, yl, zl, True)
        + cell_specs(chunk, xl, yl, zl, False)
        + face_specs(chunk, yl, zl, lanes_of(max(xl, zl)), 7),
        out_specs=pl.BlockSpec((yl, chunk, zl), lambda i: (0, i, 0)),
        out_shape=jax.ShapeDtypeStruct((yl, xl, zl), jnp.float32),
        scratch_shapes=[pltpu.VMEM((4, chunk + 2, yl, zl), jnp.float32)],
        compiler_params=kernel_params,
    )(a, a, a, c, c, c, *faces)


def adjoint_cells_call(velocity, adjoint_seed, faces):
    _, xl, yl, zl = velocity.shape
    chunk = 8
    three = cell_specs(chunk, xl, yl, zl, True)
    v, a = velocity, adjoint_seed
    return pl.pallas_call(
        functools.partial(adjoint_cells_body, chunk),
        grid=(xl // chunk,),
        in_specs=three + three + face_specs(chunk, yl, zl, lanes_of(max(xl, zl)), 6),
        out_specs=three[0],
        out_shape=jax.ShapeDtypeStruct(v.shape, jnp.float32),
        scratch_shapes=[pltpu.VMEM((6, chunk + 2, yl, zl), jnp.float32)],
        compiler_params=kernel_params,
    )(v, v, v, a, a, a, *faces)


def next_cells_call(velocity, energy, susceptibility, faces, energy_faces):
    xl, yl, zl = susceptibility.shape
    chunk = 8
    three = cell_specs(chunk, xl, yl, zl, True)
    one = cell_specs(chunk, xl, yl, zl, False)
    width = lanes_of(max(xl, zl))
    energy_specs = [
        pl.BlockSpec((yl, zl), lambda i: (0, 0)),
        pl.BlockSpec((chunk, zl), lambda i: (i, 0)),
        pl.BlockSpec((yl, width), lambda i: (0, 0)),
    ]
    energy_specs = [spec for spec in energy_specs for _ in range(2)]
    v, e, c = velocity, energy, susceptibility
    return pl.pallas_call(
        functools.partial(next_cells_body, chunk),
        grid=(xl // chunk,),
        in_specs=three + one + one[:1] + face_specs(chunk, yl, zl, width, 3) + energy_specs,
        out_specs=three[0],
        out_shape=jax.ShapeDtypeStruct(v.shape, jnp.float32),
        scratch_shapes=[pltpu.VMEM((4, chunk + 2, yl, zl), jnp.float32)],
        compiler_params=kernel_params,
    )(v, v, v, e, e, e, c, *faces, *energy_faces)


def on_device(mesh, velocity, adjoint_seed, susceptibility, remanence, region_bounds, step_id):
    plan = Plan(mesh, susceptibility.shape)
    tables = make_tables(plan)
    places = [
        lax.axis_index(a) * n + jnp.arange(n, dtype=jnp.int32)
        for a, n in zip(axes, susceptibility.shape)
    ]
    inside = [
        (place >= region_bounds[0, d]) & (place < region_bounds[1, d])
        for d, place in enumerate(places)
    ]
    region_mask = (
        inside[0][:, None, None] & inside[1][None, :, None] & inside[2][None, None, :]
    ).astype(jnp.float32)
    def end_layers(done):
        ends = [
            jnp.concatenate([velocity[:, x], adjoint_seed[:, x], susceptibility[None, x]], axis=0)
            for x in (0, plan.xl - 1)
        ]
        return ends, faces_call(velocity, adjoint_seed, susceptibility)

    def neighbours(done):
        ends, (ylo, yhi, zlo, zhi) = done[0]
        faces = [
            *to_neighbours(*ends, "gx"), *to_neighbours(ylo, yhi, "gy"), *to_neighbours(zlo, zhi, "gz"),
        ]
        return faces, field_tables(plan, tables)

    def source_of(done):
        return source_call(adjoint_seed, susceptibility, done[1][0])

    def other_tables(done):
        angle = full_turn * (step_id[0] % field_period).astype(jnp.float32) / field_period
        applied = jnp.stack([jnp.cos(angle), jnp.sin(angle), jnp.zeros((), jnp.float32)])
        return applied, adjoint_tables(plan, tables)

    octant, done = gather_octant(
        plan,
        (remanence * region_mask).transpose(1, 0, 2),
        [end_layers, neighbours, source_of, other_tables],
    )
    _, (faces, there), source, (applied, back) = done
    own, other = field_call(plan, there, octant)
    field_adjoint, energy, ylo, yhi, zlo, zhi = combine_call(applied, own, swapped(other), source)
    energy_faces = [
        *to_neighbours(energy[0], energy[-1], "gx"), *to_neighbours(ylo, yhi, "gy"), *to_neighbours(zlo, zhi, "gz"),
    ]
    other, energy_faces = together(swapped(field_adjoint), energy_faces)
    sums = adjoint_call(plan, back, field_adjoint, other)
    sums, energy, faces = together(sums, energy, faces)

    def next_cells():
        return next_cells_call(velocity, energy, susceptibility, faces, energy_faces)

    def adjoint_cells():
        return adjoint_cells_call(velocity, adjoint_seed, faces)

    gradient, (next_velocity, velocity_adjoint) = owners_sum(plan, sums, [next_cells, adjoint_cells])
    design_gradient = region_mask * gradient.transpose(1, 0, 2)
    return (next_velocity, velocity_adjoint, design_gradient)


def solution(mesh):
    cells = P(*axes)
    vectors = P(None, *axes)
    return jax.shard_map(
        functools.partial(on_device, mesh),
        mesh=mesh,
        in_specs=(vectors, vectors, cells, cells, P(), P()),
        out_specs=(vectors, vectors, cells),
        check_vma=False,
    )
```

time: 838 us -> 516 us (0.62)
  Pallas kernels: 455 us -> 269 us
  waiting for transfers between devices: 265 us -> 101 us
  starting transfers between devices: 50 us -> 80.3 us
  between operations: 15.6 us -> 2.89 us
  local copies, waits for them, and re-layouts: 24.7 us -> 37.3 us
    pallas_call x2 -> x4, Pallas kernels: 384 us -> 200 us  [the longest x1 87.9 us: field_call(): pl.pallas_call(functools.partial(field_body, plan, group), out_shape=[sha...]
    reduce_scatter x1 -> x0, waiting for transfers between devices: 182 us -> none  [on_device(): lax.psum_scatter(partial_sums.reshape(-1, plan.px, plan.py, plan.zl), axe...]
    ppermute x12 -> x48, starting transfers between devices: 21.4 us -> 51.4 us  [the longest x8 13.2 us: along(): lax.ppermute(array, 'gy', [(2 * a + c, 2 * b + c) for a, b in pairs for c...]
    ppermute x12 -> x48, waiting for transfers between devices: 68.9 us -> 94 us  [the longest x2 17.8 us: across_sums(): a = a + lax.ppermute(ay, 'gx', flip)]
  transfers between devices with their start and end apart: 26 -> 60, of which waited for: 11 -> 19; matrix products, arithmetic and copies ran while one was open for 3% -> 8% of each run, Pallas kernels for 9% -> 17%
where the time goes in v2:
time: 516 us; the launch traced here: 510 us
  Pallas kernels  269 us (52%)
  waiting for transfers between devices  101 us (20%)
  starting transfers between devices  80.3 us (16%)
  local copies, waits for them, and re-layouts  37.3 us (7%)
  other arithmetic  19.7 us (4%)
    pallas_call x1, Pallas kernels, field_call(): pl.pallas_call(functools.partial(field_body, plan, group), out_shape=[sha...  87.9 us
    pallas_call x1, Pallas kernels, adjoint_call(): pl.pallas_call(functools.partial(adjoint_body, plan, group), out_shape=[j...  79.6 us
    pallas_call x1, Pallas kernels, adjoint_cells_call(): pl.pallas_call(functools.partial(adjoint_cells_body, chunk), grid=(xl //...  28.3 us
    pallas_call x1, Pallas kernels, next_cells_call(): pl.pallas_call(functools.partial(next_cells_body, chunk), grid=(xl // chu...  23.6 us
    pallas_call x1, Pallas kernels, source_call(): pl.pallas_call(functools.partial(source_body, chunk), grid=(xl // chunk,)...  19.3 us
    ppermute x6, starting transfers between devices, to_neighbours(): above = lax.ppermute(low_face, axis, [(i + 1, i) for i in range(count - 1)])  18.4 us
    ppermute x2, waiting for transfers between devices, across_sums(): a = a + lax.ppermute(ay, 'gx', flip)  17.8 us
    ppermute x3, waiting for transfers between devices, relay_sums(): lax.ppermute(first, ('gx', 'gz'), [(r, 0)])  17.3 us
  transfers between devices with their start and end apart: 60, of which 19 were waited for; matrix products, arithmetic and copies ran while one was open for 8% of the time, Pallas kernels for 17%

profile of v2, /device:TPU:12, one launch (start us, length us, event | category | flops | bytes accessed | tf_op | source)
XLA Modules:
  0.0 510.2 jit_solution(6091019683274907967)
XLA Ops:
  0.6 1.5 fusion.10
  2.2 1.3 compare_and_fusion.2
  3.4 1.3 compare_and_fusion.1
  4.8 1.2 compare_and_fusion
  6.6 2.9 fusion
  12.7 1.4 collective-permute-start.1
  15.2 1.5 collective-permute-start.2
  25.0 1.4 dynamic-slice_bitcast_fusion.12
  26.4 1.5 dynamic-slice_bitcast_fusion.10
  32.2 16.9 %shard_map.454 = (f32[7,128,128]{2,1,0:T(8,128)}, f32[7,128,128]{2,1,0:T(8,128)}, f32[7,32,128]{2,1,0:T(8,128)}, f32[7,32,128]{2,1,0:T(8,128)}) custom-call(f32[3,128,32,128]{3,2,1,0:T(8,128)} %va_ref.3, f32[3,128,32,128]{3,2,1,0:T(8,128)} %aa_ref.3, f32[128,32,128]{2,1,0:T(8,128)} %c_ref.5), custom_call_target="tpu_custom_call" | custom-call | tf_op jit(solution)/shard_map/pallas_call | solution.py:659
  49.4 1.6 dynamic-slice_bitcast_fusion.fy_ref
  54.2 3.6 collective-permute-start.3
  57.8 1.3 constant_dynamic-update-slice_fusion.g_ref
  59.2 1.9 collective-permute-start.6
  61.1 3.6 collective-permute-start.7
  66.0 1.3 collective-permute-start.4
  67.3 5.9 %collective-permute-start.5 = (f32[7,32,128]{2,1,0:T(8,128)S(1)}, f32[7,32,128]{2,1,0:T(8,128)S(1)}, u32[]{:S(2)}, u32[]{:S(2)}) collective-permute-start(f32[7,32,128]{2,1,0:T(8,128)S(1)} %get-tuple-element.115), channel_id=1, source_target_pairs={{16,0},{17,1},{18,2},{19,3},{20,4},{21,5},{22,6},{23,7},{24,8},{25... | collective-permute-start | bytes 344072 | tf_op jit(solution)/shard_map/ppermute | solution.py:672
  74.1 1.3 collective-permute-start.8
  75.6 1.3 collective-permute-start.9
  76.9 1.8 concatenate.90.g_ref
  78.7 1.5 dynamic-slice_bitcast_fusion.3.fx_ref
  80.3 2.2 collective-permute-done.9.zhi_ref
  82.5 1.3 collective-permute-start.10
  84.7 1.6 dynamic-slice_bitcast_fusion.2.fx_ref
  87.6 1.6 dynamic-slice_bitcast_fusion.1.fy_ref
  89.1 2.2 collective-permute-start.16
  91.4 19.3 %shard_map.455.source_ref = f32[32,128,128]{2,1,0:T(8,128)} custom-call(f32[3,128,32,128]{3,2,1,0:T(8,128)} %aa_ref.3, f32[3,128,32,128]{3,2,1,0:T(8,128)} %aa_ref.3, f32[3,128,32,128]{3,2,1,0:T(8,128)} %aa_ref.3, f32[128,32,128]{2,1,0:T(8,128)} %c_ref.5, f32[128,32,128]{2,1,0:T(8,128)} %c_ref.5, f32[128,32,128]{2,1,0:T(8,128)} %c_ref.5, ...), custom_call_target="tpu_custom_call" | custom-call | tf_op jit(solution)/shard_map/pallas_call | solution.py:876
  115.3 2.5 collective-permute-start.14
  117.9 3.6 collective-permute-done.12
  121.6 2.5 collective-permute-start.13
  125.2 7.4 %collective-permute-done.17 = f32[512,128]{1,0:T(8,128)S(1)} collective-permute-done((f32[512,128]{1,0:T(8,128)S(1)}, f32[512,128]{1,0:T(8,128)S(1)}, u32[]{:S(2)}, u32[]{:S(2)}) %collective-permute-start.17) | collective-permute-done | bytes 262176 | tf_op jit(solution)/shard_map/ppermute | solution.py:591
  133.5 8.8 %collective-permute-done.19 = f32[512,128]{1,0:T(8,128)S(1)} collective-permute-done((f32[512,128]{1,0:T(8,128)S(1)}, f32[512,128]{1,0:T(8,128)S(1)}, u32[]{:S(2)}, u32[]{:S(2)}) %collective-permute-start.19) | collective-permute-done | bytes 262176 | tf_op jit(solution)/shard_map/ppermute | solution.py:592
  142.3 1.8 collective-permute-start.18
  146.3 10.5 %collective-permute-done.18.refs_5_ = f32[1024,128]{1,0:T(8,128)S(1)} collective-permute-done((f32[1024,128]{1,0:T(8,128)S(1)}, f32[1024,128]{1,0:T(8,128)S(1)}, u32[]{:S(2)}, u32[]{:S(2)}) %collective-permute-start.18) | collective-permute-done | bytes 524320 | tf_op jit(solution)/shard_map/ppermute | solution.py:593
  156.8 1.5 collective-permute-done.20.refs_7_
  160.4 87.9 %shard_map.456 = (f32[12288,128]{1,0:T(8,128)}, f32[12288,128]{1,0:T(8,128)}) custom-call(f32[128]{0:T(128)} %fusion.4.w1_ref, bf16[128,384]{1,0:T(8,128)(2,1)} %dynamic-slice_bitcast_fusion.3.fx_ref, bf16[384,256]{1,0:T(8,128)(2,1)} %constant.402.clone.ez_ref, bf16[256,384]{1,0:T(8,128)(2,1)} %dynamic-slice_bitcast_fusion.fy_ref, ...), custom_call_target="tpu_custom_call" | custom-call | tf_op jit(solution)/shard_map/pallas_call | solution.py:450
  248.8 10.1 %collective-permute-done.29.arrived_ref = f32[3,32,128,128]{3,2,1,0:T(8,128)} collective-permute-done((f32[3,32,128,128]{3,2,1,0:T(8,128)}, f32[3,32,128,128]{3,2,1,0:T(8,128)}, u32[]{:S(2)}, u32[]{:S(2)}) %collective-permute-start.29) | collective-permute-done | bytes 6291488 | tf_op jit(solution)/shard_map/ppermute | solution.py:511
  259.0 13.6 %shard_map.457 = (f32[3,32,128,128]{3,2,1,0:T(8,128)}, f32[128,32,128]{2,1,0:T(8,128)}, f32[128,128]{1,0:T(8,128)}, f32[128,128]{1,0:T(8,128)}, f32[32,128]{1,0:T(8,128)}, /*index=5*/f32[32,128]{1,0:T(8,128)}) custom-call(f32[3]{0:T(128)} %pad_maximum_fusion.16.app_ref, f32[3,32,128,128]{3,2,1,0:T(8,128)} %bitcast.87, ...), custom_call_target="tpu_custom_call" | custom-call | tf_op jit(solution)/shard_map/pallas_call | solution.py:713
  273.0 2.7 collective-permute-start.35
  275.7 1.3 collective-permute-start.36
  277.0 1.9 collective-permute-start.33
  279.0 3.6 collective-permute-start.34
  283.4 2.6 collective-permute-start.32
  286.0 1.5 collective-permute-start.31
  287.5 4.1 collective-permute-done.31.exlo_ref
  292.2 79.6 %shard_map.458 = (f32[1024,128]{1,0:T(8,128)}, f32[1024,128]{1,0:T(8,128)}, f32[1024,128]{1,0:T(8,128)}, f32[1024,128]{1,0:T(8,128)}, f32[1024,128]{1,0:T(8,128)...) custom-call(f32[128]{0:T(128)} %fusion.4.w1_ref, ...), custom_call_target="tpu_custom_call" | custom-call | tf_op jit(solution)/shard_map/pallas_call | solution.py:497
  371.9 3.1 collective-permute-start.38
  379.4 2.7 collective-permute-start.43
  383.0 9.1 %collective-permute-done.39 = f32[1024,128]{1,0:T(8,128)S(1)} collective-permute-done((f32[1024,128]{1,0:T(8,128)S(1)}, f32[1024,128]{1,0:T(8,128)S(1)}, u32[]{:S(2)}, u32[]{:S(2)}) %collective-permute-start.39) | collective-permute-done | bytes 524320 | tf_op jit(solution)/shard_map/ppermute | solution.py:599
  392.5 2.7 collective-permute-start.52
  396.3 2.0 collective-permute-start.44
  398.3 8.7 %collective-permute-done.48 = f32[1024,128]{1,0:T(8,128)S(1)} collective-permute-done((f32[1024,128]{1,0:T(8,128)S(1)}, f32[1024,128]{1,0:T(8,128)S(1)}, u32[]{:S(2)}, u32[]{:S(2)}) %collective-permute-start.48) | collective-permute-done | bytes 524320 | tf_op jit(solution)/shard_map/ppermute | solution.py:599
  407.0 2.7 collective-permute-start.49
  409.7 3.9 collective-permute-done.40
  415.3 1.8 collective-permute-start.53
  417.0 23.6 %shard_map.459 = f32[3,128,32,128]{3,2,1,0:T(8,128)} custom-call(f32[3,128,32,128]{3,2,1,0:T(8,128)} %va_ref.3, f32[3,128,32,128]{3,2,1,0:T(8,128)} %va_ref.3, f32[3,128,32,128]{3,2,1,0:T(8,128)} %va_ref.3, f32[128,32,128]{2,1,0:T(8,128)} %get-tuple-element.186.e_ref.eb_ref.ea_ref, f32[128,32,128]{2,1,0:T(8,128)} %get-tuple-element.186.e_ref.eb_ref.ea_ref, ...), custom_call_target="tpu_custom_call" | custom-call | tf_op jit(solution)/shard_map/pallas_call | solution.py:918
  440.8 1.3 collective-permute-start.54
  442.1 28.3 %shard_map.460 = f32[3,128,32,128]{3,2,1,0:T(8,128)} custom-call(f32[3,128,32,128]{3,2,1,0:T(8,128)} %va_ref.3, f32[3,128,32,128]{3,2,1,0:T(8,128)} %va_ref.3, f32[3,128,32,128]{3,2,1,0:T(8,128)} %va_ref.3, f32[3,128,32,128]{3,2,1,0:T(8,128)} %aa_ref.3, f32[3,128,32,128]{3,2,1,0:T(8,128)} %aa_ref.3, f32[3,128,32,128]{3,2,1,0:T(8,128)} %aa_ref.3, ...), custom_call_target="tpu_custom_call" | custom-call | tf_op jit(solution)/shard_map/pallas_call | solution.py:894
  470.5 1.9 collective-permute-start.56
  472.5 1.3 collective-permute-start.55
  473.8 11.0 %collective-permute-done.56 = f32[1024,128]{1,0:T(8,128)S(1)} collective-permute-done((f32[1024,128]{1,0:T(8,128)S(1)}, f32[1024,128]{1,0:T(8,128)S(1)}, u32[]{:S(2)}, u32[]{:S(2)}) %collective-permute-start.56) | collective-permute-done | bytes 524320 | tf_op jit(solution)/shard_map/ppermute | solution.py:557
  485.9 3.3 collective-permute-start.58
  490.6 17.3 %collective-permute-done.58 = f32[1024,128]{1,0:T(8,128)S(1)} collective-permute-done((f32[1024,128]{1,0:T(8,128)S(1)}, f32[1024,128]{1,0:T(8,128)S(1)}, u32[]{:S(2)}, u32[]{:S(2)}) %collective-permute-start.58) | collective-permute-done | bytes 524320 | tf_op jit(solution)/shard_map/ppermute | solution.py:619
  508.5 1.7 and_select_fusion
  (264 shorter events, 49.2 us)
Async XLA Ops:
  10.9 42.2 %collective-permute-start = (f32[1024,128]{1,0:T(8,128)}, f32[1024,128]{1,0:T(8,128)S(1)}, u32[]{:S(2)}, u32[]{:S(2)}) collective-permute-start(f32[1024,128]{1,0:T(8,128)} %bitcast.8), channel_id=1, source_target_pairs={{0,1},{2,3},{4,5},{6,7},{8,9},{10,11},{12,13},{14,15}} | collective-permute-start | bytes 1572872 | tf_op jit(solution)/shard_map/ppermute | solution.py:568
  12.7 40.3 %collective-permute-start.1 = (f32[1024,128]{1,0:T(8,128)}, f32[1024,128]{1,0:T(8,128)S(1)}, u32[]{:S(2)}, u32[]{:S(2)}) collective-permute-start(f32[1024,128]{1,0:T(8,128)} %bitcast.9), channel_id=1, source_target_pairs={{0,16},{2,18},{4,20},{6,22},{8,24},{10,26},{12,28},{14,30}} | collective-permute-start | bytes 1572872 | tf_op jit(solution)/shard_map/ppermute | solution.py:568
  15.2 37.8 %collective-permute-start.2 = (f32[1024,128]{1,0:T(8,128)}, f32[1024,128]{1,0:T(8,128)}, u32[]{:S(2)}, u32[]{:S(2)}) collective-permute-start(f32[1024,128]{1,0:T(8,128)} %bitcast.10), channel_id=1, source_target_pairs={{0,17},{2,19},{4,21},{6,23},{8,25},{10,27},{12,29},{14,31}} | collective-permute-start | bytes 1572872 | tf_op jit(solution)/shard_map/ppermute | solution.py:568
  54.2 32.1 %copy-start.32 = (bf16[128,128]{1,0:T(8,128)(2,1)S(1)}, bf16[128,128]{1,0:T(8,128)(2,1)}, u32[]{:S(2)}) copy-start(bf16[128,128]{1,0:T(8,128)(2,1)} %get-tuple-element.265) | copy-start | bytes 98308
  54.2 28.3 %collective-permute-start.3 = (f32[1024,128]{1,0:T(8,128)S(1)}, f32[1024,128]{1,0:T(8,128)S(1)}, u32[]{:S(2)}, u32[]{:S(2)}) collective-permute-start(f32[1024,128]{1,0:T(8,128)S(1)} %fusion.2), channel_id=1, source_target_pairs={{0,4},{2,6},{4,8},{6,10},{1,5},{3,7},{5,9},{7,11},{16,20},{18,22},... | collective-permute-start | bytes 1572872 | tf_op jit(solution)/shard_map/ppermute | solution.py:557
  59.2 23.3 %collective-permute-start.6 = (f32[7,128,128]{2,1,0:T(8,128)}, f32[7,128,128]{2,1,0:T(8,128)S(1)}, u32[]{:S(2)}, u32[]{:S(2)}) collective-permute-start(f32[7,128,128]{2,1,0:T(8,128)} %get-tuple-element.116), channel_id=1, source_target_pairs={{0,2},{2,4},{4,6},{6,8},{8,10},{10,12},{12,14},{1,3},{3,5},{5,7},{... | collective-permute-start | bytes 1376264 | tf_op jit(solution)/shard_map/ppermute | solution.py:671
  61.1 21.4 %collective-permute-start.7 = (f32[7,128,128]{2,1,0:T(8,128)}, f32[7,128,128]{2,1,0:T(8,128)S(1)}, u32[]{:S(2)}, u32[]{:S(2)}) collective-permute-start(f32[7,128,128]{2,1,0:T(8,128)} %get-tuple-element.117), channel_id=1, source_target_pairs={{2,0},{4,2},{6,4},{8,6},{10,8},{12,10},{14,12},{3,1},{5,3},{7,5},{... | collective-permute-start | bytes 1376264 | tf_op jit(solution)/shard_map/ppermute | solution.py:672
  66.0 8.0 %collective-permute-start.4 = (f32[7,32,128]{2,1,0:T(8,128)S(1)}, f32[7,32,128]{2,1,0:T(8,128)S(1)}, u32[]{:S(2)}, u32[]{:S(2)}) collective-permute-start(f32[7,32,128]{2,1,0:T(8,128)S(1)} %get-tuple-element.114), channel_id=1, source_target_pairs={{0,16},{1,17},{2,18},{3,19},{4,20},{5,21},{6,22},{7,23},{8,24},{9,... | collective-permute-start | bytes 344072 | tf_op jit(solution)/shard_map/ppermute | solution.py:671
  67.3 8.3 %collective-permute-start.5 = (f32[7,32,128]{2,1,0:T(8,128)S(1)}, f32[7,32,128]{2,1,0:T(8,128)S(1)}, u32[]{:S(2)}, u32[]{:S(2)}) collective-permute-start(f32[7,32,128]{2,1,0:T(8,128)S(1)} %get-tuple-element.115), channel_id=1, source_target_pairs={{16,0},{17,1},{18,2},{19,3},{20,4},{21,5},{22,6},{23,7},{24,8},{25... | collective-permute-start | bytes 344072 | tf_op jit(solution)/shard_map/ppermute | solution.py:672
  74.1 6.2 %collective-permute-start.8 = (f32[7,32,128]{2,1,0:T(8,128)}, f32[7,32,128]{2,1,0:T(8,128)S(1)}, u32[]{:S(2)}, u32[]{:S(2)}) collective-permute-start(f32[7,32,128]{2,1,0:T(8,128)} %get-tuple-element.118), channel_id=1, source_target_pairs={{0,1},{2,3},{4,5},{6,7},{8,9},{10,11},{12,13},{14,15},{16,17},{18,... | collective-permute-start | bytes 344072 | tf_op jit(solution)/shard_map/ppermute | solution.py:671
  75.6 6.9 %collective-permute-start.9 = (f32[7,32,128]{2,1,0:T(8,128)}, f32[7,32,128]{2,1,0:T(8,128)S(1)}, u32[]{:S(2)}, u32[]{:S(2)}) collective-permute-start(f32[7,32,128]{2,1,0:T(8,128)} %get-tuple-element.119), channel_id=1, source_target_pairs={{1,0},{3,2},{5,4},{7,6},{9,8},{11,10},{13,12},{15,14},{17,16},{19,... | collective-permute-start | bytes 344072 | tf_op jit(solution)/shard_map/ppermute | solution.py:672
  82.5 28.2 %collective-permute-start.10 = (f32[1024,128]{1,0:T(8,128)S(1)}, f32[1024,128]{1,0:T(8,128)S(1)}, u32[]{:S(2)}, u32[]{:S(2)}) collective-permute-start(f32[1024,128]{1,0:T(8,128)S(1)} %collective-permute-done.3), channel_id=1, source_target_pairs={{4,8},{6,10},{8,12},{10,14},{5,9},{7,11},{9,13},{11,15},{20,24},{2... | collective-permute-start | bytes 1572872 | tf_op jit(solution)/shard_map/ppermute | solution.py:557
  89.1 25.5 %collective-permute-start.16 = (f32[1024,128]{1,0:T(8,128)S(1)}, f32[1024,128]{1,0:T(8,128)}, u32[]{:S(2)}, u32[]{:S(2)}) collective-permute-start(f32[1024,128]{1,0:T(8,128)S(1)} %fusion.2), channel_id=1, source_target_pairs={{4,0},{6,2},{5,1},{7,3},{20,16},{22,18},{21,17},{23,19}} | collective-permute-start | bytes 1572872 | tf_op jit(solution)/shard_map/ppermute | solution.py:557
  110.7 4.0 collective-permute-start.11
  114.9 6.6 %collective-permute-start.12 = (f32[512,128]{1,0:T(8,128)S(1)}, f32[512,128]{1,0:T(8,128)S(1)}, u32[]{:S(2)}, u32[]{:S(2)}) collective-permute-start(f32[512,128]{1,0:T(8,128)S(1)} %get-tuple-element.230), channel_id=1, source_target_pairs={{0,1},{1,0},{2,3},{3,2},{4,5},{5,4},{6,7},{7,6},{8,9},{9,8},{10,11... | collective-permute-start | bytes 786440 | tf_op jit(solution)/shard_map/ppermute | solution.py:591
  115.3 9.7 %collective-permute-start.14 = (f32[512,128]{1,0:T(8,128)S(1)}, f32[512,128]{1,0:T(8,128)S(1)}, u32[]{:S(2)}, u32[]{:S(2)}) collective-permute-start(f32[512,128]{1,0:T(8,128)S(1)} %get-tuple-element.229), channel_id=1, source_target_pairs={{0,16},{16,0},{1,17},{17,1},{2,18},{18,2},{3,19},{19,3},{4,20},{20... | collective-permute-start | bytes 786440 | tf_op jit(solution)/shard_map/ppermute | solution.py:592
  121.5 20.8 %collective-permute-start.21 = (f32[1024,128]{1,0:T(8,128)S(1)}, f32[1024,128]{1,0:T(8,128)S(1)}, u32[]{:S(2)}, u32[]{:S(2)}) collective-permute-start(f32[1024,128]{1,0:T(8,128)S(1)} %pad_maximum_fusion.refs_0_), channel_id=1, source_target_pairs={{0,2},{2,0},{4,6},{6,4},{8,10},{10,8},{12,14},{14,12},{1,3},{3,1},... | collective-permute-start | bytes 1572872 | tf_op jit(solution)/shard_map/ppermute | solution.py:511
  121.6 22.6 %collective-permute-start.13 = (f32[1024,128]{1,0:T(8,128)S(1)}, f32[1024,128]{1,0:T(8,128)S(1)}, u32[]{:S(2)}, u32[]{:S(2)}) collective-permute-start(f32[1024,128]{1,0:T(8,128)S(1)} %pad_maximum_fusion.refs_0_), channel_id=1, source_target_pairs={{0,16},{16,0},{1,17},{17,1},{2,18},{18,2},{3,19},{19,3},{4,20},{20... | collective-permute-start | bytes 1572872 | tf_op jit(solution)/shard_map/ppermute | solution.py:593
  124.2 8.4 %collective-permute-start.17 = (f32[512,128]{1,0:T(8,128)S(1)}, f32[512,128]{1,0:T(8,128)S(1)}, u32[]{:S(2)}, u32[]{:S(2)}) collective-permute-start(f32[512,128]{1,0:T(8,128)S(1)} %get-tuple-element.228), channel_id=1, source_target_pairs={{0,1},{1,0},{2,3},{3,2},{4,5},{5,4},{6,7},{7,6},{8,9},{9,8},{10,11... | collective-permute-start | bytes 786440 | tf_op jit(solution)/shard_map/ppermute | solution.py:591
  125.1 17.2 %collective-permute-start.19 = (f32[512,128]{1,0:T(8,128)S(1)}, f32[512,128]{1,0:T(8,128)S(1)}, u32[]{:S(2)}, u32[]{:S(2)}) collective-permute-start(f32[512,128]{1,0:T(8,128)S(1)} %get-tuple-element.227), channel_id=1, source_target_pairs={{0,16},{16,0},{1,17},{17,1},{2,18},{18,2},{3,19},{19,3},{4,20},{20... | collective-permute-start | bytes 786440 | tf_op jit(solution)/shard_map/ppermute | solution.py:592
  125.1 35.2 %copy-start.3 = (f32[1024,128]{1,0:T(8,128)}, f32[1024,128]{1,0:T(8,128)S(1)}, u32[]{:S(2)}) copy-start(f32[1024,128]{1,0:T(8,128)S(1)} %pad_maximum_fusion.1.refs_2_) | copy-start | bytes 1572868
  125.1 19.9 %collective-permute-start.23 = (f32[1024,128]{1,0:T(8,128)S(1)}, f32[1024,128]{1,0:T(8,128)S(1)}, u32[]{:S(2)}, u32[]{:S(2)}) collective-permute-start(f32[1024,128]{1,0:T(8,128)S(1)} %pad_maximum_fusion.1.refs_2_), channel_id=1, source_target_pairs={{0,2},{2,0},{4,6},{6,4},{8,10},{10,8},{12,14},{14,12},{1,3},{3,1},... | collective-permute-start | bytes 1572872 | tf_op jit(solution)/shard_map/ppermute | solution.py:511
  132.6 13.2 %collective-permute-start.15 = (f32[1024,128]{1,0:T(8,128)S(1)}, f32[1024,128]{1,0:T(8,128)S(1)}, u32[]{:S(2)}, u32[]{:S(2)}) collective-permute-start(f32[1024,128]{1,0:T(8,128)S(1)} %pad_maximum_fusion.1.refs_2_), channel_id=1, source_target_pairs={{0,1},{1,0},{2,3},{3,2},{4,5},{5,4},{6,7},{7,6},{8,9},{9,8},{10,11... | collective-permute-start | bytes 1572872 | tf_op jit(solution)/shard_map/ppermute | solution.py:593
  142.3 3.5 collective-permute-start.25
  142.3 14.4 %collective-permute-start.18 = (f32[1024,128]{1,0:T(8,128)S(1)}, f32[1024,128]{1,0:T(8,128)S(1)}, u32[]{:S(2)}, u32[]{:S(2)}) collective-permute-start(f32[1024,128]{1,0:T(8,128)S(1)} %pad_maximum_fusion.2.refs_4_), channel_id=1, source_target_pairs={{0,16},{16,0},{1,17},{17,1},{2,18},{18,2},{3,19},{19,3},{4,20},{20... | collective-permute-start | bytes 1572872 | tf_op jit(solution)/shard_map/ppermute | solution.py:593
  144.2 14.1 %collective-permute-start.20 = (f32[1024,128]{1,0:T(8,128)S(1)}, f32[1024,128]{1,0:T(8,128)S(1)}, u32[]{:S(2)}, u32[]{:S(2)}) collective-permute-start(f32[1024,128]{1,0:T(8,128)S(1)} %pad_maximum_fusion.3.refs_6_), channel_id=1, source_target_pairs={{0,1},{1,0},{2,3},{3,2},{4,5},{5,4},{6,7},{7,6},{8,9},{9,8},{10,11... | collective-permute-start | bytes 1572872 | tf_op jit(solution)/shard_map/ppermute | solution.py:593
  145.0 13.2 %collective-permute-start.27 = (f32[1024,128]{1,0:T(8,128)S(1)}, f32[1024,128]{1,0:T(8,128)S(1)}, u32[]{:S(2)}, u32[]{:S(2)}) collective-permute-start(f32[1024,128]{1,0:T(8,128)S(1)} %pad_maximum_fusion.3.refs_6_), channel_id=1, source_target_pairs={{0,2},{2,0},{4,6},{6,4},{8,10},{10,8},{12,14},{14,12},{1,3},{3,1},... | collective-permute-start | bytes 1572872 | tf_op jit(solution)/shard_map/ppermute | solution.py:511
  145.8 12.5 %collective-permute-start.22 = (f32[1024,128]{1,0:T(8,128)S(1)}, f32[1024,128]{1,0:T(8,128)S(1)}, u32[]{:S(2)}, u32[]{:S(2)}) collective-permute-start(f32[1024,128]{1,0:T(8,128)S(1)} %collective-permute-done.13.refs_1_), channel_id=1, source_target_pairs={{0,2},{2,0},{4,6},{6,4},{8,10},{10,8},{12,14},{14,12},{1,3},{3,1},... | collective-permute-start | bytes 1572872 | tf_op jit(solution)/shard_map/ppermute | solution.py:511
  145.8 12.5 %collective-permute-start.24 = (f32[1024,128]{1,0:T(8,128)S(1)}, f32[1024,128]{1,0:T(8,128)S(1)}, u32[]{:S(2)}, u32[]{:S(2)}) collective-permute-start(f32[1024,128]{1,0:T(8,128)S(1)} %collective-permute-done.15.refs_3_), channel_id=1, source_target_pairs={{0,2},{2,0},{4,6},{6,4},{8,10},{10,8},{12,14},{14,12},{1,3},{3,1},... | collective-permute-start | bytes 1572872 | tf_op jit(solution)/shard_map/ppermute | solution.py:511
  156.8 1.9 collective-permute-start.26
  158.2 2.1 collective-permute-start.28
  248.3 10.7 %collective-permute-start.29 = (f32[3,32,128,128]{3,2,1,0:T(8,128)}, f32[3,32,128,128]{3,2,1,0:T(8,128)}, u32[]{:S(2)}, u32[]{:S(2)}) collective-permute-start(f32[3,32,128,128]{3,2,1,0:T(8,128)} %bitcast.92), channel_id=1, source_target_pairs={{0,2},{2,0},{4,6},{6,4},{8,10},{10,8},{12,14},{14,12},{1,3},{3,1},... | collective-permute-start | bytes 18874376 | tf_op jit(solution)/shard_map/ppermute | solution.py:511
  272.6 19.1 %collective-permute-start.30 = (f32[3,32,128,128]{3,2,1,0:T(8,128)}, f32[3,32,128,128]{3,2,1,0:T(8,128)}, u32[]{:S(2)}, u32[]{:S(2)}) collective-permute-start(f32[3,32,128,128]{3,2,1,0:T(8,128)} %get-tuple-element.145), channel_id=1, source_target_pairs={{0,2},{2,0},{4,6},{6,4},{8,10},{10,8},{12,14},{14,12},{1,3},{3,1},... | collective-permute-start | bytes 18874376 | tf_op jit(solution)/shard_map/ppermute | solution.py:511
  273.0 10.3 %collective-permute-start.35 = (f32[32,128]{1,0:T(8,128)}, f32[32,128]{1,0:T(8,128)S(1)}, u32[]{:S(2)}, u32[]{:S(2)}) collective-permute-start(f32[32,128]{1,0:T(8,128)} %get-tuple-element.149), channel_id=1, source_target_pairs={{0,1},{2,3},{4,5},{6,7},{8,9},{10,11},{12,13},{14,15},{16,17},{18,... | collective-permute-start | bytes 49160 | tf_op jit(solution)/shard_map/ppermute | solution.py:671
  275.7 10.2 %collective-permute-start.36 = (f32[32,128]{1,0:T(8,128)}, f32[32,128]{1,0:T(8,128)S(1)}, u32[]{:S(2)}, u32[]{:S(2)}) collective-permute-start(f32[32,128]{1,0:T(8,128)} %get-tuple-element.150), channel_id=1, source_target_pairs={{1,0},{3,2},{5,4},{7,6},{9,8},{11,10},{13,12},{15,14},{17,16},{19,... | collective-permute-start | bytes 49160 | tf_op jit(solution)/shard_map/ppermute | solution.py:672
  277.0 14.6 %collective-permute-start.33 = (f32[128,128]{1,0:T(8,128)}, f32[128,128]{1,0:T(8,128)S(1)}, u32[]{:S(2)}, u32[]{:S(2)}) collective-permute-start(f32[128,128]{1,0:T(8,128)} %get-tuple-element.147), channel_id=1, source_target_pairs={{0,2},{2,4},{4,6},{6,8},{8,10},{10,12},{12,14},{1,3},{3,5},{5,7},{... | collective-permute-start | bytes 196616 | tf_op jit(solution)/shard_map/ppermute | solution.py:671
  279.0 12.6 %collective-permute-start.34 = (f32[128,128]{1,0:T(8,128)}, f32[128,128]{1,0:T(8,128)S(1)}, u32[]{:S(2)}, u32[]{:S(2)}) collective-permute-start(f32[128,128]{1,0:T(8,128)} %get-tuple-element.148), channel_id=1, source_target_pairs={{2,0},{4,2},{6,4},{8,6},{10,8},{12,10},{14,12},{3,1},{5,3},{7,5},{... | collective-permute-start | bytes 196616 | tf_op jit(solution)/shard_map/ppermute | solution.py:672
  283.4 4.1 collective-permute-start.32
  286.0 5.6 %collective-permute-start.31 = (f32[32,128]{1,0:T(8,128)S(1)}, f32[32,128]{1,0:T(8,128)S(1)}, u32[]{:S(2)}, u32[]{:S(2)}) collective-permute-start(f32[32,128]{1,0:T(8,128)S(1)} %get-tuple-element.218), channel_id=1, source_target_pairs={{0,16},{1,17},{2,18},{3,19},{4,20},{5,21},{6,22},{7,23},{8,24},{9,... | collective-permute-start | bytes 49160 | tf_op jit(solution)/shard_map/ppermute | solution.py:671
  291.6 80.2 %copy-start.38 = (f32[128,128]{1,0:T(8,128)}, f32[128,128]{1,0:T(8,128)S(1)}, u32[]{:S(2)}) copy-start(f32[128,128]{1,0:T(8,128)S(1)} %collective-permute-done.33.eylo_ref) | copy-start | bytes 196612
  291.6 80.2 %copy-start.39 = (f32[128,128]{1,0:T(8,128)}, f32[128,128]{1,0:T(8,128)S(1)}, u32[]{:S(2)}) copy-start(f32[128,128]{1,0:T(8,128)S(1)} %collective-permute-done.34.eyhi_ref) | copy-start | bytes 196612
  371.9 4.8 collective-permute-start.38
  374.9 3.0 collective-permute-start.42
  375.0 4.4 collective-permute-start.47
  375.4 6.8 %collective-permute-start.51 = (f32[1024,128]{1,0:T(8,128)}, f32[1024,128]{1,0:T(8,128)S(1)}, u32[]{:S(2)}, u32[]{:S(2)}) collective-permute-start(f32[1024,128]{1,0:T(8,128)} %get-tuple-element.207), channel_id=1, source_target_pairs={{0,2},{2,0},{4,6},{6,4},{8,10},{10,8},{12,14},{14,12},{1,3},{3,1},... | collective-permute-start | bytes 1572872 | tf_op jit(solution)/shard_map/ppermute | solution.py:511
  375.5 6.9 %collective-permute-start.37 = (f32[1024,128]{1,0:T(8,128)}, f32[1024,128]{1,0:T(8,128)S(1)}, u32[]{:S(2)}, u32[]{:S(2)}) collective-permute-start(f32[1024,128]{1,0:T(8,128)} %get-tuple-element.179), channel_id=1, source_target_pairs={{0,2},{2,0},{4,6},{6,4},{8,10},{10,8},{12,14},{14,12},{1,3},{3,1},... | collective-permute-start | bytes 1572872 | tf_op jit(solution)/shard_map/ppermute | solution.py:511
  377.8 14.3 %collective-permute-start.39 = (f32[1024,128]{1,0:T(8,128)S(1)}, f32[1024,128]{1,0:T(8,128)S(1)}, u32[]{:S(2)}, u32[]{:S(2)}) collective-permute-start(f32[1024,128]{1,0:T(8,128)S(1)} %add.266), channel_id=1, source_target_pairs={{0,16},{16,0},{1,17},{17,1},{2,18},{18,2},{3,19},{19,3},{4,20},{20... | collective-permute-start | bytes 1572872 | tf_op jit(solution)/shard_map/ppermute | solution.py:599
  377.9 14.6 %collective-permute-start.41 = (f32[1024,128]{1,0:T(8,128)}, f32[1024,128]{1,0:T(8,128)S(1)}, u32[]{:S(2)}, u32[]{:S(2)}) collective-permute-start(f32[1024,128]{1,0:T(8,128)} %get-tuple-element.183), channel_id=1, source_target_pairs={{0,2},{2,0},{4,6},{6,4},{8,10},{10,8},{12,14},{14,12},{1,3},{3,1},... | collective-permute-start | bytes 1572872 | tf_op jit(solution)/shard_map/ppermute | solution.py:511
  379.4 15.8 %collective-permute-start.43 = (f32[1024,128]{1,0:T(8,128)S(1)}, f32[1024,128]{1,0:T(8,128)S(1)}, u32[]{:S(2)}, u32[]{:S(2)}) collective-permute-start(f32[1024,128]{1,0:T(8,128)S(1)} %add.270), channel_id=1, source_target_pairs={{0,1},{1,0},{2,3},{3,2},{4,5},{5,4},{6,7},{7,6},{8,9},{9,8},{10,11... | collective-permute-start | bytes 1572872 | tf_op jit(solution)/shard_map/ppermute | solution.py:600
  382.2 14.0 %collective-permute-start.46 = (f32[1024,128]{1,0:T(8,128)S(1)}, f32[1024,128]{1,0:T(8,128)S(1)}, u32[]{:S(2)}, u32[]{:S(2)}) collective-permute-start(f32[1024,128]{1,0:T(8,128)S(1)} %copy-done.53), channel_id=1, source_target_pairs={{0,2},{2,0},{4,6},{6,4},{8,10},{10,8},{12,14},{14,12},{1,3},{3,1},... | collective-permute-start | bytes 1572872 | tf_op jit(solution)/shard_map/ppermute | solution.py:511
  382.4 32.0 %collective-permute-start.50 = (f32[1024,128]{1,0:T(8,128)S(1)}, f32[1024,128]{1,0:T(8,128)S(1)}, u32[]{:S(2)}, u32[]{:S(2)}) collective-permute-start(f32[1024,128]{1,0:T(8,128)S(1)} %copy-done.52), channel_id=1, source_target_pairs={{0,2},{2,0},{4,6},{6,4},{8,10},{10,8},{12,14},{14,12},{1,3},{3,1},... | collective-permute-start | bytes 1572872 | tf_op jit(solution)/shard_map/ppermute | solution.py:511
  392.1 14.8 %collective-permute-start.48 = (f32[1024,128]{1,0:T(8,128)S(1)}, f32[1024,128]{1,0:T(8,128)S(1)}, u32[]{:S(2)}, u32[]{:S(2)}) collective-permute-start(f32[1024,128]{1,0:T(8,128)S(1)} %add.274), channel_id=1, source_target_pairs={{0,16},{16,0},{1,17},{17,1},{2,18},{18,2},{3,19},{19,3},{4,20},{20... | collective-permute-start | bytes 1572872 | tf_op jit(solution)/shard_map/ppermute | solution.py:599
  392.5 22.0 %collective-permute-start.52 = (f32[1024,128]{1,0:T(8,128)S(1)}, f32[1024,128]{1,0:T(8,128)S(1)}, u32[]{:S(2)}, u32[]{:S(2)}) collective-permute-start(f32[1024,128]{1,0:T(8,128)S(1)} %add.278), channel_id=1, source_target_pairs={{0,1},{1,0},{2,3},{3,2},{4,5},{5,4},{6,7},{7,6},{8,9},{9,8},{10,11... | collective-permute-start | bytes 1572872 | tf_op jit(solution)/shard_map/ppermute | solution.py:600
  395.2 18.4 %collective-permute-start.40 = (f32[512,128]{1,0:T(8,128)S(1)}, f32[512,128]{1,0:T(8,128)S(1)}, u32[]{:S(2)}, u32[]{:S(2)}) collective-permute-start(f32[512,128]{1,0:T(8,128)S(1)} %slice.129), channel_id=1, source_target_pairs={{0,1},{1,0},{2,3},{3,2},{4,5},{5,4},{6,7},{7,6},{8,9},{9,8},{10,11... | collective-permute-start | bytes 786440 | tf_op jit(solution)/shard_map/ppermute | solution.py:601
  396.3 17.4 %collective-permute-start.44 = (f32[512,128]{1,0:T(8,128)S(1)}, f32[512,128]{1,0:T(8,128)S(1)}, u32[]{:S(2)}, u32[]{:S(2)}) collective-permute-start(f32[512,128]{1,0:T(8,128)S(1)} %slice.131), channel_id=1, source_target_pairs={{0,16},{16,0},{1,17},{17,1},{2,18},{18,2},{3,19},{19,3},{4,20},{20... | collective-permute-start | bytes 786440 | tf_op jit(solution)/shard_map/ppermute | solution.py:602
  407.0 33.6 %collective-permute-start.49 = (f32[512,128]{1,0:T(8,128)S(1)}, f32[512,128]{1,0:T(8,128)S(1)}, u32[]{:S(2)}, u32[]{:S(2)}) collective-permute-start(f32[512,128]{1,0:T(8,128)S(1)} %slice.133), channel_id=1, source_target_pairs={{0,1},{1,0},{2,3},{3,2},{4,5},{5,4},{6,7},{7,6},{8,9},{9,8},{10,11... | collective-permute-start | bytes 786440 | tf_op jit(solution)/shard_map/ppermute | solution.py:601
  413.7 27.0 %collective-permute-start.45 = (f32[1024,128]{1,0:T(8,128)S(1)}, f32[1024,128]{1,0:T(8,128)S(1)}, u32[]{:S(2)}, u32[]{:S(2)}) collective-permute-start(f32[1024,128]{1,0:T(8,128)S(1)} %pad_maximum_fusion.4), channel_id=1, source_target_pairs={{12,8},{14,10},{13,9},{15,11},{28,24},{30,26},{29,25},{31,27}} | collective-permute-start | bytes 1572872 | tf_op jit(solution)/shard_map/ppermute | solution.py:557
  415.3 25.4 %collective-permute-start.53 = (f32[512,128]{1,0:T(8,128)}, f32[512,128]{1,0:T(8,128)S(1)}, u32[]{:S(2)}, u32[]{:S(2)}) collective-permute-start(f32[512,128]{1,0:T(8,128)} %slice.135), channel_id=1, source_target_pairs={{0,16},{16,0},{1,17},{17,1},{2,18},{18,2},{3,19},{19,3},{4,20},{20... | collective-permute-start | bytes 786440 | tf_op jit(solution)/shard_map/ppermute | solution.py:602
  440.8 29.6 %collective-permute-start.54 = (f32[1024,128]{1,0:T(8,128)S(1)}, f32[1024,128]{1,0:T(8,128)S(1)}, u32[]{:S(2)}, u32[]{:S(2)}) collective-permute-start(f32[1024,128]{1,0:T(8,128)S(1)} %fusion.3), channel_id=1, source_target_pairs={{12,8},{14,10},{8,4},{10,6},{13,9},{15,11},{9,5},{11,7},{28,24},{3... | collective-permute-start | bytes 1572872 | tf_op jit(solution)/shard_map/ppermute | solution.py:557
  470.5 14.2 %collective-permute-start.56 = (f32[1024,128]{1,0:T(8,128)S(1)}, f32[1024,128]{1,0:T(8,128)S(1)}, u32[]{:S(2)}, u32[]{:S(2)}) collective-permute-start(f32[1024,128]{1,0:T(8,128)S(1)} %get-tuple-element.211), channel_id=1, source_target_pairs={{8,4},{10,6},{4,0},{6,2},{9,5},{11,7},{5,1},{7,3},{24,20},{26,22},... | collective-permute-start | bytes 1572872 | tf_op jit(solution)/shard_map/ppermute | solution.py:557
  472.5 12.6 %collective-permute-start.55 = (f32[1024,128]{1,0:T(8,128)S(1)}, f32[1024,128]{1,0:T(8,128)S(1)}, u32[]{:S(2)}, u32[]{:S(2)}) collective-permute-start(f32[1024,128]{1,0:T(8,128)S(1)} %get-tuple-element.212), channel_id=1, source_target_pairs={{0,4},{2,6},{1,5},{3,7},{16,20},{18,22},{17,21},{19,23}} | collective-permute-start | bytes 1572872 | tf_op jit(solution)/shard_map/ppermute | solution.py:557
  485.2 5.1 collective-permute-start.59
  485.9 22.0 %collective-permute-start.58 = (f32[1024,128]{1,0:T(8,128)S(1)}, f32[1024,128]{1,0:T(8,128)S(1)}, u32[]{:S(2)}, u32[]{:S(2)}) collective-permute-start(f32[1024,128]{1,0:T(8,128)S(1)} %add_add_fusion), channel_id=1, source_target_pairs={{16,0},{18,2},{20,4},{22,6},{24,8},{26,10},{28,12},{30,14}} | collective-permute-start | bytes 1572872 | tf_op jit(solution)/shard_map/ppermute | solution.py:619
  489.2 18.9 %collective-permute-start.57 = (f32[1024,128]{1,0:T(8,128)S(1)}, f32[1024,128]{1,0:T(8,128)S(1)}, u32[]{:S(2)}, u32[]{:S(2)}) collective-permute-start(f32[1024,128]{1,0:T(8,128)S(1)} %add_add_fusion), channel_id=1, source_target_pairs={{1,0},{3,2},{5,4},{7,6},{9,8},{11,10},{13,12},{15,14}} | collective-permute-start | bytes 1572872 | tf_op jit(solution)/shard_map/ppermute | solution.py:619
  (51 other events, 639.4 us)

commit v3 on v2

--- a/solution.py
+++ b/solution.py
@@ -48,6 +48,18 @@
     return jnp.dot(left, right, preferred_element_type=jnp.float32)
 
 
+def twice_rows(table):
+    high, low = two_parts(table)
+    top = np.concatenate([high, high], axis=-1)
+    return np.concatenate([top, np.concatenate([low, np.zeros_like(low)], axis=-1)], axis=-2)
+
+
+def dot_rows(table, values):
+    both = dot(table, jnp.concatenate(split(values), axis=0))
+    half = both.shape[0] // 2
+    return both[:half] + both[half:]
+
+
 class Plan:
     def __init__(self, mesh, local):
         self.gx, self.gy, self.gz = (mesh.shape[a] for a in axes)
@@ -58,6 +70,7 @@
         self.yc = 2 * self.yl
         self.pitch = self.kx + 8
         self.px, self.py = self.xl // 4, self.yl // 2
+        self.unroll = 2 if self.py % 4 == 0 else 1
         self.relay = (self.gx, self.gy, self.gz) == (2, 8, 2)
         self.arrays = 16 if self.relay else 1
         self.segments = self.relay_segments() if self.relay else self.gathered_segments()
@@ -174,36 +187,41 @@
 
 
 def field_body(
-    plan, group, w1_ref, fx_ref, ez_ref, fy_ref, g_ref, z13_ref, z2_ref, z1n_ref, xs_ref, xb_ref, base_ref, *refs,
+    plan, group, places_ref, w1_ref,
+    fx_ref, ez_ref, fy_ref, g_ref, z13_ref, z2_ref, z1n_ref, xs_ref, xb_ref, base_ref, *refs,
 ):
     kx, kh, pitch = plan.kx, plan.kh, plan.pitch
+    w1_at = places_ref[8] * kx
     y2, z2, xl, yl, yc, zl = plan.y2, plan.z2, plan.xl, plan.yl, plan.yc, plan.zl
     span = yc * pitch
     m_refs, (own_ref, other_ref, s_ref, r_ref) = refs[: plan.arrays], refs[plan.arrays :]
 
     def along_x(number, segment):
-        def body(pair, carry):
-            planes = [load_plane(m_refs, plan, segment, 2 * pair + k) for k in range(2)]
-            high, low = split(pair_lanes(*planes))
-            out = dot(fx_ref[...], pair_rows(high, low, high))
-            row = (number * plan.py + 2 * pair) * pitch
-            s_ref[pl.ds(row, kx), :] = out[:, :z2]
-            s_ref[pl.ds(row + pitch, kx), :] = out[:, z2:]
+        def body(step, carry):
+            for pair in [plan.unroll * step + k for k in range(plan.unroll)]:
+                planes = [load_plane(m_refs, plan, segment, 2 * pair + k) for k in range(2)]
+                out = dot_rows(fx_ref[...], pair_lanes(*planes))
+                row = (number * plan.py + 2 * pair) * pitch
+                s_ref[pl.ds(row, kx), :] = out[:, :z2]
+                s_ref[pl.ds(row + pitch, kx), :] = out[:, z2:]
             return carry
 
-        lax.fori_loop(0, plan.py // 2, body, 0)
+        lax.fori_loop(0, plan.py // 2 // plan.unroll, body, 0)
 
     for number, segment in enumerate(plan.segments):
         along_x(number, segment)
 
-    def depth_waves(slots):
-        rows = pair_rows(*[s_ref[pl.ds(slot, y2, stride=pitch), :] for slot in slots])
-        high, low = split(rows)
+    def row_waves(slots):
+        planes = pair_lanes(*[s_ref[pl.ds(slot, y2, stride=pitch), :] for slot in slots])
+        out = dot_rows(fy_ref[...], planes)
+        return [out[:, part * z2 : (part + 1) * z2] for part in range(len(slots))]
+
+    def depth_waves(planes):
+        high, low = split(pair_rows(*planes))
         return dot(pair_lanes(high, low, high), ez_ref[...])
 
-    def one_slab(plane, kern):
-        high, low = split(plane)
-        high, low = split(dot(fy_ref[...], pair_rows(high, low, high)) * kern)
+    def one_slab(spectrum, kern):
+        high, low = split(spectrum * kern)
         both = dot(g_ref[...], high)
         return both[: 2 * yc] + both[2 * yc :] + dot(g_ref[: 2 * yc], low)
 
@@ -229,24 +247,24 @@
     def waves(step, carry):
         first = step * group
         slots = [first + k + part for k in range(group) for part in (0, kh)]
-        planes = depth_waves(slots)
+        planes = sum([row_waves(slots[2 * k : 2 * k + 2]) for k in range(group)], [])
+        spectra = depth_waves(planes)
         slabs = []
         for k in range(group):
-            kern = 1.0 / (base_ref[...] + w1_ref[first + k])
+            kern = 1.0 / (base_ref[...] + w1_ref[w1_at + first + k])
             for part in range(2):
-                at = (2 * k + part) * y2
-                slabs.append(one_slab(planes[at : at + y2], kern))
+                at = (2 * k + part) * plan.ny
+                slabs.append(one_slab(spectra[at : at + plan.ny], kern))
         depth_cells(slots, slabs, False)
         return carry
 
     lax.fori_loop(0, kh // group, waves, 0)
 
-    slab = one_slab(depth_waves([kh]), 1.0 / (base_ref[...] + w1_ref[kh]))
-    depth_cells([kh], [slab], True)
+    spectrum = depth_waves(row_waves([kh]))
+    depth_cells([kh], [one_slab(spectrum, 1.0 / (base_ref[...] + w1_ref[w1_at + kh]))], True)
 
     def back_x(mat_ref, values):
-        high, low = split(values)
-        return dot(mat_ref[...], pair_rows(high, low, high))
+        return dot_rows(mat_ref[...], values)
 
     def cells(out_ref, shift):
         def body(pair, carry):
@@ -270,16 +288,17 @@
 
 
 def adjoint_body(
-    plan, group, w1_ref, own_ref, other_ref, xs_ref, xb_ref, z13_ref, z2_ref, z1n_ref, g_ref, fy_ref, ez_ref, fx_ref, base_ref, *refs,
+    plan, group, places_ref, w1_ref,
+    fx_ref, ez_ref, fy_ref, g_ref, z13_ref, z2_ref, z1n_ref, xs_ref, xb_ref, base_ref, own_ref, other_ref, *refs,
 ):
     kx, kh, pitch = plan.kx, plan.kh, plan.pitch
+    w1_at = places_ref[8] * kx
     y2, z2, xl, yl, yc, zl = plan.y2, plan.z2, plan.xl, plan.yl, plan.yc, plan.zl
     span = yc * pitch
     m_refs, (s_ref, r_ref) = refs[: plan.arrays], refs[plan.arrays :]
 
     def along_x(mat_ref, values):
-        high, low = split(values)
-        return dot(mat_ref[...], pair_rows(high, low, high))
+        return dot_rows(mat_ref[...], values)
 
     def cells(f_ref, shift):
         def body(pair, carry):
@@ -317,47 +336,52 @@
         return jnp.where(first, q2, q1), jnp.where(first, 0.0, q2)
 
     def one_slab(q1, q2, kern):
-        high, low = split(pair_rows(q1, q2))
-        high, low = split(dot(g_ref[...], pair_rows(high, low, high)) * kern)
+        return dot_rows(g_ref[...], pair_rows(q1, q2)) * kern
+
+    def depth_cells(spectra):
+        high, low = split(pair_rows(*spectra))
+        out = dot(high, ez_ref[...])
+        return out[:, :z2] + out[:, z2:] + dot(low, ez_ref[:, :z2])
+
+    def row_cells(slots, planes):
+        high, low = split(pair_lanes(*planes))
         both = dot(fy_ref[...], high)
-        return both[:y2] + both[y2:] + dot(fy_ref[:y2], low)
-
-    def depth_cells(slots, slabs):
-        high, low = split(pair_rows(*slabs))
-        out = dot(high, ez_ref[...])
-        out = out[:, :z2] + out[:, z2:] + dot(low, ez_ref[:, :z2])
-        for place, slot in enumerate(slots):
-            s_ref[pl.ds(slot, y2, stride=pitch), :] = out[place * y2 : (place + 1) * y2]
+        out = both[:y2] + both[y2:] + dot(fy_ref[:y2], low)
+        for part, slot in enumerate(slots):
+            s_ref[pl.ds(slot, y2, stride=pitch), :] = out[:, part * z2 : (part + 1) * z2]
 
     def waves(step, carry):
         first = step * group
         slots = [first + k + part for k in range(group) for part in (0, kh)]
         q1, q2 = depth_waves(slots, False)
-        slabs = []
+        spectra = []
         for k in range(group):
-            kern = 1.0 / (base_ref[...] + w1_ref[first + k])
+            kern = 1.0 / (base_ref[...] + w1_ref[w1_at + first + k])
             for part in range(2):
                 take = slice((2 * k + part) * yc, (2 * k + part + 1) * yc)
-                slabs.append(one_slab(q1[take], q2[take], kern))
-        depth_cells(slots, slabs)
+                spectra.append(one_slab(q1[take], q2[take], kern))
+        planes = depth_cells(spectra)
+        planes = [planes[k * plan.ny : (k + 1) * plan.ny] for k in range(2 * group)]
+        for k in range(group):
+            row_cells(slots[2 * k : 2 * k + 2], planes[2 * k : 2 * k + 2])
         return carry
 
     lax.fori_loop(0, kh // group, waves, 0)
 
     q1, q2 = depth_waves([kh], True)
-    depth_cells([kh], [one_slab(q1, q2, 1.0 / (base_ref[...] + w1_ref[kh]))])
+    row_cells([kh], [depth_cells([one_slab(q1, q2, 1.0 / (base_ref[...] + w1_ref[w1_at + kh]))])])
 
     def back_x(number, segment):
-        def body(pair, carry):
-            row = (number * plan.py + 2 * pair) * pitch
-            planes = [s_ref[pl.ds(row + k * pitch, kx), :] for k in range(2)]
-            high, low = split(pair_lanes(*planes))
-            out = dot(fx_ref[...], pair_rows(high, low, high))
-            store_plane(m_refs, plan, segment, 2 * pair, out[:, :z2])
-            store_plane(m_refs, plan, segment, 2 * pair + 1, out[:, z2:])
+        def body(step, carry):
+            for pair in [plan.unroll * step + k for k in range(plan.unroll)]:
+                row = (number * plan.py + 2 * pair) * pitch
+                planes = [s_ref[pl.ds(row + k * pitch, kx), :] for k in range(2)]
+                out = dot_rows(fx_ref[...], pair_lanes(*planes))
+                store_plane(m_refs, plan, segment, 2 * pair, out[:, :z2])
+                store_plane(m_refs, plan, segment, 2 * pair + 1, out[:, z2:])
             return carry
 
-        lax.fori_loop(0, plan.py // 2, body, 0)
+        lax.fori_loop(0, plan.py // 2 // plan.unroll, body, 0)
 
     for number, segment in enumerate(plan.segments):
         back_x(number, segment)
@@ -375,135 +399,110 @@
     ]
 
 
-def side_of(plan):
-    return lax.rem(lax.axis_index("gy"), 2)
-
-
-def of_side(plan, stack):
-    return lax.dynamic_index_in_dim(jnp.asarray(stack), side_of(plan), 0, keepdims=False)
-
-
-def of_place(plan, stack, name):
-    side, place = side_of(plan), 0
-    if plan.relay and name == "fx":
-        side, place = 4 * side, 2 * lax.axis_index("gx") + lax.axis_index("gz")
-    elif plan.relay:
-        side, place = 2 * side, jnp.minimum(lax.axis_index("gy") // 2, 1)
-    elif name == "fy":
-        side = 0
-    return lax.dynamic_index_in_dim(jnp.asarray(stack), side + place, 0, keepdims=False)
-
-
-def own_block(plan, table, axis, count, dim):
-    table = jnp.asarray(table)
-    place = lax.axis_index(axis)
-    if axis != "gy":
-        return lax.dynamic_slice_in_dim(table, place * count, count, dim)
-    partner = place + 1 - 2 * lax.rem(place, 2)
-    both = [lax.dynamic_slice_in_dim(table, p * count, count, dim) for p in (place, partner)]
-    return jnp.concatenate(both, axis=dim)
-
-
-def thrice_lanes(table):
-    high, low = two_parts(table)
-    return np.concatenate([high, high, low], axis=-1)
-
-
 def thrice_rows(table):
     high, low = two_parts(table)
     return np.concatenate([high, high, low], axis=-2)
 
 
+def blocks_of(table, count, dim):
+    return np.stack(np.split(table, table.shape[dim] // count, axis=dim))
+
+
+def pair_blocks(table, count, dim):
+    blocks = blocks_of(table, count, dim)
+    order = np.arange(len(blocks))
+    return np.concatenate([blocks, blocks[order + 1 - 2 * (order % 2)]], axis=dim + 1)
+
+
+def by_side_blocks(tables, count, dim):
+    return np.concatenate([blocks_of(table, count, dim) for table in tables])
+
+
+def parts_over(table):
+    return np.concatenate(two_parts(table), axis=-2)
+
+
+def parts_beside(table):
+    return np.concatenate(two_parts(table), axis=-1)
+
+
+def places_of(plan):
+    first, second, third = [lax.axis_index(a) for a in axes]
+    side = lax.rem(second, 2)
+    fx, fy = side, jnp.zeros_like(side)
+    if plan.relay:
+        fx = 4 * side + 2 * first + third
+        fy = 2 * side + jnp.minimum(second // 2, 1)
+    x_place = side * plan.gx + first
+    return jnp.stack([fx, fy, second, third, third, side * plan.gz + third, x_place, x_place, side])
+
+
 def field_tables(plan, t):
     xl, yl, zl = plan.xl, plan.yl, plan.zl
-
-    def y_cells(part):
-        return own_block(plan, part, "gy", yl, 0)
-
-    def z_cells(part):
-        return own_block(plan, part, "gz", zl, 1)
-
-    def x_table(name):
-        high, low = [
-            own_block(plan, of_side(plan, part.swapaxes(1, 2)), "gx", xl, 0) for part in two_parts(t[name])
-        ]
-        return pair_lanes(high, high, low)
-
-    b, bl = [y_cells(part) for part in two_parts(t["by"].T)]
-    d, dl = [y_cells(part) for part in two_parts(t["dy"].T)]
-    z1, z1l = [z_cells(part) for part in two_parts(t["z1"])]
-    z2, z2l = [z_cells(part) for part in two_parts(t["z2"])]
-    z3, z3l = [z_cells(part) for part in two_parts(t["z3"])]
-    z1n, z1nl = [z_cells(of_side(plan, part)) for part in two_parts(t["z1n"])]
-    z13, z13l = pair_lanes(z1, z3), pair_lanes(z1l, z3l)
+    z13 = np.concatenate([blocks_of(t[name], zl, 1) for name in ("z1", "z3")], axis=2)
+    g = np.concatenate([pair_blocks(t[name].T, yl, 0) for name in ("by", "dy")], axis=1)
     return [
-        of_side(plan, t["w1"]), of_place(plan, thrice_lanes(t["fx"]), "fx"), jnp.asarray(thrice_rows(t["ez"].T)),
-        of_place(plan, thrice_lanes(t["fy"]), "fy"), pair_rows(b, d, bl, dl), pair_rows(z13, z13, z13l), pair_lanes(z2, z2l),
-        pair_lanes(z1n, z1nl), x_table("xs"), x_table("xb"), jnp.asarray(t["base"]),
+        twice_rows(t["fx"]), thrice_rows(t["ez"].T), twice_rows(t["fy"]), parts_over(g), thrice_rows(z13),
+        parts_beside(blocks_of(t["z2"], zl, 1)), parts_beside(by_side_blocks(t["z1n"], zl, 1)),
+        twice_rows(by_side_blocks([m.T for m in t["xs"]], xl, 0)),
+        twice_rows(by_side_blocks([m.T for m in t["xb"]], xl, 0)), t["base"],
     ]
-
-
-def field_call(plan, tables, octant):
-    xl, yl, zl = plan.xl, plan.yl, plan.zl
-    group = 4
-    shape = jax.ShapeDtypeStruct((3 * yl * xl, zl), jnp.float32)
-    own, other = pl.pallas_call(
-        functools.partial(field_body, plan, group),
-        out_shape=[shape, shape],
-        in_specs=[smem] + [vmem] * (10 + plan.arrays),
-        out_specs=[vmem, vmem],
-        scratch_shapes=scratch_of(plan),
-        compiler_params=kernel_params,
-    )(*tables, *octant)
-    return own.reshape(3, yl, xl, zl), other.reshape(3, yl, xl, zl)
 
 
 def adjoint_tables(plan, t):
     xl, yl, zl = plan.xl, plan.yl, plan.zl
-
-    def y_cells(part):
-        return own_block(plan, part, "gy", yl, 1)
-
-    def z_cells(part):
-        return own_block(plan, part, "gz", zl, 0)
-
-    def x_table(name):
-        high, low = [
-            own_block(plan, of_side(plan, part), "gx", xl, 1) for part in two_parts(t[name])
-        ]
-        return pair_lanes(high, high, low)
-
-    b, bl = [y_cells(part) for part in two_parts(t["by"])]
-    d, dl = [y_cells(part) for part in two_parts(t["dy"])]
-    z1, z1l = [z_cells(part) for part in two_parts(t["z1"].T)]
-    z2, z2l = [z_cells(part) for part in two_parts(t["z2"].T)]
-    z3, z3l = [z_cells(part) for part in two_parts(t["z3"].T)]
-    z1n, z1nl = [
-        z_cells(of_side(plan, part)) for part in two_parts((t["z1n"] - t["z1"]).swapaxes(1, 2))
+    z13 = np.concatenate([blocks_of(t[name].T, zl, 0) for name in ("z1", "z3")], axis=1)
+    g = np.concatenate([pair_blocks(t[name], yl, 1) for name in ("by", "dy")], axis=2)
+    edge = [(table - t["z1"]).T for table in t["z1n"]]
+    return [
+        twice_rows(t["fx"].swapaxes(1, 2)), parts_beside(t["ez"]), parts_over(t["fy"].swapaxes(1, 2)), twice_rows(g),
+        thrice_rows(z13), thrice_rows(blocks_of(t["z2"].T, zl, 0)), thrice_rows(by_side_blocks(edge, zl, 0)),
+        twice_rows(by_side_blocks(t["xs"], xl, 1)), twice_rows(by_side_blocks(t["xb"], xl, 1)), t["base"],
     ]
-    fy, fyl = two_parts(t["fy"].swapaxes(1, 2))
-    ez, ezl = two_parts(t["ez"])
-    return [
-        of_side(plan, t["w1"]), x_table("xs"), x_table("xb"),
-        pair_rows(z1, z3, z1, z3, z1l, z3l), pair_rows(z2, z2, z2l), pair_rows(z1n, z1n, z1nl),
-        pair_lanes(b, d, b, d, bl, dl), of_place(plan, np.concatenate([fy, fyl], axis=1), "fy"), jnp.concatenate([ez, ezl], axis=1),
-        of_place(plan, thrice_lanes(t["fx"].swapaxes(1, 2)), "fx"), jnp.asarray(t["base"]),
-    ]
-
-
-def adjoint_call(plan, tables, own, other):
+
+
+table_places = (0, None, 1, 2, 3, 4, 5, 6, 7, None)
+
+
+def spectral_call(plan, body, places, w1, tables, arrays, out_shape):
+    def table_spec(table, place):
+        if place is None:
+            return vmem
+        return pl.BlockSpec((None, *table.shape[1:]), lambda i, places_ref: (places_ref[place], 0, 0))
+
+    return pl.pallas_call(
+        functools.partial(body, plan, min(8, plan.kh)),
+        out_shape=out_shape,
+        grid_spec=pltpu.PrefetchScalarGridSpec(
+            num_scalar_prefetch=1,
+            grid=(1,),
+            in_specs=[smem]
+            + [table_spec(table, place) for table, place in zip(tables, table_places)]
+            + [vmem] * len(arrays),
+            out_specs=[vmem] * len(out_shape),
+            scratch_shapes=scratch_of(plan),
+        ),
+        compiler_params=kernel_params,
+    )(places, jnp.asarray(w1.reshape(-1)), *[jnp.asarray(table) for table in tables], *arrays)
+
+
+def field_call(plan, tables, places, octant):
+    xl, yl, zl = plan.xl, plan.yl, plan.zl
+    shape = jax.ShapeDtypeStruct((3 * yl * xl, zl), jnp.float32)
+    own, other = spectral_call(
+        plan, field_body, places, tables["w1"], field_tables(plan, tables), octant, [shape, shape]
+    )
+    return own.reshape(3, yl, xl, zl), other.reshape(3, yl, xl, zl)
+
+
+def adjoint_call(plan, tables, places, own, other):
     zl = plan.zl
-    group = 4
-    return pl.pallas_call(
-        functools.partial(adjoint_body, plan, group),
-        out_shape=[
-            jax.ShapeDtypeStruct((plan.x2 * plan.y2 * plan.z2 // zl // plan.arrays, zl), jnp.float32)
-        ] * plan.arrays,
-        in_specs=[smem] + [vmem] * 12,
-        out_specs=[vmem] * plan.arrays,
-        scratch_shapes=scratch_of(plan),
-        compiler_params=kernel_params,
-    )(tables[0], own.reshape(-1, zl), other.reshape(-1, zl), *tables[1:])
+    rows = plan.x2 * plan.y2 * plan.z2 // zl // plan.arrays
+    fields = [own.reshape(-1, zl), other.reshape(-1, zl)]
+    shape = jax.ShapeDtypeStruct((rows, zl), jnp.float32)
+    return spectral_call(
+        plan, adjoint_body, places, tables["w1"], adjoint_tables(plan, tables), fields, [shape] * plan.arrays
+    )
 
 
 def swapped(array):
@@ -529,13 +528,13 @@
     return jnp.concatenate(moved, axis=dim)
 
 
-def gather_octant(plan, block, work):
+def gather_octant(plan, quarters, work):
     if plan.relay:
-        return relay_octant(plan, block, work)
+        return relay_octant(plan, quarters, work)
     done = []
     for step in work:
         done.append(step(done))
-    piece = block
+    piece = jnp.concatenate([q.reshape(plan.yl, plan.px, plan.zl) for q in quarters], axis=1)
     for axis, dim in (("gx", 1), ("gz", 1), ("gy", 0)):
         piece = spread(piece, axis, dim)
     return [lax.all_gather(piece.reshape(plan.py * plan.px, plan.zl), axes, tiled=True)], done
@@ -544,7 +543,9 @@
 def owners_sum(plan, sums, work):
     if plan.relay:
         return relay_sums(plan, sums, work)
-    done = [step() for step in work]
+    done = []
+    for step in work:
+        done.append(step(done))
     piece = lax.psum_scatter(sums[0], axes, scatter_dimension=0, tiled=True)
     piece = piece.reshape(plan.py, plan.px, plan.zl)
     return unspread(unspread(unspread(piece, "gy", 0), "gz", 1), "gx", 1), done
@@ -561,43 +562,48 @@
     return lax.optimization_barrier(values)
 
 
-def relay_octant(plan, block, work):
+def relay_octant(plan, quarters, work):
     z = lax.axis_index("gy") // 2
     done = []
-    quarters = [block[:, r * plan.px : (r + 1) * plan.px].reshape(-1, plan.zl) for r in range(4)]
     moved = [lax.ppermute(quarters[r], ("gx", "gz"), [(0, r)]) for r in range(1, 4)]
     moved, result = together(moved, work[0](done))
     done.append(result)
     piece = quarters[0] + moved[0] + moved[1] + moved[2]
     up = along(piece, [(0, 1), (1, 2)])
     down = along(piece, [(1, 0)])
-    up, result = together(up, work[1](done))
+    up2 = along(up, [(1, 2), (2, 3)])
+    up2, result = together(up2, work[1](done))
+    up3 = along(up2, [(2, 3)])
+    first = across_once(plan, jnp.where(z < 2, piece, jnp.where(z == 2, up, up2)))
+    first, result = together(first, result)
     done.append(result)
-    up2 = along(up, [(1, 2), (2, 3)])
-    up2, result = together(up2, work[2](done))
-    done.append(result)
-    up3 = along(up2, [(2, 3)])
-    first = across(plan, jnp.where(z < 2, piece, jnp.where(z == 2, up, up2)))
-    up3, result = together(up3, work[3](done))
-    done.append(result)
+    first = across_twice(first)
+    up3, result = together(up3, [step(done) for step in work[2:]])
+    done.extend(result)
     second = jnp.where(z == 0, down, jnp.where(z == 1, up, jnp.where(z == 2, up2, up3)))
-    own = first + across(plan, second)
+    own = first + across_twice(across_once(plan, second))
     return own + [swapped(array) for array in own], done
 
 
-def across(plan, piece):
+def across_once(plan, piece):
     half = plan.py * plan.px
     low, high = piece[:half], piece[half:]
-    a = pair_rows(low, lax.ppermute(low, "gz", flip))
-    b = pair_rows(high, lax.ppermute(high, "gx", flip))
+    return pair_rows(low, lax.ppermute(low, "gz", flip)), pair_rows(high, lax.ppermute(high, "gx", flip))
+
+
+def across_twice(pairs):
+    a, b = pairs
     return [a, lax.ppermute(a, "gx", flip), b, lax.ppermute(b, "gz", flip)]
 
 
-def across_sums(plan, arrays):
+def across_halves(arrays):
+    a, ay, b, bx = arrays
+    return lax.ppermute(ay, "gx", flip), lax.ppermute(bx, "gz", flip)
+
+
+def across_sums(plan, arrays, halves):
     half = plan.py * plan.px
-    a, ay, b, bx = arrays
-    a = a + lax.ppermute(ay, "gx", flip)
-    b = b + lax.ppermute(bx, "gz", flip)
+    a, b = arrays[0] + halves[0], arrays[2] + halves[1]
     low = a[:half] + lax.ppermute(a[half:], "gz", flip)
     high = b[:half] + lax.ppermute(b[half:], "gx", flip)
     return pair_rows(low, high)
@@ -605,20 +611,59 @@
 
 def relay_sums(plan, sums, work):
     z = lax.axis_index("gy") // 2
-    own = [sums[i] + swapped(sums[i + 8]) for i in range(8)]
-    second = across_sums(plan, own[4:])
-    moved = along(second, [(3, 2)])
-    moved, result0 = together(moved, work[0]())
-    first = across_sums(plan, own[:4])
-    second = second + moved
-    moved = along(jnp.where(z == 3, first, second), [(3, 2), (2, 1)])
-    moved, result1 = together(moved, work[1]())
-    first = first + jnp.where(z == 2, moved, 0.0)
-    second = second + jnp.where(z == 1, moved, 0.0)
-    first = first + along(second, [(0, 1)]) + along(jnp.where(z == 2, first, second), [(2, 1), (1, 0)])
+    own = [sums[i] + swapped(sums[i + 8]) for i in (4, 5, 6, 7, 0, 1, 2, 3)]
+    done = []
+    halves, result = together(across_halves(own[:4]), work[0](done))
+    done.append(result)
+    second, *own[4:] = together(across_sums(plan, own[:4], halves), *own[4:])
+    down = along(second, [(3, 2)])
+    up = along(second, [(0, 1)])
+    halves = across_halves(own[4:])
+    down, halves, result = together(down, halves, work[1](done))
+    done.append(result)
+    second = second + down
+    down = along(second, [(2, 1)])
+    first = across_sums(plan, own[4:], halves)
+    down, first, result = together(down, first, work[2](done))
+    done.append(result)
+    second = second + down
+    down = along(second, [(1, 0)])
+    down2 = along(first, [(3, 2)])
+    down, down2, result = together(down, down2, work[3](done))
+    done.append(result)
+    first = first + down2
+    first = first + up + down + along(first, [(2, 1)])
     quarters = [first] + [lax.ppermute(first, ("gx", "gz"), [(r, 0)]) for r in range(1, 4)]
     block = jnp.concatenate([q.reshape(plan.yl, plan.px, plan.zl) for q in quarters], axis=1)
-    return block, [result0, result1]
+    return block, done
+
+
+def magnet_body(plan, from_ref, to_ref, rem_ref, *out_refs):
+    yl, px, zl = plan.yl, plan.px, plan.zl
+    lane = lax.broadcasted_iota(jnp.int32, (px, zl), 1)
+    row = lax.broadcasted_iota(jnp.int32, (px, zl), 0)
+    in_z = (lane >= from_ref[2]) & (lane < to_ref[2])
+    for r, out_ref in enumerate(out_refs):
+        inside = in_z & (row + r * px >= from_ref[0]) & (row + r * px < to_ref[0])
+
+        def plane(y, carry, inside=inside, out_ref=out_ref, r=r):
+            here = inside & (y >= from_ref[1]) & (y < to_ref[1])
+            values = rem_ref[pl.ds(r * px * yl + y, px, stride=yl), :]
+            out_ref[pl.ds(y * px, px), :] = jnp.where(here, values, 0.0)
+            return carry
+
+        lax.fori_loop(0, yl, plane, 0)
+
+
+def magnet_call(plan, remanence, bounds):
+    shape = jax.ShapeDtypeStruct((plan.yl * plan.px, plan.zl), jnp.float32)
+    return pl.pallas_call(
+        functools.partial(magnet_body, plan),
+        out_shape=[shape] * 4,
+        in_specs=[smem, smem, vmem],
+        out_specs=[vmem] * 4,
+        compiler_params=kernel_params,
+    )(bounds[0], bounds[1], remanence.reshape(-1, plan.zl))
 
 
 def lanes_of(count):
@@ -668,6 +713,10 @@
 
 def to_neighbours(low_face, high_face, axis):
     count = lax.axis_size(axis)
+    if count == 2:
+        lower = lax.axis_index(axis) == 0
+        other = lax.ppermute(jnp.where(lower, high_face, low_face), axis, [(0, 1), (1, 0)])
+        return jnp.where(lower, 0.0, other), jnp.where(lower, other, 0.0)
     below = lax.ppermute(high_face, axis, [(i, i + 1) for i in range(count - 1)])
     above = lax.ppermute(low_face, axis, [(i + 1, i) for i in range(count - 1)])
     return below, above
@@ -704,7 +753,7 @@
 
 def combine_call(applied, own, arrived, source):
     _, yl, xl, zl = own.shape
-    chunk = 8
+    chunk = 16
     width = lanes_of(max(xl, zl))
     three = pl.BlockSpec((3, yl, chunk, zl), lambda i: (0, 0, i, 0))
     y_spec = pl.BlockSpec((chunk, zl), lambda i: (i, 0))
@@ -751,8 +800,9 @@
         return beside + self.more[2] + self.less[2] - 6.0 * self.mid
 
 
-def fill_window(window, chunk, field, before, block, after, x_below, x_above):
-    step, last = pl.program_id(0), pl.num_programs(0) - 1
+def fill_window(window, chunk, field, before, block, after, x_below, x_above, step=None, last=None):
+    step = pl.program_id(0) if step is None else step
+    last = pl.num_programs(0) - 1 if last is None else last
     for k in range(chunk):
         window[field, k + 1] = block(k)
     window[field, 0] = jnp.where(step == 0, x_below, before)
@@ -785,13 +835,15 @@
 
 
 def adjoint_cells_body(
-    chunk, v_ref, vb_ref, va_ref, a_ref, ab_ref, aa_ref,
-    xlo_ref, xhi_ref, ylo_ref, yhi_ref, zlo_ref, zhi_ref, out_ref, window,
+    chunk, begin, last, v_ref, vb_ref, va_ref, a_ref, ab_ref, aa_ref,
+    xlo_ref, xhi_ref, ylo_ref, yhi_ref, zlo_ref, zhi_ref, *refs,
 ):
+    out_ref, window = refs[-2:]
+    step = pl.program_id(0) + begin
     for j in range(3):
-        fill_window(window, chunk, j, vb_ref[j, 0], lambda k: v_ref[j, k], va_ref[j, 0], xlo_ref[j], xhi_ref[j])
-        fill_window(window, chunk, 3 + j, ab_ref[j, 0], lambda k: a_ref[j, k], aa_ref[j, 0], xlo_ref[3 + j], xhi_ref[3 + j])
-    start = pl.program_id(0) * chunk
+        fill_window(window, chunk, j, vb_ref[j, 0], lambda k: v_ref[j, k], va_ref[j, 0], xlo_ref[j], xhi_ref[j], step, last)
+        fill_window(window, chunk, 3 + j, ab_ref[j, 0], lambda k: a_ref[j, k], aa_ref[j, 0], xlo_ref[3 + j], xhi_ref[3 + j], step, last)
+    start = step * chunk
 
     def plane(k, carry):
         at = [
@@ -814,14 +866,16 @@
 
 
 def next_cells_body(
-    chunk, v_ref, vb_ref, va_ref, e_ref, eb_ref, ea_ref, c_ref,
+    chunk, begin, last, v_ref, vb_ref, va_ref, e_ref, eb_ref, ea_ref, c_ref,
     xlo_ref, xhi_ref, ylo_ref, yhi_ref, zlo_ref, zhi_ref,
-    exlo_ref, exhi_ref, eylo_ref, eyhi_ref, ezlo_ref, ezhi_ref, out_ref, window,
+    exlo_ref, exhi_ref, eylo_ref, eyhi_ref, ezlo_ref, ezhi_ref, *refs,
 ):
+    out_ref, window = refs[-2:]
+    step = pl.program_id(0) + begin
     for j in range(3):
-        fill_window(window, chunk, j, vb_ref[j, 0], lambda k: v_ref[j, k], va_ref[j, 0], xlo_ref[j], xhi_ref[j])
-    fill_window(window, chunk, 3, eb_ref[0], lambda k: e_ref[k], ea_ref[0], exlo_ref[...], exhi_ref[...])
-    start = pl.program_id(0) * chunk
+        fill_window(window, chunk, j, vb_ref[j, 0], lambda k: v_ref[j, k], va_ref[j, 0], xlo_ref[j], xhi_ref[j], step, last)
+    fill_window(window, chunk, 3, eb_ref[0], lambda k: e_ref[k], ea_ref[0], exlo_ref[...], exhi_ref[...], step, last)
+    start = step * chunk
 
     def plane(k, carry):
         v = [
@@ -846,11 +900,11 @@
     lax.fori_loop(0, chunk, plane, 0)
 
 
-def cell_specs(chunk, xl, yl, zl, lead):
+def cell_specs(chunk, xl, yl, zl, lead, begin=0):
     def at(block, place):
         if lead:
-            return pl.BlockSpec((3, block, yl, zl), lambda i: (0, place(i), 0, 0))
-        return pl.BlockSpec((block, yl, zl), lambda i: (place(i), 0, 0))
+            return pl.BlockSpec((3, block, yl, zl), lambda i: (0, place(i + begin), 0, 0))
+        return pl.BlockSpec((block, yl, zl), lambda i: (place(i + begin), 0, 0))
 
     return [
         at(chunk, lambda i: i),
@@ -859,12 +913,12 @@
     ]
 
 
-def face_specs(chunk, yl, zl, width, fields):
+def face_specs(chunk, yl, zl, width, fields, begin=0):
     def spec(shape, index):
         return pl.BlockSpec((fields, *shape), lambda i: (0, *index(i)))
 
     x_spec = spec((yl, zl), lambda i: (0, 0))
-    y_spec = spec((chunk, zl), lambda i: (i, 0))
+    y_spec = spec((chunk, zl), lambda i: (i + begin, 0))
     z_spec = spec((yl, width), lambda i: (0, 0))
     return [x_spec, x_spec, y_spec, y_spec, z_spec, z_spec]
 
@@ -886,60 +940,69 @@
     )(a, a, a, c, c, c, *faces)
 
 
-def adjoint_cells_call(velocity, adjoint_seed, faces):
+def adjoint_cells_call(velocity, adjoint_seed, faces, part, earlier):
     _, xl, yl, zl = velocity.shape
     chunk = 8
-    three = cell_specs(chunk, xl, yl, zl, True)
+    steps = xl // chunk // 2
+    begin = part * steps
+    specs = cell_specs(chunk, xl, yl, zl, True, begin)
     v, a = velocity, adjoint_seed
     return pl.pallas_call(
-        functools.partial(adjoint_cells_body, chunk),
-        grid=(xl // chunk,),
-        in_specs=three + three + face_specs(chunk, yl, zl, lanes_of(max(xl, zl)), 6),
-        out_specs=three[0],
+        functools.partial(adjoint_cells_body, chunk, begin, xl // chunk - 1),
+        grid=(steps,),
+        in_specs=specs
+        + specs
+        + face_specs(chunk, yl, zl, lanes_of(max(xl, zl)), 6, begin)
+        + [pl.BlockSpec(memory_space=pl.ANY)] * part,
+        out_specs=specs[0],
         out_shape=jax.ShapeDtypeStruct(v.shape, jnp.float32),
         scratch_shapes=[pltpu.VMEM((6, chunk + 2, yl, zl), jnp.float32)],
+        input_output_aliases={12: 0} if part else {},
         compiler_params=kernel_params,
-    )(v, v, v, a, a, a, *faces)
-
-
-def next_cells_call(velocity, energy, susceptibility, faces, energy_faces):
+    )(v, v, v, a, a, a, *faces, *earlier)
+
+
+def next_cells_call(velocity, energy, susceptibility, faces, energy_faces, part, earlier):
     xl, yl, zl = susceptibility.shape
     chunk = 8
-    three = cell_specs(chunk, xl, yl, zl, True)
-    one = cell_specs(chunk, xl, yl, zl, False)
+    steps = xl // chunk // 2
+    begin = part * steps
+    three = cell_specs(chunk, xl, yl, zl, True, begin)
+    one = cell_specs(chunk, xl, yl, zl, False, begin)
     width = lanes_of(max(xl, zl))
     energy_specs = [
         pl.BlockSpec((yl, zl), lambda i: (0, 0)),
-        pl.BlockSpec((chunk, zl), lambda i: (i, 0)),
+        pl.BlockSpec((chunk, zl), lambda i: (i + begin, 0)),
         pl.BlockSpec((yl, width), lambda i: (0, 0)),
     ]
     energy_specs = [spec for spec in energy_specs for _ in range(2)]
     v, e, c = velocity, energy, susceptibility
     return pl.pallas_call(
-        functools.partial(next_cells_body, chunk),
-        grid=(xl // chunk,),
-        in_specs=three + one + one[:1] + face_specs(chunk, yl, zl, width, 3) + energy_specs,
+        functools.partial(next_cells_body, chunk, begin, xl // chunk - 1),
+        grid=(steps,),
+        in_specs=three
+        + one
+        + one[:1]
+        + face_specs(chunk, yl, zl, width, 3, begin)
+        + energy_specs
+        + [pl.BlockSpec(memory_space=pl.ANY)] * part,
         out_specs=three[0],
         out_shape=jax.ShapeDtypeStruct(v.shape, jnp.float32),
         scratch_shapes=[pltpu.VMEM((4, chunk + 2, yl, zl), jnp.float32)],
+        input_output_aliases={19: 0} if part else {},
         compiler_params=kernel_params,
-    )(v, v, v, e, e, e, c, *faces, *energy_faces)
+    )(v, v, v, e, e, e, c, *faces, *energy_faces, *earlier)
 
 
 def on_device(mesh, velocity, adjoint_seed, susceptibility, remanence, region_bounds, step_id):
     plan = Plan(mesh, susceptibility.shape)
     tables = make_tables(plan)
-    places = [
-        lax.axis_index(a) * n + jnp.arange(n, dtype=jnp.int32)
-        for a, n in zip(axes, susceptibility.shape)
-    ]
-    inside = [
-        (place >= region_bounds[0, d]) & (place < region_bounds[1, d])
-        for d, place in enumerate(places)
-    ]
-    region_mask = (
-        inside[0][:, None, None] & inside[1][None, :, None] & inside[2][None, None, :]
-    ).astype(jnp.float32)
+    corner = jnp.stack([lax.axis_index(a) * n for a, n in zip(axes, susceptibility.shape)])
+    bounds = region_bounds - corner[None, :]
+    place = [jnp.arange(n, dtype=jnp.int32) for n in susceptibility.shape]
+    inside = [(p >= bounds[0, d]) & (p < bounds[1, d]) for d, p in enumerate(place)]
+    region_mask = inside[0][:, None, None] & inside[1][None, :, None] & inside[2][None, None, :]
+
     def end_layers(done):
         ends = [
             jnp.concatenate([velocity[:, x], adjoint_seed[:, x], susceptibility[None, x]], axis=0)
@@ -952,39 +1015,45 @@
         faces = [
             *to_neighbours(*ends, "gx"), *to_neighbours(ylo, yhi, "gy"), *to_neighbours(zlo, zhi, "gz"),
         ]
-        return faces, field_tables(plan, tables)
+        return faces, places_of(plan)
 
     def source_of(done):
         return source_call(adjoint_seed, susceptibility, done[1][0])
 
-    def other_tables(done):
+    def applied_field(done):
         angle = full_turn * (step_id[0] % field_period).astype(jnp.float32) / field_period
         applied = jnp.stack([jnp.cos(angle), jnp.sin(angle), jnp.zeros((), jnp.float32)])
-        return applied, adjoint_tables(plan, tables)
+        return applied
 
     octant, done = gather_octant(
         plan,
-        (remanence * region_mask).transpose(1, 0, 2),
-        [end_layers, neighbours, source_of, other_tables],
+        magnet_call(plan, remanence, bounds),
+        [end_layers, neighbours, source_of, applied_field],
     )
-    _, (faces, there), source, (applied, back) = done
-    own, other = field_call(plan, there, octant)
+    _, (faces, places), source, applied = done
+    own, other = field_call(plan, tables, places, octant)
     field_adjoint, energy, ylo, yhi, zlo, zhi = combine_call(applied, own, swapped(other), source)
     energy_faces = [
         *to_neighbours(energy[0], energy[-1], "gx"), *to_neighbours(ylo, yhi, "gy"), *to_neighbours(zlo, zhi, "gz"),
     ]
     other, energy_faces = together(swapped(field_adjoint), energy_faces)
-    sums = adjoint_call(plan, back, field_adjoint, other)
+    sums = adjoint_call(plan, tables, places, field_adjoint, other)
     sums, energy, faces = together(sums, energy, faces)
 
-    def next_cells():
-        return next_cells_call(velocity, energy, susceptibility, faces, energy_faces)
-
-    def adjoint_cells():
-        return adjoint_cells_call(velocity, adjoint_seed, faces)
-
-    gradient, (next_velocity, velocity_adjoint) = owners_sum(plan, sums, [next_cells, adjoint_cells])
-    design_gradient = region_mask * gradient.transpose(1, 0, 2)
+    def next_cells(part):
+        return lambda done: next_cells_call(
+            velocity, energy, susceptibility, faces, energy_faces, part, done[:part]
+        )
+
+    def adjoint_cells(part):
+        return lambda done: adjoint_cells_call(
+            velocity, adjoint_seed, faces, part, done[2 : 2 + part]
+        )
+
+    gradient, (_, next_velocity, _, velocity_adjoint) = owners_sum(
+        plan, sums, [next_cells(0), next_cells(1), adjoint_cells(0), adjoint_cells(1)]
+    )
+    design_gradient = jnp.where(region_mask, gradient.transpose(1, 0, 2), 0.0)
     return (next_velocity, velocity_adjoint, design_gradient)
 
 

time: 516 us -> 417 us (0.81)
  Pallas kernels: 269 us -> 227 us
  local copies, waits for them, and re-layouts: 37.3 us -> 8.25 us
  waiting for transfers between devices: 101 us -> 82.6 us
  starting transfers between devices: 80.3 us -> 74 us
    pallas_call x4 -> x7, Pallas kernels: 219 us -> 179 us  [the longest x2 117 us: spectral_call(): pl.pallas_call(functools.partial(body, plan, min(8, plan.kh)), out_shape=...]
    ppermute x12 -> x16, waiting for transfers between devices: 50.3 us -> 25.1 us  [the longest x4 11.7 us: across_twice(): return [a, lax.ppermute(a, 'gx', flip), b, lax.ppermute(b, 'gz', flip)]]
    ppermute x12 -> x16, starting transfers between devices: 15.7 us -> 29.1 us  [the longest x4 14.2 us: to_neighbours(): lax.ppermute(jnp.where(lower, high_face, low_face), axis, [(0, 1), (1, 0)])]
    ppermute x8 -> x10, waiting for transfers between devices: 11.3 us -> 24 us  [along(): lax.ppermute(array, 'gy', [(2 * a + c, 2 * b + c) for a, b in pairs for c...]
    ppermute x6 -> x2, starting transfers between devices: 18.4 us -> 7.4 us  [to_neighbours(): above = lax.ppermute(low_face, axis, [(i + 1, i) for i in range(count - 1)])]
    dynamic_slice x12 -> x0, local copies, waits for them, and re-layouts: 9.41 us -> none  [the longest x10 7.52 us: own_block(): return lax.dynamic_slice_in_dim(table, place * count, count, dim)]
    squeeze x6 -> x1, local copies, waits for them, and re-layouts: 7.53 us -> 0.58 us  [magnet_call(): bounds[1]]
    ppermute x6 -> x2, starting transfers between devices: 10.6 us -> 3.88 us  [to_neighbours(): lax.ppermute(high_face, axis, [(i, i + 1) for i in range(count - 1)])]
  transfers between devices with their start and end apart: 60 -> 58, of which waited for: 19 -> 17; matrix products, arithmetic and copies ran while one was open for 8% -> 5% of each run, Pallas kernels for 17% -> 22%
where the time goes in v3:
time: 417 us; the launch traced here: 413 us
  Pallas kernels  227 us (54%)
  waiting for transfers between devices  82.6 us (20%)
  starting transfers between devices  74 us (18%)
  other arithmetic  18 us (4%)
  local copies, waits for them, and re-layouts  8.25 us (2%)
    pallas_call x2, Pallas kernels, spectral_call(): pl.pallas_call(functools.partial(body, plan, min(8, plan.kh)), out_shape=...  117 us
    pallas_call x2, Pallas kernels, adjoint_cells_call(): pl.pallas_call(functools.partial(adjoint_cells_body, chunk, begin, xl //...  30.3 us
    pallas_call x2, Pallas kernels, next_cells_call(): pl.pallas_call(functools.partial(next_cells_body, chunk, begin, xl // chu...  25.5 us
    ppermute x10, waiting for transfers between devices, along(): lax.ppermute(array, 'gy', [(2 * a + c, 2 * b + c) for a, b in pairs for c...  24 us
    pallas_call x1, Pallas kernels, source_call(): pl.pallas_call(functools.partial(source_body, chunk), grid=(xl // chunk,)...  19.3 us
    ppermute x10, starting transfers between devices, along(): lax.ppermute(array, 'gy', [(2 * a + c, 2 * b + c) for a, b in pairs for c...  17.5 us
    pallas_call x1, Pallas kernels, faces_call(): pl.pallas_call(functools.partial(faces_body, chunk), grid=(xl // chunk,),...  17 us
    ppermute x4, starting transfers between devices, to_neighbours(): lax.ppermute(jnp.where(lower, high_face, low_face), axis, [(0, 1), (1, 0)])  14.2 us
  transfers between devices with their start and end apart: 58, of which 17 were waited for; matrix products, arithmetic and copies ran while one was open for 5% of the time, Pallas kernels for 22%

profile of v3, /device:TPU:12, one launch (start us, length us, event | category | flops | bytes accessed | tf_op | source)
XLA Modules:
  0.0 412.7 jit_solution(5525037887340241456)
XLA Ops:
  2.0 6.0 %shard_map.274 = (f32[1024,128]{1,0:T(8,128)}, f32[1024,128]{1,0:T(8,128)}, f32[1024,128]{1,0:T(8,128)}, f32[1024,128]{1,0:T(8,128)}) custom-call(s32[3]{0:T(128)} %get-tuple-element.246.from_ref, s32[3]{0:T(128)} %get-tuple-element.245.to_ref, f32[4096,128]{1,0:T(8,128)} %bitcast.57), custom_call_target="tpu_custom_call" | custom-call | tf_op jit(solution)/shard_map/pallas_call | solution.py:660
  8.7 1.3 collective-permute-start.1
  10.7 0.8 slice_bitcast_fusion
  11.5 17.0 %shard_map.275 = (f32[7,128,128]{2,1,0:T(8,128)}, f32[7,128,128]{2,1,0:T(8,128)}, f32[7,32,128]{2,1,0:T(8,128)}, f32[7,32,128]{2,1,0:T(8,128)}) custom-call(f32[3,128,32,128]{3,2,1,0:T(8,128)} %va_ref.7, f32[3,128,32,128]{3,2,1,0:T(8,128)} %aa_ref.5, f32[128,32,128]{2,1,0:T(8,128)} %c_ref.7), custom_call_target="tpu_custom_call" | custom-call | tf_op jit(solution)/shard_map/pallas_call | solution.py:704
  29.3 0.8 slice_bitcast_fusion.1
  30.3 3.5 collective-permute-start.3
  34.5 3.2 collective-permute-start.14
  37.7 4.5 %collective-permute-start.5 = (f32[7,32,128]{2,1,0:T(8,128)S(1)}, f32[7,32,128]{2,1,0:T(8,128)S(1)}, u32[]{:S(2)}, u32[]{:S(2)}) collective-permute-start(f32[7,32,128]{2,1,0:T(8,128)S(1)} %broadcast_select_fusion.5), channel_id=1, source_target_pairs={{0,16},{16,0},{1,17},{17,1},{2,18},{18,2},{3,19},{19,3},{4,20},{20... | collective-permute-start | bytes 344072 | tf_op jit(solution)/shard_map/ppermute | solution.py:718
  42.2 1.9 collective-permute-start.6
  44.1 3.6 collective-permute-start.7
  47.7 2.8 collective-permute-start.4
  50.6 6.3 %collective-permute-start.8 = (f32[7,32,128]{2,1,0:T(8,128)S(1)}, f32[7,32,128]{2,1,0:T(8,128)S(1)}, u32[]{:S(2)}, u32[]{:S(2)}) collective-permute-start(f32[7,32,128]{2,1,0:T(8,128)S(1)} %broadcast_select_fusion.4), channel_id=1, source_target_pairs={{0,1},{1,0},{2,3},{3,2},{4,5},{5,4},{6,7},{7,6},{8,9},{9,8},{10,11... | collective-permute-start | bytes 344072 | tf_op jit(solution)/shard_map/ppermute | solution.py:718
  57.6 2.0 collective-permute-done.8
  61.1 1.5 collective-permute-start.11
  62.7 5.4 %collective-permute-start.9 = (f32[512,128]{1,0:T(8,128)S(1)}, f32[512,128]{1,0:T(8,128)S(1)}, u32[]{:S(2)}, u32[]{:S(2)}) collective-permute-start(f32[512,128]{1,0:T(8,128)S(1)} %get-tuple-element.230), channel_id=1, source_target_pairs={{0,1},{1,0},{2,3},{3,2},{4,5},{5,4},{6,7},{7,6},{8,9},{9,8},{10,11... | collective-permute-start | bytes 786440 | tf_op jit(solution)/shard_map/ppermute | solution.py:591
  69.5 3.0 collective-permute-done.9
  72.6 2.8 collective-permute-done.10
  75.6 19.3 %shard_map.276.source_ref = f32[32,128,128]{2,1,0:T(8,128)} custom-call(f32[3,128,32,128]{3,2,1,0:T(8,128)} %aa_ref.5, f32[3,128,32,128]{3,2,1,0:T(8,128)} %aa_ref.5, f32[3,128,32,128]{3,2,1,0:T(8,128)} %aa_ref.5, f32[128,32,128]{2,1,0:T(8,128)} %c_ref.7, f32[128,32,128]{2,1,0:T(8,128)} %c_ref.7, f32[128,32,128]{2,1,0:T(8,128)} %c_ref.7, ...), custom_call_target="tpu_custom_call" | custom-call | tf_op jit(solution)/shard_map/pallas_call | solution.py:930
  94.9 1.2 select_select_fusion
  96.1 2.0 collective-permute-start.15
  98.1 1.9 collective-permute-start.17
  100.1 2.5 collective-permute-done.15
  102.6 1.9 collective-permute-done.17
  104.5 1.9 collective-permute-start.16
  107.3 9.9 %collective-permute-done.16.refs_5_ = f32[1024,128]{1,0:T(8,128)S(1)} collective-permute-done((f32[1024,128]{1,0:T(8,128)S(1)}, f32[1024,128]{1,0:T(8,128)S(1)}, u32[]{:S(2)}, u32[]{:S(2)}) %collective-permute-start.16) | collective-permute-done | bytes 524320 | tf_op jit(solution)/shard_map/ppermute | solution.py:596
  117.2 1.8 collective-permute-done.18.refs_7_
  119.6 1.3 collective-permute-done.24.refs_13_
  121.0 0.8 copy-done.21
  121.9 61.6 %shard_map.277 = (f32[12288,128]{1,0:T(8,128)}, f32[12288,128]{1,0:T(8,128)}) custom-call(s32[9]{0:T(128)} %stack.58.places_ref, f32[256]{0:T(256)} %constant.97.clone.w1_ref, bf16[8,256,256]{2,1,0:T(8,128)(2,1)} %constant.98.clone.fx_ref, bf16[384,256]{1,0:T(8,128)(2,1)} %constant.99.clone.ez_ref, bf16[4,512,256]{2,1,0:T(8,128)(2,1)} %constant.100.clone.fy_ref, ...), custom_call_target="tpu_custom_call" | custom-call | tf_op jit(solution)/shard_map/pallas_call | solution.py:473
  183.6 10.4 %collective-permute-done.27.arrived_ref = f32[3,32,128,128]{3,2,1,0:T(8,128)} collective-permute-done((f32[3,32,128,128]{3,2,1,0:T(8,128)}, f32[3,32,128,128]{3,2,1,0:T(8,128)}, u32[]{:S(2)}, u32[]{:S(2)}) %collective-permute-start.27) | collective-permute-done | bytes 6291488 | tf_op jit(solution)/shard_map/ppermute | solution.py:510
  194.0 12.0 %shard_map.278 = (f32[3,32,128,128]{3,2,1,0:T(8,128)}, f32[128,32,128]{2,1,0:T(8,128)}, f32[128,128]{1,0:T(8,128)}, f32[128,128]{1,0:T(8,128)}, f32[32,128]{1,0:T(8,128)}, /*index=5*/f32[32,128]{1,0:T(8,128)}) custom-call(f32[3]{0:T(128)} %pad_maximum_fusion.8.app_ref, f32[3,32,128,128]{3,2,1,0:T(8,128)} %bitcast.54, ...), custom_call_target="tpu_custom_call" | custom-call | tf_op jit(solution)/shard_map/pallas_call | solution.py:762
  207.0 1.5 collective-permute-start.29
  208.5 2.0 collective-permute-start.30
  210.5 3.8 collective-permute-start.31
  215.0 1.9 collective-permute-start.32
  217.5 1.2 collective-permute-done.32
  219.3 55.8 %shard_map.279 = (f32[1024,128]{1,0:T(8,128)}, f32[1024,128]{1,0:T(8,128)}, f32[1024,128]{1,0:T(8,128)}, f32[1024,128]{1,0:T(8,128)}, f32[1024,128]{1,0:T(8,128)...) custom-call(s32[9]{0:T(128)} %stack.58.places_ref, ...), custom_call_target="tpu_custom_call" | custom-call | tf_op jit(solution)/shard_map/pallas_call | solution.py:473
  275.7 1.6 collective-permute-done.34
  277.3 1.1 add.105
  279.1 1.1 add.106
  280.2 1.8 collective-permute-start.37
  282.5 12.7 %shard_map.280.refs_0_ = f32[3,128,32,128]{3,2,1,0:T(8,128)} custom-call(f32[3,128,32,128]{3,2,1,0:T(8,128)} %va_ref.7, f32[3,128,32,128]{3,2,1,0:T(8,128)} %va_ref.7, f32[3,128,32,128]{3,2,1,0:T(8,128)} %va_ref.7, f32[128,32,128]{2,1,0:T(8,128)} %get-tuple-element.180.e_ref.eb_ref.ea_ref, f32[128,32,128]{2,1,0:T(8,128)} %get-tuple-element.180.e_ref.eb_ref.ea_ref, ...), custom_call_target="tpu_custom_call" | custom-call | tf_op jit(solution)/shard_map/pallas_call | solution.py:980
  296.4 1.3 add_add_fusion.1
  297.7 1.7 collective-permute-start.40
  300.8 5.3 %collective-permute-done.40 = f32[512,128]{1,0:T(8,128)S(1)} collective-permute-done((f32[512,128]{1,0:T(8,128)S(1)}, f32[512,128]{1,0:T(8,128)S(1)}, u32[]{:S(2)}, u32[]{:S(2)}) %collective-permute-start.40) | collective-permute-done | bytes 262176 | tf_op jit(solution)/shard_map/ppermute | solution.py:608
  306.1 1.5 collective-permute-done.38
  309.1 12.7 %shard_map.281 = f32[3,128,32,128]{3,2,1,0:T(8,128)} custom-call(f32[3,128,32,128]{3,2,1,0:T(8,128)} %va_ref.7, f32[3,128,32,128]{3,2,1,0:T(8,128)} %va_ref.7, f32[3,128,32,128]{3,2,1,0:T(8,128)} %va_ref.7, f32[128,32,128]{2,1,0:T(8,128)} %get-tuple-element.180.e_ref.eb_ref.ea_ref, ...), custom_call_target="tpu_custom_call", output_to_operand_aliasing={{}: (19, {})} | custom-call | tf_op jit(solution)/shard_map/pallas_call | solution.py:980
  322.7 1.2 add.119
  323.9 1.7 collective-permute-start.50
  325.7 1.8 collective-permute-start.49
  327.5 15.1 %shard_map.282.refs_0_ = f32[3,128,32,128]{3,2,1,0:T(8,128)} custom-call(f32[3,128,32,128]{3,2,1,0:T(8,128)} %va_ref.7, f32[3,128,32,128]{3,2,1,0:T(8,128)} %va_ref.7, f32[3,128,32,128]{3,2,1,0:T(8,128)} %va_ref.7, f32[3,128,32,128]{3,2,1,0:T(8,128)} %aa_ref.5, f32[3,128,32,128]{3,2,1,0:T(8,128)} %aa_ref.5, f32[3,128,32,128]{3,2,1,0:T(8,128)} %aa_ref.5, ...), custom_call_target="tpu_custom_call" | custom-call | tf_op jit(solution)/shard_map/pallas_call | solution.py:950
  342.7 1.3 collective-permute-start.48
  344.1 12.4 %collective-permute-done.48 = f32[1024,128]{1,0:T(8,128)S(1)} collective-permute-done((f32[1024,128]{1,0:T(8,128)S(1)}, f32[1024,128]{1,0:T(8,128)S(1)}, u32[]{:S(2)}, u32[]{:S(2)}) %collective-permute-start.48) | collective-permute-done | bytes 524320 | tf_op jit(solution)/shard_map/ppermute | solution.py:558
  356.6 1.3 collective-permute-start.51
  358.6 1.3 collective-permute-start.53
  359.9 15.2 %shard_map.283 = f32[3,128,32,128]{3,2,1,0:T(8,128)} custom-call(f32[3,128,32,128]{3,2,1,0:T(8,128)} %va_ref.7, f32[3,128,32,128]{3,2,1,0:T(8,128)} %va_ref.7, f32[3,128,32,128]{3,2,1,0:T(8,128)} %va_ref.7, f32[3,128,32,128]{3,2,1,0:T(8,128)} %aa_ref.5, f32[3,128,32,128]{3,2,1,0:T(8,128)} %aa_ref.5, ...), custom_call_target="tpu_custom_call", output_to_operand_aliasing={{}: (12, {})} | custom-call | tf_op jit(solution)/shard_map/pallas_call | solution.py:950
  375.2 1.3 collective-permute-start.54
  377.1 10.9 %collective-permute-done.54 = f32[1024,128]{1,0:T(8,128)S(1)} collective-permute-done((f32[1024,128]{1,0:T(8,128)S(1)}, f32[1024,128]{1,0:T(8,128)S(1)}, u32[]{:S(2)}, u32[]{:S(2)}) %collective-permute-start.54) | collective-permute-done | bytes 524320 | tf_op jit(solution)/shard_map/ppermute | solution.py:558
  388.9 3.0 collective-permute-start.56
  392.6 1.2 compare_and_fusion
  393.9 1.2 compare_and_fusion.1
  395.1 1.3 compare_and_fusion.2
  397.2 13.2 %collective-permute-done.56 = f32[1024,128]{1,0:T(8,128)S(1)} collective-permute-done((f32[1024,128]{1,0:T(8,128)S(1)}, f32[1024,128]{1,0:T(8,128)S(1)}, u32[]{:S(2)}, u32[]{:S(2)}) %collective-permute-start.56) | collective-permute-done | bytes 524320 | tf_op jit(solution)/shard_map/ppermute | solution.py:636
  411.0 1.7 fusion
  (184 shorter events, 23.0 us)
Async XLA Ops:
  8.0 22.2 %collective-permute-start = (f32[1024,128]{1,0:T(8,128)}, f32[1024,128]{1,0:T(8,128)S(1)}, u32[]{:S(2)}, u32[]{:S(2)}) collective-permute-start(f32[1024,128]{1,0:T(8,128)} %get-tuple-element.113), channel_id=1, source_target_pairs={{0,1},{2,3},{4,5},{6,7},{8,9},{10,11},{12,13},{14,15}} | collective-permute-start | bytes 1572872 | tf_op jit(solution)/shard_map/ppermute | solution.py:568
  8.7 21.5 %collective-permute-start.1 = (f32[1024,128]{1,0:T(8,128)}, f32[1024,128]{1,0:T(8,128)S(1)}, u32[]{:S(2)}, u32[]{:S(2)}) collective-permute-start(f32[1024,128]{1,0:T(8,128)} %get-tuple-element.114), channel_id=1, source_target_pairs={{0,16},{2,18},{4,20},{6,22},{8,24},{10,26},{12,28},{14,30}} | collective-permute-start | bytes 1572872 | tf_op jit(solution)/shard_map/ppermute | solution.py:568
  10.0 20.2 %collective-permute-start.2 = (f32[1024,128]{1,0:T(8,128)}, f32[1024,128]{1,0:T(8,128)S(1)}, u32[]{:S(2)}, u32[]{:S(2)}) collective-permute-start(f32[1024,128]{1,0:T(8,128)} %get-tuple-element.115), channel_id=1, source_target_pairs={{0,17},{2,19},{4,21},{6,23},{8,25},{10,27},{12,29},{14,31}} | collective-permute-start | bytes 1572872 | tf_op jit(solution)/shard_map/ppermute | solution.py:568
  28.5 22.0 %copy-start.28 = (f32[7,32,128]{2,1,0:T(8,128)S(1)}, f32[7,32,128]{2,1,0:T(8,128)}, u32[]{:S(2)}) copy-start(f32[7,32,128]{2,1,0:T(8,128)} %get-tuple-element.128) | copy-start | bytes 344068
  28.5 22.0 %copy-start.29 = (f32[7,32,128]{2,1,0:T(8,128)S(1)}, f32[7,32,128]{2,1,0:T(8,128)}, u32[]{:S(2)}) copy-start(f32[7,32,128]{2,1,0:T(8,128)} %get-tuple-element.127) | copy-start | bytes 344068
  30.3 17.4 %collective-permute-start.3 = (f32[1024,128]{1,0:T(8,128)S(1)}, f32[1024,128]{1,0:T(8,128)S(1)}, u32[]{:S(2)}, u32[]{:S(2)}) collective-permute-start(f32[1024,128]{1,0:T(8,128)S(1)} %add_add_fusion.3), channel_id=1, source_target_pairs={{0,4},{2,6},{4,8},{6,10},{1,5},{3,7},{5,9},{7,11},{16,20},{18,22},... | collective-permute-start | bytes 1572872 | tf_op jit(solution)/shard_map/ppermute | solution.py:558
  34.5 60.4 %collective-permute-start.14 = (f32[1024,128]{1,0:T(8,128)S(1)}, f32[1024,128]{1,0:T(8,128)}, u32[]{:S(2)}, u32[]{:S(2)}) collective-permute-start(f32[1024,128]{1,0:T(8,128)S(1)} %add_add_fusion.3), channel_id=1, source_target_pairs={{4,0},{6,2},{5,1},{7,3},{20,16},{22,18},{21,17},{23,19}} | collective-permute-start | bytes 1572872 | tf_op jit(solution)/shard_map/ppermute | solution.py:558
  37.7 12.9 %collective-permute-start.5 = (f32[7,32,128]{2,1,0:T(8,128)S(1)}, f32[7,32,128]{2,1,0:T(8,128)S(1)}, u32[]{:S(2)}, u32[]{:S(2)}) collective-permute-start(f32[7,32,128]{2,1,0:T(8,128)S(1)} %broadcast_select_fusion.5), channel_id=1, source_target_pairs={{0,16},{16,0},{1,17},{17,1},{2,18},{18,2},{3,19},{19,3},{4,20},{20... | collective-permute-start | bytes 344072 | tf_op jit(solution)/shard_map/ppermute | solution.py:718
  42.2 18.2 %collective-permute-start.6 = (f32[7,128,128]{2,1,0:T(8,128)}, f32[7,128,128]{2,1,0:T(8,128)S(1)}, u32[]{:S(2)}, u32[]{:S(2)}) collective-permute-start(f32[7,128,128]{2,1,0:T(8,128)} %get-tuple-element.125), channel_id=1, source_target_pairs={{0,2},{2,4},{4,6},{6,8},{8,10},{10,12},{12,14},{1,3},{3,5},{5,7},{... | collective-permute-start | bytes 1376264 | tf_op jit(solution)/shard_map/ppermute | solution.py:720
  44.1 16.3 %collective-permute-start.7 = (f32[7,128,128]{2,1,0:T(8,128)S(1)}, f32[7,128,128]{2,1,0:T(8,128)S(1)}, u32[]{:S(2)}, u32[]{:S(2)}) collective-permute-start(f32[7,128,128]{2,1,0:T(8,128)S(1)} %copy-done.30), channel_id=1, source_target_pairs={{2,0},{4,2},{6,4},{8,6},{10,8},{12,10},{14,12},{3,1},{5,3},{7,5},{... | collective-permute-start | bytes 1376264 | tf_op jit(solution)/shard_map/ppermute | solution.py:721
  47.7 13.4 %collective-permute-start.4 = (f32[1024,128]{1,0:T(8,128)S(1)}, f32[1024,128]{1,0:T(8,128)S(1)}, u32[]{:S(2)}, u32[]{:S(2)}) collective-permute-start(f32[1024,128]{1,0:T(8,128)S(1)} %collective-permute-done.3), channel_id=1, source_target_pairs={{4,8},{6,10},{8,12},{10,14},{5,9},{7,11},{9,13},{11,15},{20,24},{2... | collective-permute-start | bytes 1572872 | tf_op jit(solution)/shard_map/ppermute | solution.py:558
  50.6 9.1 %collective-permute-start.8 = (f32[7,32,128]{2,1,0:T(8,128)S(1)}, f32[7,32,128]{2,1,0:T(8,128)S(1)}, u32[]{:S(2)}, u32[]{:S(2)}) collective-permute-start(f32[7,32,128]{2,1,0:T(8,128)S(1)} %broadcast_select_fusion.4), channel_id=1, source_target_pairs={{0,1},{1,0},{2,3},{3,2},{4,5},{5,4},{6,7},{7,6},{8,9},{9,8},{10,11... | collective-permute-start | bytes 344072 | tf_op jit(solution)/shard_map/ppermute | solution.py:718
  61.1 33.8 %collective-permute-start.11 = (f32[1024,128]{1,0:T(8,128)S(1)}, f32[1024,128]{1,0:T(8,128)}, u32[]{:S(2)}, u32[]{:S(2)}) collective-permute-start(f32[1024,128]{1,0:T(8,128)S(1)} %collective-permute-done.4), channel_id=1, source_target_pairs={{8,12},{10,14},{9,13},{11,15},{24,28},{26,30},{25,29},{27,31}} | collective-permute-start | bytes 1572872 | tf_op jit(solution)/shard_map/ppermute | solution.py:558
  62.7 9.8 %collective-permute-start.9 = (f32[512,128]{1,0:T(8,128)S(1)}, f32[512,128]{1,0:T(8,128)S(1)}, u32[]{:S(2)}, u32[]{:S(2)}) collective-permute-start(f32[512,128]{1,0:T(8,128)S(1)} %get-tuple-element.230), channel_id=1, source_target_pairs={{0,1},{1,0},{2,3},{3,2},{4,5},{5,4},{6,7},{7,6},{8,9},{9,8},{10,11... | collective-permute-start | bytes 786440 | tf_op jit(solution)/shard_map/ppermute | solution.py:591
  68.1 7.3 %collective-permute-start.10 = (f32[512,128]{1,0:T(8,128)S(1)}, f32[512,128]{1,0:T(8,128)S(1)}, u32[]{:S(2)}, u32[]{:S(2)}) collective-permute-start(f32[512,128]{1,0:T(8,128)S(1)} %get-tuple-element.229), channel_id=1, source_target_pairs={{0,16},{16,0},{1,17},{17,1},{2,18},{18,2},{3,19},{19,3},{4,20},{20... | collective-permute-start | bytes 786440 | tf_op jit(solution)/shard_map/ppermute | solution.py:591
  72.6 27.5 %copy-start.2 = (f32[1024,128]{1,0:T(8,128)}, f32[1024,128]{1,0:T(8,128)S(1)}, u32[]{:S(2)}) copy-start(f32[1024,128]{1,0:T(8,128)S(1)} %pad_maximum_fusion.refs_0_) | copy-start | bytes 1572868
  75.4 27.2 %copy-start.3 = (f32[1024,128]{1,0:T(8,128)}, f32[1024,128]{1,0:T(8,128)S(1)}, u32[]{:S(2)}) copy-start(f32[1024,128]{1,0:T(8,128)S(1)} %pad_maximum_fusion.1.refs_2_) | copy-start | bytes 1572868
  75.4 31.1 %collective-permute-start.12 = (f32[1024,128]{1,0:T(8,128)S(1)}, f32[1024,128]{1,0:T(8,128)S(1)}, u32[]{:S(2)}, u32[]{:S(2)}) collective-permute-start(f32[1024,128]{1,0:T(8,128)S(1)} %pad_maximum_fusion.refs_0_), channel_id=1, source_target_pairs={{0,16},{16,0},{1,17},{17,1},{2,18},{18,2},{3,19},{19,3},{4,20},{20... | collective-permute-start | bytes 1572872 | tf_op jit(solution)/shard_map/ppermute | solution.py:596
  75.5 31.2 %collective-permute-start.13 = (f32[1024,128]{1,0:T(8,128)S(1)}, f32[1024,128]{1,0:T(8,128)S(1)}, u32[]{:S(2)}, u32[]{:S(2)}) collective-permute-start(f32[1024,128]{1,0:T(8,128)S(1)} %pad_maximum_fusion.1.refs_2_), channel_id=1, source_target_pairs={{0,1},{1,0},{2,3},{3,2},{4,5},{5,4},{6,7},{7,6},{8,9},{9,8},{10,11... | collective-permute-start | bytes 1572872 | tf_op jit(solution)/shard_map/ppermute | solution.py:596
  96.1 6.4 %collective-permute-start.15 = (f32[512,128]{1,0:T(8,128)S(1)}, f32[512,128]{1,0:T(8,128)S(1)}, u32[]{:S(2)}, u32[]{:S(2)}) collective-permute-start(f32[512,128]{1,0:T(8,128)S(1)} %get-tuple-element.228), channel_id=1, source_target_pairs={{0,1},{1,0},{2,3},{3,2},{4,5},{5,4},{6,7},{7,6},{8,9},{9,8},{10,11... | collective-permute-start | bytes 786440 | tf_op jit(solution)/shard_map/ppermute | solution.py:591
  98.1 6.4 %collective-permute-start.17 = (f32[512,128]{1,0:T(8,128)S(1)}, f32[512,128]{1,0:T(8,128)S(1)}, u32[]{:S(2)}, u32[]{:S(2)}) collective-permute-start(f32[512,128]{1,0:T(8,128)S(1)} %get-tuple-element.227), channel_id=1, source_target_pairs={{0,16},{16,0},{1,17},{17,1},{2,18},{18,2},{3,19},{19,3},{4,20},{20... | collective-permute-start | bytes 786440 | tf_op jit(solution)/shard_map/ppermute | solution.py:591
  100.1 6.6 %collective-permute-start.19 = (f32[1024,128]{1,0:T(8,128)S(1)}, f32[1024,128]{1,0:T(8,128)S(1)}, u32[]{:S(2)}, u32[]{:S(2)}) collective-permute-start(f32[1024,128]{1,0:T(8,128)S(1)} %pad_maximum_fusion.refs_0_), channel_id=1, source_target_pairs={{0,2},{2,0},{4,6},{6,4},{8,10},{10,8},{12,14},{14,12},{1,3},{3,1},... | collective-permute-start | bytes 1572872 | tf_op jit(solution)/shard_map/ppermute | solution.py:510
  102.6 4.7 %collective-permute-start.21 = (f32[1024,128]{1,0:T(8,128)S(1)}, f32[1024,128]{1,0:T(8,128)S(1)}, u32[]{:S(2)}, u32[]{:S(2)}) collective-permute-start(f32[1024,128]{1,0:T(8,128)S(1)} %pad_maximum_fusion.1.refs_2_), channel_id=1, source_target_pairs={{0,2},{2,0},{4,6},{6,4},{8,10},{10,8},{12,14},{14,12},{1,3},{3,1},... | collective-permute-start | bytes 1572872 | tf_op jit(solution)/shard_map/ppermute | solution.py:510
  104.5 12.7 %collective-permute-start.16 = (f32[1024,128]{1,0:T(8,128)S(1)}, f32[1024,128]{1,0:T(8,128)S(1)}, u32[]{:S(2)}, u32[]{:S(2)}) collective-permute-start(f32[1024,128]{1,0:T(8,128)S(1)} %pad_maximum_fusion.2.refs_4_), channel_id=1, source_target_pairs={{0,16},{16,0},{1,17},{17,1},{2,18},{18,2},{3,19},{19,3},{4,20},{20... | collective-permute-start | bytes 1572872 | tf_op jit(solution)/shard_map/ppermute | solution.py:596
  106.5 12.5 %collective-permute-start.18 = (f32[1024,128]{1,0:T(8,128)S(1)}, f32[1024,128]{1,0:T(8,128)S(1)}, u32[]{:S(2)}, u32[]{:S(2)}) collective-permute-start(f32[1024,128]{1,0:T(8,128)S(1)} %pad_maximum_fusion.3.refs_6_), channel_id=1, source_target_pairs={{0,1},{1,0},{2,3},{3,2},{4,5},{5,4},{6,7},{7,6},{8,9},{9,8},{10,11... | collective-permute-start | bytes 1572872 | tf_op jit(solution)/shard_map/ppermute | solution.py:596
  106.7 12.3 %collective-permute-start.20 = (f32[1024,128]{1,0:T(8,128)S(1)}, f32[1024,128]{1,0:T(8,128)S(1)}, u32[]{:S(2)}, u32[]{:S(2)}) collective-permute-start(f32[1024,128]{1,0:T(8,128)S(1)} %collective-permute-done.12.refs_1_), channel_id=1, source_target_pairs={{0,2},{2,0},{4,6},{6,4},{8,10},{10,8},{12,14},{14,12},{1,3},{3,1},... | collective-permute-start | bytes 1572872 | tf_op jit(solution)/shard_map/ppermute | solution.py:510
  106.7 12.8 %collective-permute-start.23 = (f32[1024,128]{1,0:T(8,128)S(1)}, f32[1024,128]{1,0:T(8,128)S(1)}, u32[]{:S(2)}, u32[]{:S(2)}) collective-permute-start(f32[1024,128]{1,0:T(8,128)S(1)} %pad_maximum_fusion.2.refs_4_), channel_id=1, source_target_pairs={{0,2},{2,0},{4,6},{6,4},{8,10},{10,8},{12,14},{14,12},{1,3},{3,1},... | collective-permute-start | bytes 1572872 | tf_op jit(solution)/shard_map/ppermute | solution.py:510
  107.2 12.3 %collective-permute-start.25 = (f32[1024,128]{1,0:T(8,128)S(1)}, f32[1024,128]{1,0:T(8,128)S(1)}, u32[]{:S(2)}, u32[]{:S(2)}) collective-permute-start(f32[1024,128]{1,0:T(8,128)S(1)} %pad_maximum_fusion.3.refs_6_), channel_id=1, source_target_pairs={{0,2},{2,0},{4,6},{6,4},{8,10},{10,8},{12,14},{14,12},{1,3},{3,1},... | collective-permute-start | bytes 1572872 | tf_op jit(solution)/shard_map/ppermute | solution.py:510
  117.2 2.3 collective-permute-start.22
  119.0 1.9 collective-permute-start.24
  119.1 2.8 collective-permute-start.26
  183.4 10.6 %collective-permute-start.27 = (f32[3,32,128,128]{3,2,1,0:T(8,128)}, f32[3,32,128,128]{3,2,1,0:T(8,128)}, u32[]{:S(2)}, u32[]{:S(2)}) collective-permute-start(f32[3,32,128,128]{3,2,1,0:T(8,128)} %bitcast.61), channel_id=1, source_target_pairs={{0,2},{2,0},{4,6},{6,4},{8,10},{10,8},{12,14},{14,12},{1,3},{3,1},... | collective-permute-start | bytes 18874376 | tf_op jit(solution)/shard_map/ppermute | solution.py:510
  206.0 13.3 %collective-permute-start.28 = (f32[3,32,128,128]{3,2,1,0:T(8,128)}, f32[3,32,128,128]{3,2,1,0:T(8,128)}, u32[]{:S(2)}, u32[]{:S(2)}) collective-permute-start(f32[3,32,128,128]{3,2,1,0:T(8,128)} %get-tuple-element.151), channel_id=1, source_target_pairs={{0,2},{2,0},{4,6},{6,4},{8,10},{10,8},{12,14},{14,12},{1,3},{3,1},... | collective-permute-start | bytes 18874376 | tf_op jit(solution)/shard_map/ppermute | solution.py:510
  207.0 9.9 %collective-permute-start.29 = (f32[32,128]{1,0:T(8,128)S(1)}, f32[32,128]{1,0:T(8,128)S(1)}, u32[]{:S(2)}, u32[]{:S(2)}) collective-permute-start(f32[32,128]{1,0:T(8,128)S(1)} %select_bitcast_fusion), channel_id=1, source_target_pairs={{0,16},{16,0},{1,17},{17,1},{2,18},{18,2},{3,19},{19,3},{4,20},{20... | collective-permute-start | bytes 49160 | tf_op jit(solution)/shard_map/ppermute | solution.py:718
  208.5 10.8 %collective-permute-start.30 = (f32[128,128]{1,0:T(8,128)}, f32[128,128]{1,0:T(8,128)S(1)}, u32[]{:S(2)}, u32[]{:S(2)}) collective-permute-start(f32[128,128]{1,0:T(8,128)} %get-tuple-element.153), channel_id=1, source_target_pairs={{0,2},{2,4},{4,6},{6,8},{8,10},{10,12},{12,14},{1,3},{3,5},{5,7},{... | collective-permute-start | bytes 196616 | tf_op jit(solution)/shard_map/ppermute | solution.py:720
  210.5 8.9 %collective-permute-start.31 = (f32[128,128]{1,0:T(8,128)}, f32[128,128]{1,0:T(8,128)S(1)}, u32[]{:S(2)}, u32[]{:S(2)}) collective-permute-start(f32[128,128]{1,0:T(8,128)} %get-tuple-element.154), channel_id=1, source_target_pairs={{2,0},{4,2},{6,4},{8,6},{10,8},{12,10},{14,12},{3,1},{5,3},{7,5},{... | collective-permute-start | bytes 196616 | tf_op jit(solution)/shard_map/ppermute | solution.py:721
  215.0 3.7 collective-permute-start.32
  219.3 55.8 %copy-start.26 = (f32[128,128]{1,0:T(8,128)}, f32[128,128]{1,0:T(8,128)S(1)}, u32[]{:S(2)}) copy-start(f32[128,128]{1,0:T(8,128)S(1)} %collective-permute-done.30.eylo_ref) | copy-start | bytes 196612
  219.3 55.8 %copy-start.27 = (f32[128,128]{1,0:T(8,128)}, f32[128,128]{1,0:T(8,128)S(1)}, u32[]{:S(2)}) copy-start(f32[128,128]{1,0:T(8,128)S(1)} %collective-permute-done.31.eyhi_ref) | copy-start | bytes 196612
  275.2 2.2 collective-permute-start.34
  275.2 3.8 collective-permute-start.36
  278.5 16.8 %collective-permute-start.35 = (f32[1024,128]{1,0:T(8,128)S(1)}, f32[1024,128]{1,0:T(8,128)S(1)}, u32[]{:S(2)}, u32[]{:S(2)}) collective-permute-start(f32[1024,128]{1,0:T(8,128)S(1)} %add.105), channel_id=1, source_target_pairs={{0,16},{16,0},{1,17},{17,1},{2,18},{18,2},{3,19},{19,3},{4,20},{20... | collective-permute-start | bytes 1572872 | tf_op jit(solution)/shard_map/ppermute | solution.py:601
  280.2 15.7 %collective-permute-start.37 = (f32[1024,128]{1,0:T(8,128)S(1)}, f32[1024,128]{1,0:T(8,128)}, u32[]{:S(2)}, u32[]{:S(2)}) collective-permute-start(f32[1024,128]{1,0:T(8,128)S(1)} %add.106), channel_id=1, source_target_pairs={{0,1},{1,0},{2,3},{3,2},{4,5},{5,4},{6,7},{7,6},{8,9},{9,8},{10,11... | collective-permute-start | bytes 1572872 | tf_op jit(solution)/shard_map/ppermute | solution.py:601
  282.0 13.9 %collective-permute-start.39 = (f32[1024,128]{1,0:T(8,128)}, f32[1024,128]{1,0:T(8,128)}, u32[]{:S(2)}, u32[]{:S(2)}) collective-permute-start(f32[1024,128]{1,0:T(8,128)} %get-tuple-element.195), channel_id=1, source_target_pairs={{0,2},{2,0},{4,6},{6,4},{8,10},{10,8},{12,14},{14,12},{1,3},{3,1},... | collective-permute-start | bytes 1572872 | tf_op jit(solution)/shard_map/ppermute | solution.py:510
  282.0 15.7 %collective-permute-start.33 = (f32[1024,128]{1,0:T(8,128)}, f32[1024,128]{1,0:T(8,128)S(1)}, u32[]{:S(2)}, u32[]{:S(2)}) collective-permute-start(f32[1024,128]{1,0:T(8,128)} %get-tuple-element.175), channel_id=1, source_target_pairs={{0,2},{2,0},{4,6},{6,4},{8,10},{10,8},{12,14},{14,12},{1,3},{3,1},... | collective-permute-start | bytes 1572872 | tf_op jit(solution)/shard_map/ppermute | solution.py:510
  282.5 17.0 %collective-permute-start.41 = (f32[1024,128]{1,0:T(8,128)}, f32[1024,128]{1,0:T(8,128)S(1)}, u32[]{:S(2)}, u32[]{:S(2)}) collective-permute-start(f32[1024,128]{1,0:T(8,128)} %get-tuple-element.198), channel_id=1, source_target_pairs={{0,2},{2,0},{4,6},{6,4},{8,10},{10,8},{12,14},{14,12},{1,3},{3,1},... | collective-permute-start | bytes 1572872 | tf_op jit(solution)/shard_map/ppermute | solution.py:510
  295.3 4.5 %collective-permute-start.42 = (f32[1024,128]{1,0:T(8,128)}, f32[1024,128]{1,0:T(8,128)S(1)}, u32[]{:S(2)}, u32[]{:S(2)}) collective-permute-start(f32[1024,128]{1,0:T(8,128)} %get-tuple-element.200), channel_id=1, source_target_pairs={{0,2},{2,0},{4,6},{6,4},{8,10},{10,8},{12,14},{14,12},{1,3},{3,1},... | collective-permute-start | bytes 1572872 | tf_op jit(solution)/shard_map/ppermute | solution.py:510
  295.8 4.0 collective-permute-start.43
  295.9 4.7 %collective-permute-start.44 = (f32[1024,128]{1,0:T(8,128)}, f32[1024,128]{1,0:T(8,128)S(1)}, u32[]{:S(2)}, u32[]{:S(2)}) collective-permute-start(f32[1024,128]{1,0:T(8,128)} %get-tuple-element.204), channel_id=1, source_target_pairs={{0,2},{2,0},{4,6},{6,4},{8,10},{10,8},{12,14},{14,12},{1,3},{3,1},... | collective-permute-start | bytes 1572872 | tf_op jit(solution)/shard_map/ppermute | solution.py:510
  297.7 8.4 %collective-permute-start.40 = (f32[512,128]{1,0:T(8,128)S(1)}, f32[512,128]{1,0:T(8,128)S(1)}, u32[]{:S(2)}, u32[]{:S(2)}) collective-permute-start(f32[512,128]{1,0:T(8,128)S(1)} %slice.119), channel_id=1, source_target_pairs={{0,16},{16,0},{1,17},{17,1},{2,18},{18,2},{3,19},{19,3},{4,20},{20... | collective-permute-start | bytes 786440 | tf_op jit(solution)/shard_map/ppermute | solution.py:608
  299.6 8.1 %collective-permute-start.38 = (f32[512,128]{1,0:T(8,128)S(1)}, f32[512,128]{1,0:T(8,128)S(1)}, u32[]{:S(2)}, u32[]{:S(2)}) collective-permute-start(f32[512,128]{1,0:T(8,128)S(1)} %slice.117), channel_id=1, source_target_pairs={{0,1},{1,0},{2,3},{3,2},{4,5},{5,4},{6,7},{7,6},{8,9},{9,8},{10,11... | collective-permute-start | bytes 786440 | tf_op jit(solution)/shard_map/ppermute | solution.py:607
  307.7 14.2 %collective-permute-start.45 = (f32[1024,128]{1,0:T(8,128)S(1)}, f32[1024,128]{1,0:T(8,128)S(1)}, u32[]{:S(2)}, u32[]{:S(2)}) collective-permute-start(f32[1024,128]{1,0:T(8,128)S(1)} %pad_maximum_fusion.4), channel_id=1, source_target_pairs={{12,8},{14,10},{13,9},{15,11},{28,24},{30,26},{29,25},{31,27}} | collective-permute-start | bytes 1572872 | tf_op jit(solution)/shard_map/ppermute | solution.py:558
  308.4 13.5 %collective-permute-start.46 = (f32[1024,128]{1,0:T(8,128)S(1)}, f32[1024,128]{1,0:T(8,128)S(1)}, u32[]{:S(2)}, u32[]{:S(2)}) collective-permute-start(f32[1024,128]{1,0:T(8,128)S(1)} %add.113), channel_id=1, source_target_pairs={{0,16},{16,0},{1,17},{17,1},{2,18},{18,2},{3,19},{19,3},{4,20},{20... | collective-permute-start | bytes 1572872 | tf_op jit(solution)/shard_map/ppermute | solution.py:601
  308.9 13.9 %collective-permute-start.47 = (f32[1024,128]{1,0:T(8,128)S(1)}, f32[1024,128]{1,0:T(8,128)}, u32[]{:S(2)}, u32[]{:S(2)}) collective-permute-start(f32[1024,128]{1,0:T(8,128)S(1)} %add.115), channel_id=1, source_target_pairs={{0,1},{1,0},{2,3},{3,2},{4,5},{5,4},{6,7},{7,6},{8,9},{9,8},{10,11... | collective-permute-start | bytes 1572872 | tf_op jit(solution)/shard_map/ppermute | solution.py:601
  323.9 20.1 %collective-permute-start.50 = (f32[512,128]{1,0:T(8,128)S(1)}, f32[512,128]{1,0:T(8,128)S(1)}, u32[]{:S(2)}, u32[]{:S(2)}) collective-permute-start(f32[512,128]{1,0:T(8,128)S(1)} %slice.123), channel_id=1, source_target_pairs={{0,16},{16,0},{1,17},{17,1},{2,18},{18,2},{3,19},{19,3},{4,20},{20... | collective-permute-start | bytes 786440 | tf_op jit(solution)/shard_map/ppermute | solution.py:608
  325.7 18.3 %collective-permute-start.49 = (f32[512,128]{1,0:T(8,128)S(1)}, f32[512,128]{1,0:T(8,128)S(1)}, u32[]{:S(2)}, u32[]{:S(2)}) collective-permute-start(f32[512,128]{1,0:T(8,128)S(1)} %slice.121), channel_id=1, source_target_pairs={{0,1},{1,0},{2,3},{3,2},{4,5},{5,4},{6,7},{7,6},{8,9},{9,8},{10,11... | collective-permute-start | bytes 786440 | tf_op jit(solution)/shard_map/ppermute | solution.py:607
  342.7 13.8 %collective-permute-start.48 = (f32[1024,128]{1,0:T(8,128)S(1)}, f32[1024,128]{1,0:T(8,128)S(1)}, u32[]{:S(2)}, u32[]{:S(2)}) collective-permute-start(f32[1024,128]{1,0:T(8,128)S(1)} %add.116), channel_id=1, source_target_pairs={{8,4},{10,6},{9,5},{11,7},{24,20},{26,22},{25,21},{27,23}} | collective-permute-start | bytes 1572872 | tf_op jit(solution)/shard_map/ppermute | solution.py:558
  356.6 18.5 %collective-permute-start.51 = (f32[1024,128]{1,0:T(8,128)S(1)}, f32[1024,128]{1,0:T(8,128)S(1)}, u32[]{:S(2)}, u32[]{:S(2)}) collective-permute-start(f32[1024,128]{1,0:T(8,128)S(1)} %add.121), channel_id=1, source_target_pairs={{4,0},{6,2},{5,1},{7,3},{20,16},{22,18},{21,17},{23,19}} | collective-permute-start | bytes 1572872 | tf_op jit(solution)/shard_map/ppermute | solution.py:558
  357.9 17.2 %collective-permute-start.52 = (f32[1024,128]{1,0:T(8,128)S(1)}, f32[1024,128]{1,0:T(8,128)S(1)}, u32[]{:S(2)}, u32[]{:S(2)}) collective-permute-start(f32[1024,128]{1,0:T(8,128)S(1)} %pad_maximum_fusion.5), channel_id=1, source_target_pairs={{12,8},{14,10},{13,9},{15,11},{28,24},{30,26},{29,25},{31,27}} | collective-permute-start | bytes 1572872 | tf_op jit(solution)/shard_map/ppermute | solution.py:558
  358.6 18.5 %collective-permute-start.53 = (f32[1024,128]{1,0:T(8,128)S(1)}, f32[1024,128]{1,0:T(8,128)S(1)}, u32[]{:S(2)}, u32[]{:S(2)}) collective-permute-start(f32[1024,128]{1,0:T(8,128)S(1)} %pad_maximum_fusion.4), channel_id=1, source_target_pairs={{0,4},{2,6},{1,5},{3,7},{16,20},{18,22},{17,21},{19,23}} | collective-permute-start | bytes 1572872 | tf_op jit(solution)/shard_map/ppermute | solution.py:558
  375.2 12.9 %collective-permute-start.54 = (f32[1024,128]{1,0:T(8,128)S(1)}, f32[1024,128]{1,0:T(8,128)S(1)}, u32[]{:S(2)}, u32[]{:S(2)}) collective-permute-start(f32[1024,128]{1,0:T(8,128)S(1)} %add.122), channel_id=1, source_target_pairs={{8,4},{10,6},{9,5},{11,7},{24,20},{26,22},{25,21},{27,23}} | collective-permute-start | bytes 1572872 | tf_op jit(solution)/shard_map/ppermute | solution.py:558
  388.2 8.7 %collective-permute-start.57 = (f32[1024,128]{1,0:T(8,128)S(1)}, f32[1024,128]{1,0:T(8,128)S(1)}, u32[]{:S(2)}, u32[]{:S(2)}) collective-permute-start(f32[1024,128]{1,0:T(8,128)S(1)} %add_add_fusion), channel_id=1, source_target_pairs={{17,0},{19,2},{21,4},{23,6},{25,8},{27,10},{29,12},{31,14}} | collective-permute-start | bytes 1572872 | tf_op jit(solution)/shard_map/ppermute | solution.py:636
  388.9 21.5 %collective-permute-start.56 = (f32[1024,128]{1,0:T(8,128)S(1)}, f32[1024,128]{1,0:T(8,128)S(1)}, u32[]{:S(2)}, u32[]{:S(2)}) collective-permute-start(f32[1024,128]{1,0:T(8,128)S(1)} %add_add_fusion), channel_id=1, source_target_pairs={{16,0},{18,2},{20,4},{22,6},{24,8},{26,10},{28,12},{30,14}} | collective-permute-start | bytes 1572872 | tf_op jit(solution)/shard_map/ppermute | solution.py:636
  391.9 18.8 %collective-permute-start.55 = (f32[1024,128]{1,0:T(8,128)S(1)}, f32[1024,128]{1,0:T(8,128)S(1)}, u32[]{:S(2)}, u32[]{:S(2)}) collective-permute-start(f32[1024,128]{1,0:T(8,128)S(1)} %add_add_fusion), channel_id=1, source_target_pairs={{1,0},{3,2},{5,4},{7,6},{9,8},{11,10},{13,12},{15,14}} | collective-permute-start | bytes 1572872 | tf_op jit(solution)/shard_map/ppermute | solution.py:636
  (25 other events, 195.9 us)

commit v4 on v3

--- a/solution.py
+++ b/solution.py
@@ -540,12 +540,11 @@
     return [lax.all_gather(piece.reshape(plan.py * plan.px, plan.zl), axes, tiled=True)], done
 
 
-def owners_sum(plan, sums, work):
+def owners_sum(plan, sums, work, late):
     if plan.relay:
-        return relay_sums(plan, sums, work)
-    done = []
-    for step in work:
-        done.append(step(done))
+        return relay_sums(plan, sums, work, late)
+    done = [work[0]([])]
+    done += [work[1](done), work[2](late)]
     piece = lax.psum_scatter(sums[0], axes, scatter_dimension=0, tiled=True)
     piece = piece.reshape(plan.py, plan.px, plan.zl)
     return unspread(unspread(unspread(piece, "gy", 0), "gz", 1), "gx", 1), done
@@ -562,26 +561,33 @@
     return lax.optimization_barrier(values)
 
 
+def to_column(array, start, end):
+    return lax.ppermute(array, ("gx", "gz"), [(start, end)])
+
+
 def relay_octant(plan, quarters, work):
     z = lax.axis_index("gy") // 2
     done = []
-    moved = [lax.ppermute(quarters[r], ("gx", "gz"), [(0, r)]) for r in range(1, 4)]
-    moved, result = together(moved, work[0](done))
-    done.append(result)
-    piece = quarters[0] + moved[0] + moved[1] + moved[2]
+    half = plan.py * plan.px
+    near = [to_column(quarters[r], 0, r) for r in (1, 2)]
+    via = [to_column(quarters[3][:half], 0, 1), to_column(quarters[3][half:], 0, 2)]
+    via = [to_column(via[0], 1, 3), to_column(via[1], 2, 3)]
+    piece = quarters[0] + near[0] + near[1] + pair_rows(*via)
     up = along(piece, [(0, 1), (1, 2)])
     down = along(piece, [(1, 0)])
+    up, result = together(up, work[0](done))
+    done.append(result)
     up2 = along(up, [(1, 2), (2, 3)])
-    up2, result = together(up2, work[1](done))
     up3 = along(up2, [(2, 3)])
     first = across_once(plan, jnp.where(z < 2, piece, jnp.where(z == 2, up, up2)))
-    first, result = together(first, result)
+    first, result = together(first, work[1](done))
     done.append(result)
     first = across_twice(first)
-    up3, result = together(up3, [step(done) for step in work[2:]])
+    second = jnp.where(z == 0, down, jnp.where(z == 1, up, jnp.where(z == 2, up2, up3)))
+    second, done[1] = together(across_once(plan, second), done[1])
+    second, result = together(across_twice(second), [step(done) for step in work[2:]])
     done.extend(result)
-    second = jnp.where(z == 0, down, jnp.where(z == 1, up, jnp.where(z == 2, up2, up3)))
-    own = first + across_twice(across_once(plan, second))
+    own = first + second
     return own + [swapped(array) for array in own], done
 
 
@@ -609,7 +615,7 @@
     return pair_rows(low, high)
 
 
-def relay_sums(plan, sums, work):
+def relay_sums(plan, sums, work, late):
     z = lax.axis_index("gy") // 2
     own = [sums[i] + swapped(sums[i + 8]) for i in (4, 5, 6, 7, 0, 1, 2, 3)]
     done = []
@@ -624,16 +630,19 @@
     second = second + down
     down = along(second, [(2, 1)])
     first = across_sums(plan, own[4:], halves)
-    down, first, result = together(down, first, work[2](done))
-    done.append(result)
+    down2 = along(first, [(3, 2)])
     second = second + down
     down = along(second, [(1, 0)])
-    down2 = along(first, [(3, 2)])
-    down, down2, result = together(down, down2, work[3](done))
-    done.append(result)
     first = first + down2
     first = first + up + down + along(first, [(2, 1)])
-    quarters = [first] + [lax.ppermute(first, ("gx", "gz"), [(r, 0)]) for r in range(1, 4)]
+    half = plan.py * plan.px
+    first, late = together(first, late)
+    near = [to_column(first, r, 0) for r in (1, 2)]
+    via = [to_column(first[:half], 3, 1), to_column(first[half:], 3, 2)]
+    via = [to_column(via[0], 1, 0), to_column(via[1], 2, 0)]
+    near, via, result = together(near, via, work[2](late))
+    done.append(result)
+    quarters = [first, *near, pair_rows(*via)]
     block = jnp.concatenate([q.reshape(plan.yl, plan.px, plan.zl) for q in quarters], axis=1)
     return block, done
 
@@ -652,7 +661,7 @@
             out_ref[pl.ds(y * px, px), :] = jnp.where(here, values, 0.0)
             return carry
 
-        lax.fori_loop(0, yl, plane, 0)
+        lax.fori_loop(0, yl, plane, 0, unroll=4)
 
 
 def magnet_call(plan, remanence, bounds):
@@ -695,7 +704,7 @@
 
 def faces_call(velocity, adjoint_seed, susceptibility):
     xl, yl, zl = susceptibility.shape
-    chunk = 8
+    chunk = 16
     three = pl.BlockSpec((3, chunk, yl, zl), lambda i: (0, i, 0, 0))
     y_spec = pl.BlockSpec((7, chunk, zl), lambda i: (0, i, 0))
     z_spec = pl.BlockSpec((7, yl, lanes_of(max(xl, zl))), lambda i: (0, 0, 0))
@@ -753,7 +762,7 @@
 
 def combine_call(applied, own, arrived, source):
     _, yl, xl, zl = own.shape
-    chunk = 16
+    chunk = 32
     width = lanes_of(max(xl, zl))
     three = pl.BlockSpec((3, yl, chunk, zl), lambda i: (0, 0, i, 0))
     y_spec = pl.BlockSpec((chunk, zl), lambda i: (i, 0))
@@ -831,7 +840,7 @@
         source_ref[:, k, :] = (-0.5 * time_step) * (flux[0] + flux[1] + flux[2])
         return carry
 
-    lax.fori_loop(0, chunk, plane, 0)
+    lax.fori_loop(0, chunk, plane, 0, unroll=4)
 
 
 def adjoint_cells_body(
@@ -862,7 +871,7 @@
             )
         return carry
 
-    lax.fori_loop(0, chunk, plane, 0)
+    lax.fori_loop(0, chunk, plane, 0, unroll=4)
 
 
 def next_cells_body(
@@ -897,7 +906,7 @@
             )
         return carry
 
-    lax.fori_loop(0, chunk, plane, 0)
+    lax.fori_loop(0, chunk, plane, 0, unroll=2)
 
 
 def cell_specs(chunk, xl, yl, zl, lead, begin=0):
@@ -925,7 +934,7 @@
 
 def source_call(adjoint_seed, susceptibility, faces):
     xl, yl, zl = susceptibility.shape
-    chunk = 8
+    chunk = 16
     a, c = adjoint_seed, susceptibility
     return pl.pallas_call(
         functools.partial(source_body, chunk),
@@ -1022,8 +1031,7 @@
 
     def applied_field(done):
         angle = full_turn * (step_id[0] % field_period).astype(jnp.float32) / field_period
-        applied = jnp.stack([jnp.cos(angle), jnp.sin(angle), jnp.zeros((), jnp.float32)])
-        return applied
+        return jnp.stack([jnp.cos(angle), jnp.sin(angle), jnp.zeros((), jnp.float32)])
 
     octant, done = gather_octant(
         plan,
@@ -1036,7 +1044,9 @@
     energy_faces = [
         *to_neighbours(energy[0], energy[-1], "gx"), *to_neighbours(ylo, yhi, "gy"), *to_neighbours(zlo, zhi, "gz"),
     ]
-    other, energy_faces = together(swapped(field_adjoint), energy_faces)
+    field_adjoint, faces = together(field_adjoint, faces)
+    half_adjoint = adjoint_cells_call(velocity, adjoint_seed, faces, 0, [])
+    other, energy_faces, half_adjoint = together(swapped(field_adjoint), energy_faces, half_adjoint)
     sums = adjoint_call(plan, tables, places, field_adjoint, other)
     sums, energy, faces = together(sums, energy, faces)
 
@@ -1045,13 +1055,11 @@
             velocity, energy, susceptibility, faces, energy_faces, part, done[:part]
         )
 
-    def adjoint_cells(part):
-        return lambda done: adjoint_cells_call(
-            velocity, adjoint_seed, faces, part, done[2 : 2 + part]
-        )
-
-    gradient, (_, next_velocity, _, velocity_adjoint) = owners_sum(
-        plan, sums, [next_cells(0), next_cells(1), adjoint_cells(0), adjoint_cells(1)]
+    def adjoint_rest(late):
+        return adjoint_cells_call(velocity, adjoint_seed, late[0], 1, late[1:])
+
+    gradient, (_, next_velocity, velocity_adjoint) = owners_sum(
+        plan, sums, [next_cells(0), next_cells(1), adjoint_rest], [faces, half_adjoint]
     )
     design_gradient = jnp.where(region_mask, gradient.transpose(1, 0, 2), 0.0)
     return (next_velocity, velocity_adjoint, design_gradient)

time: 417 us -> 389 us (0.933)
  Pallas kernels: 227 us -> 203 us
  starting transfers between devices: 74 us -> 64 us
  waiting for transfers between devices: 82.6 us -> 92.2 us
    ppermute x10, waiting for transfers between devices: 24 us -> 35.6 us  [along(): lax.ppermute(array, 'gy', [(2 * a + c, 2 * b + c) for a, b in pairs for c...]
    ppermute x4, starting transfers between devices: 14.2 us -> 2.75 us  [to_neighbours(): lax.ppermute(jnp.where(lower, high_face, low_face), axis, [(0, 1), (1, 0)])]
    pallas_call x1, Pallas kernels: 19.3 us -> 11.6 us  [source_call(): pl.pallas_call(functools.partial(source_body, chunk), grid=(xl // chunk,)...]
    ppermute x6 -> x12, starting transfers between devices: 7.1 us -> 14.5 us  [to_column(): return lax.ppermute(array, ('gx', 'gz'), [(start, end)])]
    ppermute x2, waiting for transfers between devices: 1.55 us -> 8.5 us  [across_sums(): low = a[:half] + lax.ppermute(a[half:], 'gz', flip)]
    pallas_call x2, Pallas kernels: 30.3 us -> 23.8 us  [adjoint_cells_call(): pl.pallas_call(functools.partial(adjoint_cells_body, chunk, begin, xl //...]
    ppermute x6 -> x12, waiting for transfers between devices: 13.2 us -> 7.96 us  [to_column(): return lax.ppermute(array, ('gx', 'gz'), [(start, end)])]
    ppermute x2, starting transfers between devices: 7.41 us -> 2.4 us  [across_once(): lax.ppermute(low, 'gz', flip)]
  transfers between devices with their start and end apart: 58 -> 64, of which waited for: 17 -> 27; matrix products, arithmetic and copies ran while one was open for 5% -> 4% of each run, Pallas kernels for 22% -> 18%
where the time goes in v4:
time: 389 us; the launch traced here: 387 us
  Pallas kernels  203 us (52%)
  waiting for transfers between devices  92.2 us (24%)
  starting transfers between devices  64 us (16%)
  other arithmetic  17.1 us (4%)
  local copies, waits for them, and re-layouts  8.22 us (2%)
    pallas_call x2, Pallas kernels, spectral_call(): pl.pallas_call(functools.partial(body, plan, min(8, plan.kh)), out_shape=...  117 us
    ppermute x10, waiting for transfers between devices, along(): lax.ppermute(array, 'gy', [(2 * a + c, 2 * b + c) for a, b in pairs for c...  35.6 us
    pallas_call x2, Pallas kernels, adjoint_cells_call(): pl.pallas_call(functools.partial(adjoint_cells_body, chunk, begin, xl //...  23.8 us
    pallas_call x2, Pallas kernels, next_cells_call(): pl.pallas_call(functools.partial(next_cells_body, chunk, begin, xl // chu...  21.6 us
    ppermute x18, waiting for transfers between devices, swapped(): lax.ppermute(array, 'gy', [(i, i + 1 - 2 * (i % 2)) for i in range(count)])  15.9 us
    ppermute x10, starting transfers between devices, along(): lax.ppermute(array, 'gy', [(2 * a + c, 2 * b + c) for a, b in pairs for c...  15.7 us
    ppermute x12, starting transfers between devices, to_column(): return lax.ppermute(array, ('gx', 'gz'), [(start, end)])  14.5 us
    pallas_call x1, Pallas kernels, faces_call(): pl.pallas_call(functools.partial(faces_body, chunk), grid=(xl // chunk,),...  13.6 us
  transfers between devices with their start and end apart: 64, of which 27 were waited for; matrix products, arithmetic and copies ran while one was open for 4% of the time, Pallas kernels for 18%

profile of v4, /device:TPU:12, one launch (start us, length us, event | category | flops | bytes accessed | tf_op | source)
XLA Modules:
  0.0 387.0 jit_solution(35537025576993878)
XLA Ops:
  1.9 4.8 %shard_map.274 = (f32[1024,128]{1,0:T(8,128)}, f32[1024,128]{1,0:T(8,128)}, f32[1024,128]{1,0:T(8,128)}, f32[1024,128]{1,0:T(8,128)}) custom-call(s32[3]{0:T(128)} %get-tuple-element.286.from_ref, s32[3]{0:T(128)} %get-tuple-element.285.to_ref, f32[4096,128]{1,0:T(8,128)} %bitcast.57), custom_call_target="tpu_custom_call" | custom-call | tf_op jit(solution)/shard_map/pallas_call | solution.py:669
  7.8 1.4 collective-permute-start.2
  9.1 1.3 collective-permute-start.4
  11.1 1.4 collective-permute-start.1
  13.3 7.7 %collective-permute-done.4 = f32[512,128]{1,0:T(8,128)} collective-permute-done((f32[512,128]{1,0:T(8,128)S(1)}, f32[512,128]{1,0:T(8,128)}, u32[]{:S(2)}, u32[]{:S(2)}) %collective-permute-start.4) | collective-permute-done | bytes 262176 | tf_op jit(solution)/shard_map/ppermute | solution.py:565
  20.9 1.3 collective-permute-start.5
  22.2 13.6 %shard_map.275 = (f32[7,128,128]{2,1,0:T(8,128)}, f32[7,128,128]{2,1,0:T(8,128)}, f32[7,32,128]{2,1,0:T(8,128)}, f32[7,32,128]{2,1,0:T(8,128)}) custom-call(f32[3,128,32,128]{3,2,1,0:T(8,128)} %va_ref.7, f32[3,128,32,128]{3,2,1,0:T(8,128)} %aa_ref.5, f32[128,32,128]{2,1,0:T(8,128)} %c_ref.7), custom_call_target="tpu_custom_call" | custom-call | tf_op jit(solution)/shard_map/pallas_call | solution.py:713
  36.9 3.6 collective-permute-start.7
  42.1 8.5 %collective-permute-done.7 = f32[1024,128]{1,0:T(8,128)S(1)} collective-permute-done((f32[1024,128]{1,0:T(8,128)S(1)}, f32[1024,128]{1,0:T(8,128)S(1)}, u32[]{:S(2)}, u32[]{:S(2)}) %collective-permute-start.7) | collective-permute-done | bytes 524320 | tf_op jit(solution)/shard_map/ppermute | solution.py:557
  50.5 3.5 collective-permute-start.8
  54.7 1.3 collective-permute-start.6
  56.0 6.2 %collective-permute-done.8 = f32[1024,128]{1,0:T(8,128)S(1)} collective-permute-done((f32[1024,128]{1,0:T(8,128)S(1)}, f32[1024,128]{1,0:T(8,128)S(1)}, u32[]{:S(2)}, u32[]{:S(2)}) %collective-permute-start.8) | collective-permute-done | bytes 524320 | tf_op jit(solution)/shard_map/ppermute | solution.py:557
  63.8 1.9 collective-permute-start.15
  65.8 2.1 collective-permute-done.17
  67.8 2.1 collective-permute-start.16
  71.9 2.0 collective-permute-start.12
  74.8 4.1 %collective-permute-done.13 = f32[512,128]{1,0:T(8,128)S(1)} collective-permute-done((f32[512,128]{1,0:T(8,128)S(1)}, f32[512,128]{1,0:T(8,128)S(1)}, u32[]{:S(2)}, u32[]{:S(2)}) %collective-permute-start.13) | collective-permute-done | bytes 262176 | tf_op jit(solution)/shard_map/ppermute | solution.py:597
  79.7 4.9 %collective-permute-done.11 = f32[512,128]{1,0:T(8,128)S(1)} collective-permute-done((f32[512,128]{1,0:T(8,128)S(1)}, f32[512,128]{1,0:T(8,128)S(1)}, u32[]{:S(2)}, u32[]{:S(2)}) %collective-permute-start.11) | collective-permute-done | bytes 262176 | tf_op jit(solution)/shard_map/ppermute | solution.py:597
  84.6 2.1 collective-permute-done.10
  86.8 1.9 collective-permute-start.19
  90.3 1.4 collective-permute-start.22
  92.8 11.6 %shard_map.276.source_ref = f32[32,128,128]{2,1,0:T(8,128)} custom-call(f32[3,128,32,128]{3,2,1,0:T(8,128)} %aa_ref.5, f32[3,128,32,128]{3,2,1,0:T(8,128)} %aa_ref.5, f32[3,128,32,128]{3,2,1,0:T(8,128)} %aa_ref.5, f32[128,32,128]{2,1,0:T(8,128)} %c_ref.7, f32[128,32,128]{2,1,0:T(8,128)} %c_ref.7, f32[128,32,128]{2,1,0:T(8,128)} %c_ref.7, ...), custom_call_target="tpu_custom_call" | custom-call | tf_op jit(solution)/shard_map/pallas_call | solution.py:939
  104.9 7.6 %collective-permute-done.20.refs_1_ = f32[1024,128]{1,0:T(8,128)S(1)} collective-permute-done((f32[1024,128]{1,0:T(8,128)S(1)}, f32[1024,128]{1,0:T(8,128)S(1)}, u32[]{:S(2)}, u32[]{:S(2)}) %collective-permute-start.20) | collective-permute-done | bytes 524320 | tf_op jit(solution)/shard_map/ppermute | solution.py:602
  114.4 1.5 collective-permute-done.28.refs_14_
  116.1 1.3 collective-permute-done.23.refs_9_
  119.0 61.5 %shard_map.277 = (f32[12288,128]{1,0:T(8,128)}, f32[12288,128]{1,0:T(8,128)}) custom-call(s32[9]{0:T(128)} %stack.58.places_ref, f32[256]{0:T(256)} %constant.97.clone.w1_ref, bf16[8,256,256]{2,1,0:T(8,128)(2,1)} %constant.98.clone.fx_ref, bf16[384,256]{1,0:T(8,128)(2,1)} %constant.99.clone.ez_ref, bf16[4,512,256]{2,1,0:T(8,128)(2,1)} %constant.100.clone.fy_ref, ...), custom_call_target="tpu_custom_call" | custom-call | tf_op jit(solution)/shard_map/pallas_call | solution.py:473
  180.8 10.4 %collective-permute-done.30.arrived_ref = f32[3,32,128,128]{3,2,1,0:T(8,128)} collective-permute-done((f32[3,32,128,128]{3,2,1,0:T(8,128)}, f32[3,32,128,128]{3,2,1,0:T(8,128)}, u32[]{:S(2)}, u32[]{:S(2)}) %collective-permute-start.30) | collective-permute-done | bytes 6291488 | tf_op jit(solution)/shard_map/ppermute | solution.py:510
  191.1 10.5 %shard_map.278 = (f32[3,32,128,128]{3,2,1,0:T(8,128)}, f32[128,32,128]{2,1,0:T(8,128)}, f32[128,128]{1,0:T(8,128)}, f32[128,128]{1,0:T(8,128)}, f32[32,128]{1,0:T(8,128)}, /*index=5*/f32[32,128]{1,0:T(8,128)}) custom-call(f32[3]{0:T(128)} %pad_maximum_fusion.9.app_ref, f32[3,32,128,128]{3,2,1,0:T(8,128)} %bitcast.54, ...), custom_call_target="tpu_custom_call" | custom-call | tf_op jit(solution)/shard_map/pallas_call | solution.py:771
  205.2 1.9 collective-permute-start.33
  207.1 3.9 collective-permute-start.34
  211.0 11.9 %shard_map.279.refs_0_ = f32[3,128,32,128]{3,2,1,0:T(8,128)} custom-call(f32[3,128,32,128]{3,2,1,0:T(8,128)} %va_ref.7, f32[3,128,32,128]{3,2,1,0:T(8,128)} %va_ref.7, f32[3,128,32,128]{3,2,1,0:T(8,128)} %va_ref.7, f32[3,128,32,128]{3,2,1,0:T(8,128)} %aa_ref.5, f32[3,128,32,128]{3,2,1,0:T(8,128)} %aa_ref.5, f32[3,128,32,128]{3,2,1,0:T(8,128)} %aa_ref.5, ...), custom_call_target="tpu_custom_call" | custom-call | tf_op jit(solution)/shard_map/pallas_call | solution.py:959
  224.2 55.8 %shard_map.280 = (f32[1024,128]{1,0:T(8,128)}, f32[1024,128]{1,0:T(8,128)}, f32[1024,128]{1,0:T(8,128)}, f32[1024,128]{1,0:T(8,128)}, f32[1024,128]{1,0:T(8,128)...) custom-call(s32[9]{0:T(128)} %stack.58.places_ref, ...), custom_call_target="tpu_custom_call" | custom-call | tf_op jit(solution)/shard_map/pallas_call | solution.py:473
  280.5 1.6 collective-permute-done.39
  282.1 1.1 add.106
  283.3 1.5 collective-permute-start.40
  284.8 1.1 add.105
  287.2 10.9 %shard_map.281.refs_0_ = f32[3,128,32,128]{3,2,1,0:T(8,128)} custom-call(f32[3,128,32,128]{3,2,1,0:T(8,128)} %va_ref.7, f32[3,128,32,128]{3,2,1,0:T(8,128)} %va_ref.7, f32[3,128,32,128]{3,2,1,0:T(8,128)} %va_ref.7, f32[128,32,128]{2,1,0:T(8,128)} %get-tuple-element.206.e_ref.eb_ref.ea_ref, f32[128,32,128]{2,1,0:T(8,128)} %get-tuple-element.206.e_ref.eb_ref.ea_ref, ...), custom_call_target="tpu_custom_call" | custom-call | tf_op jit(solution)/shard_map/pallas_call | solution.py:989
  300.2 1.2 add_add_fusion.2
  302.2 1.1 collective-permute-start.43
  303.6 6.0 %collective-permute-done.41 = f32[512,128]{1,0:T(8,128)S(1)} collective-permute-done((f32[512,128]{1,0:T(8,128)S(1)}, f32[512,128]{1,0:T(8,128)S(1)}, u32[]{:S(2)}, u32[]{:S(2)}) %collective-permute-start.41) | collective-permute-done | bytes 262176 | tf_op jit(solution)/shard_map/ppermute | solution.py:613
  311.0 1.1 collective-permute-start.49
  312.1 1.1 collective-permute-start.50
  313.2 10.7 %shard_map.282 = f32[3,128,32,128]{3,2,1,0:T(8,128)} custom-call(f32[3,128,32,128]{3,2,1,0:T(8,128)} %va_ref.7, f32[3,128,32,128]{3,2,1,0:T(8,128)} %va_ref.7, f32[3,128,32,128]{3,2,1,0:T(8,128)} %va_ref.7, f32[128,32,128]{2,1,0:T(8,128)} %get-tuple-element.206.e_ref.eb_ref.ea_ref, ...), custom_call_target="tpu_custom_call", output_to_operand_aliasing={{}: (19, {})} | custom-call | tf_op jit(solution)/shard_map/pallas_call | solution.py:989
  324.5 1.1 add.116
  325.6 1.2 collective-permute-start.51
  326.9 1.3 collective-permute-start.52
  328.3 1.3 collective-permute-start.55
  329.6 2.5 collective-permute-done.51
  332.1 1.2 collective-permute-done.52
  334.1 1.3 collective-permute-start.54
  335.4 7.0 %collective-permute-done.55 = f32[1024,128]{1,0:T(8,128)S(1)} collective-permute-done((f32[1024,128]{1,0:T(8,128)S(1)}, f32[1024,128]{1,0:T(8,128)S(1)}, u32[]{:S(2)}, u32[]{:S(2)}) %collective-permute-start.55) | collective-permute-done | bytes 524320 | tf_op jit(solution)/shard_map/ppermute | solution.py:557
  342.5 1.3 collective-permute-start.56
  343.9 1.3 collective-permute-start.57
  345.2 1.2 collective-permute-done.54
  346.5 5.5 %collective-permute-done.56 = f32[1024,128]{1,0:T(8,128)S(1)} collective-permute-done((f32[1024,128]{1,0:T(8,128)S(1)}, f32[1024,128]{1,0:T(8,128)S(1)}, u32[]{:S(2)}, u32[]{:S(2)}) %collective-permute-start.56) | collective-permute-done | bytes 524320 | tf_op jit(solution)/shard_map/ppermute | solution.py:557
  352.0 7.1 %collective-permute-done.57 = f32[1024,128]{1,0:T(8,128)S(1)} collective-permute-done((f32[1024,128]{1,0:T(8,128)S(1)}, f32[1024,128]{1,0:T(8,128)S(1)}, u32[]{:S(2)}, u32[]{:S(2)}) %collective-permute-start.57) | collective-permute-done | bytes 524320 | tf_op jit(solution)/shard_map/ppermute | solution.py:557
  359.9 1.3 collective-permute-start.62
  362.6 2.6 collective-permute-start.59
  365.2 1.3 compare_and_fusion.1
  366.5 1.3 compare_and_fusion.2
  368.8 1.9 collective-permute-start.63
  370.7 1.3 compare_and_fusion
  372.4 11.9 %shard_map.283 = f32[3,128,32,128]{3,2,1,0:T(8,128)} custom-call(f32[3,128,32,128]{3,2,1,0:T(8,128)} %va_ref.7, f32[3,128,32,128]{3,2,1,0:T(8,128)} %va_ref.7, f32[3,128,32,128]{3,2,1,0:T(8,128)} %va_ref.7, f32[3,128,32,128]{3,2,1,0:T(8,128)} %aa_ref.5, f32[3,128,32,128]{3,2,1,0:T(8,128)} %aa_ref.5, ...), custom_call_target="tpu_custom_call", output_to_operand_aliasing={{}: (12, {})} | custom-call | tf_op jit(solution)/shard_map/pallas_call | solution.py:959
  385.3 1.7 fusion
  (192 shorter events, 35.7 us)
Async XLA Ops:
  7.8 4.8 %collective-permute-start.2 = (f32[512,128]{1,0:T(8,128)S(1)}, f32[512,128]{1,0:T(8,128)}, u32[]{:S(2)}, u32[]{:S(2)}) collective-permute-start(f32[512,128]{1,0:T(8,128)S(1)} %get-tuple-element.269), channel_id=1, source_target_pairs={{0,1},{2,3},{4,5},{6,7},{8,9},{10,11},{12,13},{14,15}} | collective-permute-start | bytes 786440 | tf_op jit(solution)/shard_map/ppermute | solution.py:565
  9.1 11.8 %collective-permute-start.4 = (f32[512,128]{1,0:T(8,128)S(1)}, f32[512,128]{1,0:T(8,128)}, u32[]{:S(2)}, u32[]{:S(2)}) collective-permute-start(f32[512,128]{1,0:T(8,128)S(1)} %get-tuple-element.270), channel_id=1, source_target_pairs={{0,16},{2,18},{4,20},{6,22},{8,24},{10,26},{12,28},{14,30}} | collective-permute-start | bytes 786440 | tf_op jit(solution)/shard_map/ppermute | solution.py:565
  10.4 26.3 %collective-permute-start = (f32[1024,128]{1,0:T(8,128)}, f32[1024,128]{1,0:T(8,128)S(1)}, u32[]{:S(2)}, u32[]{:S(2)}) collective-permute-start(f32[1024,128]{1,0:T(8,128)} %get-tuple-element.130), channel_id=1, source_target_pairs={{0,1},{2,3},{4,5},{6,7},{8,9},{10,11},{12,13},{14,15}} | collective-permute-start | bytes 1572872 | tf_op jit(solution)/shard_map/ppermute | solution.py:565
  11.1 25.6 %collective-permute-start.1 = (f32[1024,128]{1,0:T(8,128)}, f32[1024,128]{1,0:T(8,128)S(1)}, u32[]{:S(2)}, u32[]{:S(2)}) collective-permute-start(f32[1024,128]{1,0:T(8,128)} %get-tuple-element.131), channel_id=1, source_target_pairs={{0,16},{2,18},{4,20},{6,22},{8,24},{10,26},{12,28},{14,30}} | collective-permute-start | bytes 1572872 | tf_op jit(solution)/shard_map/ppermute | solution.py:565
  12.6 24.1 %collective-permute-start.3 = (f32[512,128]{1,0:T(8,128)}, f32[512,128]{1,0:T(8,128)S(1)}, u32[]{:S(2)}, u32[]{:S(2)}) collective-permute-start(f32[512,128]{1,0:T(8,128)} %collective-permute-done.2), channel_id=1, source_target_pairs={{1,17},{3,19},{5,21},{7,23},{9,25},{11,27},{13,29},{15,31}} | collective-permute-start | bytes 786440 | tf_op jit(solution)/shard_map/ppermute | solution.py:565
  20.9 15.8 %collective-permute-start.5 = (f32[512,128]{1,0:T(8,128)}, f32[512,128]{1,0:T(8,128)S(1)}, u32[]{:S(2)}, u32[]{:S(2)}) collective-permute-start(f32[512,128]{1,0:T(8,128)} %collective-permute-done.4), channel_id=1, source_target_pairs={{16,17},{18,19},{20,21},{22,23},{24,25},{26,27},{28,29},{30,31}} | collective-permute-start | bytes 786440 | tf_op jit(solution)/shard_map/ppermute | solution.py:565
  36.9 13.7 %collective-permute-start.7 = (f32[1024,128]{1,0:T(8,128)S(1)}, f32[1024,128]{1,0:T(8,128)S(1)}, u32[]{:S(2)}, u32[]{:S(2)}) collective-permute-start(f32[1024,128]{1,0:T(8,128)S(1)} %maximum_add_fusion), channel_id=1, source_target_pairs={{0,4},{2,6},{4,8},{6,10},{1,5},{3,7},{5,9},{7,11},{16,20},{18,22},... | collective-permute-start | bytes 1572872 | tf_op jit(solution)/shard_map/ppermute | solution.py:557
  50.5 11.7 %collective-permute-start.8 = (f32[1024,128]{1,0:T(8,128)S(1)}, f32[1024,128]{1,0:T(8,128)S(1)}, u32[]{:S(2)}, u32[]{:S(2)}) collective-permute-start(f32[1024,128]{1,0:T(8,128)S(1)} %collective-permute-done.7), channel_id=1, source_target_pairs={{4,8},{6,10},{8,12},{10,14},{5,9},{7,11},{9,13},{11,15},{20,24},{2... | collective-permute-start | bytes 1572872 | tf_op jit(solution)/shard_map/ppermute | solution.py:557
  54.7 16.0 %collective-permute-start.6 = (f32[1024,128]{1,0:T(8,128)S(1)}, f32[1024,128]{1,0:T(8,128)S(1)}, u32[]{:S(2)}, u32[]{:S(2)}) collective-permute-start(f32[1024,128]{1,0:T(8,128)S(1)} %maximum_add_fusion), channel_id=1, source_target_pairs={{4,0},{6,2},{5,1},{7,3},{20,16},{22,18},{21,17},{23,19}} | collective-permute-start | bytes 1572872 | tf_op jit(solution)/shard_map/ppermute | solution.py:557
  62.2 8.4 %collective-permute-start.9 = (f32[1024,128]{1,0:T(8,128)S(1)}, f32[1024,128]{1,0:T(8,128)S(1)}, u32[]{:S(2)}, u32[]{:S(2)}) collective-permute-start(f32[1024,128]{1,0:T(8,128)S(1)} %collective-permute-done.8), channel_id=1, source_target_pairs={{8,12},{10,14},{9,13},{11,15},{24,28},{26,30},{25,29},{27,31}} | collective-permute-start | bytes 1572872 | tf_op jit(solution)/shard_map/ppermute | solution.py:557
  63.0 4.9 %collective-permute-start.17 = (f32[7,32,128]{2,1,0:T(8,128)S(1)}, f32[7,32,128]{2,1,0:T(8,128)S(1)}, u32[]{:S(2)}, u32[]{:S(2)}) collective-permute-start(f32[7,32,128]{2,1,0:T(8,128)S(1)} %broadcast_select_fusion.4), channel_id=1, source_target_pairs={{0,1},{1,0},{2,3},{3,2},{4,5},{5,4},{6,7},{7,6},{8,9},{9,8},{10,11... | collective-permute-start | bytes 344072 | tf_op jit(solution)/shard_map/ppermute | solution.py:727
  63.1 10.9 %collective-permute-start.14 = (f32[7,32,128]{2,1,0:T(8,128)S(1)}, f32[7,32,128]{2,1,0:T(8,128)S(1)}, u32[]{:S(2)}, u32[]{:S(2)}) collective-permute-start(f32[7,32,128]{2,1,0:T(8,128)S(1)} %broadcast_select_fusion.5), channel_id=1, source_target_pairs={{0,16},{16,0},{1,17},{17,1},{2,18},{18,2},{3,19},{19,3},{4,20},{20... | collective-permute-start | bytes 344072 | tf_op jit(solution)/shard_map/ppermute | solution.py:727
  63.8 15.8 %collective-permute-start.15 = (f32[7,128,128]{2,1,0:T(8,128)S(1)}, f32[7,128,128]{2,1,0:T(8,128)S(1)}, u32[]{:S(2)}, u32[]{:S(2)}) collective-permute-start(f32[7,128,128]{2,1,0:T(8,128)S(1)} %copy-done.27), channel_id=1, source_target_pairs={{0,2},{2,4},{4,6},{6,8},{8,10},{10,12},{12,14},{1,3},{3,5},{5,7},{... | collective-permute-start | bytes 1376264 | tf_op jit(solution)/shard_map/ppermute | solution.py:729
  67.8 11.8 %collective-permute-start.16 = (f32[7,128,128]{2,1,0:T(8,128)S(1)}, f32[7,128,128]{2,1,0:T(8,128)S(1)}, u32[]{:S(2)}, u32[]{:S(2)}) collective-permute-start(f32[7,128,128]{2,1,0:T(8,128)S(1)} %copy-done.26), channel_id=1, source_target_pairs={{2,0},{4,2},{6,4},{8,6},{10,8},{12,10},{14,12},{3,1},{5,3},{7,5},{... | collective-permute-start | bytes 1376264 | tf_op jit(solution)/shard_map/ppermute | solution.py:730
  70.8 8.1 %collective-permute-start.13 = (f32[512,128]{1,0:T(8,128)S(1)}, f32[512,128]{1,0:T(8,128)S(1)}, u32[]{:S(2)}, u32[]{:S(2)}) collective-permute-start(f32[512,128]{1,0:T(8,128)S(1)} %get-tuple-element.265), channel_id=1, source_target_pairs={{0,16},{16,0},{1,17},{17,1},{2,18},{18,2},{3,19},{19,3},{4,20},{20... | collective-permute-start | bytes 786440 | tf_op jit(solution)/shard_map/ppermute | solution.py:597
  71.9 7.7 %collective-permute-start.12 = (f32[512,128]{1,0:T(8,128)S(1)}, f32[512,128]{1,0:T(8,128)S(1)}, u32[]{:S(2)}, u32[]{:S(2)}) collective-permute-start(f32[512,128]{1,0:T(8,128)S(1)} %get-tuple-element.266), channel_id=1, source_target_pairs={{0,1},{1,0},{2,3},{3,2},{4,5},{5,4},{6,7},{7,6},{8,9},{9,8},{10,11... | collective-permute-start | bytes 786440 | tf_op jit(solution)/shard_map/ppermute | solution.py:597
  73.9 10.6 %collective-permute-start.11 = (f32[512,128]{1,0:T(8,128)S(1)}, f32[512,128]{1,0:T(8,128)S(1)}, u32[]{:S(2)}, u32[]{:S(2)}) collective-permute-start(f32[512,128]{1,0:T(8,128)S(1)} %get-tuple-element.267), channel_id=1, source_target_pairs={{0,16},{16,0},{1,17},{17,1},{2,18},{18,2},{3,19},{19,3},{4,20},{20... | collective-permute-start | bytes 786440 | tf_op jit(solution)/shard_map/ppermute | solution.py:597
  78.9 7.7 %collective-permute-start.10 = (f32[512,128]{1,0:T(8,128)S(1)}, f32[512,128]{1,0:T(8,128)S(1)}, u32[]{:S(2)}, u32[]{:S(2)}) collective-permute-start(f32[512,128]{1,0:T(8,128)S(1)} %get-tuple-element.268), channel_id=1, source_target_pairs={{0,1},{1,0},{2,3},{3,2},{4,5},{5,4},{6,7},{7,6},{8,9},{9,8},{10,11... | collective-permute-start | bytes 786440 | tf_op jit(solution)/shard_map/ppermute | solution.py:597
  86.7 17.6 %collective-permute-start.18 = (f32[1024,128]{1,0:T(8,128)S(1)}, f32[1024,128]{1,0:T(8,128)S(1)}, u32[]{:S(2)}, u32[]{:S(2)}) collective-permute-start(f32[1024,128]{1,0:T(8,128)S(1)} %pad_maximum_fusion.refs_4_), channel_id=1, source_target_pairs={{0,16},{16,0},{1,17},{17,1},{2,18},{18,2},{3,19},{19,3},{4,20},{20... | collective-permute-start | bytes 1572872 | tf_op jit(solution)/shard_map/ppermute | solution.py:602
  86.8 17.6 %collective-permute-start.19 = (f32[1024,128]{1,0:T(8,128)S(1)}, f32[1024,128]{1,0:T(8,128)}, u32[]{:S(2)}, u32[]{:S(2)}) collective-permute-start(f32[1024,128]{1,0:T(8,128)S(1)} %pad_maximum_fusion.1.refs_6_), channel_id=1, source_target_pairs={{0,1},{1,0},{2,3},{3,2},{4,5},{5,4},{6,7},{7,6},{8,9},{9,8},{10,11... | collective-permute-start | bytes 1572872 | tf_op jit(solution)/shard_map/ppermute | solution.py:602
  90.2 22.3 %collective-permute-start.20 = (f32[1024,128]{1,0:T(8,128)S(1)}, f32[1024,128]{1,0:T(8,128)S(1)}, u32[]{:S(2)}, u32[]{:S(2)}) collective-permute-start(f32[1024,128]{1,0:T(8,128)S(1)} %pad_maximum_fusion.2.refs_0_), channel_id=1, source_target_pairs={{0,16},{16,0},{1,17},{17,1},{2,18},{18,2},{3,19},{19,3},{4,20},{20... | collective-permute-start | bytes 1572872 | tf_op jit(solution)/shard_map/ppermute | solution.py:602
  90.3 22.7 %collective-permute-start.22 = (f32[1024,128]{1,0:T(8,128)S(1)}, f32[1024,128]{1,0:T(8,128)}, u32[]{:S(2)}, u32[]{:S(2)}) collective-permute-start(f32[1024,128]{1,0:T(8,128)S(1)} %pad_maximum_fusion.2.refs_0_), channel_id=1, source_target_pairs={{0,2},{2,0},{4,6},{6,4},{8,10},{10,8},{12,14},{14,12},{1,3},{3,1},... | collective-permute-start | bytes 1572872 | tf_op jit(solution)/shard_map/ppermute | solution.py:510
  91.7 20.9 %collective-permute-start.21 = (f32[1024,128]{1,0:T(8,128)S(1)}, f32[1024,128]{1,0:T(8,128)}, u32[]{:S(2)}, u32[]{:S(2)}) collective-permute-start(f32[1024,128]{1,0:T(8,128)S(1)} %pad_maximum_fusion.3.refs_2_), channel_id=1, source_target_pairs={{0,1},{1,0},{2,3},{3,2},{4,5},{5,4},{6,7},{7,6},{8,9},{9,8},{10,11... | collective-permute-start | bytes 1572872 | tf_op jit(solution)/shard_map/ppermute | solution.py:602
  104.3 8.8 %collective-permute-start.24 = (f32[1024,128]{1,0:T(8,128)S(1)}, f32[1024,128]{1,0:T(8,128)S(1)}, u32[]{:S(2)}, u32[]{:S(2)}) collective-permute-start(f32[1024,128]{1,0:T(8,128)S(1)} %pad_maximum_fusion.3.refs_2_), channel_id=1, source_target_pairs={{0,2},{2,0},{4,6},{6,4},{8,10},{10,8},{12,14},{14,12},{1,3},{3,1},... | collective-permute-start | bytes 1572872 | tf_op jit(solution)/shard_map/ppermute | solution.py:510
  104.4 9.1 %collective-permute-start.26 = (f32[1024,128]{1,0:T(8,128)S(1)}, f32[1024,128]{1,0:T(8,128)S(1)}, u32[]{:S(2)}, u32[]{:S(2)}) collective-permute-start(f32[1024,128]{1,0:T(8,128)S(1)} %pad_maximum_fusion.refs_4_), channel_id=1, source_target_pairs={{0,2},{2,0},{4,6},{6,4},{8,10},{10,8},{12,14},{14,12},{1,3},{3,1},... | collective-permute-start | bytes 1572872 | tf_op jit(solution)/shard_map/ppermute | solution.py:510
  112.5 1.9 collective-permute-start.27
  112.7 3.3 collective-permute-start.28
  113.0 3.1 collective-permute-start.29
  113.2 4.3 %collective-permute-start.23 = (f32[1024,128]{1,0:T(8,128)S(1)}, f32[1024,128]{1,0:T(8,128)S(1)}, u32[]{:S(2)}, u32[]{:S(2)}) collective-permute-start(f32[1024,128]{1,0:T(8,128)S(1)} %collective-permute-done.20.refs_1_), channel_id=1, source_target_pairs={{0,2},{2,0},{4,6},{6,4},{8,10},{10,8},{12,14},{14,12},{1,3},{3,1},... | collective-permute-start | bytes 1572872 | tf_op jit(solution)/shard_map/ppermute | solution.py:510
  113.6 4.1 %collective-permute-start.25 = (f32[1024,128]{1,0:T(8,128)}, f32[1024,128]{1,0:T(8,128)S(1)}, u32[]{:S(2)}, u32[]{:S(2)}) collective-permute-start(f32[1024,128]{1,0:T(8,128)} %collective-permute-done.21.refs_3_), channel_id=1, source_target_pairs={{0,2},{2,0},{4,6},{6,4},{8,10},{10,8},{12,14},{14,12},{1,3},{3,1},... | collective-permute-start | bytes 1572872 | tf_op jit(solution)/shard_map/ppermute | solution.py:510
  180.6 10.6 %collective-permute-start.30 = (f32[3,32,128,128]{3,2,1,0:T(8,128)}, f32[3,32,128,128]{3,2,1,0:T(8,128)}, u32[]{:S(2)}, u32[]{:S(2)}) collective-permute-start(f32[3,32,128,128]{3,2,1,0:T(8,128)} %bitcast.61), channel_id=1, source_target_pairs={{0,2},{2,0},{4,6},{6,4},{8,10},{10,8},{12,14},{14,12},{1,3},{3,1},... | collective-permute-start | bytes 18874376 | tf_op jit(solution)/shard_map/ppermute | solution.py:510
  201.6 22.5 %collective-permute-start.31 = (f32[3,32,128,128]{3,2,1,0:T(8,128)}, f32[3,32,128,128]{3,2,1,0:T(8,128)}, u32[]{:S(2)}, u32[]{:S(2)}) collective-permute-start(f32[3,32,128,128]{3,2,1,0:T(8,128)} %get-tuple-element.171), channel_id=1, source_target_pairs={{0,2},{2,0},{4,6},{6,4},{8,10},{10,8},{12,14},{14,12},{1,3},{3,1},... | collective-permute-start | bytes 18874376 | tf_op jit(solution)/shard_map/ppermute | solution.py:510
  202.6 20.3 %collective-permute-start.35 = (f32[32,128]{1,0:T(8,128)S(1)}, f32[32,128]{1,0:T(8,128)S(1)}, u32[]{:S(2)}, u32[]{:S(2)}) collective-permute-start(f32[32,128]{1,0:T(8,128)S(1)} %broadcast_select_fusion.10), channel_id=1, source_target_pairs={{0,1},{1,0},{2,3},{3,2},{4,5},{5,4},{6,7},{7,6},{8,9},{9,8},{10,11... | collective-permute-start | bytes 49160 | tf_op jit(solution)/shard_map/ppermute | solution.py:727
  204.2 19.3 %collective-permute-start.32 = (f32[32,128]{1,0:T(8,128)S(1)}, f32[32,128]{1,0:T(8,128)S(1)}, u32[]{:S(2)}, u32[]{:S(2)}) collective-permute-start(f32[32,128]{1,0:T(8,128)S(1)} %select_bitcast_fusion), channel_id=1, source_target_pairs={{0,16},{16,0},{1,17},{17,1},{2,18},{18,2},{3,19},{19,3},{4,20},{20... | collective-permute-start | bytes 49160 | tf_op jit(solution)/shard_map/ppermute | solution.py:727
  205.2 18.9 %collective-permute-start.33 = (f32[128,128]{1,0:T(8,128)}, f32[128,128]{1,0:T(8,128)S(1)}, u32[]{:S(2)}, u32[]{:S(2)}) collective-permute-start(f32[128,128]{1,0:T(8,128)} %get-tuple-element.173), channel_id=1, source_target_pairs={{0,2},{2,4},{4,6},{6,8},{8,10},{10,12},{12,14},{1,3},{3,5},{5,7},{... | collective-permute-start | bytes 196616 | tf_op jit(solution)/shard_map/ppermute | solution.py:729
  207.1 17.0 %collective-permute-start.34 = (f32[128,128]{1,0:T(8,128)}, f32[128,128]{1,0:T(8,128)S(1)}, u32[]{:S(2)}, u32[]{:S(2)}) collective-permute-start(f32[128,128]{1,0:T(8,128)} %get-tuple-element.174), channel_id=1, source_target_pairs={{2,0},{4,2},{6,4},{8,6},{10,8},{12,10},{14,12},{3,1},{5,3},{7,5},{... | collective-permute-start | bytes 196616 | tf_op jit(solution)/shard_map/ppermute | solution.py:730
  280.0 2.2 collective-permute-start.39
  280.0 4.7 %collective-permute-start.37 = (f32[1024,128]{1,0:T(8,128)}, f32[1024,128]{1,0:T(8,128)S(1)}, u32[]{:S(2)}, u32[]{:S(2)}) collective-permute-start(f32[1024,128]{1,0:T(8,128)} %get-tuple-element.203), channel_id=1, source_target_pairs={{0,2},{2,0},{4,6},{6,4},{8,10},{10,8},{12,14},{14,12},{1,3},{3,1},... | collective-permute-start | bytes 1572872 | tf_op jit(solution)/shard_map/ppermute | solution.py:510
  283.3 14.8 %collective-permute-start.40 = (f32[1024,128]{1,0:T(8,128)S(1)}, f32[1024,128]{1,0:T(8,128)S(1)}, u32[]{:S(2)}, u32[]{:S(2)}) collective-permute-start(f32[1024,128]{1,0:T(8,128)S(1)} %add.106), channel_id=1, source_target_pairs={{0,1},{1,0},{2,3},{3,2},{4,5},{5,4},{6,7},{7,6},{8,9},{9,8},{10,11... | collective-permute-start | bytes 1572872 | tf_op jit(solution)/shard_map/ppermute | solution.py:607
  285.9 13.8 %collective-permute-start.38 = (f32[1024,128]{1,0:T(8,128)S(1)}, f32[1024,128]{1,0:T(8,128)S(1)}, u32[]{:S(2)}, u32[]{:S(2)}) collective-permute-start(f32[1024,128]{1,0:T(8,128)S(1)} %add.105), channel_id=1, source_target_pairs={{0,16},{16,0},{1,17},{17,1},{2,18},{18,2},{3,19},{19,3},{4,20},{20... | collective-permute-start | bytes 1572872 | tf_op jit(solution)/shard_map/ppermute | solution.py:607
  286.7 12.9 %collective-permute-start.36 = (f32[1024,128]{1,0:T(8,128)}, f32[1024,128]{1,0:T(8,128)}, u32[]{:S(2)}, u32[]{:S(2)}) collective-permute-start(f32[1024,128]{1,0:T(8,128)} %get-tuple-element.201), channel_id=1, source_target_pairs={{0,2},{2,0},{4,6},{6,4},{8,10},{10,8},{12,14},{14,12},{1,3},{3,1},... | collective-permute-start | bytes 1572872 | tf_op jit(solution)/shard_map/ppermute | solution.py:510
  286.7 14.7 %collective-permute-start.42 = (f32[1024,128]{1,0:T(8,128)}, f32[1024,128]{1,0:T(8,128)S(1)}, u32[]{:S(2)}, u32[]{:S(2)}) collective-permute-start(f32[1024,128]{1,0:T(8,128)} %get-tuple-element.221), channel_id=1, source_target_pairs={{0,2},{2,0},{4,6},{6,4},{8,10},{10,8},{12,14},{14,12},{1,3},{3,1},... | collective-permute-start | bytes 1572872 | tf_op jit(solution)/shard_map/ppermute | solution.py:510
  287.2 15.0 %collective-permute-start.47 = (f32[1024,128]{1,0:T(8,128)}, f32[1024,128]{1,0:T(8,128)S(1)}, u32[]{:S(2)}, u32[]{:S(2)}) collective-permute-start(f32[1024,128]{1,0:T(8,128)} %get-tuple-element.230), channel_id=1, source_target_pairs={{0,2},{2,0},{4,6},{6,4},{8,10},{10,8},{12,14},{14,12},{1,3},{3,1},... | collective-permute-start | bytes 1572872 | tf_op jit(solution)/shard_map/ppermute | solution.py:510
  298.1 5.3 %collective-permute-start.46 = (f32[1024,128]{1,0:T(8,128)}, f32[1024,128]{1,0:T(8,128)S(1)}, u32[]{:S(2)}, u32[]{:S(2)}) collective-permute-start(f32[1024,128]{1,0:T(8,128)} %get-tuple-element.228), channel_id=1, source_target_pairs={{0,2},{2,0},{4,6},{6,4},{8,10},{10,8},{12,14},{14,12},{1,3},{3,1},... | collective-permute-start | bytes 1572872 | tf_op jit(solution)/shard_map/ppermute | solution.py:510
  299.7 3.8 collective-permute-start.45
  299.7 3.9 %collective-permute-start.44 = (f32[1024,128]{1,0:T(8,128)}, f32[1024,128]{1,0:T(8,128)S(1)}, u32[]{:S(2)}, u32[]{:S(2)}) collective-permute-start(f32[1024,128]{1,0:T(8,128)} %get-tuple-element.224), channel_id=1, source_target_pairs={{0,2},{2,0},{4,6},{6,4},{8,10},{10,8},{12,14},{14,12},{1,3},{3,1},... | collective-permute-start | bytes 1572872 | tf_op jit(solution)/shard_map/ppermute | solution.py:510
  301.4 8.3 %collective-permute-start.41 = (f32[512,128]{1,0:T(8,128)S(1)}, f32[512,128]{1,0:T(8,128)S(1)}, u32[]{:S(2)}, u32[]{:S(2)}) collective-permute-start(f32[512,128]{1,0:T(8,128)S(1)} %slice.133), channel_id=1, source_target_pairs={{0,1},{1,0},{2,3},{3,2},{4,5},{5,4},{6,7},{7,6},{8,9},{9,8},{10,11... | collective-permute-start | bytes 786440 | tf_op jit(solution)/shard_map/ppermute | solution.py:613
  302.2 8.0 %collective-permute-start.43 = (f32[512,128]{1,0:T(8,128)S(1)}, f32[512,128]{1,0:T(8,128)S(1)}, u32[]{:S(2)}, u32[]{:S(2)}) collective-permute-start(f32[512,128]{1,0:T(8,128)S(1)} %slice.135), channel_id=1, source_target_pairs={{0,16},{16,0},{1,17},{17,1},{2,18},{18,2},{3,19},{19,3},{4,20},{20... | collective-permute-start | bytes 786440 | tf_op jit(solution)/shard_map/ppermute | solution.py:614
  310.3 13.7 %collective-permute-start.48 = (f32[1024,128]{1,0:T(8,128)S(1)}, f32[1024,128]{1,0:T(8,128)S(1)}, u32[]{:S(2)}, u32[]{:S(2)}) collective-permute-start(f32[1024,128]{1,0:T(8,128)S(1)} %pad_maximum_fusion.4), channel_id=1, source_target_pairs={{12,8},{14,10},{13,9},{15,11},{28,24},{30,26},{29,25},{31,27}} | collective-permute-start | bytes 1572872 | tf_op jit(solution)/shard_map/ppermute | solution.py:557
  311.0 13.0 %collective-permute-start.49 = (f32[1024,128]{1,0:T(8,128)S(1)}, f32[1024,128]{1,0:T(8,128)}, u32[]{:S(2)}, u32[]{:S(2)}) collective-permute-start(f32[1024,128]{1,0:T(8,128)S(1)} %add.113), channel_id=1, source_target_pairs={{0,16},{16,0},{1,17},{17,1},{2,18},{18,2},{3,19},{19,3},{4,20},{20... | collective-permute-start | bytes 1572872 | tf_op jit(solution)/shard_map/ppermute | solution.py:607
  312.1 12.4 %collective-permute-start.50 = (f32[1024,128]{1,0:T(8,128)S(1)}, f32[1024,128]{1,0:T(8,128)S(1)}, u32[]{:S(2)}, u32[]{:S(2)}) collective-permute-start(f32[1024,128]{1,0:T(8,128)S(1)} %add.115), channel_id=1, source_target_pairs={{0,1},{1,0},{2,3},{3,2},{4,5},{5,4},{6,7},{7,6},{8,9},{9,8},{10,11... | collective-permute-start | bytes 1572872 | tf_op jit(solution)/shard_map/ppermute | solution.py:607
  325.6 6.4 %collective-permute-start.51 = (f32[512,128]{1,0:T(8,128)S(1)}, f32[512,128]{1,0:T(8,128)S(1)}, u32[]{:S(2)}, u32[]{:S(2)}) collective-permute-start(f32[512,128]{1,0:T(8,128)S(1)} %slice.137), channel_id=1, source_target_pairs={{0,1},{1,0},{2,3},{3,2},{4,5},{5,4},{6,7},{7,6},{8,9},{9,8},{10,11... | collective-permute-start | bytes 786440 | tf_op jit(solution)/shard_map/ppermute | solution.py:613
  326.9 6.4 %collective-permute-start.52 = (f32[512,128]{1,0:T(8,128)S(1)}, f32[512,128]{1,0:T(8,128)S(1)}, u32[]{:S(2)}, u32[]{:S(2)}) collective-permute-start(f32[512,128]{1,0:T(8,128)S(1)} %slice.139), channel_id=1, source_target_pairs={{0,16},{16,0},{1,17},{17,1},{2,18},{18,2},{3,19},{19,3},{4,20},{20... | collective-permute-start | bytes 786440 | tf_op jit(solution)/shard_map/ppermute | solution.py:614
  328.3 14.2 %collective-permute-start.55 = (f32[1024,128]{1,0:T(8,128)S(1)}, f32[1024,128]{1,0:T(8,128)S(1)}, u32[]{:S(2)}, u32[]{:S(2)}) collective-permute-start(f32[1024,128]{1,0:T(8,128)S(1)} %add.122), channel_id=1, source_target_pairs={{8,4},{10,6},{9,5},{11,7},{24,20},{26,22},{25,21},{27,23}} | collective-permute-start | bytes 1572872 | tf_op jit(solution)/shard_map/ppermute | solution.py:557
  333.4 10.4 %collective-permute-start.53 = (f32[1024,128]{1,0:T(8,128)S(1)}, f32[1024,128]{1,0:T(8,128)S(1)}, u32[]{:S(2)}, u32[]{:S(2)}) collective-permute-start(f32[1024,128]{1,0:T(8,128)S(1)} %pad_maximum_fusion.5), channel_id=1, source_target_pairs={{12,8},{14,10},{13,9},{15,11},{28,24},{30,26},{29,25},{31,27}} | collective-permute-start | bytes 1572872 | tf_op jit(solution)/shard_map/ppermute | solution.py:557
  334.1 12.3 %collective-permute-start.54 = (f32[1024,128]{1,0:T(8,128)S(1)}, f32[1024,128]{1,0:T(8,128)S(1)}, u32[]{:S(2)}, u32[]{:S(2)}) collective-permute-start(f32[1024,128]{1,0:T(8,128)S(1)} %pad_maximum_fusion.4), channel_id=1, source_target_pairs={{0,4},{2,6},{1,5},{3,7},{16,20},{18,22},{17,21},{19,23}} | collective-permute-start | bytes 1572872 | tf_op jit(solution)/shard_map/ppermute | solution.py:557
  342.5 9.4 %collective-permute-start.56 = (f32[1024,128]{1,0:T(8,128)S(1)}, f32[1024,128]{1,0:T(8,128)S(1)}, u32[]{:S(2)}, u32[]{:S(2)}) collective-permute-start(f32[1024,128]{1,0:T(8,128)S(1)} %add.123), channel_id=1, source_target_pairs={{4,0},{6,2},{5,1},{7,3},{20,16},{22,18},{21,17},{23,19}} | collective-permute-start | bytes 1572872 | tf_op jit(solution)/shard_map/ppermute | solution.py:557
  343.9 15.2 %collective-permute-start.57 = (f32[1024,128]{1,0:T(8,128)S(1)}, f32[1024,128]{1,0:T(8,128)S(1)}, u32[]{:S(2)}, u32[]{:S(2)}) collective-permute-start(f32[1024,128]{1,0:T(8,128)S(1)} %fusion.1), channel_id=1, source_target_pairs={{8,4},{10,6},{9,5},{11,7},{24,20},{26,22},{25,21},{27,23}} | collective-permute-start | bytes 1572872 | tf_op jit(solution)/shard_map/ppermute | solution.py:557
  359.3 8.6 %collective-permute-start.60 = (f32[512,128]{1,0:T(8,128)S(1)}, f32[512,128]{1,0:T(8,128)S(1)}, u32[]{:S(2)}, u32[]{:S(2)}) collective-permute-start(f32[512,128]{1,0:T(8,128)S(1)} %get-tuple-element.264), channel_id=1, source_target_pairs={{17,1},{19,3},{21,5},{23,7},{25,9},{27,11},{29,13},{31,15}} | collective-permute-start | bytes 786440 | tf_op jit(solution)/shard_map/ppermute | solution.py:565
  359.9 8.9 %collective-permute-start.62 = (f32[512,128]{1,0:T(8,128)S(1)}, f32[512,128]{1,0:T(8,128)S(1)}, u32[]{:S(2)}, u32[]{:S(2)}) collective-permute-start(f32[512,128]{1,0:T(8,128)S(1)} %get-tuple-element.263), channel_id=1, source_target_pairs={{17,16},{19,18},{21,20},{23,22},{25,24},{27,26},{29,28},{31,30}} | collective-permute-start | bytes 786440 | tf_op jit(solution)/shard_map/ppermute | solution.py:565
  361.9 22.4 %collective-permute-start.58 = (f32[1024,128]{1,0:T(8,128)S(1)}, f32[1024,128]{1,0:T(8,128)S(1)}, u32[]{:S(2)}, u32[]{:S(2)}) collective-permute-start(f32[1024,128]{1,0:T(8,128)S(1)} %add_add_fusion), channel_id=1, source_target_pairs={{1,0},{3,2},{5,4},{7,6},{9,8},{11,10},{13,12},{15,14}} | collective-permute-start | bytes 1572872 | tf_op jit(solution)/shard_map/ppermute | solution.py:565
  362.6 21.7 %collective-permute-start.59 = (f32[1024,128]{1,0:T(8,128)S(1)}, f32[1024,128]{1,0:T(8,128)S(1)}, u32[]{:S(2)}, u32[]{:S(2)}) collective-permute-start(f32[1024,128]{1,0:T(8,128)S(1)} %add_add_fusion), channel_id=1, source_target_pairs={{16,0},{18,2},{20,4},{22,6},{24,8},{26,10},{28,12},{30,14}} | collective-permute-start | bytes 1572872 | tf_op jit(solution)/shard_map/ppermute | solution.py:565
  367.9 16.5 %collective-permute-start.61 = (f32[512,128]{1,0:T(8,128)S(1)}, f32[512,128]{1,0:T(8,128)S(1)}, u32[]{:S(2)}, u32[]{:S(2)}) collective-permute-start(f32[512,128]{1,0:T(8,128)S(1)} %collective-permute-done.60), channel_id=1, source_target_pairs={{1,0},{3,2},{5,4},{7,6},{9,8},{11,10},{13,12},{15,14}} | collective-permute-start | bytes 786440 | tf_op jit(solution)/shard_map/ppermute | solution.py:565
  368.8 15.5 %collective-permute-start.63 = (f32[512,128]{1,0:T(8,128)S(1)}, f32[512,128]{1,0:T(8,128)S(1)}, u32[]{:S(2)}, u32[]{:S(2)}) collective-permute-start(f32[512,128]{1,0:T(8,128)S(1)} %collective-permute-done.62), channel_id=1, source_target_pairs={{16,0},{18,2},{20,4},{22,6},{24,8},{26,10},{28,12},{30,14}} | collective-permute-start | bytes 786440 | tf_op jit(solution)/shard_map/ppermute | solution.py:565
  (28 other events, 430.7 us)

commit v5 on v4

--- a/solution.py
+++ b/solution.py
@@ -194,7 +194,7 @@
     w1_at = places_ref[8] * kx
     y2, z2, xl, yl, yc, zl = plan.y2, plan.z2, plan.xl, plan.yl, plan.yc, plan.zl
     span = yc * pitch
-    m_refs, (own_ref, other_ref, s_ref, r_ref) = refs[: plan.arrays], refs[plan.arrays :]
+    m_refs, (own_out, other_out, s_ref, r_ref, own_ref, other_ref, sem) = refs[: plan.arrays], refs[plan.arrays :]
 
     def along_x(number, segment):
         def body(step, carry):
@@ -284,18 +284,29 @@
         lax.fori_loop(0, yl // 2, body, 0)
 
     cells(other_ref, yl)
+    away = pltpu.make_async_copy(other_ref, other_out, sem.at[0])
+    away.start()
     cells(own_ref, 0)
+    kept = pltpu.make_async_copy(own_ref, own_out, sem.at[1])
+    kept.start()
+    away.wait()
+    kept.wait()
 
 
 def adjoint_body(
     plan, group, places_ref, w1_ref,
-    fx_ref, ez_ref, fy_ref, g_ref, z13_ref, z2_ref, z1n_ref, xs_ref, xb_ref, base_ref, own_ref, other_ref, *refs,
+    fx_ref, ez_ref, fy_ref, g_ref, z13_ref, z2_ref, z1n_ref, xs_ref, xb_ref, base_ref, own_in, other_in, *refs,
 ):
     kx, kh, pitch = plan.kx, plan.kh, plan.pitch
     w1_at = places_ref[8] * kx
     y2, z2, xl, yl, yc, zl = plan.y2, plan.z2, plan.xl, plan.yl, plan.yc, plan.zl
     span = yc * pitch
-    m_refs, (s_ref, r_ref) = refs[: plan.arrays], refs[plan.arrays :]
+    m_outs, (s_ref, r_ref, own_ref, other_ref, sem) = refs[: plan.arrays], refs[plan.arrays : plan.arrays + 5]
+    m_refs, out_sem = refs[plan.arrays + 5 : -1], refs[-1]
+    here = pltpu.make_async_copy(own_in, own_ref, sem.at[0])
+    there = pltpu.make_async_copy(other_in, other_ref, sem.at[1])
+    here.start()
+    there.start()
 
     def along_x(mat_ref, values):
         return dot_rows(mat_ref[...], values)
@@ -316,7 +327,9 @@
 
         lax.fori_loop(0, yl // 2, body, 0)
 
+    here.wait()
     cells(own_ref, 0)
+    there.wait()
     cells(other_ref, yl)
 
     def depth_waves(slots, edge):
@@ -383,8 +396,17 @@
 
         lax.fori_loop(0, plan.py // 2 // plan.unroll, body, 0)
 
+    copies = [
+        pltpu.make_async_copy(m_refs[k], m_outs[k], out_sem.at[k]) for k in range(plan.arrays)
+    ]
+    last = {array: n for n, runs in enumerate(plan.segments) for array, _ in sum(runs, [])}
     for number, segment in enumerate(plan.segments):
         back_x(number, segment)
+        for array in range(plan.arrays):
+            if last[array] == number:
+                copies[array].start()
+    for copy in copies:
+        copy.wait()
 
 
 vmem = pl.BlockSpec(memory_space=pltpu.VMEM)
@@ -394,8 +416,11 @@
 
 def scratch_of(plan):
     return [
-        pltpu.VMEM((plan.y2 * plan.pitch, plan.z2), jnp.float32),
-        pltpu.VMEM((3 * plan.yc * plan.pitch, plan.zl), jnp.float32),
+        pltpu.VMEM(((plan.y2 + 1) * plan.pitch, plan.z2), jnp.float32),
+        pltpu.VMEM(((3 * plan.yc + 1) * plan.pitch, plan.zl), jnp.float32),
+        pltpu.VMEM((3 * plan.yl * plan.xl, plan.zl), jnp.float32),
+        pltpu.VMEM((3 * plan.yl * plan.xl, plan.zl), jnp.float32),
+        pltpu.SemaphoreType.DMA((2,)),
     ]
 
 
@@ -464,7 +489,7 @@
 table_places = (0, None, 1, 2, 3, 4, 5, 6, 7, None)
 
 
-def spectral_call(plan, body, places, w1, tables, arrays, out_shape):
+def spectral_call(plan, body, places, w1, tables, arrays, out_shape, in_space, scratch):
     def table_spec(table, place):
         if place is None:
             return vmem
@@ -478,9 +503,9 @@
             grid=(1,),
             in_specs=[smem]
             + [table_spec(table, place) for table, place in zip(tables, table_places)]
-            + [vmem] * len(arrays),
-            out_specs=[vmem] * len(out_shape),
-            scratch_shapes=scratch_of(plan),
+            + [pl.BlockSpec(memory_space=in_space)] * len(arrays),
+            out_specs=[pl.BlockSpec(memory_space=pl.ANY)] * len(out_shape),
+            scratch_shapes=scratch_of(plan) + scratch,
         ),
         compiler_params=kernel_params,
     )(places, jnp.asarray(w1.reshape(-1)), *[jnp.asarray(table) for table in tables], *arrays)
@@ -490,7 +515,8 @@
     xl, yl, zl = plan.xl, plan.yl, plan.zl
     shape = jax.ShapeDtypeStruct((3 * yl * xl, zl), jnp.float32)
     own, other = spectral_call(
-        plan, field_body, places, tables["w1"], field_tables(plan, tables), octant, [shape, shape]
+        plan, field_body, places, tables["w1"], field_tables(plan, tables), octant, [shape, shape],
+        pltpu.VMEM, [],
     )
     return own.reshape(3, yl, xl, zl), other.reshape(3, yl, xl, zl)
 
@@ -501,7 +527,8 @@
     fields = [own.reshape(-1, zl), other.reshape(-1, zl)]
     shape = jax.ShapeDtypeStruct((rows, zl), jnp.float32)
     return spectral_call(
-        plan, adjoint_body, places, tables["w1"], adjoint_tables(plan, tables), fields, [shape] * plan.arrays
+        plan, adjoint_body, places, tables["w1"], adjoint_tables(plan, tables), fields, [shape] * plan.arrays,
+        pl.ANY, [pltpu.VMEM((rows, zl), jnp.float32)] * plan.arrays + [pltpu.SemaphoreType.DMA((plan.arrays,))],
     )
 
 

time: 389 us -> 385 us (0.990)
  Pallas kernels: 203 us -> 198 us
    pallas_call x2, Pallas kernels: 117 us -> 112 us  [spectral_call(): pl.pallas_call(functools.partial(body, plan, min(8, plan.kh)), out_shape=...]
  transfers between devices with their start and end apart: 64 -> 64, of which waited for: 27 -> 27; matrix products, arithmetic and copies ran while one was open for 4% -> 5% of each run, Pallas kernels for 18% -> 18%
where the time goes in v5:
time: 385 us; the launch traced here: 382 us
  Pallas kernels  198 us (51%)
  waiting for transfers between devices  92.2 us (24%)
  starting transfers between devices  64 us (17%)
  other arithmetic  17.1 us (4%)
  local copies, waits for them, and re-layouts  8.22 us (2%)
    pallas_call x2, Pallas kernels, spectral_call(): pl.pallas_call(functools.partial(body, plan, min(8, plan.kh)), out_shape=...  112 us
    ppermute x10, waiting for transfers between devices, along(): lax.ppermute(array, 'gy', [(2 * a + c, 2 * b + c) for a, b in pairs for c...  35.6 us
    pallas_call x2, Pallas kernels, adjoint_cells_call(): pl.pallas_call(functools.partial(adjoint_cells_body, chunk, begin, xl //...  23.8 us
    pallas_call x2, Pallas kernels, next_cells_call(): pl.pallas_call(functools.partial(next_cells_body, chunk, begin, xl // chu...  21.6 us
    ppermute x18, waiting for transfers between devices, swapped(): lax.ppermute(array, 'gy', [(i, i + 1 - 2 * (i % 2)) for i in range(count)])  15.9 us
    ppermute x10, starting transfers between devices, along(): lax.ppermute(array, 'gy', [(2 * a + c, 2 * b + c) for a, b in pairs for c...  15.7 us
    ppermute x12, starting transfers between devices, to_column(): return lax.ppermute(array, ('gx', 'gz'), [(start, end)])  14.5 us
    pallas_call x1, Pallas kernels, faces_call(): pl.pallas_call(functools.partial(faces_body, chunk), grid=(xl // chunk,),...  13.6 us
  transfers between devices with their start and end apart: 64, of which 27 were waited for; matrix products, arithmetic and copies ran while one was open for 5% of the time, Pallas kernels for 18%

profile of v5, /device:TPU:12, one launch (start us, length us, event | category | flops | bytes accessed | tf_op | source)
XLA Modules:
  0.0 382.2 jit_solution(13826348619975401636)
XLA Ops:
  1.9 4.8 %shard_map.274 = (f32[1024,128]{1,0:T(8,128)}, f32[1024,128]{1,0:T(8,128)}, f32[1024,128]{1,0:T(8,128)}, f32[1024,128]{1,0:T(8,128)}) custom-call(s32[3]{0:T(128)} %get-tuple-element.286.from_ref, s32[3]{0:T(128)} %get-tuple-element.285.to_ref, f32[4096,128]{1,0:T(8,128)} %bitcast.57), custom_call_target="tpu_custom_call" | custom-call | tf_op jit(solution)/shard_map/pallas_call | solution.py:696
  7.8 1.4 collective-permute-start.2
  9.1 1.3 collective-permute-start.4
  11.1 1.4 collective-permute-start.1
  13.3 7.7 %collective-permute-done.4 = f32[512,128]{1,0:T(8,128)} collective-permute-done((f32[512,128]{1,0:T(8,128)S(1)}, f32[512,128]{1,0:T(8,128)}, u32[]{:S(2)}, u32[]{:S(2)}) %collective-permute-start.4) | collective-permute-done | bytes 262176 | tf_op jit(solution)/shard_map/ppermute | solution.py:592
  20.9 1.3 collective-permute-start.5
  22.2 13.6 %shard_map.275 = (f32[7,128,128]{2,1,0:T(8,128)}, f32[7,128,128]{2,1,0:T(8,128)}, f32[7,32,128]{2,1,0:T(8,128)}, f32[7,32,128]{2,1,0:T(8,128)}) custom-call(f32[3,128,32,128]{3,2,1,0:T(8,128)} %va_ref.7, f32[3,128,32,128]{3,2,1,0:T(8,128)} %aa_ref.5, f32[128,32,128]{2,1,0:T(8,128)} %c_ref.7), custom_call_target="tpu_custom_call" | custom-call | tf_op jit(solution)/shard_map/pallas_call | solution.py:740
  36.9 3.6 collective-permute-start.7
  42.1 8.5 %collective-permute-done.7 = f32[1024,128]{1,0:T(8,128)S(1)} collective-permute-done((f32[1024,128]{1,0:T(8,128)S(1)}, f32[1024,128]{1,0:T(8,128)S(1)}, u32[]{:S(2)}, u32[]{:S(2)}) %collective-permute-start.7) | collective-permute-done | bytes 524320 | tf_op jit(solution)/shard_map/ppermute | solution.py:584
  50.5 3.5 collective-permute-start.8
  54.7 1.3 collective-permute-start.6
  56.0 6.2 %collective-permute-done.8 = f32[1024,128]{1,0:T(8,128)S(1)} collective-permute-done((f32[1024,128]{1,0:T(8,128)S(1)}, f32[1024,128]{1,0:T(8,128)S(1)}, u32[]{:S(2)}, u32[]{:S(2)}) %collective-permute-start.8) | collective-permute-done | bytes 524320 | tf_op jit(solution)/shard_map/ppermute | solution.py:584
  63.8 1.9 collective-permute-start.15
  65.8 2.1 collective-permute-done.17
  67.8 2.1 collective-permute-start.16
  71.9 2.0 collective-permute-start.12
  74.8 4.1 %collective-permute-done.13 = f32[512,128]{1,0:T(8,128)S(1)} collective-permute-done((f32[512,128]{1,0:T(8,128)S(1)}, f32[512,128]{1,0:T(8,128)S(1)}, u32[]{:S(2)}, u32[]{:S(2)}) %collective-permute-start.13) | collective-permute-done | bytes 262176 | tf_op jit(solution)/shard_map/ppermute | solution.py:624
  79.7 4.9 %collective-permute-done.11 = f32[512,128]{1,0:T(8,128)S(1)} collective-permute-done((f32[512,128]{1,0:T(8,128)S(1)}, f32[512,128]{1,0:T(8,128)S(1)}, u32[]{:S(2)}, u32[]{:S(2)}) %collective-permute-start.11) | collective-permute-done | bytes 262176 | tf_op jit(solution)/shard_map/ppermute | solution.py:624
  84.6 2.1 collective-permute-done.10
  86.8 1.9 collective-permute-start.19
  90.3 1.4 collective-permute-start.22
  92.8 11.6 %shard_map.276.source_ref = f32[32,128,128]{2,1,0:T(8,128)} custom-call(f32[3,128,32,128]{3,2,1,0:T(8,128)} %aa_ref.5, f32[3,128,32,128]{3,2,1,0:T(8,128)} %aa_ref.5, f32[3,128,32,128]{3,2,1,0:T(8,128)} %aa_ref.5, f32[128,32,128]{2,1,0:T(8,128)} %c_ref.7, f32[128,32,128]{2,1,0:T(8,128)} %c_ref.7, f32[128,32,128]{2,1,0:T(8,128)} %c_ref.7, ...), custom_call_target="tpu_custom_call" | custom-call | tf_op jit(solution)/shard_map/pallas_call | solution.py:966
  104.9 7.6 %collective-permute-done.20.refs_1_ = f32[1024,128]{1,0:T(8,128)S(1)} collective-permute-done((f32[1024,128]{1,0:T(8,128)S(1)}, f32[1024,128]{1,0:T(8,128)S(1)}, u32[]{:S(2)}, u32[]{:S(2)}) %collective-permute-start.20) | collective-permute-done | bytes 524320 | tf_op jit(solution)/shard_map/ppermute | solution.py:629
  114.4 1.5 collective-permute-done.28.refs_14_
  116.1 1.3 collective-permute-done.23.refs_9_
  119.0 59.7 %shard_map.277 = (f32[12288,128]{1,0:T(8,128)}, f32[12288,128]{1,0:T(8,128)}) custom-call(s32[9]{0:T(128)} %stack.58.places_ref, f32[256]{0:T(256)} %constant.97.clone.w1_ref, bf16[8,256,256]{2,1,0:T(8,128)(2,1)} %constant.98.clone.fx_ref, bf16[384,256]{1,0:T(8,128)(2,1)} %constant.99.clone.ez_ref, bf16[4,512,256]{2,1,0:T(8,128)(2,1)} %constant.100.clone.fy_ref, ...), custom_call_target="tpu_custom_call" | custom-call | tf_op jit(solution)/shard_map/pallas_call | solution.py:498
  179.0 10.3 %collective-permute-done.30.arrived_ref = f32[3,32,128,128]{3,2,1,0:T(8,128)} collective-permute-done((f32[3,32,128,128]{3,2,1,0:T(8,128)}, f32[3,32,128,128]{3,2,1,0:T(8,128)}, u32[]{:S(2)}, u32[]{:S(2)}) %collective-permute-start.30) | collective-permute-done | bytes 6291488 | tf_op jit(solution)/shard_map/ppermute | solution.py:537
  189.4 10.5 %shard_map.278 = (f32[3,32,128,128]{3,2,1,0:T(8,128)}, f32[128,32,128]{2,1,0:T(8,128)}, f32[128,128]{1,0:T(8,128)}, f32[128,128]{1,0:T(8,128)}, f32[32,128]{1,0:T(8,128)}, /*index=5*/f32[32,128]{1,0:T(8,128)}) custom-call(f32[3]{0:T(128)} %pad_maximum_fusion.9.app_ref, f32[3,32,128,128]{3,2,1,0:T(8,128)} %bitcast.54, ...), custom_call_target="tpu_custom_call" | custom-call | tf_op jit(solution)/shard_map/pallas_call | solution.py:798
  203.4 1.9 collective-permute-start.33
  205.4 3.9 %collective-permute-start.34 = (f32[128,128]{1,0:T(8,128)}, f32[128,128]{1,0:T(8,128)S(1)}, u32[]{:S(2)}, u32[]{:S(2)}) collective-permute-start(f32[128,128]{1,0:T(8,128)} %get-tuple-element.174), channel_id=1, source_target_pairs={{2,0},{4,2},{6,4},{8,6},{10,8},{12,10},{14,12},{3,1},{5,3},{7,5},{... | collective-permute-start | bytes 196616 | tf_op jit(solution)/shard_map/ppermute | solution.py:757
  209.2 11.9 %shard_map.279.refs_0_ = f32[3,128,32,128]{3,2,1,0:T(8,128)} custom-call(f32[3,128,32,128]{3,2,1,0:T(8,128)} %va_ref.7, f32[3,128,32,128]{3,2,1,0:T(8,128)} %va_ref.7, f32[3,128,32,128]{3,2,1,0:T(8,128)} %va_ref.7, f32[3,128,32,128]{3,2,1,0:T(8,128)} %aa_ref.5, f32[3,128,32,128]{3,2,1,0:T(8,128)} %aa_ref.5, f32[3,128,32,128]{3,2,1,0:T(8,128)} %aa_ref.5, ...), custom_call_target="tpu_custom_call" | custom-call | tf_op jit(solution)/shard_map/pallas_call | solution.py:986
  222.4 52.7 %shard_map.280 = (f32[1024,128]{1,0:T(8,128)}, f32[1024,128]{1,0:T(8,128)}, f32[1024,128]{1,0:T(8,128)}, f32[1024,128]{1,0:T(8,128)}, f32[1024,128]{1,0:T(8,128)...) custom-call(s32[9]{0:T(128)} %stack.58.places_ref, ...), custom_call_target="tpu_custom_call" | custom-call | tf_op jit(solution)/shard_map/pallas_call | solution.py:498
  275.7 1.6 collective-permute-done.39
  277.3 1.1 add.106
  278.5 1.5 collective-permute-start.40
  280.0 1.1 add.105
  282.4 10.9 %shard_map.281.refs_0_ = f32[3,128,32,128]{3,2,1,0:T(8,128)} custom-call(f32[3,128,32,128]{3,2,1,0:T(8,128)} %va_ref.7, f32[3,128,32,128]{3,2,1,0:T(8,128)} %va_ref.7, f32[3,128,32,128]{3,2,1,0:T(8,128)} %va_ref.7, f32[128,32,128]{2,1,0:T(8,128)} %get-tuple-element.206.e_ref.eb_ref.ea_ref, f32[128,32,128]{2,1,0:T(8,128)} %get-tuple-element.206.e_ref.eb_ref.ea_ref, ...), custom_call_target="tpu_custom_call" | custom-call | tf_op jit(solution)/shard_map/pallas_call | solution.py:1016
  295.4 1.2 add_add_fusion.2
  297.4 1.1 collective-permute-start.43
  298.8 6.1 %collective-permute-done.41 = f32[512,128]{1,0:T(8,128)S(1)} collective-permute-done((f32[512,128]{1,0:T(8,128)S(1)}, f32[512,128]{1,0:T(8,128)S(1)}, u32[]{:S(2)}, u32[]{:S(2)}) %collective-permute-start.41) | collective-permute-done | bytes 262176 | tf_op jit(solution)/shard_map/ppermute | solution.py:640
  306.2 1.1 collective-permute-start.49
  307.3 1.1 collective-permute-start.50
  308.4 10.7 %shard_map.282 = f32[3,128,32,128]{3,2,1,0:T(8,128)} custom-call(f32[3,128,32,128]{3,2,1,0:T(8,128)} %va_ref.7, f32[3,128,32,128]{3,2,1,0:T(8,128)} %va_ref.7, f32[3,128,32,128]{3,2,1,0:T(8,128)} %va_ref.7, f32[128,32,128]{2,1,0:T(8,128)} %get-tuple-element.206.e_ref.eb_ref.ea_ref, ...), custom_call_target="tpu_custom_call", output_to_operand_aliasing={{}: (19, {})} | custom-call | tf_op jit(solution)/shard_map/pallas_call | solution.py:1016
  319.7 1.1 add.116
  320.8 1.2 collective-permute-start.51
  322.1 1.4 collective-permute-start.52
  323.5 1.3 collective-permute-start.55
  324.8 2.4 collective-permute-done.51
  327.3 1.2 collective-permute-done.52
  329.3 1.3 collective-permute-start.54
  330.6 7.1 %collective-permute-done.55 = f32[1024,128]{1,0:T(8,128)S(1)} collective-permute-done((f32[1024,128]{1,0:T(8,128)S(1)}, f32[1024,128]{1,0:T(8,128)S(1)}, u32[]{:S(2)}, u32[]{:S(2)}) %collective-permute-start.55) | collective-permute-done | bytes 524320 | tf_op jit(solution)/shard_map/ppermute | solution.py:584
  337.7 1.3 collective-permute-start.56
  339.2 1.3 collective-permute-start.57
  340.5 1.2 collective-permute-done.54
  341.7 5.5 %collective-permute-done.56 = f32[1024,128]{1,0:T(8,128)S(1)} collective-permute-done((f32[1024,128]{1,0:T(8,128)S(1)}, f32[1024,128]{1,0:T(8,128)S(1)}, u32[]{:S(2)}, u32[]{:S(2)}) %collective-permute-start.56) | collective-permute-done | bytes 524320 | tf_op jit(solution)/shard_map/ppermute | solution.py:584
  347.2 7.1 %collective-permute-done.57 = f32[1024,128]{1,0:T(8,128)S(1)} collective-permute-done((f32[1024,128]{1,0:T(8,128)S(1)}, f32[1024,128]{1,0:T(8,128)S(1)}, u32[]{:S(2)}, u32[]{:S(2)}) %collective-permute-start.57) | collective-permute-done | bytes 524320 | tf_op jit(solution)/shard_map/ppermute | solution.py:584
  355.2 1.3 collective-permute-start.62
  357.8 2.6 collective-permute-start.59
  360.4 1.3 compare_and_fusion.1
  361.7 1.3 compare_and_fusion.2
  364.0 1.9 collective-permute-start.63
  365.9 1.3 compare_and_fusion
  367.6 11.9 %shard_map.283 = f32[3,128,32,128]{3,2,1,0:T(8,128)} custom-call(f32[3,128,32,128]{3,2,1,0:T(8,128)} %va_ref.7, f32[3,128,32,128]{3,2,1,0:T(8,128)} %va_ref.7, f32[3,128,32,128]{3,2,1,0:T(8,128)} %va_ref.7, f32[3,128,32,128]{3,2,1,0:T(8,128)} %aa_ref.5, f32[3,128,32,128]{3,2,1,0:T(8,128)} %aa_ref.5, ...), custom_call_target="tpu_custom_call", output_to_operand_aliasing={{}: (12, {})} | custom-call | tf_op jit(solution)/shard_map/pallas_call | solution.py:986
  380.5 1.7 fusion
  (192 shorter events, 35.7 us)
Async XLA Ops:
  7.8 4.8 %collective-permute-start.2 = (f32[512,128]{1,0:T(8,128)S(1)}, f32[512,128]{1,0:T(8,128)}, u32[]{:S(2)}, u32[]{:S(2)}) collective-permute-start(f32[512,128]{1,0:T(8,128)S(1)} %get-tuple-element.269), channel_id=1, source_target_pairs={{0,1},{2,3},{4,5},{6,7},{8,9},{10,11},{12,13},{14,15}} | collective-permute-start | bytes 786440 | tf_op jit(solution)/shard_map/ppermute | solution.py:592
  9.1 11.8 %collective-permute-start.4 = (f32[512,128]{1,0:T(8,128)S(1)}, f32[512,128]{1,0:T(8,128)}, u32[]{:S(2)}, u32[]{:S(2)}) collective-permute-start(f32[512,128]{1,0:T(8,128)S(1)} %get-tuple-element.270), channel_id=1, source_target_pairs={{0,16},{2,18},{4,20},{6,22},{8,24},{10,26},{12,28},{14,30}} | collective-permute-start | bytes 786440 | tf_op jit(solution)/shard_map/ppermute | solution.py:592
  10.4 26.3 %collective-permute-start = (f32[1024,128]{1,0:T(8,128)}, f32[1024,128]{1,0:T(8,128)S(1)}, u32[]{:S(2)}, u32[]{:S(2)}) collective-permute-start(f32[1024,128]{1,0:T(8,128)} %get-tuple-element.130), channel_id=1, source_target_pairs={{0,1},{2,3},{4,5},{6,7},{8,9},{10,11},{12,13},{14,15}} | collective-permute-start | bytes 1572872 | tf_op jit(solution)/shard_map/ppermute | solution.py:592
  11.1 25.6 %collective-permute-start.1 = (f32[1024,128]{1,0:T(8,128)}, f32[1024,128]{1,0:T(8,128)S(1)}, u32[]{:S(2)}, u32[]{:S(2)}) collective-permute-start(f32[1024,128]{1,0:T(8,128)} %get-tuple-element.131), channel_id=1, source_target_pairs={{0,16},{2,18},{4,20},{6,22},{8,24},{10,26},{12,28},{14,30}} | collective-permute-start | bytes 1572872 | tf_op jit(solution)/shard_map/ppermute | solution.py:592
  12.6 24.1 %collective-permute-start.3 = (f32[512,128]{1,0:T(8,128)}, f32[512,128]{1,0:T(8,128)S(1)}, u32[]{:S(2)}, u32[]{:S(2)}) collective-permute-start(f32[512,128]{1,0:T(8,128)} %collective-permute-done.2), channel_id=1, source_target_pairs={{1,17},{3,19},{5,21},{7,23},{9,25},{11,27},{13,29},{15,31}} | collective-permute-start | bytes 786440 | tf_op jit(solution)/shard_map/ppermute | solution.py:592
  20.9 15.8 %collective-permute-start.5 = (f32[512,128]{1,0:T(8,128)}, f32[512,128]{1,0:T(8,128)S(1)}, u32[]{:S(2)}, u32[]{:S(2)}) collective-permute-start(f32[512,128]{1,0:T(8,128)} %collective-permute-done.4), channel_id=1, source_target_pairs={{16,17},{18,19},{20,21},{22,23},{24,25},{26,27},{28,29},{30,31}} | collective-permute-start | bytes 786440 | tf_op jit(solution)/shard_map/ppermute | solution.py:592
  36.9 13.7 %collective-permute-start.7 = (f32[1024,128]{1,0:T(8,128)S(1)}, f32[1024,128]{1,0:T(8,128)S(1)}, u32[]{:S(2)}, u32[]{:S(2)}) collective-permute-start(f32[1024,128]{1,0:T(8,128)S(1)} %maximum_add_fusion), channel_id=1, source_target_pairs={{0,4},{2,6},{4,8},{6,10},{1,5},{3,7},{5,9},{7,11},{16,20},{18,22},... | collective-permute-start | bytes 1572872 | tf_op jit(solution)/shard_map/ppermute | solution.py:584
  50.5 11.7 %collective-permute-start.8 = (f32[1024,128]{1,0:T(8,128)S(1)}, f32[1024,128]{1,0:T(8,128)S(1)}, u32[]{:S(2)}, u32[]{:S(2)}) collective-permute-start(f32[1024,128]{1,0:T(8,128)S(1)} %collective-permute-done.7), channel_id=1, source_target_pairs={{4,8},{6,10},{8,12},{10,14},{5,9},{7,11},{9,13},{11,15},{20,24},{2... | collective-permute-start | bytes 1572872 | tf_op jit(solution)/shard_map/ppermute | solution.py:584
  54.7 16.0 %collective-permute-start.6 = (f32[1024,128]{1,0:T(8,128)S(1)}, f32[1024,128]{1,0:T(8,128)S(1)}, u32[]{:S(2)}, u32[]{:S(2)}) collective-permute-start(f32[1024,128]{1,0:T(8,128)S(1)} %maximum_add_fusion), channel_id=1, source_target_pairs={{4,0},{6,2},{5,1},{7,3},{20,16},{22,18},{21,17},{23,19}} | collective-permute-start | bytes 1572872 | tf_op jit(solution)/shard_map/ppermute | solution.py:584
  62.2 8.4 %collective-permute-start.9 = (f32[1024,128]{1,0:T(8,128)S(1)}, f32[1024,128]{1,0:T(8,128)S(1)}, u32[]{:S(2)}, u32[]{:S(2)}) collective-permute-start(f32[1024,128]{1,0:T(8,128)S(1)} %collective-permute-done.8), channel_id=1, source_target_pairs={{8,12},{10,14},{9,13},{11,15},{24,28},{26,30},{25,29},{27,31}} | collective-permute-start | bytes 1572872 | tf_op jit(solution)/shard_map/ppermute | solution.py:584
  63.0 4.9 %collective-permute-start.17 = (f32[7,32,128]{2,1,0:T(8,128)S(1)}, f32[7,32,128]{2,1,0:T(8,128)S(1)}, u32[]{:S(2)}, u32[]{:S(2)}) collective-permute-start(f32[7,32,128]{2,1,0:T(8,128)S(1)} %broadcast_select_fusion.4), channel_id=1, source_target_pairs={{0,1},{1,0},{2,3},{3,2},{4,5},{5,4},{6,7},{7,6},{8,9},{9,8},{10,11... | collective-permute-start | bytes 344072 | tf_op jit(solution)/shard_map/ppermute | solution.py:754
  63.1 10.9 %collective-permute-start.14 = (f32[7,32,128]{2,1,0:T(8,128)S(1)}, f32[7,32,128]{2,1,0:T(8,128)S(1)}, u32[]{:S(2)}, u32[]{:S(2)}) collective-permute-start(f32[7,32,128]{2,1,0:T(8,128)S(1)} %broadcast_select_fusion.5), channel_id=1, source_target_pairs={{0,16},{16,0},{1,17},{17,1},{2,18},{18,2},{3,19},{19,3},{4,20},{20... | collective-permute-start | bytes 344072 | tf_op jit(solution)/shard_map/ppermute | solution.py:754
  63.8 15.8 %collective-permute-start.15 = (f32[7,128,128]{2,1,0:T(8,128)S(1)}, f32[7,128,128]{2,1,0:T(8,128)S(1)}, u32[]{:S(2)}, u32[]{:S(2)}) collective-permute-start(f32[7,128,128]{2,1,0:T(8,128)S(1)} %copy-done.27), channel_id=1, source_target_pairs={{0,2},{2,4},{4,6},{6,8},{8,10},{10,12},{12,14},{1,3},{3,5},{5,7},{... | collective-permute-start | bytes 1376264 | tf_op jit(solution)/shard_map/ppermute | solution.py:756
  67.8 11.8 %collective-permute-start.16 = (f32[7,128,128]{2,1,0:T(8,128)S(1)}, f32[7,128,128]{2,1,0:T(8,128)S(1)}, u32[]{:S(2)}, u32[]{:S(2)}) collective-permute-start(f32[7,128,128]{2,1,0:T(8,128)S(1)} %copy-done.26), channel_id=1, source_target_pairs={{2,0},{4,2},{6,4},{8,6},{10,8},{12,10},{14,12},{3,1},{5,3},{7,5},{... | collective-permute-start | bytes 1376264 | tf_op jit(solution)/shard_map/ppermute | solution.py:757
  70.8 8.1 %collective-permute-start.13 = (f32[512,128]{1,0:T(8,128)S(1)}, f32[512,128]{1,0:T(8,128)S(1)}, u32[]{:S(2)}, u32[]{:S(2)}) collective-permute-start(f32[512,128]{1,0:T(8,128)S(1)} %get-tuple-element.265), channel_id=1, source_target_pairs={{0,16},{16,0},{1,17},{17,1},{2,18},{18,2},{3,19},{19,3},{4,20},{20... | collective-permute-start | bytes 786440 | tf_op jit(solution)/shard_map/ppermute | solution.py:624
  71.9 7.7 %collective-permute-start.12 = (f32[512,128]{1,0:T(8,128)S(1)}, f32[512,128]{1,0:T(8,128)S(1)}, u32[]{:S(2)}, u32[]{:S(2)}) collective-permute-start(f32[512,128]{1,0:T(8,128)S(1)} %get-tuple-element.266), channel_id=1, source_target_pairs={{0,1},{1,0},{2,3},{3,2},{4,5},{5,4},{6,7},{7,6},{8,9},{9,8},{10,11... | collective-permute-start | bytes 786440 | tf_op jit(solution)/shard_map/ppermute | solution.py:624
  73.9 10.6 %collective-permute-start.11 = (f32[512,128]{1,0:T(8,128)S(1)}, f32[512,128]{1,0:T(8,128)S(1)}, u32[]{:S(2)}, u32[]{:S(2)}) collective-permute-start(f32[512,128]{1,0:T(8,128)S(1)} %get-tuple-element.267), channel_id=1, source_target_pairs={{0,16},{16,0},{1,17},{17,1},{2,18},{18,2},{3,19},{19,3},{4,20},{20... | collective-permute-start | bytes 786440 | tf_op jit(solution)/shard_map/ppermute | solution.py:624
  78.9 7.7 %collective-permute-start.10 = (f32[512,128]{1,0:T(8,128)S(1)}, f32[512,128]{1,0:T(8,128)S(1)}, u32[]{:S(2)}, u32[]{:S(2)}) collective-permute-start(f32[512,128]{1,0:T(8,128)S(1)} %get-tuple-element.268), channel_id=1, source_target_pairs={{0,1},{1,0},{2,3},{3,2},{4,5},{5,4},{6,7},{7,6},{8,9},{9,8},{10,11... | collective-permute-start | bytes 786440 | tf_op jit(solution)/shard_map/ppermute | solution.py:624
  86.7 17.6 %collective-permute-start.18 = (f32[1024,128]{1,0:T(8,128)S(1)}, f32[1024,128]{1,0:T(8,128)S(1)}, u32[]{:S(2)}, u32[]{:S(2)}) collective-permute-start(f32[1024,128]{1,0:T(8,128)S(1)} %pad_maximum_fusion.refs_4_), channel_id=1, source_target_pairs={{0,16},{16,0},{1,17},{17,1},{2,18},{18,2},{3,19},{19,3},{4,20},{20... | collective-permute-start | bytes 1572872 | tf_op jit(solution)/shard_map/ppermute | solution.py:629
  86.8 17.6 %collective-permute-start.19 = (f32[1024,128]{1,0:T(8,128)S(1)}, f32[1024,128]{1,0:T(8,128)}, u32[]{:S(2)}, u32[]{:S(2)}) collective-permute-start(f32[1024,128]{1,0:T(8,128)S(1)} %pad_maximum_fusion.1.refs_6_), channel_id=1, source_target_pairs={{0,1},{1,0},{2,3},{3,2},{4,5},{5,4},{6,7},{7,6},{8,9},{9,8},{10,11... | collective-permute-start | bytes 1572872 | tf_op jit(solution)/shard_map/ppermute | solution.py:629
  90.2 22.3 %collective-permute-start.20 = (f32[1024,128]{1,0:T(8,128)S(1)}, f32[1024,128]{1,0:T(8,128)S(1)}, u32[]{:S(2)}, u32[]{:S(2)}) collective-permute-start(f32[1024,128]{1,0:T(8,128)S(1)} %pad_maximum_fusion.2.refs_0_), channel_id=1, source_target_pairs={{0,16},{16,0},{1,17},{17,1},{2,18},{18,2},{3,19},{19,3},{4,20},{20... | collective-permute-start | bytes 1572872 | tf_op jit(solution)/shard_map/ppermute | solution.py:629
  90.3 22.7 %collective-permute-start.22 = (f32[1024,128]{1,0:T(8,128)S(1)}, f32[1024,128]{1,0:T(8,128)}, u32[]{:S(2)}, u32[]{:S(2)}) collective-permute-start(f32[1024,128]{1,0:T(8,128)S(1)} %pad_maximum_fusion.2.refs_0_), channel_id=1, source_target_pairs={{0,2},{2,0},{4,6},{6,4},{8,10},{10,8},{12,14},{14,12},{1,3},{3,1},... | collective-permute-start | bytes 1572872 | tf_op jit(solution)/shard_map/ppermute | solution.py:537
  91.7 20.9 %collective-permute-start.21 = (f32[1024,128]{1,0:T(8,128)S(1)}, f32[1024,128]{1,0:T(8,128)}, u32[]{:S(2)}, u32[]{:S(2)}) collective-permute-start(f32[1024,128]{1,0:T(8,128)S(1)} %pad_maximum_fusion.3.refs_2_), channel_id=1, source_target_pairs={{0,1},{1,0},{2,3},{3,2},{4,5},{5,4},{6,7},{7,6},{8,9},{9,8},{10,11... | collective-permute-start | bytes 1572872 | tf_op jit(solution)/shard_map/ppermute | solution.py:629
  104.3 8.8 %collective-permute-start.24 = (f32[1024,128]{1,0:T(8,128)S(1)}, f32[1024,128]{1,0:T(8,128)S(1)}, u32[]{:S(2)}, u32[]{:S(2)}) collective-permute-start(f32[1024,128]{1,0:T(8,128)S(1)} %pad_maximum_fusion.3.refs_2_), channel_id=1, source_target_pairs={{0,2},{2,0},{4,6},{6,4},{8,10},{10,8},{12,14},{14,12},{1,3},{3,1},... | collective-permute-start | bytes 1572872 | tf_op jit(solution)/shard_map/ppermute | solution.py:537
  104.4 9.1 %collective-permute-start.26 = (f32[1024,128]{1,0:T(8,128)S(1)}, f32[1024,128]{1,0:T(8,128)S(1)}, u32[]{:S(2)}, u32[]{:S(2)}) collective-permute-start(f32[1024,128]{1,0:T(8,128)S(1)} %pad_maximum_fusion.refs_4_), channel_id=1, source_target_pairs={{0,2},{2,0},{4,6},{6,4},{8,10},{10,8},{12,14},{14,12},{1,3},{3,1},... | collective-permute-start | bytes 1572872 | tf_op jit(solution)/shard_map/ppermute | solution.py:537
  112.5 1.9 collective-permute-start.27
  112.7 3.3 collective-permute-start.28
  113.0 3.1 collective-permute-start.29
  113.2 4.3 %collective-permute-start.23 = (f32[1024,128]{1,0:T(8,128)S(1)}, f32[1024,128]{1,0:T(8,128)S(1)}, u32[]{:S(2)}, u32[]{:S(2)}) collective-permute-start(f32[1024,128]{1,0:T(8,128)S(1)} %collective-permute-done.20.refs_1_), channel_id=1, source_target_pairs={{0,2},{2,0},{4,6},{6,4},{8,10},{10,8},{12,14},{14,12},{1,3},{3,1},... | collective-permute-start | bytes 1572872 | tf_op jit(solution)/shard_map/ppermute | solution.py:537
  113.6 4.1 %collective-permute-start.25 = (f32[1024,128]{1,0:T(8,128)}, f32[1024,128]{1,0:T(8,128)S(1)}, u32[]{:S(2)}, u32[]{:S(2)}) collective-permute-start(f32[1024,128]{1,0:T(8,128)} %collective-permute-done.21.refs_3_), channel_id=1, source_target_pairs={{0,2},{2,0},{4,6},{6,4},{8,10},{10,8},{12,14},{14,12},{1,3},{3,1},... | collective-permute-start | bytes 1572872 | tf_op jit(solution)/shard_map/ppermute | solution.py:537
  178.8 10.6 %collective-permute-start.30 = (f32[3,32,128,128]{3,2,1,0:T(8,128)}, f32[3,32,128,128]{3,2,1,0:T(8,128)}, u32[]{:S(2)}, u32[]{:S(2)}) collective-permute-start(f32[3,32,128,128]{3,2,1,0:T(8,128)} %bitcast.61), channel_id=1, source_target_pairs={{0,2},{2,0},{4,6},{6,4},{8,10},{10,8},{12,14},{14,12},{1,3},{3,1},... | collective-permute-start | bytes 18874376 | tf_op jit(solution)/shard_map/ppermute | solution.py:537
  199.8 22.5 %collective-permute-start.31 = (f32[3,32,128,128]{3,2,1,0:T(8,128)}, f32[3,32,128,128]{3,2,1,0:T(8,128)}, u32[]{:S(2)}, u32[]{:S(2)}) collective-permute-start(f32[3,32,128,128]{3,2,1,0:T(8,128)} %get-tuple-element.171), channel_id=1, source_target_pairs={{0,2},{2,0},{4,6},{6,4},{8,10},{10,8},{12,14},{14,12},{1,3},{3,1},... | collective-permute-start | bytes 18874376 | tf_op jit(solution)/shard_map/ppermute | solution.py:537
  200.8 20.3 %collective-permute-start.35 = (f32[32,128]{1,0:T(8,128)S(1)}, f32[32,128]{1,0:T(8,128)S(1)}, u32[]{:S(2)}, u32[]{:S(2)}) collective-permute-start(f32[32,128]{1,0:T(8,128)S(1)} %broadcast_select_fusion.10), channel_id=1, source_target_pairs={{0,1},{1,0},{2,3},{3,2},{4,5},{5,4},{6,7},{7,6},{8,9},{9,8},{10,11... | collective-permute-start | bytes 49160 | tf_op jit(solution)/shard_map/ppermute | solution.py:754
  202.4 19.3 %collective-permute-start.32 = (f32[32,128]{1,0:T(8,128)S(1)}, f32[32,128]{1,0:T(8,128)S(1)}, u32[]{:S(2)}, u32[]{:S(2)}) collective-permute-start(f32[32,128]{1,0:T(8,128)S(1)} %select_bitcast_fusion), channel_id=1, source_target_pairs={{0,16},{16,0},{1,17},{17,1},{2,18},{18,2},{3,19},{19,3},{4,20},{20... | collective-permute-start | bytes 49160 | tf_op jit(solution)/shard_map/ppermute | solution.py:754
  203.4 18.9 %collective-permute-start.33 = (f32[128,128]{1,0:T(8,128)}, f32[128,128]{1,0:T(8,128)S(1)}, u32[]{:S(2)}, u32[]{:S(2)}) collective-permute-start(f32[128,128]{1,0:T(8,128)} %get-tuple-element.173), channel_id=1, source_target_pairs={{0,2},{2,4},{4,6},{6,8},{8,10},{10,12},{12,14},{1,3},{3,5},{5,7},{... | collective-permute-start | bytes 196616 | tf_op jit(solution)/shard_map/ppermute | solution.py:756
  205.4 17.0 %collective-permute-start.34 = (f32[128,128]{1,0:T(8,128)}, f32[128,128]{1,0:T(8,128)S(1)}, u32[]{:S(2)}, u32[]{:S(2)}) collective-permute-start(f32[128,128]{1,0:T(8,128)} %get-tuple-element.174), channel_id=1, source_target_pairs={{2,0},{4,2},{6,4},{8,6},{10,8},{12,10},{14,12},{3,1},{5,3},{7,5},{... | collective-permute-start | bytes 196616 | tf_op jit(solution)/shard_map/ppermute | solution.py:757
  275.2 2.2 collective-permute-start.39
  275.2 4.7 %collective-permute-start.37 = (f32[1024,128]{1,0:T(8,128)}, f32[1024,128]{1,0:T(8,128)S(1)}, u32[]{:S(2)}, u32[]{:S(2)}) collective-permute-start(f32[1024,128]{1,0:T(8,128)} %get-tuple-element.203), channel_id=1, source_target_pairs={{0,2},{2,0},{4,6},{6,4},{8,10},{10,8},{12,14},{14,12},{1,3},{3,1},... | collective-permute-start | bytes 1572872 | tf_op jit(solution)/shard_map/ppermute | solution.py:537
  278.5 14.8 %collective-permute-start.40 = (f32[1024,128]{1,0:T(8,128)S(1)}, f32[1024,128]{1,0:T(8,128)S(1)}, u32[]{:S(2)}, u32[]{:S(2)}) collective-permute-start(f32[1024,128]{1,0:T(8,128)S(1)} %add.106), channel_id=1, source_target_pairs={{0,1},{1,0},{2,3},{3,2},{4,5},{5,4},{6,7},{7,6},{8,9},{9,8},{10,11... | collective-permute-start | bytes 1572872 | tf_op jit(solution)/shard_map/ppermute | solution.py:634
  281.1 13.8 %collective-permute-start.38 = (f32[1024,128]{1,0:T(8,128)S(1)}, f32[1024,128]{1,0:T(8,128)S(1)}, u32[]{:S(2)}, u32[]{:S(2)}) collective-permute-start(f32[1024,128]{1,0:T(8,128)S(1)} %add.105), channel_id=1, source_target_pairs={{0,16},{16,0},{1,17},{17,1},{2,18},{18,2},{3,19},{19,3},{4,20},{20... | collective-permute-start | bytes 1572872 | tf_op jit(solution)/shard_map/ppermute | solution.py:634
  281.9 13.0 %collective-permute-start.36 = (f32[1024,128]{1,0:T(8,128)}, f32[1024,128]{1,0:T(8,128)}, u32[]{:S(2)}, u32[]{:S(2)}) collective-permute-start(f32[1024,128]{1,0:T(8,128)} %get-tuple-element.201), channel_id=1, source_target_pairs={{0,2},{2,0},{4,6},{6,4},{8,10},{10,8},{12,14},{14,12},{1,3},{3,1},... | collective-permute-start | bytes 1572872 | tf_op jit(solution)/shard_map/ppermute | solution.py:537
  281.9 14.7 %collective-permute-start.42 = (f32[1024,128]{1,0:T(8,128)}, f32[1024,128]{1,0:T(8,128)S(1)}, u32[]{:S(2)}, u32[]{:S(2)}) collective-permute-start(f32[1024,128]{1,0:T(8,128)} %get-tuple-element.221), channel_id=1, source_target_pairs={{0,2},{2,0},{4,6},{6,4},{8,10},{10,8},{12,14},{14,12},{1,3},{3,1},... | collective-permute-start | bytes 1572872 | tf_op jit(solution)/shard_map/ppermute | solution.py:537
  282.4 15.0 %collective-permute-start.47 = (f32[1024,128]{1,0:T(8,128)}, f32[1024,128]{1,0:T(8,128)S(1)}, u32[]{:S(2)}, u32[]{:S(2)}) collective-permute-start(f32[1024,128]{1,0:T(8,128)} %get-tuple-element.230), channel_id=1, source_target_pairs={{0,2},{2,0},{4,6},{6,4},{8,10},{10,8},{12,14},{14,12},{1,3},{3,1},... | collective-permute-start | bytes 1572872 | tf_op jit(solution)/shard_map/ppermute | solution.py:537
  293.3 5.3 %collective-permute-start.46 = (f32[1024,128]{1,0:T(8,128)}, f32[1024,128]{1,0:T(8,128)S(1)}, u32[]{:S(2)}, u32[]{:S(2)}) collective-permute-start(f32[1024,128]{1,0:T(8,128)} %get-tuple-element.228), channel_id=1, source_target_pairs={{0,2},{2,0},{4,6},{6,4},{8,10},{10,8},{12,14},{14,12},{1,3},{3,1},... | collective-permute-start | bytes 1572872 | tf_op jit(solution)/shard_map/ppermute | solution.py:537
  294.9 3.8 collective-permute-start.45
  294.9 3.9 %collective-permute-start.44 = (f32[1024,128]{1,0:T(8,128)}, f32[1024,128]{1,0:T(8,128)S(1)}, u32[]{:S(2)}, u32[]{:S(2)}) collective-permute-start(f32[1024,128]{1,0:T(8,128)} %get-tuple-element.224), channel_id=1, source_target_pairs={{0,2},{2,0},{4,6},{6,4},{8,10},{10,8},{12,14},{14,12},{1,3},{3,1},... | collective-permute-start | bytes 1572872 | tf_op jit(solution)/shard_map/ppermute | solution.py:537
  296.6 8.3 %collective-permute-start.41 = (f32[512,128]{1,0:T(8,128)S(1)}, f32[512,128]{1,0:T(8,128)S(1)}, u32[]{:S(2)}, u32[]{:S(2)}) collective-permute-start(f32[512,128]{1,0:T(8,128)S(1)} %slice.133), channel_id=1, source_target_pairs={{0,1},{1,0},{2,3},{3,2},{4,5},{5,4},{6,7},{7,6},{8,9},{9,8},{10,11... | collective-permute-start | bytes 786440 | tf_op jit(solution)/shard_map/ppermute | solution.py:640
  297.4 8.0 %collective-permute-start.43 = (f32[512,128]{1,0:T(8,128)S(1)}, f32[512,128]{1,0:T(8,128)S(1)}, u32[]{:S(2)}, u32[]{:S(2)}) collective-permute-start(f32[512,128]{1,0:T(8,128)S(1)} %slice.135), channel_id=1, source_target_pairs={{0,16},{16,0},{1,17},{17,1},{2,18},{18,2},{3,19},{19,3},{4,20},{20... | collective-permute-start | bytes 786440 | tf_op jit(solution)/shard_map/ppermute | solution.py:641
  305.5 13.7 %collective-permute-start.48 = (f32[1024,128]{1,0:T(8,128)S(1)}, f32[1024,128]{1,0:T(8,128)S(1)}, u32[]{:S(2)}, u32[]{:S(2)}) collective-permute-start(f32[1024,128]{1,0:T(8,128)S(1)} %pad_maximum_fusion.4), channel_id=1, source_target_pairs={{12,8},{14,10},{13,9},{15,11},{28,24},{30,26},{29,25},{31,27}} | collective-permute-start | bytes 1572872 | tf_op jit(solution)/shard_map/ppermute | solution.py:584
  306.2 13.0 %collective-permute-start.49 = (f32[1024,128]{1,0:T(8,128)S(1)}, f32[1024,128]{1,0:T(8,128)}, u32[]{:S(2)}, u32[]{:S(2)}) collective-permute-start(f32[1024,128]{1,0:T(8,128)S(1)} %add.113), channel_id=1, source_target_pairs={{0,16},{16,0},{1,17},{17,1},{2,18},{18,2},{3,19},{19,3},{4,20},{20... | collective-permute-start | bytes 1572872 | tf_op jit(solution)/shard_map/ppermute | solution.py:634
  307.3 12.4 %collective-permute-start.50 = (f32[1024,128]{1,0:T(8,128)S(1)}, f32[1024,128]{1,0:T(8,128)S(1)}, u32[]{:S(2)}, u32[]{:S(2)}) collective-permute-start(f32[1024,128]{1,0:T(8,128)S(1)} %add.115), channel_id=1, source_target_pairs={{0,1},{1,0},{2,3},{3,2},{4,5},{5,4},{6,7},{7,6},{8,9},{9,8},{10,11... | collective-permute-start | bytes 1572872 | tf_op jit(solution)/shard_map/ppermute | solution.py:634
  320.8 6.4 %collective-permute-start.51 = (f32[512,128]{1,0:T(8,128)S(1)}, f32[512,128]{1,0:T(8,128)S(1)}, u32[]{:S(2)}, u32[]{:S(2)}) collective-permute-start(f32[512,128]{1,0:T(8,128)S(1)} %slice.137), channel_id=1, source_target_pairs={{0,1},{1,0},{2,3},{3,2},{4,5},{5,4},{6,7},{7,6},{8,9},{9,8},{10,11... | collective-permute-start | bytes 786440 | tf_op jit(solution)/shard_map/ppermute | solution.py:640
  322.1 6.4 %collective-permute-start.52 = (f32[512,128]{1,0:T(8,128)S(1)}, f32[512,128]{1,0:T(8,128)S(1)}, u32[]{:S(2)}, u32[]{:S(2)}) collective-permute-start(f32[512,128]{1,0:T(8,128)S(1)} %slice.139), channel_id=1, source_target_pairs={{0,16},{16,0},{1,17},{17,1},{2,18},{18,2},{3,19},{19,3},{4,20},{20... | collective-permute-start | bytes 786440 | tf_op jit(solution)/shard_map/ppermute | solution.py:641
  323.5 14.1 %collective-permute-start.55 = (f32[1024,128]{1,0:T(8,128)S(1)}, f32[1024,128]{1,0:T(8,128)S(1)}, u32[]{:S(2)}, u32[]{:S(2)}) collective-permute-start(f32[1024,128]{1,0:T(8,128)S(1)} %add.122), channel_id=1, source_target_pairs={{8,4},{10,6},{9,5},{11,7},{24,20},{26,22},{25,21},{27,23}} | collective-permute-start | bytes 1572872 | tf_op jit(solution)/shard_map/ppermute | solution.py:584
  328.6 10.4 %collective-permute-start.53 = (f32[1024,128]{1,0:T(8,128)S(1)}, f32[1024,128]{1,0:T(8,128)S(1)}, u32[]{:S(2)}, u32[]{:S(2)}) collective-permute-start(f32[1024,128]{1,0:T(8,128)S(1)} %pad_maximum_fusion.5), channel_id=1, source_target_pairs={{12,8},{14,10},{13,9},{15,11},{28,24},{30,26},{29,25},{31,27}} | collective-permute-start | bytes 1572872 | tf_op jit(solution)/shard_map/ppermute | solution.py:584
  329.3 12.3 %collective-permute-start.54 = (f32[1024,128]{1,0:T(8,128)S(1)}, f32[1024,128]{1,0:T(8,128)S(1)}, u32[]{:S(2)}, u32[]{:S(2)}) collective-permute-start(f32[1024,128]{1,0:T(8,128)S(1)} %pad_maximum_fusion.4), channel_id=1, source_target_pairs={{0,4},{2,6},{1,5},{3,7},{16,20},{18,22},{17,21},{19,23}} | collective-permute-start | bytes 1572872 | tf_op jit(solution)/shard_map/ppermute | solution.py:584
  337.7 9.4 %collective-permute-start.56 = (f32[1024,128]{1,0:T(8,128)S(1)}, f32[1024,128]{1,0:T(8,128)S(1)}, u32[]{:S(2)}, u32[]{:S(2)}) collective-permute-start(f32[1024,128]{1,0:T(8,128)S(1)} %add.123), channel_id=1, source_target_pairs={{4,0},{6,2},{5,1},{7,3},{20,16},{22,18},{21,17},{23,19}} | collective-permute-start | bytes 1572872 | tf_op jit(solution)/shard_map/ppermute | solution.py:584
  339.2 15.2 %collective-permute-start.57 = (f32[1024,128]{1,0:T(8,128)S(1)}, f32[1024,128]{1,0:T(8,128)S(1)}, u32[]{:S(2)}, u32[]{:S(2)}) collective-permute-start(f32[1024,128]{1,0:T(8,128)S(1)} %fusion.1), channel_id=1, source_target_pairs={{8,4},{10,6},{9,5},{11,7},{24,20},{26,22},{25,21},{27,23}} | collective-permute-start | bytes 1572872 | tf_op jit(solution)/shard_map/ppermute | solution.py:584
  354.5 8.6 %collective-permute-start.60 = (f32[512,128]{1,0:T(8,128)S(1)}, f32[512,128]{1,0:T(8,128)S(1)}, u32[]{:S(2)}, u32[]{:S(2)}) collective-permute-start(f32[512,128]{1,0:T(8,128)S(1)} %get-tuple-element.264), channel_id=1, source_target_pairs={{17,1},{19,3},{21,5},{23,7},{25,9},{27,11},{29,13},{31,15}} | collective-permute-start | bytes 786440 | tf_op jit(solution)/shard_map/ppermute | solution.py:592
  355.2 8.9 %collective-permute-start.62 = (f32[512,128]{1,0:T(8,128)S(1)}, f32[512,128]{1,0:T(8,128)S(1)}, u32[]{:S(2)}, u32[]{:S(2)}) collective-permute-start(f32[512,128]{1,0:T(8,128)S(1)} %get-tuple-element.263), channel_id=1, source_target_pairs={{17,16},{19,18},{21,20},{23,22},{25,24},{27,26},{29,28},{31,30}} | collective-permute-start | bytes 786440 | tf_op jit(solution)/shard_map/ppermute | solution.py:592
  357.1 22.4 %collective-permute-start.58 = (f32[1024,128]{1,0:T(8,128)S(1)}, f32[1024,128]{1,0:T(8,128)S(1)}, u32[]{:S(2)}, u32[]{:S(2)}) collective-permute-start(f32[1024,128]{1,0:T(8,128)S(1)} %add_add_fusion), channel_id=1, source_target_pairs={{1,0},{3,2},{5,4},{7,6},{9,8},{11,10},{13,12},{15,14}} | collective-permute-start | bytes 1572872 | tf_op jit(solution)/shard_map/ppermute | solution.py:592
  357.8 21.7 %collective-permute-start.59 = (f32[1024,128]{1,0:T(8,128)S(1)}, f32[1024,128]{1,0:T(8,128)S(1)}, u32[]{:S(2)}, u32[]{:S(2)}) collective-permute-start(f32[1024,128]{1,0:T(8,128)S(1)} %add_add_fusion), channel_id=1, source_target_pairs={{16,0},{18,2},{20,4},{22,6},{24,8},{26,10},{28,12},{30,14}} | collective-permute-start | bytes 1572872 | tf_op jit(solution)/shard_map/ppermute | solution.py:592
  363.1 16.5 %collective-permute-start.61 = (f32[512,128]{1,0:T(8,128)S(1)}, f32[512,128]{1,0:T(8,128)S(1)}, u32[]{:S(2)}, u32[]{:S(2)}) collective-permute-start(f32[512,128]{1,0:T(8,128)S(1)} %collective-permute-done.60), channel_id=1, source_target_pairs={{1,0},{3,2},{5,4},{7,6},{9,8},{11,10},{13,12},{15,14}} | collective-permute-start | bytes 786440 | tf_op jit(solution)/shard_map/ppermute | solution.py:592
  364.0 15.5 %collective-permute-start.63 = (f32[512,128]{1,0:T(8,128)S(1)}, f32[512,128]{1,0:T(8,128)S(1)}, u32[]{:S(2)}, u32[]{:S(2)}) collective-permute-start(f32[512,128]{1,0:T(8,128)S(1)} %collective-permute-done.62), channel_id=1, source_target_pairs={{16,0},{18,2},{20,4},{22,6},{24,8},{26,10},{28,12},{30,14}} | collective-permute-start | bytes 786440 | tf_op jit(solution)/shard_map/ppermute | solution.py:592
  (28 other events, 424.6 us)
